TPU v7x, 32 devices: a whole 2x2x4 slice. The times are simulated.
32 devices in a mesh: groups: 2 (over y), tp: 4 (over z), seq: 4 (over x, core).
Axes of the slice: x: 2, y: 2, z: 4, core: 2. Of those that a mesh axis runs over, the one named last changes fastest.
Arguments:
- tokens_values: bfloat16 [1024, 8192], P(('groups', 'seq'), 'tp'), parts along dimension 0, may hold values from -1 to 1
- tokens_scales: float32 [1024, 64], P(('groups', 'seq'), 'tp'), parts along dimension 0, may hold values from 0.25 to 4
- gate_weight: bfloat16 [8192, 16384], P('seq', 'tp'), may hold values from -0.0625 to 0.0625
- up_weight: bfloat16 [8192, 16384], P('seq', 'tp'), may hold values from -0.0625 to 0.0625
- down_weight: bfloat16 [16384, 8192], P('tp', 'seq'), may hold values from -0.0625 to 0.0625
Outputs:
- mixed_values: bfloat16 [1024, 8192], P(('groups', 'seq'), 'tp'), parts along dimension 0
- mixed_scales: float32 [1024, 64], P(('groups', 'seq'), 'tp'), parts along dimension 0
There are 2 independent parts, one for each index of `groups`. A program takes and returns all parts, laid end to end along the dimension named above; an argument that names none is the same for every part. Nothing has to cross between parts.
All inputs are finite; a program needn't handle non-finite values.
Results may differ from a plain program's by a relative error of at most 0.02.
Values may be sent and summed in bfloat16 or wider, within the bound.
No kernel may reach another device: no remote copies, remote signals or barrier semaphores. Data moves between devices by JAX's collectives and lax.ppermute only.
A program may use at most 512 MiB of HBM per device.

v0:
```python
import functools

import jax
import jax.numpy as jnp
from jax import lax
from jax.experimental import pallas as pl
from jax.experimental.pallas import tpu as pltpu
from jax.sharding import PartitionSpec as P

ROWS = (48, 48, 32)
ORDER = (
    "far0", "load3", "load1", "sel0", "far1", "load2", "arr0", "sel1", "far2", "load0", "take0", "a0", "c0",
    "arr1", "b0", "sel2", "d0", "take1", "a1", "c1", "arr2", "hide0", "b1", "d1", "own0", "take2", "a2", "c2",
    "forward0", "b2", "d2", "hide1", "rest0", "out0", "hide2", "own1", "mix0", "forward1", "own2", "far_out0",
    "rest1", "forward2", "out1", "end0", "rest2", "out2", "mix1", "mix2", "far_out1", "far_out2", "end1",
    "end2",
)
TILE = 256
COST = 1 << 33
VMEM = 10 << 20


def blocks(array):
    return array.reshape(array.shape[0], array.shape[1] // 128, 128)


def block_scale(array):
    return jnp.max(jnp.abs(blocks(array)), axis=2) + 1e-06


def expand(values, scales):
    return (blocks(values.astype(jnp.float32)) * scales[:, :, None]).reshape(values.shape)


def scaled(total):
    scales = block_scale(total)
    values = (blocks(total) / scales[:, :, None]).reshape(total.shape).astype(jnp.bfloat16)
    return values, scales


def wide(array):
    return array.astype(jnp.float32)


def narrow(array):
    return array.astype(jnp.bfloat16)


def dot(a, b):
    return jnp.dot(a, b, preferred_element_type=jnp.float32)


def any_shards(tokens_values, tokens_scales, gate_weight, up_weight, down_weight):
    mine = narrow(expand(tokens_values, tokens_scales))
    mine = lax.all_gather(mine, "tp", axis=1, tiled=True)
    inputs = lax.all_to_all(mine, "seq", split_axis=1, concat_axis=0, tiled=True)
    gate = narrow(dot(inputs, gate_weight))
    up = narrow(dot(inputs, up_weight))
    gate = wide(lax.psum_scatter(gate, "seq", scatter_dimension=0, tiled=True))
    up = wide(lax.psum_scatter(up, "seq", scatter_dimension=0, tiled=True))
    hidden = narrow(jax.nn.silu(gate) * up)
    hidden = lax.all_gather(hidden, "seq", axis=0, tiled=True)
    partial_sum = narrow(dot(hidden, down_weight))
    partial_sum = lax.all_to_all(partial_sum, "seq", split_axis=0, concat_axis=1, tiled=True)
    return scaled(wide(lax.psum_scatter(partial_sum, "tp", scatter_dimension=1, tiled=True)))


def over_seq(array, bit):
    return lax.ppermute(array, "seq", [(i, i ^ bit) for i in range(4)])


def over_tp(array, bit):
    return lax.ppermute(array, "tp", [(i, i ^ bit) for i in range(4)])


def device(tp, seq):
    return tp * 4 + seq


FIRST_IN, SECOND, FIRST_OUT = [], [], []
for tp in range(4):
    for seq in range(4):
        if (tp ^ seq) & 1:
            FIRST_IN.append((device(tp, seq), device(tp, seq ^ 1)))
            SECOND.append((device(tp, seq), device(tp ^ 1, seq ^ 1)))
            FIRST_OUT.append((device(tp, seq), device(tp ^ 1, seq)))
        else:
            FIRST_IN.append((device(tp, seq), device(tp ^ 1, seq)))
            FIRST_OUT.append((device(tp, seq), device(tp, seq ^ 1)))


def over_both(array, pairs):
    return lax.ppermute(array, ("tp", "seq"), pairs)


def arrange(low_first, one, other):
    return jnp.concatenate([jnp.where(low_first, one, other), jnp.where(low_first, other, one)], axis=0)


def load_kernel(quarter, gate_weight, up_weight, out, done):
    width = out.shape[2]
    here = pl.ds(pl.multiple_of(quarter[0] * width, width), width)
    pieces = done.shape[1]
    rows = out.shape[1] // pieces
    copies = [
        pltpu.make_async_copy(weight.at[pl.ds(i * rows, rows), here], out.at[k, pl.ds(i * rows, rows)], done.at[k, i])
        for k, weight in enumerate((gate_weight, up_weight))
        for i in range(pieces)
    ]
    for copy in copies:
        copy.start()
    for copy in copies:
        copy.wait()


def load(gate_weight, up_weight, quarter):
    deep, width = gate_weight.shape
    far = pl.BlockSpec(memory_space=pl.ANY)
    return pl.pallas_call(
        load_kernel,
        out_shape=jax.ShapeDtypeStruct((2, deep, width // 4), gate_weight.dtype),
        in_specs=[pl.BlockSpec(memory_space=pltpu.SMEM), far, far],
        out_specs=far,
        scratch_shapes=[pltpu.SemaphoreType.DMA((2, 4))],
        cost_estimate=pl.CostEstimate(flops=COST, bytes_accessed=1, transcendentals=0),
    )(quarter.reshape(1).astype(jnp.int32), gate_weight, up_weight)


def sums_kernel(has_got, some, weights, *rest):
    out = rest[-1]

    @pl.loop(0, 2)
    def side(k):
        value = dot(some[...], weights[k])
        if has_got:
            value += wide(rest[0][k])
        out[k] = value.astype(out.dtype)


def sums(some, weights, got=None, kind=jnp.bfloat16):
    near = pl.BlockSpec(memory_space=pltpu.VMEM)
    return pl.pallas_call(
        functools.partial(sums_kernel, got is not None),
        out_shape=jax.ShapeDtypeStruct((2, some.shape[0], weights.shape[2]), kind),
        in_specs=[near] * (2 + (got is not None)),
        out_specs=near,
        compiler_params=pltpu.CompilerParams(vmem_limit_bytes=VMEM),
        cost_estimate=pl.CostEstimate(flops=COST, bytes_accessed=1, transcendentals=0),
    )(some, weights, *([] if got is None else [got]))


def products_kernel(has_total, quarters, one, two, weight, *rest):
    out, near, done = rest[-3:]
    deep, tile = near.shape[2], near.shape[3]
    pieces = one, two
    copies = [
        [
            pltpu.make_async_copy(
                weight.at[pl.ds(pl.multiple_of(quarters[k] * deep, deep), deep), pl.ds(j * tile, tile)],
                near.at[k, j],
                done.at[k, j],
            )
            for k in range(2)
        ]
        for j in range(near.shape[1])
    ]
    for pair in copies:
        for copy in pair:
            copy.start()
    for j, pair in enumerate(copies):
        here = pl.ds(j * tile, tile)
        for copy in pair:
            copy.wait()
        value = sum(dot(pieces[k][...], near[k, j]) for k in range(2))
        if has_total:
            value += rest[0][:, here]
        out[:, here] = value


def products(pieces, weight, quarters, total=None):
    rows, deep = pieces[0].shape
    tiles = weight.shape[1] // (2 * TILE)
    near = pl.BlockSpec(memory_space=pltpu.VMEM)
    return pl.pallas_call(
        functools.partial(products_kernel, total is not None),
        out_shape=jax.ShapeDtypeStruct((rows, weight.shape[1]), jnp.float32),
        in_specs=[pl.BlockSpec(memory_space=pltpu.SMEM), near, near, pl.BlockSpec(memory_space=pl.ANY)]
        + [near] * (total is not None),
        out_specs=near,
        scratch_shapes=[
            pltpu.VMEM((2, tiles, deep, 2 * TILE), weight.dtype),
            pltpu.SemaphoreType.DMA((2, tiles)),
        ],
        compiler_params=pltpu.CompilerParams(vmem_limit_bytes=VMEM),
        cost_estimate=pl.CostEstimate(flops=COST, bytes_accessed=1, transcendentals=0),
    )(jnp.stack(quarters).astype(jnp.int32), *pieces, weight, *([] if total is None else [total]))


def hide_kernel(held, got, out):
    rows = 32

    @pl.loop(0, out.shape[0] // rows)
    def strip(i):
        here = pl.ds(pl.multiple_of(i * rows, rows), rows)
        gate = held[0, here] + wide(got[0, here])
        up = held[1, here] + wide(got[1, here])
        out[here] = narrow(jax.nn.silu(gate) * up)


def hide(held, got):
    near = pl.BlockSpec(memory_space=pltpu.VMEM)
    return pl.pallas_call(
        hide_kernel,
        out_shape=jax.ShapeDtypeStruct(held.shape[1:], got.dtype),
        in_specs=[near] * 2,
        out_specs=near,
        compiler_params=pltpu.CompilerParams(vmem_limit_bytes=VMEM),
        cost_estimate=pl.CostEstimate(flops=COST, bytes_accessed=1, transcendentals=0),
    )(held, got)


def end_kernel(kept, got, values, scales):
    for j in range(scales.shape[1]):
        here = pl.ds(j * 128, 128)
        total = kept[:, here] + wide(got[:, here])
        scale = jnp.max(jnp.abs(total), axis=1, keepdims=True) + 1e-06
        values[:, here] = narrow(total / scale)
        scales[:, pl.ds(j, 1)] = scale


def end(kept, got):
    rows, width = kept.shape
    near = pl.BlockSpec(memory_space=pltpu.VMEM)
    return pl.pallas_call(
        end_kernel,
        out_shape=(
            jax.ShapeDtypeStruct((rows, width), got.dtype),
            jax.ShapeDtypeStruct((rows, width // 128), kept.dtype),
        ),
        in_specs=[near] * 2,
        out_specs=(near, near),
        compiler_params=pltpu.CompilerParams(vmem_limit_bytes=VMEM),
        cost_estimate=pl.CostEstimate(flops=COST, bytes_accessed=1, transcendentals=0),
    )(kept, got)


class Steps:

    def __init__(self, tokens_values, tokens_scales, gate_weight, up_weight, down_weight):
        tp, seq = lax.axis_index("tp"), lax.axis_index("seq")
        self.seq, self.x, self.core = seq, seq >> 1, seq & 1
        self.high, self.even = tp >> 1, (tp ^ seq) & 1 == 0
        self.gate_weight = pltpu.with_memory_space_constraint(gate_weight, pltpu.HBM)
        self.up_weight = pltpu.with_memory_space_constraint(up_weight, pltpu.HBM)
        self.down_weight = pltpu.with_memory_space_constraint(down_weight, pltpu.HBM)
        self.mine = narrow(expand(tokens_values, tokens_scales))
        unit = tokens_values.shape[0] // sum(ROWS)
        self.starts = [sum(ROWS[:i]) * unit for i in range(len(ROWS) + 1)]
        self.last = self.mine
        self.held = {}

    def run(self, order):
        for step in order:
            with jax.named_scope(step):
                getattr(self, step[:-1])(int(step[-1]))
        return tuple(
            jnp.concatenate([self.held["end", i][k] for i in range(len(ROWS))], axis=0) for k in range(2)
        )

    def now(self, array):
        return lax.optimization_barrier((array, self.last))[0]

    def far(self, i):
        part = self.now(self.mine[self.starts[i] : self.starts[i + 1]])
        self.held["far", i] = part, over_tp(part, 2)

    def sel(self, i):
        part, other = self.held["far", i]
        other = self.now(other)
        sent = jnp.where(self.high == self.x, other, part)
        kept = jnp.where(self.high == self.x, part, other)
        self.held["sel", i] = kept, over_seq(sent, 2)
        self.last = sent

    def arr(self, i):
        kept, got = self.held["sel", i]
        pair = arrange(self.x == 0, kept, self.now(got))
        self.held["arr", i] = pair, over_both(pair, FIRST_IN), over_both(pair, SECOND)
        self.last = pair

    def take(self, i):
        pair, first, second = self.held["arr", i]
        first = self.now(first)
        own = jnp.where(self.even, pair, first)
        others = jnp.where(self.even, first, second)
        self.held["take", i] = self.last = arrange(self.core == 0, own, others)

    def load(self, bits):
        gate_weight = self.now(self.gate_weight)
        self.held["load", bits] = self.last = load(gate_weight, self.up_weight, self.seq ^ bits)

    def part(self, i, bits, got=None, kind=jnp.bfloat16):
        some = self.now(self.held["take", i])
        self.last = sums(some, self.held["load", bits], got, kind)
        return self.last

    def a(self, i):
        self.held["a", i] = over_seq(self.part(i, 3), 1)

    def c(self, i):
        self.held["c", i] = over_seq(self.part(i, 1), 1)

    def b(self, i):
        self.held["b", i] = over_seq(self.part(i, 2, self.held["a", i]), 2)

    def d(self, i):
        self.held["d", i] = self.part(i, 0, self.held["c", i], jnp.float32)

    def hide(self, i):
        hidden = hide(self.held["d", i], self.now(self.held["b", i]))
        far = over_seq(hidden, 2)
        self.held["hide", i] = hidden, far, over_seq(hidden, 1)
        self.last = hidden

    def down(self, pieces, bits, total=None):
        return products(pieces, self.down_weight, [self.seq ^ bit for bit in bits], total)

    def own(self, i):
        hidden, far, near = self.held["hide", i]
        self.held["own", i] = self.last = self.down((self.now(hidden), near), (0, 1))

    def forward(self, i):
        far = self.now(self.held["hide", i][1])
        self.held["pass", i] = far, over_seq(far, 1)

    def rest(self, i):
        far, last = self.held["pass", i]
        self.held["rest", i] = self.last = self.down((self.now(far), last), (2, 3), self.held["own", i])

    def out(self, i):
        partial_sum = self.now(self.held["rest", i])
        half = partial_sum.shape[0] // 2
        low, top = partial_sum[:half], partial_sum[half:]
        own = jnp.where(self.core == 0, low, top)
        others = jnp.where(self.core == 0, top, low)
        one, two = narrow(jnp.where(self.even, others, own)), narrow(others)
        self.held["out", i] = own, over_both(one, FIRST_OUT), over_both(two, SECOND)
        self.last = one

    def mix(self, i):
        own, first, second = self.held["out", i]
        pair = wide(self.now(first)) + jnp.where(self.even, own, wide(second))
        rows = pair.shape[0] // 2
        low, top = pair[:rows], pair[rows:]
        kept = jnp.where(self.x == 0, low, top)
        sent = narrow(jnp.where(self.x == 0, top, low))
        self.held["mix", i] = kept, over_seq(sent, 2)
        self.last = sent

    def far_out(self, i):
        kept, got = self.held["mix", i]
        got = self.now(got)
        sent = jnp.where(self.high == self.x, got, narrow(kept))
        kept = jnp.where(self.high == self.x, kept, wide(got))
        self.held["far_out", i] = kept, over_tp(sent, 2)
        self.last = sent

    def end(self, i):
        kept, got = self.held["far_out", i]
        self.held["end", i] = end(kept, self.now(got))
        self.last = self.held["end", i][0]


def four_shards(*arrays):
    return Steps(*arrays).run(ORDER)


def solution(mesh):
    placed = (
        P(("groups", "seq"), "tp"),
        P(("groups", "seq"), "tp"),
        P("seq", "tp"),
        P("seq", "tp"),
        P("tp", "seq"),
    )
    fours = mesh.shape["tp"] == 4 and mesh.shape["seq"] == 4
    return jax.shard_map(
        four_shards if fours else any_shards,
        mesh=mesh,
        in_specs=placed,
        out_specs=(P(("groups", "seq"), "tp"), P(("groups", "seq"), "tp")),
        check_vma=False,
    )
```

profile of v0, /device:TPU:1, one launch (start us, length us, event | category | flops | bytes accessed | tf_op | source)
XLA Modules:
  0.0 1184.8 jit_solution(18227350839805401036)
XLA Ops:
  3.2 3.2 collective-permute-start
  6.4 255.3 %load3.1.weights = bf16[2,2048,1024]{2,1,0:T(8,128)(2,1)} custom-call(s32[1]{0:T(128)} %bitcast.1.quarter, bf16[2048,4096]{1,0:T(8,128)(2,1)} %gate_weight.3, bf16[2048,4096]{1,0:T(8,128)(2,1)} %up_weight.7), custom_call_target="tpu_custom_call" | custom-call | flops 8589934592 | bytes 1 | tf_op jit(solution)/shard_map/load3/pallas_call | solution.py:119
  261.7 255.3 %load1.1.weights = bf16[2,2048,1024]{2,1,0:T(8,128)(2,1)} custom-call(s32[1]{0:T(128)} %bitcast.2.quarter, bf16[2048,4096]{1,0:T(8,128)(2,1)} %gate_weight.3, bf16[2048,4096]{1,0:T(8,128)(2,1)} %up_weight.7), custom_call_target="tpu_custom_call" | custom-call | flops 8589934592 | bytes 1 | tf_op jit(solution)/shard_map/load1/pallas_call | solution.py:119
  518.5 255.3 %load2.1.weights = bf16[2,2048,1024]{2,1,0:T(8,128)(2,1)} custom-call(s32[1]{0:T(128)} %bitcast.quarter, bf16[2048,4096]{1,0:T(8,128)(2,1)} %gate_weight.3, bf16[2048,4096]{1,0:T(8,128)(2,1)} %up_weight.7), custom_call_target="tpu_custom_call" | custom-call | flops 8589934592 | bytes 1 | tf_op jit(solution)/shard_map/load2/pallas_call | solution.py:119
  775.6 3.1 collective-permute-start.4
  778.7 6.1 collective-permute-done.3
  785.1 255.3 %load0.1.weights = bf16[2,2048,1024]{2,1,0:T(8,128)(2,1)} custom-call(s32[1]{0:T(128)} %bitcast.3.quarter, bf16[2048,4096]{1,0:T(8,128)(2,1)} %gate_weight.3, bf16[2048,4096]{1,0:T(8,128)(2,1)} %up_weight.7), custom_call_target="tpu_custom_call" | custom-call | flops 8589934592 | bytes 1 | tf_op jit(solution)/shard_map/load0/pallas_call | solution.py:119
  1040.8 3.4 copy-done
  1044.2 2.0 a0.1
  1048.2 3.4 copy-done.1
  1051.6 2.0 c0.1
  1054.3 3.6 collective-permute-start.12
  1058.0 2.0 b0.1
  1061.6 2.0 d0.1.held
  1065.5 2.0 a1.1
  1068.7 2.0 c1.1
  1071.4 4.6 collective-permute-start.18
  1075.9 5.6 collective-permute-done.9.got
  1082.0 2.0 b1.1
  1085.5 2.0 d1.1.held
  1087.5 4.7 own0.1.rest_0_
  1096.5 14.6 %collective-permute-done.13.one = bf16[192,1024]{1,0:T(8,128)(2,1)S(1)} collective-permute-done((bf16[192,1024]{1,0:T(8,128)(2,1)S(1)}, bf16[192,1024]{1,0:T(8,128)(2,1)S(1)}, u32[]{:S(2)}, u32[]{:S(2)}) %collective-permute-start.13) | collective-permute-done | bytes 393248 | tf_op jit(solution)/shard_map/hide0/ppermute | solution.py:69
  1117.6 4.7 rest0.1
  1122.4 4.2 collective-permute-start.26
  1128.9 4.7 own1.1.rest_0_
  1136.7 4.5 own2.1.rest_0_
  1142.7 4.7 rest1.1
  1150.1 2.3 collective-permute-start.35
  1153.1 4.5 rest2.1
  1157.8 4.0 collective-permute-start.38
  1164.5 2.2 collective-permute-done.38
  1172.1 9.2 collective-permute-done.39.got
  (146 shorter events, 49.0 us)
Async XLA Ops:
  3.2 514.0 %collective-permute-start = (bf16[48,2048]{1,0:T(8,128)(2,1)S(1)}, bf16[48,2048]{1,0:T(8,128)(2,1)S(1)}, u32[]{:S(2)}, u32[]{:S(2)}) collective-permute-start(bf16[48,2048]{1,0:T(8,128)(2,1)S(1)} %get-tuple-element.58), channel_id=1, source_target_pairs={{0,8},{4,12},{8,0},{12,4},{1,9},{5,13},{9,1},{13,5},{2,10},{6,14},... | collective-permute-start | bytes 589832 | tf_op jit(solution)/shard_map/far0/ppermute | solution.py:73
  517.2 256.7 %collective-permute-start.1 = (bf16[48,2048]{1,0:T(8,128)(2,1)S(1)}, bf16[48,2048]{1,0:T(8,128)(2,1)S(1)}, u32[]{:S(2)}, u32[]{:S(2)}) collective-permute-start(bf16[48,2048]{1,0:T(8,128)(2,1)S(1)} %broadcast_select_fusion.18), channel_id=1, source_target_pairs={{0,2},{1,3},{2,0},{3,1},{4,6},{5,7},{6,4},{7,5},{8,10},{9,11},{10,... | collective-permute-start | bytes 589832 | tf_op jit(solution)/shard_map/sel0/ppermute | solution.py:69
  773.8 11.0 collective-permute-start.3
  774.0 266.5 %collective-permute-start.2 = (bf16[96,2048]{1,0:T(8,128)(2,1)S(1)}, bf16[96,2048]{1,0:T(8,128)(2,1)S(1)}, u32[]{:S(2)}, u32[]{:S(2)}) collective-permute-start(bf16[96,2048]{1,0:T(8,128)(2,1)S(1)} %pad_maximum_fusion.4), channel_id=1, source_target_pairs={{0,4},{1,0},{2,6},{3,2},{4,5},{5,1},{6,7},{7,3},{8,12},{9,8},{10,1... | collective-permute-start | bytes 1179656 | tf_op jit(solution)/shard_map/arr0/ppermute | solution.py:93
  775.6 265.0 %collective-permute-start.4 = (bf16[96,2048]{1,0:T(8,128)(2,1)S(1)}, bf16[96,2048]{1,0:T(8,128)(2,1)S(1)}, u32[]{:S(2)}, u32[]{:S(2)}) collective-permute-start(bf16[96,2048]{1,0:T(8,128)(2,1)S(1)} %pad_maximum_fusion.4), channel_id=1, source_target_pairs={{1,4},{3,6},{4,1},{6,3},{9,12},{11,14},{12,9},{14,11},{17,20},{19,... | collective-permute-start | bytes 1179656 | tf_op jit(solution)/shard_map/arr0/ppermute | solution.py:93
  784.8 269.0 %collective-permute-start.6 = (bf16[48,2048]{1,0:T(8,128)(2,1)S(1)}, bf16[48,2048]{1,0:T(8,128)(2,1)S(1)}, u32[]{:S(2)}, u32[]{:S(2)}) collective-permute-start(bf16[48,2048]{1,0:T(8,128)(2,1)S(1)} %broadcast_select_fusion.17), channel_id=1, source_target_pairs={{0,2},{1,3},{2,0},{3,1},{4,6},{5,7},{6,4},{7,5},{8,10},{9,11},{10,... | collective-permute-start | bytes 589832 | tf_op jit(solution)/shard_map/sel1/ppermute | solution.py:69
  1040.4 19.6 %collective-permute-start.5 = (bf16[32,2048]{1,0:T(8,128)(2,1)S(1)}, bf16[32,2048]{1,0:T(8,128)(2,1)S(1)}, u32[]{:S(2)}, u32[]{:S(2)}) collective-permute-start(bf16[32,2048]{1,0:T(8,128)(2,1)S(1)} %slice.62), channel_id=1, source_target_pairs={{0,8},{4,12},{8,0},{12,4},{1,9},{5,13},{9,1},{13,5},{2,10},{6,14},... | collective-permute-start | bytes 393224 | tf_op jit(solution)/shard_map/far2/ppermute | solution.py:73
  1046.2 11.7 collective-permute-start.7
  1053.9 9.7 collective-permute-start.11
  1054.3 10.8 collective-permute-start.12
  1060.1 10.7 collective-permute-start.10
  1061.4 20.2 %collective-permute-start.9 = (bf16[2,192,1024]{2,1,0:T(8,128)(2,1)S(1)}, bf16[2,192,1024]{2,1,0:T(8,128)(2,1)S(1)}, u32[]{:S(2)}, u32[]{:S(2)}) collective-permute-start(bf16[2,192,1024]{2,1,0:T(8,128)(2,1)S(1)} %b0.1), channel_id=1, source_target_pairs={{0,2},{1,3},{2,0},{3,1},{4,6},{5,7},{6,4},{7,5},{8,10},{9,11},{10,... | collective-permute-start | bytes 2359304 | tf_op jit(solution)/shard_map/b0/ppermute | solution.py:69
  1067.5 14.5 %collective-permute-start.15 = (bf16[2,192,1024]{2,1,0:T(8,128)(2,1)S(1)}, bf16[2,192,1024]{2,1,0:T(8,128)(2,1)S(1)}, u32[]{:S(2)}, u32[]{:S(2)}) collective-permute-start(bf16[2,192,1024]{2,1,0:T(8,128)(2,1)S(1)} %a1.1), channel_id=1, source_target_pairs={{0,1},{1,0},{2,3},{3,2},{4,5},{5,4},{6,7},{7,6},{8,9},{9,8},{10,11... | collective-permute-start | bytes 2359304 | tf_op jit(solution)/shard_map/a1/ppermute | solution.py:69
  1070.7 14.7 %collective-permute-start.16 = (bf16[2,192,1024]{2,1,0:T(8,128)(2,1)S(1)}, bf16[2,192,1024]{2,1,0:T(8,128)(2,1)S(1)}, u32[]{:S(2)}, u32[]{:S(2)}) collective-permute-start(bf16[2,192,1024]{2,1,0:T(8,128)(2,1)S(1)} %c1.1), channel_id=1, source_target_pairs={{0,1},{1,0},{2,3},{3,2},{4,5},{5,4},{6,7},{7,6},{8,9},{9,8},{10,11... | collective-permute-start | bytes 2359304 | tf_op jit(solution)/shard_map/c1/ppermute | solution.py:69
  1070.8 21.4 %collective-permute-start.14 = (bf16[64,2048]{1,0:T(8,128)(2,1)S(1)}, bf16[64,2048]{1,0:T(8,128)(2,1)S(1)}, u32[]{:S(2)}, u32[]{:S(2)}) collective-permute-start(bf16[64,2048]{1,0:T(8,128)(2,1)S(1)} %pad_maximum_fusion.6), channel_id=1, source_target_pairs={{0,4},{1,0},{2,6},{3,2},{4,5},{5,1},{6,7},{7,3},{8,12},{9,8},{10,1... | collective-permute-start | bytes 786440 | tf_op jit(solution)/shard_map/arr2/ppermute | solution.py:93
  1071.4 20.8 %collective-permute-start.18 = (bf16[64,2048]{1,0:T(8,128)(2,1)S(1)}, bf16[64,2048]{1,0:T(8,128)(2,1)S(1)}, u32[]{:S(2)}, u32[]{:S(2)}) collective-permute-start(bf16[64,2048]{1,0:T(8,128)(2,1)S(1)} %pad_maximum_fusion.6), channel_id=1, source_target_pairs={{1,4},{3,6},{4,1},{6,3},{9,12},{11,14},{12,9},{14,11},{17,20},{19,... | collective-permute-start | bytes 786440 | tf_op jit(solution)/shard_map/arr2/ppermute | solution.py:93
  1084.0 32.7 %collective-permute-start.19 = (bf16[2,192,1024]{2,1,0:T(8,128)(2,1)S(1)}, bf16[2,192,1024]{2,1,0:T(8,128)(2,1)S(1)}, u32[]{:S(2)}, u32[]{:S(2)}) collective-permute-start(bf16[2,192,1024]{2,1,0:T(8,128)(2,1)S(1)} %b1.1), channel_id=1, source_target_pairs={{0,2},{1,3},{2,0},{3,1},{4,6},{5,7},{6,4},{7,5},{8,10},{9,11},{10,... | collective-permute-start | bytes 2359304 | tf_op jit(solution)/shard_map/b1/ppermute | solution.py:69
  1085.3 25.8 %collective-permute-start.13 = (bf16[192,1024]{1,0:T(8,128)(2,1)S(1)}, bf16[192,1024]{1,0:T(8,128)(2,1)S(1)}, u32[]{:S(2)}, u32[]{:S(2)}) collective-permute-start(bf16[192,1024]{1,0:T(8,128)(2,1)S(1)} %hide0.1.one), channel_id=1, source_target_pairs={{0,2},{1,3},{2,0},{3,1},{4,6},{5,7},{6,4},{7,5},{8,10},{9,11},{10,... | collective-permute-start | bytes 1179656 | tf_op jit(solution)/shard_map/hide0/ppermute | solution.py:69
  1093.9 18.6 %collective-permute-start.20 = (bf16[2,128,1024]{2,1,0:T(8,128)(2,1)S(1)}, bf16[2,128,1024]{2,1,0:T(8,128)(2,1)S(1)}, u32[]{:S(2)}, u32[]{:S(2)}) collective-permute-start(bf16[2,128,1024]{2,1,0:T(8,128)(2,1)S(1)} %a2.1), channel_id=1, source_target_pairs={{0,1},{1,0},{2,3},{3,2},{4,5},{5,4},{6,7},{7,6},{8,9},{9,8},{10,11... | collective-permute-start | bytes 1572872 | tf_op jit(solution)/shard_map/a2/ppermute | solution.py:69
  1096.4 18.8 %collective-permute-start.21 = (bf16[2,128,1024]{2,1,0:T(8,128)(2,1)S(1)}, bf16[2,128,1024]{2,1,0:T(8,128)(2,1)S(1)}, u32[]{:S(2)}, u32[]{:S(2)}) collective-permute-start(bf16[2,128,1024]{2,1,0:T(8,128)(2,1)S(1)} %c2.1), channel_id=1, source_target_pairs={{0,1},{1,0},{2,3},{3,2},{4,5},{5,4},{6,7},{7,6},{8,9},{9,8},{10,11... | collective-permute-start | bytes 1572872 | tf_op jit(solution)/shard_map/c2/ppermute | solution.py:69
  1113.9 13.6 %collective-permute-start.24 = (bf16[2,128,1024]{2,1,0:T(8,128)(2,1)S(1)}, bf16[2,128,1024]{2,1,0:T(8,128)(2,1)S(1)}, u32[]{:S(2)}, u32[]{:S(2)}) collective-permute-start(bf16[2,128,1024]{2,1,0:T(8,128)(2,1)S(1)} %b2.1), channel_id=1, source_target_pairs={{0,2},{1,3},{2,0},{3,1},{4,6},{5,7},{6,4},{7,5},{8,10},{9,11},{10,... | collective-permute-start | bytes 1572872 | tf_op jit(solution)/shard_map/b2/ppermute | solution.py:69
  1117.0 11.9 %collective-permute-start.25 = (bf16[192,1024]{1,0:T(8,128)(2,1)S(1)}, bf16[192,1024]{1,0:T(8,128)(2,1)S(1)}, u32[]{:S(2)}, u32[]{:S(2)}) collective-permute-start(bf16[192,1024]{1,0:T(8,128)(2,1)S(1)} %hide1.1.one), channel_id=1, source_target_pairs={{0,1},{1,0},{2,3},{3,2},{4,5},{5,4},{6,7},{7,6},{8,9},{9,8},{10,11... | collective-permute-start | bytes 1179656 | tf_op jit(solution)/shard_map/hide1/ppermute | solution.py:69
  1117.4 18.9 %collective-permute-start.30 = (bf16[192,1024]{1,0:T(8,128)(2,1)S(1)}, bf16[192,1024]{1,0:T(8,128)(2,1)S(1)}, u32[]{:S(2)}, u32[]{:S(2)}) collective-permute-start(bf16[192,1024]{1,0:T(8,128)(2,1)S(1)} %hide1.1.one), channel_id=1, source_target_pairs={{0,2},{1,3},{2,0},{3,1},{4,6},{5,7},{6,4},{7,5},{8,10},{9,11},{10,... | collective-permute-start | bytes 1179656 | tf_op jit(solution)/shard_map/hide1/ppermute | solution.py:69
  1122.3 11.3 collective-permute-start.23
  1122.4 12.1 %collective-permute-start.26 = (bf16[96,2048]{1,0:T(8,128)(2,1)S(1)}, bf16[96,2048]{1,0:T(8,128)(2,1)S(1)}, u32[]{:S(2)}, u32[]{:S(2)}) collective-permute-start(bf16[96,2048]{1,0:T(8,128)(2,1)S(1)} %get-tuple-element.118), channel_id=1, source_target_pairs={{1,4},{3,6},{4,1},{6,3},{9,12},{11,14},{12,9},{14,11},{17,20},{19,... | collective-permute-start | bytes 1179656 | tf_op jit(solution)/shard_map/out0/ppermute | solution.py:93
  1127.7 9.0 collective-permute-start.28
  1136.1 12.3 %collective-permute-start.33 = (bf16[128,1024]{1,0:T(8,128)(2,1)S(1)}, bf16[128,1024]{1,0:T(8,128)(2,1)S(1)}, u32[]{:S(2)}, u32[]{:S(2)}) collective-permute-start(bf16[128,1024]{1,0:T(8,128)(2,1)S(1)} %hide2.1.one), channel_id=1, source_target_pairs={{0,2},{1,3},{2,0},{3,1},{4,6},{5,7},{6,4},{7,5},{8,10},{9,11},{10,... | collective-permute-start | bytes 786440 | tf_op jit(solution)/shard_map/hide2/ppermute | solution.py:69
  1141.6 11.2 collective-permute-start.29
  1148.4 13.4 %collective-permute-start.32 = (bf16[96,2048]{1,0:T(8,128)(2,1)}, bf16[96,2048]{1,0:T(8,128)(2,1)}, u32[]{:S(2)}, u32[]{:S(2)}) collective-permute-start(bf16[96,2048]{1,0:T(8,128)(2,1)} %get-tuple-element.117), channel_id=1, source_target_pairs={{0,1},{1,5},{2,3},{3,7},{4,0},{5,4},{6,2},{7,6},{8,9},{9,13},{10,1... | collective-permute-start | bytes 1179656 | tf_op jit(solution)/shard_map/out1/ppermute | solution.py:93
  1150.1 11.7 collective-permute-start.35
  1168.4 12.8 %collective-permute-start.39 = (bf16[48,2048]{1,0:T(8,128)(2,1)S(1)}, bf16[48,2048]{1,0:T(8,128)(2,1)S(1)}, u32[]{:S(2)}, u32[]{:S(2)}) collective-permute-start(bf16[48,2048]{1,0:T(8,128)(2,1)S(1)} %convert_select_fusion.3), channel_id=1, source_target_pairs={{0,8},{4,12},{8,0},{12,4},{1,9},{5,13},{9,1},{13,5},{2,10},{6,14},... | collective-permute-start | bytes 589832 | tf_op jit(solution)/shard_map/far_out1/ppermute | solution.py:73
  1171.1 11.8 collective-permute-start.41
  (20 other events, 127.5 us)
where the time goes:
time: 1190 us; the launch traced here: 1180 us
  Pallas kernels  1070 us (90%)
  starting transfers between devices  50 us (4%)
  waiting for transfers between devices  45.1 us (4%)
    pallas_call x4, Pallas kernels, load(): pl.pallas_call(load_kernel, out_shape=jax.ShapeDtypeStruct((2, deep, widt...  1020 us
    pallas_call x6, Pallas kernels, products(): pl.pallas_call(functools.partial(products_kernel, total is not None), out...  27.7 us
    ppermute x12, starting transfers between devices, over_both(): return lax.ppermute(array, ('tp', 'seq'), pairs)  26.2 us
  transfers between devices with their start and end apart: 42, of which 12 were waited for; matrix products, arithmetic and copies ran while one was open for 0% of the time, Pallas kernels for 90%

commit v1 on v0

--- a/solution.py
+++ b/solution.py
@@ -7,13 +7,13 @@
 from jax.experimental.pallas import tpu as pltpu
 from jax.sharding import PartitionSpec as P
 
-ROWS = (48, 48, 32)
+ROWS = (48, 32, 48)
 ORDER = (
     "far0", "load3", "load1", "sel0", "far1", "load2", "arr0", "sel1", "far2", "load0", "take0", "a0", "c0",
-    "arr1", "b0", "sel2", "d0", "take1", "a1", "c1", "arr2", "hide0", "b1", "d1", "own0", "take2", "a2", "c2",
-    "forward0", "b2", "d2", "hide1", "rest0", "out0", "hide2", "own1", "mix0", "forward1", "own2", "far_out0",
-    "rest1", "forward2", "out1", "end0", "rest2", "out2", "mix1", "mix2", "far_out1", "far_out2", "end1",
-    "end2",
+    "arr1", "b0", "d0", "sel2", "take1", "a1", "c1", "b1", "arr2", "hide0", "d1", "take2", "a2", "c2", "b2",
+    "own0", "d2", "hide1", "forward0", "hide2", "rest0", "out0", "own1", "mix0", "forward1", "own2",
+    "far_out0", "rest1", "forward2", "out1", "end0", "rest2", "out2", "mix1", "mix2", "far_out1", "far_out2",
+    "end1", "end2",
 )
 TILE = 256
 COST = 1 << 33
@@ -120,30 +120,36 @@
         load_kernel,
         out_shape=jax.ShapeDtypeStruct((2, deep, width // 4), gate_weight.dtype),
         in_specs=[pl.BlockSpec(memory_space=pltpu.SMEM), far, far],
-        out_specs=far,
+        out_specs=pl.BlockSpec(memory_space=pltpu.VMEM),
         scratch_shapes=[pltpu.SemaphoreType.DMA((2, 4))],
+        compiler_params=pltpu.CompilerParams(vmem_limit_bytes=VMEM),
         cost_estimate=pl.CostEstimate(flops=COST, bytes_accessed=1, transcendentals=0),
     )(quarter.reshape(1).astype(jnp.int32), gate_weight, up_weight)
 
 
-def sums_kernel(has_got, some, weights, *rest):
-    out = rest[-1]
-
-    @pl.loop(0, 2)
-    def side(k):
-        value = dot(some[...], weights[k])
-        if has_got:
-            value += wide(rest[0][k])
-        out[k] = value.astype(out.dtype)
-
-
-def sums(some, weights, got=None, kind=jnp.bfloat16):
+def sums_kernel(has_got, split, some, weights, *rest):
+    def value(k):
+        product = dot(some[...], weights[k])
+        return product + wide(rest[0][k]) if has_got else product
+
+    if split:
+        for k, out in enumerate(rest[-2:]):
+            out[...] = value(k).astype(out.dtype)
+    else:
+
+        @pl.loop(0, 2)
+        def side(k):
+            rest[-1][k] = value(k).astype(rest[-1].dtype)
+
+
+def sums(some, weights, got=None, kind=jnp.bfloat16, split=False):
     near = pl.BlockSpec(memory_space=pltpu.VMEM)
+    shape = some.shape[0], weights.shape[2]
     return pl.pallas_call(
-        functools.partial(sums_kernel, got is not None),
-        out_shape=jax.ShapeDtypeStruct((2, some.shape[0], weights.shape[2]), kind),
+        functools.partial(sums_kernel, got is not None, split),
+        out_shape=(jax.ShapeDtypeStruct(shape, kind),) * 2 if split else jax.ShapeDtypeStruct((2,) + shape, kind),
         in_specs=[near] * (2 + (got is not None)),
-        out_specs=near,
+        out_specs=(near, near) if split else near,
         compiler_params=pltpu.CompilerParams(vmem_limit_bytes=VMEM),
         cost_estimate=pl.CostEstimate(flops=COST, bytes_accessed=1, transcendentals=0),
     )(some, weights, *([] if got is None else [got]))
@@ -196,27 +202,27 @@
     )(jnp.stack(quarters).astype(jnp.int32), *pieces, weight, *([] if total is None else [total]))
 
 
-def hide_kernel(held, got, out):
+def hide_kernel(held, got_gate, got_up, out):
     rows = 32
 
     @pl.loop(0, out.shape[0] // rows)
     def strip(i):
         here = pl.ds(pl.multiple_of(i * rows, rows), rows)
-        gate = held[0, here] + wide(got[0, here])
-        up = held[1, here] + wide(got[1, here])
+        gate = held[0, here] + wide(got_gate[here])
+        up = held[1, here] + wide(got_up[here])
         out[here] = narrow(jax.nn.silu(gate) * up)
 
 
-def hide(held, got):
+def hide(held, got_gate, got_up):
     near = pl.BlockSpec(memory_space=pltpu.VMEM)
     return pl.pallas_call(
         hide_kernel,
-        out_shape=jax.ShapeDtypeStruct(held.shape[1:], got.dtype),
-        in_specs=[near] * 2,
+        out_shape=jax.ShapeDtypeStruct(held.shape[1:], got_up.dtype),
+        in_specs=[near] * 3,
         out_specs=near,
         compiler_params=pltpu.CompilerParams(vmem_limit_bytes=VMEM),
         cost_estimate=pl.CostEstimate(flops=COST, bytes_accessed=1, transcendentals=0),
-    )(held, got)
+    )(held, got_gate, got_up)
 
 
 def end_kernel(kept, got, values, scales):
@@ -299,10 +305,11 @@
         gate_weight = self.now(self.gate_weight)
         self.held["load", bits] = self.last = load(gate_weight, self.up_weight, self.seq ^ bits)
 
-    def part(self, i, bits, got=None, kind=jnp.bfloat16):
+    def part(self, i, bits, got=None, kind=jnp.bfloat16, split=False):
         some = self.now(self.held["take", i])
-        self.last = sums(some, self.held["load", bits], got, kind)
-        return self.last
+        result = sums(some, self.held["load", bits], got, kind, split)
+        self.last = result[0] if split else result
+        return result
 
     def a(self, i):
         self.held["a", i] = over_seq(self.part(i, 3), 1)
@@ -311,13 +318,14 @@
         self.held["c", i] = over_seq(self.part(i, 1), 1)
 
     def b(self, i):
-        self.held["b", i] = over_seq(self.part(i, 2, self.held["a", i]), 2)
+        both = self.part(i, 2, self.held["a", i], split=True)
+        self.held["b", i] = over_seq(both[0], 2), over_seq(both[1], 2)
 
     def d(self, i):
         self.held["d", i] = self.part(i, 0, self.held["c", i], jnp.float32)
 
     def hide(self, i):
-        hidden = hide(self.held["d", i], self.now(self.held["b", i]))
+        hidden = hide(self.held["d", i], *(self.now(got) for got in self.held["b", i]))
         far = over_seq(hidden, 2)
         self.held["hide", i] = hidden, far, over_seq(hidden, 1)
         self.last = hidden

time: 1190 us -> 191 us (0.16)
  Pallas kernels: 1070 us -> 64.2 us
  waiting for transfers between devices: 45.1 us -> 58.4 us
    pallas_call x4, Pallas kernels: 1020 us -> 14 us  [load(): pl.pallas_call(load_kernel, out_shape=jax.ShapeDtypeStruct((2, deep, widt...]
    ppermute x12, waiting for transfers between devices: 4.62 us -> 27.9 us  [over_both(): return lax.ppermute(array, ('tp', 'seq'), pairs)]
  transfers between devices with their start and end apart: 42 -> 45, of which waited for: 12 -> 17; matrix products, arithmetic and copies ran while one was open for 0% -> 1% of each run, Pallas kernels for 90% -> 34%
where the time goes in v1:
time: 191 us
  Pallas kernels  64.2 us (34%)
  starting transfers between devices  58.9 us (31%)
  waiting for transfers between devices  58.4 us (31%)
  other arithmetic  5.11 us (3%)
  local copies, waits for them, and re-layouts  2.78 us (1%)
    ppermute x12, waiting for transfers between devices, over_both(): return lax.ppermute(array, ('tp', 'seq'), pairs)  27.9 us
    pallas_call x6, Pallas kernels, products(): pl.pallas_call(functools.partial(products_kernel, total is not None), out...  27.7 us
    ppermute x12, starting transfers between devices, over_both(): return lax.ppermute(array, ('tp', 'seq'), pairs)  22.5 us
    ppermute x27, waiting for transfers between devices, over_seq(): return lax.ppermute(array, 'seq', [(i, i ^ bit) for i in range(4)])  21.8 us
    pallas_call x12, Pallas kernels, sums(): pl.pallas_call(functools.partial(sums_kernel, got is not None, split), ou...  21.2 us
    ppermute x27, starting transfers between devices, over_seq(): return lax.ppermute(array, 'seq', [(i, i ^ bit) for i in range(4)])  20.8 us
    ppermute x6, starting transfers between devices, over_tp(): return lax.ppermute(array, 'tp', [(i, i ^ bit) for i in range(4)])  15.6 us
    pallas_call x4, Pallas kernels, load(): pl.pallas_call(load_kernel, out_shape=jax.ShapeDtypeStruct((2, deep, widt...  14 us
  transfers between devices with their start and end apart: 45, of which 17 were waited for; matrix products, arithmetic and copies ran while one was open for 1% of the time, Pallas kernels for 34%

profile of v1, /device:TPU:1, one launch (start us, length us, event | category | flops | bytes accessed | tf_op | source)
XLA Modules:
  0.0 190.7 jit_solution(5059403373894051257)
XLA Ops:
  3.2 3.2 %collective-permute-start = (bf16[48,2048]{1,0:T(8,128)(2,1)S(1)}, bf16[48,2048]{1,0:T(8,128)(2,1)S(1)}, u32[]{:S(2)}, u32[]{:S(2)}) collective-permute-start(bf16[48,2048]{1,0:T(8,128)(2,1)S(1)} %get-tuple-element.67), channel_id=1, source_target_pairs={{0,8},{4,12},{8,0},{12,4},{1,9},{5,13},{9,1},{13,5},{2,10},{6,14},... | collective-permute-start | bytes 589832 | tf_op jit(solution)/shard_map/far0/ppermute | solution.py:73
  6.4 3.5 %load3.1.weights = bf16[2,2048,1024]{2,1,0:T(8,128)(2,1)S(1)} custom-call(s32[1]{0:T(128)} %bitcast.1.quarter, bf16[2048,4096]{1,0:T(8,128)(2,1)} %gate_weight.3, bf16[2048,4096]{1,0:T(8,128)(2,1)} %up_weight.7), custom_call_target="tpu_custom_call" | custom-call | flops 8589934592 | bytes 1 | tf_op jit(solution)/shard_map/load3/pallas_call | solution.py:119
  9.9 3.5 %load1.1.weights = bf16[2,2048,1024]{2,1,0:T(8,128)(2,1)S(1)} custom-call(s32[1]{0:T(128)} %bitcast.2.quarter, bf16[2048,4096]{1,0:T(8,128)(2,1)} %gate_weight.3, bf16[2048,4096]{1,0:T(8,128)(2,1)} %up_weight.7), custom_call_target="tpu_custom_call" | custom-call | flops 8589934592 | bytes 1 | tf_op jit(solution)/shard_map/load1/pallas_call | solution.py:119
  16.3 3.5 %load2.1.weights = bf16[2,2048,1024]{2,1,0:T(8,128)(2,1)S(1)} custom-call(s32[1]{0:T(128)} %bitcast.quarter, bf16[2048,4096]{1,0:T(8,128)(2,1)} %gate_weight.3, bf16[2048,4096]{1,0:T(8,128)(2,1)} %up_weight.7), custom_call_target="tpu_custom_call" | custom-call | flops 8589934592 | bytes 1 | tf_op jit(solution)/shard_map/load2/pallas_call | solution.py:119
  21.6 6.3 %collective-permute-start.4 = (bf16[96,2048]{1,0:T(8,128)(2,1)S(1)}, bf16[96,2048]{1,0:T(8,128)(2,1)S(1)}, u32[]{:S(2)}, u32[]{:S(2)}) collective-permute-start(bf16[96,2048]{1,0:T(8,128)(2,1)S(1)} %pad_maximum_fusion.4), channel_id=1, source_target_pairs={{1,4},{3,6},{4,1},{6,3},{9,12},{11,14},{12,9},{14,11},{17,20},{19,... | collective-permute-start | bytes 1179656 | tf_op jit(solution)/shard_map/arr0/ppermute | solution.py:93
  28.0 2.5 %collective-permute-start.9 = (bf16[48,2048]{1,0:T(8,128)(2,1)S(1)}, bf16[48,2048]{1,0:T(8,128)(2,1)S(1)}, u32[]{:S(2)}, u32[]{:S(2)}) collective-permute-start(bf16[48,2048]{1,0:T(8,128)(2,1)S(1)} %get-tuple-element.83), channel_id=1, source_target_pairs={{0,8},{4,12},{8,0},{12,4},{1,9},{5,13},{9,1},{13,5},{2,10},{6,14},... | collective-permute-start | bytes 589832 | tf_op jit(solution)/shard_map/far2/ppermute | solution.py:73
  30.5 3.5 %load0.1.weights = bf16[2,2048,1024]{2,1,0:T(8,128)(2,1)S(1)} custom-call(s32[1]{0:T(128)} %bitcast.3.quarter, bf16[2048,4096]{1,0:T(8,128)(2,1)} %gate_weight.3, bf16[2048,4096]{1,0:T(8,128)(2,1)} %up_weight.7), custom_call_target="tpu_custom_call" | custom-call | flops 8589934592 | bytes 1 | tf_op jit(solution)/shard_map/load0/pallas_call | solution.py:119
  34.0 7.7 %collective-permute-done.2 = bf16[96,2048]{1,0:T(8,128)(2,1)S(1)} collective-permute-done((bf16[96,2048]{1,0:T(8,128)(2,1)S(1)}, bf16[96,2048]{1,0:T(8,128)(2,1)S(1)}, u32[]{:S(2)}, u32[]{:S(2)}) %collective-permute-start.2) | collective-permute-done | bytes 393248 | tf_op jit(solution)/shard_map/arr0/ppermute | solution.py:93
  42.1 2.0 %a0.1 = bf16[2,192,1024]{2,1,0:T(8,128)(2,1)S(1)} custom-call(bf16[192,2048]{1,0:T(8,128)(2,1)S(1)} %pad_maximum_fusion.some, bf16[2,2048,1024]{2,1,0:T(8,128)(2,1)S(1)} %load3.1.weights), custom_call_target="tpu_custom_call" | custom-call | flops 8589934592 | bytes 1 | tf_op jit(solution)/shard_map/a0/pallas_call | solution.py:148
  44.2 2.0 %c0.1 = bf16[2,192,1024]{2,1,0:T(8,128)(2,1)S(1)} custom-call(bf16[192,2048]{1,0:T(8,128)(2,1)S(1)} %pad_maximum_fusion.some, bf16[2,2048,1024]{2,1,0:T(8,128)(2,1)S(1)} %load1.1.weights), custom_call_target="tpu_custom_call" | custom-call | flops 8589934592 | bytes 1 | tf_op jit(solution)/shard_map/c0/pallas_call | solution.py:148
  48.2 2.1 %collective-permute-start.7 = (bf16[2,192,1024]{2,1,0:T(8,128)(2,1)S(1)}, bf16[2,192,1024]{2,1,0:T(8,128)(2,1)S(1)}, u32[]{:S(2)}, u32[]{:S(2)}) collective-permute-start(bf16[2,192,1024]{2,1,0:T(8,128)(2,1)S(1)} %c0.1), channel_id=1, source_target_pairs={{0,1},{1,0},{2,3},{3,2},{4,5},{5,4},{6,7},{7,6},{8,9},{9,8},{10,11... | collective-permute-start | bytes 2359304 | tf_op jit(solution)/shard_map/c0/ppermute | solution.py:69
  63.1 4.1 %collective-permute-done.10 = bf16[48,2048]{1,0:T(8,128)(2,1)S(1)} collective-permute-done((bf16[48,2048]{1,0:T(8,128)(2,1)S(1)}, bf16[48,2048]{1,0:T(8,128)(2,1)S(1)}, u32[]{:S(2)}, u32[]{:S(2)}) %collective-permute-start.10) | collective-permute-done | bytes 196640 | tf_op jit(solution)/shard_map/sel2/ppermute | solution.py:69
  67.3 8.4 %collective-permute-done.14.got_up = bf16[192,1024]{1,0:T(8,128)(2,1)S(1)} collective-permute-done((bf16[192,1024]{1,0:T(8,128)(2,1)S(1)}, bf16[192,1024]{1,0:T(8,128)(2,1)S(1)}, u32[]{:S(2)}, u32[]{:S(2)}) %collective-permute-start.14) | collective-permute-done | bytes 393248 | tf_op jit(solution)/shard_map/b0/ppermute | solution.py:69
  82.0 9.1 %collective-permute-done.18 = bf16[96,2048]{1,0:T(8,128)(2,1)S(1)} collective-permute-done((bf16[96,2048]{1,0:T(8,128)(2,1)S(1)}, bf16[96,2048]{1,0:T(8,128)(2,1)S(1)}, u32[]{:S(2)}, u32[]{:S(2)}) %collective-permute-start.18) | collective-permute-done | bytes 393248 | tf_op jit(solution)/shard_map/arr2/ppermute | solution.py:93
  91.8 2.0 %a2.1 = bf16[2,192,1024]{2,1,0:T(8,128)(2,1)S(1)} custom-call(bf16[192,2048]{1,0:T(8,128)(2,1)S(1)} %pad_maximum_fusion.1.some, bf16[2,2048,1024]{2,1,0:T(8,128)(2,1)S(1)} %load3.1.weights), custom_call_target="tpu_custom_call" | custom-call | flops 8589934592 | bytes 1 | tf_op jit(solution)/shard_map/a2/pallas_call | solution.py:148
  99.5 4.7 %own0.1.rest_0_ = f32[192,2048]{1,0:T(8,128)S(1)} custom-call(s32[2]{0:T(128)S(1)} %pad_add_fusion.1.quarters, bf16[192,1024]{1,0:T(8,128)(2,1)S(1)} %hide0.1.one, bf16[192,1024]{1,0:T(8,128)(2,1)S(1)} %collective-permute-done.21.two, bf16[4096,2048]{1,0:T(8,128)(2,1)} %weight.11), custom_call_target="tpu_custom_call" | custom-call | flops 8589934592 | bytes 1 | tf_op jit(solution)/shard_map/own0/pallas_call | solution.py:190
  109.0 8.2 %collective-permute-done.25.got_up = bf16[192,1024]{1,0:T(8,128)(2,1)S(1)} collective-permute-done((bf16[192,1024]{1,0:T(8,128)(2,1)S(1)}, bf16[192,1024]{1,0:T(8,128)(2,1)S(1)}, u32[]{:S(2)}, u32[]{:S(2)}) %collective-permute-start.25) | collective-permute-done | bytes 393248 | tf_op jit(solution)/shard_map/b2/ppermute | solution.py:69
  120.7 4.7 %rest0.1 = f32[192,2048]{1,0:T(8,128)S(1)} custom-call(s32[2]{0:T(128)S(1)} %pad_add_fusion.quarters, bf16[192,1024]{1,0:T(8,128)(2,1)S(1)} %collective-permute-done.15.one, bf16[192,1024]{1,0:T(8,128)(2,1)S(1)} %collective-permute-done.26.two, bf16[4096,2048]{1,0:T(8,128)(2,1)} %weight.11, f32[192,2048]{1,0:T(8,128)S(1)} %own0.1.rest_0_), custom_call_target="tpu_custom_call" | custom-call | flops 8589934592 | bytes 1 | tf_op jit(solution)/shard_map/rest0/pallas_call | solution.py:190
  126.3 3.0 %collective-permute-start.29 = (bf16[96,2048]{1,0:T(8,128)(2,1)S(1)}, bf16[96,2048]{1,0:T(8,128)(2,1)S(1)}, u32[]{:S(2)}, u32[]{:S(2)}) collective-permute-start(bf16[96,2048]{1,0:T(8,128)(2,1)S(1)} %get-tuple-element.137), channel_id=1, source_target_pairs={{1,4},{3,6},{4,1},{6,3},{9,12},{11,14},{12,9},{14,11},{17,20},{19,... | collective-permute-start | bytes 1179656 | tf_op jit(solution)/shard_map/out0/ppermute | solution.py:93
  129.3 4.5 %own1.1.rest_0_ = f32[128,2048]{1,0:T(8,128)S(1)} custom-call(s32[2]{0:T(128)S(1)} %pad_add_fusion.1.quarters, bf16[128,1024]{1,0:T(8,128)(2,1)S(1)} %hide1.1.one, bf16[128,1024]{1,0:T(8,128)(2,1)S(1)} %collective-permute-done.28.two, bf16[4096,2048]{1,0:T(8,128)(2,1)} %weight.11), custom_call_target="tpu_custom_call" | custom-call | flops 8589934592 | bytes 1 | tf_op jit(solution)/shard_map/own1/pallas_call | solution.py:190
  133.9 3.3 %collective-permute-done.29 = bf16[96,2048]{1,0:T(8,128)(2,1)S(1)} collective-permute-done((bf16[96,2048]{1,0:T(8,128)(2,1)S(1)}, bf16[96,2048]{1,0:T(8,128)(2,1)S(1)}, u32[]{:S(2)}, u32[]{:S(2)}) %collective-permute-start.29) | collective-permute-done | bytes 393248 | tf_op jit(solution)/shard_map/out0/ppermute | solution.py:93
  137.7 4.7 %own2.1.rest_0_ = f32[192,2048]{1,0:T(8,128)S(1)} custom-call(s32[2]{0:T(128)S(1)} %pad_add_fusion.1.quarters, bf16[192,1024]{1,0:T(8,128)(2,1)S(1)} %hide2.1.one, bf16[192,1024]{1,0:T(8,128)(2,1)S(1)} %collective-permute-done.31.two, bf16[4096,2048]{1,0:T(8,128)(2,1)} %weight.11), custom_call_target="tpu_custom_call" | custom-call | flops 8589934592 | bytes 1 | tf_op jit(solution)/shard_map/own2/pallas_call | solution.py:190
  142.5 3.3 %collective-permute-start.32 = (bf16[48,2048]{1,0:T(8,128)(2,1)S(1)}, bf16[48,2048]{1,0:T(8,128)(2,1)S(1)}, u32[]{:S(2)}, u32[]{:S(2)}) collective-permute-start(bf16[48,2048]{1,0:T(8,128)(2,1)S(1)} %convert_select_fusion.4), channel_id=1, source_target_pairs={{0,8},{4,12},{8,0},{12,4},{1,9},{5,13},{9,1},{13,5},{2,10},{6,14},... | collective-permute-start | bytes 589832 | tf_op jit(solution)/shard_map/far_out0/ppermute | solution.py:73
  145.8 4.5 %rest1.1 = f32[128,2048]{1,0:T(8,128)S(1)} custom-call(s32[2]{0:T(128)S(1)} %pad_add_fusion.quarters, bf16[128,1024]{1,0:T(8,128)(2,1)S(1)} %collective-permute-done.33.one, bf16[128,1024]{1,0:T(8,128)(2,1)S(1)} %collective-permute-done.34.two, bf16[4096,2048]{1,0:T(8,128)(2,1)} %weight.11, f32[128,2048]{1,0:T(8,128)S(1)} %own1.1.rest_0_), custom_call_target="tpu_custom_call" | custom-call | flops 8589934592 | bytes 1 | tf_op jit(solution)/shard_map/rest1/pallas_call | solution.py:190
  151.3 3.5 %collective-permute-start.38 = (bf16[64,2048]{1,0:T(8,128)(2,1)S(1)}, bf16[64,2048]{1,0:T(8,128)(2,1)S(1)}, u32[]{:S(2)}, u32[]{:S(2)}) collective-permute-start(bf16[64,2048]{1,0:T(8,128)(2,1)S(1)} %get-tuple-element.142), channel_id=1, source_target_pairs={{1,4},{3,6},{4,1},{6,3},{9,12},{11,14},{12,9},{14,11},{17,20},{19,... | collective-permute-start | bytes 786440 | tf_op jit(solution)/shard_map/out1/ppermute | solution.py:93
  156.6 4.7 %rest2.1 = f32[192,2048]{1,0:T(8,128)S(1)} custom-call(s32[2]{0:T(128)S(1)} %pad_add_fusion.quarters, bf16[192,1024]{1,0:T(8,128)(2,1)S(1)} %collective-permute-done.36.one, bf16[192,1024]{1,0:T(8,128)(2,1)S(1)} %collective-permute-done.37.two, bf16[4096,2048]{1,0:T(8,128)(2,1)} %weight.11, f32[192,2048]{1,0:T(8,128)S(1)} %copy-done.1), custom_call_target="tpu_custom_call" | custom-call | flops 8589934592 | bytes 1 | tf_op jit(solution)/shard_map/rest2/pallas_call | solution.py:190
  162.3 3.5 %collective-permute-start.41 = (bf16[96,2048]{1,0:T(8,128)(2,1)S(1)}, bf16[96,2048]{1,0:T(8,128)(2,1)S(1)}, u32[]{:S(2)}, u32[]{:S(2)}) collective-permute-start(bf16[96,2048]{1,0:T(8,128)(2,1)S(1)} %get-tuple-element.135), channel_id=1, source_target_pairs={{1,4},{3,6},{4,1},{6,3},{9,12},{11,14},{12,9},{14,11},{17,20},{19,... | collective-permute-start | bytes 1179656 | tf_op jit(solution)/shard_map/out2/ppermute | solution.py:93
  167.1 6.9 %collective-permute-done.41 = bf16[96,2048]{1,0:T(8,128)(2,1)S(1)} collective-permute-done((bf16[96,2048]{1,0:T(8,128)(2,1)S(1)}, bf16[96,2048]{1,0:T(8,128)(2,1)S(1)}, u32[]{:S(2)}, u32[]{:S(2)}) %collective-permute-start.41) | collective-permute-done | bytes 393248 | tf_op jit(solution)/shard_map/out2/ppermute | solution.py:93
  175.2 3.4 %collective-permute-start.42 = (bf16[32,2048]{1,0:T(8,128)(2,1)S(1)}, bf16[32,2048]{1,0:T(8,128)(2,1)S(1)}, u32[]{:S(2)}, u32[]{:S(2)}) collective-permute-start(bf16[32,2048]{1,0:T(8,128)(2,1)S(1)} %convert_select_fusion.5), channel_id=1, source_target_pairs={{0,8},{4,12},{8,0},{12,4},{1,9},{5,13},{9,1},{13,5},{2,10},{6,14},... | collective-permute-start | bytes 393224 | tf_op jit(solution)/shard_map/far_out1/ppermute | solution.py:73
  178.8 3.1 %collective-permute-start.44 = (bf16[48,2048]{1,0:T(8,128)(2,1)S(1)}, bf16[48,2048]{1,0:T(8,128)(2,1)S(1)}, u32[]{:S(2)}, u32[]{:S(2)}) collective-permute-start(bf16[48,2048]{1,0:T(8,128)(2,1)S(1)} %convert_select_fusion.3), channel_id=1, source_target_pairs={{0,8},{4,12},{8,0},{12,4},{1,9},{5,13},{9,1},{13,5},{2,10},{6,14},... | collective-permute-start | bytes 589832 | tf_op jit(solution)/shard_map/far_out2/ppermute | solution.py:73
  181.9 2.3 %collective-permute-done.42.got = bf16[32,2048]{1,0:T(8,128)(2,1)S(1)} collective-permute-done((bf16[32,2048]{1,0:T(8,128)(2,1)S(1)}, bf16[32,2048]{1,0:T(8,128)(2,1)S(1)}, u32[]{:S(2)}, u32[]{:S(2)}) %collective-permute-start.42) | collective-permute-done | bytes 131104 | tf_op jit(solution)/shard_map/far_out1/ppermute | solution.py:73
  184.6 4.3 %collective-permute-done.44.got = bf16[48,2048]{1,0:T(8,128)(2,1)S(1)} collective-permute-done((bf16[48,2048]{1,0:T(8,128)(2,1)S(1)}, bf16[48,2048]{1,0:T(8,128)(2,1)S(1)}, u32[]{:S(2)}, u32[]{:S(2)}) %collective-permute-start.44) | collective-permute-done | bytes 196640 | tf_op jit(solution)/shard_map/far_out2/ppermute | solution.py:73
  (132 shorter events, 53.3 us)
Async XLA Ops:
  3.2 12.0 %collective-permute-start = (bf16[48,2048]{1,0:T(8,128)(2,1)S(1)}, bf16[48,2048]{1,0:T(8,128)(2,1)S(1)}, u32[]{:S(2)}, u32[]{:S(2)}) collective-permute-start(bf16[48,2048]{1,0:T(8,128)(2,1)S(1)} %get-tuple-element.67), channel_id=1, source_target_pairs={{0,8},{4,12},{8,0},{12,4},{1,9},{5,13},{9,1},{13,5},{2,10},{6,14},... | collective-permute-start | bytes 589832 | tf_op jit(solution)/shard_map/far0/ppermute | solution.py:73
  21.0 25.1 %collective-permute-start.5 = (bf16[32,2048]{1,0:T(8,128)(2,1)S(1)}, bf16[32,2048]{1,0:T(8,128)(2,1)S(1)}, u32[]{:S(2)}, u32[]{:S(2)}) collective-permute-start(bf16[32,2048]{1,0:T(8,128)(2,1)S(1)} %broadcast_select_fusion.23), channel_id=1, source_target_pairs={{0,2},{1,3},{2,0},{3,1},{4,6},{5,7},{6,4},{7,5},{8,10},{9,11},{10,... | collective-permute-start | bytes 393224 | tf_op jit(solution)/shard_map/sel1/ppermute | solution.py:69
  21.6 20.2 %collective-permute-start.4 = (bf16[96,2048]{1,0:T(8,128)(2,1)S(1)}, bf16[96,2048]{1,0:T(8,128)(2,1)S(1)}, u32[]{:S(2)}, u32[]{:S(2)}) collective-permute-start(bf16[96,2048]{1,0:T(8,128)(2,1)S(1)} %pad_maximum_fusion.4), channel_id=1, source_target_pairs={{1,4},{3,6},{4,1},{6,3},{9,12},{11,14},{12,9},{14,11},{17,20},{19,... | collective-permute-start | bytes 1179656 | tf_op jit(solution)/shard_map/arr0/ppermute | solution.py:93
  27.9 13.9 %collective-permute-start.2 = (bf16[96,2048]{1,0:T(8,128)(2,1)S(1)}, bf16[96,2048]{1,0:T(8,128)(2,1)S(1)}, u32[]{:S(2)}, u32[]{:S(2)}) collective-permute-start(bf16[96,2048]{1,0:T(8,128)(2,1)S(1)} %pad_maximum_fusion.4), channel_id=1, source_target_pairs={{0,4},{1,0},{2,6},{3,2},{4,5},{5,1},{6,7},{7,3},{8,12},{9,8},{10,1... | collective-permute-start | bytes 1179656 | tf_op jit(solution)/shard_map/arr0/ppermute | solution.py:93
  28.0 27.5 %collective-permute-start.9 = (bf16[48,2048]{1,0:T(8,128)(2,1)S(1)}, bf16[48,2048]{1,0:T(8,128)(2,1)S(1)}, u32[]{:S(2)}, u32[]{:S(2)}) collective-permute-start(bf16[48,2048]{1,0:T(8,128)(2,1)S(1)} %get-tuple-element.83), channel_id=1, source_target_pairs={{0,8},{4,12},{8,0},{12,4},{1,9},{5,13},{9,1},{13,5},{2,10},{6,14},... | collective-permute-start | bytes 589832 | tf_op jit(solution)/shard_map/far2/ppermute | solution.py:73
  46.2 10.3 %collective-permute-start.12 = (bf16[64,2048]{1,0:T(8,128)(2,1)S(1)}, bf16[64,2048]{1,0:T(8,128)(2,1)S(1)}, u32[]{:S(2)}, u32[]{:S(2)}) collective-permute-start(bf16[64,2048]{1,0:T(8,128)(2,1)S(1)} %pad_maximum_fusion.6), channel_id=1, source_target_pairs={{1,4},{3,6},{4,1},{6,3},{9,12},{11,14},{12,9},{14,11},{17,20},{19,... | collective-permute-start | bytes 786440 | tf_op jit(solution)/shard_map/arr1/ppermute | solution.py:93
  52.2 23.5 %collective-permute-start.8 = (bf16[192,1024]{1,0:T(8,128)(2,1)S(1)}, bf16[192,1024]{1,0:T(8,128)(2,1)S(1)}, u32[]{:S(2)}, u32[]{:S(2)}) collective-permute-start(bf16[192,1024]{1,0:T(8,128)(2,1)S(1)} %get-tuple-element.81), channel_id=1, source_target_pairs={{0,2},{1,3},{2,0},{3,1},{4,6},{5,7},{6,4},{7,5},{8,10},{9,11},{10,... | collective-permute-start | bytes 1179656 | tf_op jit(solution)/shard_map/b0/ppermute | solution.py:69
  55.5 11.7 %collective-permute-start.10 = (bf16[48,2048]{1,0:T(8,128)(2,1)S(1)}, bf16[48,2048]{1,0:T(8,128)(2,1)S(1)}, u32[]{:S(2)}, u32[]{:S(2)}) collective-permute-start(bf16[48,2048]{1,0:T(8,128)(2,1)S(1)} %broadcast_select_fusion.16), channel_id=1, source_target_pairs={{0,2},{1,3},{2,0},{3,1},{4,6},{5,7},{6,4},{7,5},{8,10},{9,11},{10,... | collective-permute-start | bytes 589832 | tf_op jit(solution)/shard_map/sel2/ppermute | solution.py:69
  59.7 20.6 %collective-permute-start.16 = (bf16[2,128,1024]{2,1,0:T(8,128)(2,1)S(1)}, bf16[2,128,1024]{2,1,0:T(8,128)(2,1)S(1)}, u32[]{:S(2)}, u32[]{:S(2)}) collective-permute-start(bf16[2,128,1024]{2,1,0:T(8,128)(2,1)S(1)} %c1.1), channel_id=1, source_target_pairs={{0,1},{1,0},{2,3},{3,2},{4,5},{5,4},{6,7},{7,6},{8,9},{9,8},{10,11... | collective-permute-start | bytes 1572872 | tf_op jit(solution)/shard_map/c1/ppermute | solution.py:69
  60.3 15.3 %collective-permute-start.14 = (bf16[192,1024]{1,0:T(8,128)(2,1)S(1)}, bf16[192,1024]{1,0:T(8,128)(2,1)S(1)}, u32[]{:S(2)}, u32[]{:S(2)}) collective-permute-start(bf16[192,1024]{1,0:T(8,128)(2,1)S(1)} %get-tuple-element.92), channel_id=1, source_target_pairs={{0,2},{1,3},{2,0},{3,1},{4,6},{5,7},{6,4},{7,5},{8,10},{9,11},{10,... | collective-permute-start | bytes 1179656 | tf_op jit(solution)/shard_map/b0/ppermute | solution.py:69
  62.8 43.8 %collective-permute-start.17 = (bf16[128,1024]{1,0:T(8,128)(2,1)S(1)}, bf16[128,1024]{1,0:T(8,128)(2,1)S(1)}, u32[]{:S(2)}, u32[]{:S(2)}) collective-permute-start(bf16[128,1024]{1,0:T(8,128)(2,1)S(1)} %get-tuple-element.89), channel_id=1, source_target_pairs={{0,2},{1,3},{2,0},{3,1},{4,6},{5,7},{6,4},{7,5},{8,10},{9,11},{10,... | collective-permute-start | bytes 786440 | tf_op jit(solution)/shard_map/b1/ppermute | solution.py:69
  75.9 22.3 %collective-permute-start.21 = (bf16[192,1024]{1,0:T(8,128)(2,1)S(1)}, bf16[192,1024]{1,0:T(8,128)(2,1)S(1)}, u32[]{:S(2)}, u32[]{:S(2)}) collective-permute-start(bf16[192,1024]{1,0:T(8,128)(2,1)S(1)} %hide0.1.one), channel_id=1, source_target_pairs={{0,1},{1,0},{2,3},{3,2},{4,5},{5,4},{6,7},{7,6},{8,9},{9,8},{10,11... | collective-permute-start | bytes 1179656 | tf_op jit(solution)/shard_map/hide0/ppermute | solution.py:69
  77.1 31.9 %collective-permute-start.15 = (bf16[192,1024]{1,0:T(8,128)(2,1)S(1)}, bf16[192,1024]{1,0:T(8,128)(2,1)S(1)}, u32[]{:S(2)}, u32[]{:S(2)}) collective-permute-start(bf16[192,1024]{1,0:T(8,128)(2,1)S(1)} %hide0.1.one), channel_id=1, source_target_pairs={{0,2},{1,3},{2,0},{3,1},{4,6},{5,7},{6,4},{7,5},{8,10},{9,11},{10,... | collective-permute-start | bytes 1179656 | tf_op jit(solution)/shard_map/hide0/ppermute | solution.py:69
  78.3 13.1 %collective-permute-start.19 = (bf16[96,2048]{1,0:T(8,128)(2,1)S(1)}, bf16[96,2048]{1,0:T(8,128)(2,1)S(1)}, u32[]{:S(2)}, u32[]{:S(2)}) collective-permute-start(bf16[96,2048]{1,0:T(8,128)(2,1)S(1)} %pad_maximum_fusion.5), channel_id=1, source_target_pairs={{1,4},{3,6},{4,1},{6,3},{9,12},{11,14},{12,9},{14,11},{17,20},{19,... | collective-permute-start | bytes 1179656 | tf_op jit(solution)/shard_map/arr2/ppermute | solution.py:93
  80.3 10.9 %collective-permute-start.18 = (bf16[96,2048]{1,0:T(8,128)(2,1)S(1)}, bf16[96,2048]{1,0:T(8,128)(2,1)S(1)}, u32[]{:S(2)}, u32[]{:S(2)}) collective-permute-start(bf16[96,2048]{1,0:T(8,128)(2,1)S(1)} %pad_maximum_fusion.5), channel_id=1, source_target_pairs={{0,4},{1,0},{2,6},{3,2},{4,5},{5,1},{6,7},{7,3},{8,12},{9,8},{10,1... | collective-permute-start | bytes 1179656 | tf_op jit(solution)/shard_map/arr2/ppermute | solution.py:93
  91.2 15.3 %collective-permute-start.23 = (bf16[128,1024]{1,0:T(8,128)(2,1)S(1)}, bf16[128,1024]{1,0:T(8,128)(2,1)S(1)}, u32[]{:S(2)}, u32[]{:S(2)}) collective-permute-start(bf16[128,1024]{1,0:T(8,128)(2,1)S(1)} %get-tuple-element.103), channel_id=1, source_target_pairs={{0,2},{1,3},{2,0},{3,1},{4,6},{5,7},{6,4},{7,5},{8,10},{9,11},{10,... | collective-permute-start | bytes 786440 | tf_op jit(solution)/shard_map/b1/ppermute | solution.py:69
  98.2 19.0 %collective-permute-start.24 = (bf16[192,1024]{1,0:T(8,128)(2,1)S(1)}, bf16[192,1024]{1,0:T(8,128)(2,1)S(1)}, u32[]{:S(2)}, u32[]{:S(2)}) collective-permute-start(bf16[192,1024]{1,0:T(8,128)(2,1)S(1)} %get-tuple-element.99), channel_id=1, source_target_pairs={{0,2},{1,3},{2,0},{3,1},{4,6},{5,7},{6,4},{7,5},{8,10},{9,11},{10,... | collective-permute-start | bytes 1179656 | tf_op jit(solution)/shard_map/b2/ppermute | solution.py:69
  104.2 13.1 %collective-permute-start.25 = (bf16[192,1024]{1,0:T(8,128)(2,1)S(1)}, bf16[192,1024]{1,0:T(8,128)(2,1)S(1)}, u32[]{:S(2)}, u32[]{:S(2)}) collective-permute-start(bf16[192,1024]{1,0:T(8,128)(2,1)S(1)} %get-tuple-element.107), channel_id=1, source_target_pairs={{0,2},{1,3},{2,0},{3,1},{4,6},{5,7},{6,4},{7,5},{8,10},{9,11},{10,... | collective-permute-start | bytes 1179656 | tf_op jit(solution)/shard_map/b2/ppermute | solution.py:69
  106.7 31.0 %collective-permute-start.33 = (bf16[128,1024]{1,0:T(8,128)(2,1)S(1)}, bf16[128,1024]{1,0:T(8,128)(2,1)S(1)}, u32[]{:S(2)}, u32[]{:S(2)}) collective-permute-start(bf16[128,1024]{1,0:T(8,128)(2,1)S(1)} %hide1.1.one), channel_id=1, source_target_pairs={{0,2},{1,3},{2,0},{3,1},{4,6},{5,7},{6,4},{7,5},{8,10},{9,11},{10,... | collective-permute-start | bytes 786440 | tf_op jit(solution)/shard_map/hide1/ppermute | solution.py:69
  108.0 18.3 %collective-permute-start.28 = (bf16[128,1024]{1,0:T(8,128)(2,1)S(1)}, bf16[128,1024]{1,0:T(8,128)(2,1)S(1)}, u32[]{:S(2)}, u32[]{:S(2)}) collective-permute-start(bf16[128,1024]{1,0:T(8,128)(2,1)S(1)} %hide1.1.one), channel_id=1, source_target_pairs={{0,1},{1,0},{2,3},{3,2},{4,5},{5,4},{6,7},{7,6},{8,9},{9,8},{10,11... | collective-permute-start | bytes 786440 | tf_op jit(solution)/shard_map/hide1/ppermute | solution.py:69
  109.0 11.7 %collective-permute-start.26 = (bf16[192,1024]{1,0:T(8,128)(2,1)S(1)}, bf16[192,1024]{1,0:T(8,128)(2,1)S(1)}, u32[]{:S(2)}, u32[]{:S(2)}) collective-permute-start(bf16[192,1024]{1,0:T(8,128)(2,1)S(1)} %collective-permute-done.15.one), channel_id=1, source_target_pairs={{0,1},{1,0},{2,3},{3,2},{4,5},{5,4},{6,7},{7,6},{8,9},{9,8},{10,11... | collective-permute-start | bytes 1179656 | tf_op jit(solution)/shard_map/forward0/ppermute | solution.py:69
  117.6 32.9 %collective-permute-start.36 = (bf16[192,1024]{1,0:T(8,128)(2,1)S(1)}, bf16[192,1024]{1,0:T(8,128)(2,1)S(1)}, u32[]{:S(2)}, u32[]{:S(2)}) collective-permute-start(bf16[192,1024]{1,0:T(8,128)(2,1)S(1)} %hide2.1.one), channel_id=1, source_target_pairs={{0,2},{1,3},{2,0},{3,1},{4,6},{5,7},{6,4},{7,5},{8,10},{9,11},{10,... | collective-permute-start | bytes 1179656 | tf_op jit(solution)/shard_map/hide2/ppermute | solution.py:69
  118.8 18.9 %collective-permute-start.31 = (bf16[192,1024]{1,0:T(8,128)(2,1)S(1)}, bf16[192,1024]{1,0:T(8,128)(2,1)S(1)}, u32[]{:S(2)}, u32[]{:S(2)}) collective-permute-start(bf16[192,1024]{1,0:T(8,128)(2,1)S(1)} %hide2.1.one), channel_id=1, source_target_pairs={{0,1},{1,0},{2,3},{3,2},{4,5},{5,4},{6,7},{7,6},{8,9},{9,8},{10,11... | collective-permute-start | bytes 1179656 | tf_op jit(solution)/shard_map/hide2/ppermute | solution.py:69
  125.5 8.4 %collective-permute-start.27 = (bf16[96,2048]{1,0:T(8,128)(2,1)S(1)}, bf16[96,2048]{1,0:T(8,128)(2,1)S(1)}, u32[]{:S(2)}, u32[]{:S(2)}) collective-permute-start(bf16[96,2048]{1,0:T(8,128)(2,1)S(1)} %get-tuple-element.136), channel_id=1, source_target_pairs={{0,1},{1,5},{2,3},{3,7},{4,0},{5,4},{6,2},{7,6},{8,9},{9,13},{10,1... | collective-permute-start | bytes 1179656 | tf_op jit(solution)/shard_map/out0/ppermute | solution.py:93
  126.3 10.9 %collective-permute-start.29 = (bf16[96,2048]{1,0:T(8,128)(2,1)S(1)}, bf16[96,2048]{1,0:T(8,128)(2,1)S(1)}, u32[]{:S(2)}, u32[]{:S(2)}) collective-permute-start(bf16[96,2048]{1,0:T(8,128)(2,1)S(1)} %get-tuple-element.137), channel_id=1, source_target_pairs={{1,4},{3,6},{4,1},{6,3},{9,12},{11,14},{12,9},{14,11},{17,20},{19,... | collective-permute-start | bytes 1179656 | tf_op jit(solution)/shard_map/out0/ppermute | solution.py:93
  137.7 8.1 %collective-permute-start.34 = (bf16[128,1024]{1,0:T(8,128)(2,1)S(1)}, bf16[128,1024]{1,0:T(8,128)(2,1)S(1)}, u32[]{:S(2)}, u32[]{:S(2)}) collective-permute-start(bf16[128,1024]{1,0:T(8,128)(2,1)S(1)} %collective-permute-done.33.one), channel_id=1, source_target_pairs={{0,1},{1,0},{2,3},{3,2},{4,5},{5,4},{6,7},{7,6},{8,9},{9,8},{10,11... | collective-permute-start | bytes 786440 | tf_op jit(solution)/shard_map/forward1/ppermute | solution.py:69
  142.5 12.4 %collective-permute-start.32 = (bf16[48,2048]{1,0:T(8,128)(2,1)S(1)}, bf16[48,2048]{1,0:T(8,128)(2,1)S(1)}, u32[]{:S(2)}, u32[]{:S(2)}) collective-permute-start(bf16[48,2048]{1,0:T(8,128)(2,1)S(1)} %convert_select_fusion.4), channel_id=1, source_target_pairs={{0,8},{4,12},{8,0},{12,4},{1,9},{5,13},{9,1},{13,5},{2,10},{6,14},... | collective-permute-start | bytes 589832 | tf_op jit(solution)/shard_map/far_out0/ppermute | solution.py:73
  151.3 14.6 %collective-permute-start.38 = (bf16[64,2048]{1,0:T(8,128)(2,1)S(1)}, bf16[64,2048]{1,0:T(8,128)(2,1)S(1)}, u32[]{:S(2)}, u32[]{:S(2)}) collective-permute-start(bf16[64,2048]{1,0:T(8,128)(2,1)S(1)} %get-tuple-element.142), channel_id=1, source_target_pairs={{1,4},{3,6},{4,1},{6,3},{9,12},{11,14},{12,9},{14,11},{17,20},{19,... | collective-permute-start | bytes 786440 | tf_op jit(solution)/shard_map/out1/ppermute | solution.py:93
  162.3 11.6 %collective-permute-start.41 = (bf16[96,2048]{1,0:T(8,128)(2,1)S(1)}, bf16[96,2048]{1,0:T(8,128)(2,1)S(1)}, u32[]{:S(2)}, u32[]{:S(2)}) collective-permute-start(bf16[96,2048]{1,0:T(8,128)(2,1)S(1)} %get-tuple-element.135), channel_id=1, source_target_pairs={{1,4},{3,6},{4,1},{6,3},{9,12},{11,14},{12,9},{14,11},{17,20},{19,... | collective-permute-start | bytes 1179656 | tf_op jit(solution)/shard_map/out2/ppermute | solution.py:93
  166.1 9.0 %collective-permute-start.39 = (bf16[32,2048]{1,0:T(8,128)(2,1)S(1)}, bf16[32,2048]{1,0:T(8,128)(2,1)S(1)}, u32[]{:S(2)}, u32[]{:S(2)}) collective-permute-start(bf16[32,2048]{1,0:T(8,128)(2,1)S(1)} %select_convert_fusion.5), channel_id=1, source_target_pairs={{0,2},{1,3},{2,0},{3,1},{4,6},{5,7},{6,4},{7,5},{8,10},{9,11},{10,... | collective-permute-start | bytes 393224 | tf_op jit(solution)/shard_map/mix1/ppermute | solution.py:69
  175.2 9.1 %collective-permute-start.42 = (bf16[32,2048]{1,0:T(8,128)(2,1)S(1)}, bf16[32,2048]{1,0:T(8,128)(2,1)S(1)}, u32[]{:S(2)}, u32[]{:S(2)}) collective-permute-start(bf16[32,2048]{1,0:T(8,128)(2,1)S(1)} %convert_select_fusion.5), channel_id=1, source_target_pairs={{0,8},{4,12},{8,0},{12,4},{1,9},{5,13},{9,1},{13,5},{2,10},{6,14},... | collective-permute-start | bytes 393224 | tf_op jit(solution)/shard_map/far_out1/ppermute | solution.py:73
  178.8 10.1 %collective-permute-start.44 = (bf16[48,2048]{1,0:T(8,128)(2,1)S(1)}, bf16[48,2048]{1,0:T(8,128)(2,1)S(1)}, u32[]{:S(2)}, u32[]{:S(2)}) collective-permute-start(bf16[48,2048]{1,0:T(8,128)(2,1)S(1)} %convert_select_fusion.3), channel_id=1, source_target_pairs={{0,8},{4,12},{8,0},{12,4},{1,9},{5,13},{9,1},{13,5},{2,10},{6,14},... | collective-permute-start | bytes 589832 | tf_op jit(solution)/shard_map/far_out2/ppermute | solution.py:73
  (15 other events, 80.1 us)

commit v2 on v1

--- a/solution.py
+++ b/solution.py
@@ -7,16 +7,16 @@
 from jax.experimental.pallas import tpu as pltpu
 from jax.sharding import PartitionSpec as P
 
-ROWS = (48, 32, 48)
+ROWS = (32, 64, 32)
 ORDER = (
-    "far0", "load3", "load1", "sel0", "far1", "load2", "arr0", "sel1", "far2", "load0", "take0", "a0", "c0",
+    "far0", "load3", "load1", "sel0", "far1", "load2", "arr0", "load0", "sel1", "far2", "take0", "a0", "c0",
     "arr1", "b0", "d0", "sel2", "take1", "a1", "c1", "b1", "arr2", "hide0", "d1", "take2", "a2", "c2", "b2",
-    "own0", "d2", "hide1", "forward0", "hide2", "rest0", "out0", "own1", "mix0", "forward1", "own2",
-    "far_out0", "rest1", "forward2", "out1", "end0", "rest2", "out2", "mix1", "mix2", "far_out1", "far_out2",
-    "end1", "end2",
+    "d2", "down0", "own0", "down2", "hide1", "forward0", "hide2", "rest0", "out0", "own1", "mix0", "forward1",
+    "own2", "far_out0", "rest1", "forward2", "out1", "end0", "rest2", "out2", "mix1", "mix2", "far_out1",
+    "far_out2", "end1", "end2",
 )
 TILE = 256
-COST = 1 << 33
+COST = 1 << 34
 VMEM = 10 << 20
 
 
@@ -155,51 +155,80 @@
     )(some, weights, *([] if got is None else [got]))
 
 
-def products_kernel(has_total, quarters, one, two, weight, *rest):
-    out, near, done = rest[-3:]
-    deep, tile = near.shape[2], near.shape[3]
-    pieces = one, two
+def load_rows_kernel(quarters, weight, out, done):
+    rows = out.shape[1]
+    pieces = done.shape[1]
+    part = rows // pieces
     copies = [
-        [
-            pltpu.make_async_copy(
-                weight.at[pl.ds(pl.multiple_of(quarters[k] * deep, deep), deep), pl.ds(j * tile, tile)],
-                near.at[k, j],
-                done.at[k, j],
-            )
-            for k in range(2)
-        ]
-        for j in range(near.shape[1])
+        pltpu.make_async_copy(
+            weight.at[pl.ds(pl.multiple_of(quarters[k] * rows + i * part, part), part)],
+            out.at[k, pl.ds(i * part, part)],
+            done.at[k, i],
+        )
+        for k in range(2)
+        for i in range(pieces)
     ]
-    for pair in copies:
-        for copy in pair:
-            copy.start()
-    for j, pair in enumerate(copies):
-        here = pl.ds(j * tile, tile)
-        for copy in pair:
-            copy.wait()
-        value = sum(dot(pieces[k][...], near[k, j]) for k in range(2))
-        if has_total:
-            value += rest[0][:, here]
-        out[:, here] = value
-
-
-def products(pieces, weight, quarters, total=None):
-    rows, deep = pieces[0].shape
-    tiles = weight.shape[1] // (2 * TILE)
+    for copy in copies:
+        copy.start()
+    for copy in copies:
+        copy.wait()
+
+
+def load_rows(weight, quarters):
+    deep, width = weight.shape
+    return pl.pallas_call(
+        load_rows_kernel,
+        out_shape=jax.ShapeDtypeStruct((2, deep // 4, width), weight.dtype),
+        in_specs=[pl.BlockSpec(memory_space=pltpu.SMEM), pl.BlockSpec(memory_space=pl.ANY)],
+        out_specs=pl.BlockSpec(memory_space=pltpu.VMEM),
+        scratch_shapes=[pltpu.SemaphoreType.DMA((2, 4))],
+        compiler_params=pltpu.CompilerParams(vmem_limit_bytes=VMEM),
+        cost_estimate=pl.CostEstimate(flops=COST, bytes_accessed=1, transcendentals=0),
+    )(jnp.stack(quarters).astype(jnp.int32), weight)
+
+
+def products_kernel(has_total, one, two, weights, *rest):
+    tile = 4 * TILE
+
+    @pl.loop(0, weights.shape[2] // tile)
+    def strip(j):
+        here = pl.ds(pl.multiple_of(j * tile, tile), tile)
+        value = dot(one[...], weights[0, :, here]) + dot(two[...], weights[1, :, here])
+        rest[-1][:, here] = value + rest[0][:, here] if has_total else value
+
+
+def products(pieces, weights, total=None):
     near = pl.BlockSpec(memory_space=pltpu.VMEM)
     return pl.pallas_call(
         functools.partial(products_kernel, total is not None),
-        out_shape=jax.ShapeDtypeStruct((rows, weight.shape[1]), jnp.float32),
-        in_specs=[pl.BlockSpec(memory_space=pltpu.SMEM), near, near, pl.BlockSpec(memory_space=pl.ANY)]
-        + [near] * (total is not None),
+        out_shape=jax.ShapeDtypeStruct((pieces[0].shape[0], weights.shape[2]), jnp.float32),
+        in_specs=[near] * (3 + (total is not None)),
         out_specs=near,
-        scratch_shapes=[
-            pltpu.VMEM((2, tiles, deep, 2 * TILE), weight.dtype),
-            pltpu.SemaphoreType.DMA((2, tiles)),
-        ],
-        compiler_params=pltpu.CompilerParams(vmem_limit_bytes=VMEM),
-        cost_estimate=pl.CostEstimate(flops=COST, bytes_accessed=1, transcendentals=0),
-    )(jnp.stack(quarters).astype(jnp.int32), *pieces, weight, *([] if total is None else [total]))
+        compiler_params=pltpu.CompilerParams(vmem_limit_bytes=VMEM),
+        cost_estimate=pl.CostEstimate(flops=COST, bytes_accessed=1, transcendentals=0),
+    )(*pieces, weights, *([] if total is None else [total]))
+
+
+def begin_kernel(starts, values, turned_scales, *outs):
+    scales = turned_scales[...].T
+    for j in range(scales.shape[1]):
+        here = pl.ds(j * 128, 128)
+        scaled_values = narrow(wide(values[:, here]) * scales[:, j : j + 1])
+        for i, out in enumerate(outs):
+            out[:, here] = scaled_values[starts[i] : starts[i + 1]]
+
+
+def begin(values, scales, starts):
+    near = pl.BlockSpec(memory_space=pltpu.VMEM)
+    count = len(starts) - 1
+    return pl.pallas_call(
+        functools.partial(begin_kernel, starts),
+        out_shape=[jax.ShapeDtypeStruct((starts[i + 1] - starts[i], values.shape[1]), values.dtype) for i in range(count)],
+        in_specs=[near] * 2,
+        out_specs=[near] * count,
+        compiler_params=pltpu.CompilerParams(vmem_limit_bytes=VMEM),
+        cost_estimate=pl.CostEstimate(flops=COST, bytes_accessed=1, transcendentals=0),
+    )(values, scales.T)
 
 
 def hide_kernel(held, got_gate, got_up, out):
@@ -225,29 +254,42 @@
     )(held, got_gate, got_up)
 
 
-def end_kernel(kept, got, values, scales):
-    for j in range(scales.shape[1]):
+def end_kernel(count, kept, got, *rest):
+    before, (values, scales) = rest[: 2 * count], rest[2 * count :]
+    first = sum(part.shape[0] for part in before[::2])
+    rows = pl.ds(first, kept.shape[0])
+    columns = []
+    for j in range(kept.shape[1] // 128):
         here = pl.ds(j * 128, 128)
         total = kept[:, here] + wide(got[:, here])
         scale = jnp.max(jnp.abs(total), axis=1, keepdims=True) + 1e-06
-        values[:, here] = narrow(total / scale)
-        scales[:, pl.ds(j, 1)] = scale
-
-
-def end(kept, got):
+        values[rows, here] = narrow(total / scale)
+        columns.append(scale)
+    ended = jnp.concatenate(columns, axis=1)
+    if not count:
+        scales[...] = ended
+        return
+    row = 0
+    for part in before[::2]:
+        values[pl.ds(row, part.shape[0])] = part[...]
+        row += part.shape[0]
+    scales[...] = jnp.concatenate([part[...] for part in before[1::2]] + [ended], axis=0).T
+
+
+def end(kept, got, before=()):
     rows, width = kept.shape
+    count = len(before)
+    rows += sum(values.shape[0] for values, scales in before)
     near = pl.BlockSpec(memory_space=pltpu.VMEM)
-    return pl.pallas_call(
-        end_kernel,
-        out_shape=(
-            jax.ShapeDtypeStruct((rows, width), got.dtype),
-            jax.ShapeDtypeStruct((rows, width // 128), kept.dtype),
-        ),
-        in_specs=[near] * 2,
+    shape = (width // 128, rows) if count else (rows, width // 128)
+    return pl.pallas_call(
+        functools.partial(end_kernel, count),
+        out_shape=(jax.ShapeDtypeStruct((rows, width), got.dtype), jax.ShapeDtypeStruct(shape, kept.dtype)),
+        in_specs=[near] * (2 + 2 * count),
         out_specs=(near, near),
         compiler_params=pltpu.CompilerParams(vmem_limit_bytes=VMEM),
         cost_estimate=pl.CostEstimate(flops=COST, bytes_accessed=1, transcendentals=0),
-    )(kept, got)
+    )(kept, got, *(array for pair in before for array in pair))
 
 
 class Steps:
@@ -259,25 +301,23 @@
         self.gate_weight = pltpu.with_memory_space_constraint(gate_weight, pltpu.HBM)
         self.up_weight = pltpu.with_memory_space_constraint(up_weight, pltpu.HBM)
         self.down_weight = pltpu.with_memory_space_constraint(down_weight, pltpu.HBM)
-        self.mine = narrow(expand(tokens_values, tokens_scales))
         unit = tokens_values.shape[0] // sum(ROWS)
-        self.starts = [sum(ROWS[:i]) * unit for i in range(len(ROWS) + 1)]
-        self.last = self.mine
+        self.mine = begin(tokens_values, tokens_scales, [sum(ROWS[:i]) * unit for i in range(len(ROWS) + 1)])
+        self.last = self.mine[0]
         self.held = {}
 
     def run(self, order):
         for step in order:
             with jax.named_scope(step):
                 getattr(self, step[:-1])(int(step[-1]))
-        return tuple(
-            jnp.concatenate([self.held["end", i][k] for i in range(len(ROWS))], axis=0) for k in range(2)
-        )
+        values, scales = self.held["end", len(ROWS) - 1]
+        return values, scales.T
 
     def now(self, array):
         return lax.optimization_barrier((array, self.last))[0]
 
     def far(self, i):
-        part = self.now(self.mine[self.starts[i] : self.starts[i + 1]])
+        part = self.now(self.mine[i])
         self.held["far", i] = part, over_tp(part, 2)
 
     def sel(self, i):
@@ -330,12 +370,13 @@
         self.held["hide", i] = hidden, far, over_seq(hidden, 1)
         self.last = hidden
 
-    def down(self, pieces, bits, total=None):
-        return products(pieces, self.down_weight, [self.seq ^ bit for bit in bits], total)
+    def down(self, bits):
+        quarters = [self.seq ^ bits, self.seq ^ bits ^ 1]
+        self.held["down", bits] = self.last = load_rows(self.now(self.down_weight), quarters)
 
     def own(self, i):
         hidden, far, near = self.held["hide", i]
-        self.held["own", i] = self.last = self.down((self.now(hidden), near), (0, 1))
+        self.held["own", i] = self.last = products((self.now(hidden), near), self.held["down", 0])
 
     def forward(self, i):
         far = self.now(self.held["hide", i][1])
@@ -343,7 +384,7 @@
 
     def rest(self, i):
         far, last = self.held["pass", i]
-        self.held["rest", i] = self.last = self.down((self.now(far), last), (2, 3), self.held["own", i])
+        self.held["rest", i] = self.last = products((self.now(far), last), self.held["down", 2], self.held["own", i])
 
     def out(self, i):
         partial_sum = self.now(self.held["rest", i])
@@ -375,7 +416,8 @@
 
     def end(self, i):
         kept, got = self.held["far_out", i]
-        self.held["end", i] = end(kept, self.now(got))
+        before = [self.held["end", k] for k in range(i)] if i == len(ROWS) - 1 else ()
+        self.held["end", i] = end(kept, self.now(got), before)
         self.last = self.held["end", i][0]
 
 

time: 191 us -> 180 us (0.942)
  local copies, waits for them, and re-layouts: 2.78 us -> 8.34 us
  starting transfers between devices: 58.9 us -> 53.5 us
  waiting for transfers between devices: 58.4 us -> 54.2 us
  Pallas kernels: 64.2 us -> 60.3 us
  other arithmetic: 5.11 us -> 2.25 us
    pallas_call x6, Pallas kernels: 27.7 us -> 13 us  [products(): pl.pallas_call(functools.partial(products_kernel, total is not None), out...]
    ppermute x12, waiting for transfers between devices: 27.9 us -> 14.7 us  [over_both(): return lax.ppermute(array, ('tp', 'seq'), pairs)]
    ppermute x6, waiting for transfers between devices: 8.73 us -> 21 us  [over_tp(): return lax.ppermute(array, 'tp', [(i, i ^ bit) for i in range(4)])]
    pallas_call x3 -> x6, Pallas kernels: 0.53 us -> 9.84 us  [the longest x2 8.04 us: load_rows(): pl.pallas_call(load_rows_kernel, out_shape=jax.ShapeDtypeStruct((2, deep...]
    ppermute x6, starting transfers between devices: 15.6 us -> 6.57 us  [over_tp(): return lax.ppermute(array, 'tp', [(i, i ^ bit) for i in range(4)])]
    unnamed x5 -> x16, local copies, waits for them, and re-layouts: 2.22 us -> 8.34 us
    ppermute x27, waiting for transfers between devices: 21.8 us -> 18.4 us  [over_seq(): return lax.ppermute(array, 'seq', [(i, i ^ bit) for i in range(4)])]
    ppermute x27, starting transfers between devices: 20.8 us -> 23.1 us  [over_seq(): return lax.ppermute(array, 'seq', [(i, i ^ bit) for i in range(4)])]
  transfers between devices with their start and end apart: 45 -> 45, of which waited for: 17 -> 14; matrix products, arithmetic and copies ran while one was open for 1% -> 1% of each run, Pallas kernels for 34% -> 33%
where the time goes in v2:
time: 180 us
  Pallas kernels  60.3 us (34%)
  waiting for transfers between devices  54.2 us (30%)
  starting transfers between devices  53.5 us (30%)
  local copies, waits for them, and re-layouts  8.34 us (5%)
  other arithmetic  2.25 us (1%)
    ppermute x12, starting transfers between devices, over_both(): return lax.ppermute(array, ('tp', 'seq'), pairs)  23.8 us
    ppermute x27, starting transfers between devices, over_seq(): return lax.ppermute(array, 'seq', [(i, i ^ bit) for i in range(4)])  23.1 us
    pallas_call x12, Pallas kernels, sums(): pl.pallas_call(functools.partial(sums_kernel, got is not None, split), ou...  21.9 us
    ppermute x6, waiting for transfers between devices, over_tp(): return lax.ppermute(array, 'tp', [(i, i ^ bit) for i in range(4)])  21 us
    ppermute x27, waiting for transfers between devices, over_seq(): return lax.ppermute(array, 'seq', [(i, i ^ bit) for i in range(4)])  18.4 us
    ppermute x12, waiting for transfers between devices, over_both(): return lax.ppermute(array, ('tp', 'seq'), pairs)  14.7 us
    pallas_call x4, Pallas kernels, load(): pl.pallas_call(load_kernel, out_shape=jax.ShapeDtypeStruct((2, deep, widt...  14 us
    pallas_call x6, Pallas kernels, products(): pl.pallas_call(functools.partial(products_kernel, total is not None), out...  13 us
  transfers between devices with their start and end apart: 45, of which 14 were waited for; matrix products, arithmetic and copies ran while one was open for 1% of the time, Pallas kernels for 33%

profile of v2, /device:TPU:1, one launch (start us, length us, event | category | flops | bytes accessed | tf_op | source)
XLA Modules:
  0.0 179.8 jit_solution(4948213882291859621)
XLA Ops:
  2.8 3.2 %collective-permute-start = (bf16[32,2048]{1,0:T(8,128)(2,1)S(1)}, bf16[32,2048]{1,0:T(8,128)(2,1)S(1)}, u32[]{:S(2)}, u32[]{:S(2)}) collective-permute-start(bf16[32,2048]{1,0:T(8,128)(2,1)S(1)} %get-tuple-element.75), channel_id=1, source_target_pairs={{0,8},{4,12},{8,0},{12,4},{1,9},{5,13},{9,1},{13,5},{2,10},{6,14},... | collective-permute-start | bytes 393224 | tf_op jit(solution)/shard_map/far0/ppermute | solution.py:73
  6.0 3.5 %load3.1.weights = bf16[2,2048,1024]{2,1,0:T(8,128)(2,1)S(1)} custom-call(s32[1]{0:T(128)} %bitcast.2.quarter, bf16[2048,4096]{1,0:T(8,128)(2,1)} %gate_weight.3, bf16[2048,4096]{1,0:T(8,128)(2,1)} %up_weight.7), custom_call_target="tpu_custom_call" | custom-call | flops 17179869184 | bytes 1 | tf_op jit(solution)/shard_map/load3/pallas_call | solution.py:119
  9.6 3.3 %copy-done.3 = bf16[2,2048,1024]{2,1,0:T(8,128)(2,1)} copy-done((bf16[2,2048,1024]{2,1,0:T(8,128)(2,1)}, bf16[2,2048,1024]{2,1,0:T(8,128)(2,1)S(1)}, u32[]{:S(2)}) %copy-start.3) | copy-done | bytes 8388632
  12.8 3.5 %load1.1.weights = bf16[2,2048,1024]{2,1,0:T(8,128)(2,1)S(1)} custom-call(s32[1]{0:T(128)} %bitcast.1.quarter, bf16[2048,4096]{1,0:T(8,128)(2,1)} %gate_weight.3, bf16[2048,4096]{1,0:T(8,128)(2,1)} %up_weight.7), custom_call_target="tpu_custom_call" | custom-call | flops 17179869184 | bytes 1 | tf_op jit(solution)/shard_map/load1/pallas_call | solution.py:119
  16.4 3.3 %copy-done.2 = bf16[2,2048,1024]{2,1,0:T(8,128)(2,1)} copy-done((bf16[2,2048,1024]{2,1,0:T(8,128)(2,1)}, bf16[2,2048,1024]{2,1,0:T(8,128)(2,1)S(1)}, u32[]{:S(2)}) %copy-start.2) | copy-done | bytes 8388632
  21.1 3.5 %load2.1.weights = bf16[2,2048,1024]{2,1,0:T(8,128)(2,1)S(1)} custom-call(s32[1]{0:T(128)} %bitcast.4.quarter, bf16[2048,4096]{1,0:T(8,128)(2,1)} %gate_weight.3, bf16[2048,4096]{1,0:T(8,128)(2,1)} %up_weight.7), custom_call_target="tpu_custom_call" | custom-call | flops 17179869184 | bytes 1 | tf_op jit(solution)/shard_map/load2/pallas_call | solution.py:119
  26.4 3.4 %collective-permute-start.5 = (bf16[64,2048]{1,0:T(8,128)(2,1)S(1)}, bf16[64,2048]{1,0:T(8,128)(2,1)S(1)}, u32[]{:S(2)}, u32[]{:S(2)}) collective-permute-start(bf16[64,2048]{1,0:T(8,128)(2,1)S(1)} %pad_maximum_fusion.4), channel_id=1, source_target_pairs={{1,4},{3,6},{4,1},{6,3},{9,12},{11,14},{12,9},{14,11},{17,20},{19,... | collective-permute-start | bytes 786440 | tf_op jit(solution)/shard_map/arr0/ppermute | solution.py:93
  29.8 3.5 %load0.1.weights = bf16[2,2048,1024]{2,1,0:T(8,128)(2,1)S(1)} custom-call(s32[1]{0:T(128)} %bitcast.3.quarter, bf16[2048,4096]{1,0:T(8,128)(2,1)} %gate_weight.3, bf16[2048,4096]{1,0:T(8,128)(2,1)} %up_weight.7), custom_call_target="tpu_custom_call" | custom-call | flops 17179869184 | bytes 1 | tf_op jit(solution)/shard_map/load0/pallas_call | solution.py:119
  33.3 5.2 %collective-permute-done.1 = bf16[64,2048]{1,0:T(8,128)(2,1)S(1)} collective-permute-done((bf16[64,2048]{1,0:T(8,128)(2,1)S(1)}, bf16[64,2048]{1,0:T(8,128)(2,1)S(1)}, u32[]{:S(2)}, u32[]{:S(2)}) %collective-permute-start.1) | collective-permute-done | bytes 262176 | tf_op jit(solution)/shard_map/far1/ppermute | solution.py:73
  56.0 3.9 %collective-permute-done.11 = bf16[128,2048]{1,0:T(8,128)(2,1)S(1)} collective-permute-done((bf16[128,2048]{1,0:T(8,128)(2,1)S(1)}, bf16[128,2048]{1,0:T(8,128)(2,1)S(1)}, u32[]{:S(2)}, u32[]{:S(2)}) %collective-permute-start.11) | collective-permute-done | bytes 524320 | tf_op jit(solution)/shard_map/arr1/ppermute | solution.py:93
  60.4 2.6 %a1.1 = bf16[2,256,1024]{2,1,0:T(8,128)(2,1)S(1)} custom-call(bf16[256,2048]{1,0:T(8,128)(2,1)S(1)} %pad_maximum_fusion.some, bf16[2,2048,1024]{2,1,0:T(8,128)(2,1)S(1)} %bitcast.11), custom_call_target="tpu_custom_call" | custom-call | flops 17179869184 | bytes 1 | tf_op jit(solution)/shard_map/a1/pallas_call | solution.py:148
  63.0 2.6 %c1.1 = bf16[2,256,1024]{2,1,0:T(8,128)(2,1)S(1)} custom-call(bf16[256,2048]{1,0:T(8,128)(2,1)S(1)} %pad_maximum_fusion.some, bf16[2,2048,1024]{2,1,0:T(8,128)(2,1)S(1)} %bitcast.9), custom_call_target="tpu_custom_call" | custom-call | flops 17179869184 | bytes 1 | tf_op jit(solution)/shard_map/c1/pallas_call | solution.py:148
  66.2 2.4 %b1.1 = (bf16[256,1024]{1,0:T(8,128)(2,1)S(1)}, bf16[256,1024]{1,0:T(8,128)(2,1)S(1)}) custom-call(bf16[256,2048]{1,0:T(8,128)(2,1)S(1)} %pad_maximum_fusion.some, bf16[2,2048,1024]{2,1,0:T(8,128)(2,1)S(1)} %load2.1.weights, bf16[2,256,1024]{2,1,0:T(8,128)(2,1)S(1)} %collective-permute-done.12.rest_0_), custom_call_target="tpu_custom_call" | custom-call | flops 17179869184 | bytes 1 | tf_op jit(solution)/shard_map/b1/pallas_call | solution.py:148
  68.7 4.3 %collective-permute-start.17 = (bf16[64,2048]{1,0:T(8,128)(2,1)S(1)}, bf16[64,2048]{1,0:T(8,128)(2,1)S(1)}, u32[]{:S(2)}, u32[]{:S(2)}) collective-permute-start(bf16[64,2048]{1,0:T(8,128)(2,1)S(1)} %pad_maximum_fusion.5), channel_id=1, source_target_pairs={{1,4},{3,6},{4,1},{6,3},{9,12},{11,14},{12,9},{14,11},{17,20},{19,... | collective-permute-start | bytes 786440 | tf_op jit(solution)/shard_map/arr2/ppermute | solution.py:93
  75.4 2.6 %d1.1.held = f32[2,256,1024]{2,1,0:T(8,128)S(1)} custom-call(bf16[256,2048]{1,0:T(8,128)(2,1)S(1)} %pad_maximum_fusion.some, bf16[2,2048,1024]{2,1,0:T(8,128)(2,1)S(1)} %load0.1.weights, bf16[2,256,1024]{2,1,0:T(8,128)(2,1)S(1)} %collective-permute-done.16.rest_0_), custom_call_target="tpu_custom_call" | custom-call | flops 17179869184 | bytes 1 | tf_op jit(solution)/shard_map/d1/pallas_call | solution.py:148
  87.7 4.0 %down0.1.weights = bf16[2,1024,2048]{2,1,0:T(8,128)(2,1)S(1)} custom-call(s32[2]{0:T(128)S(1)} %pad_add_fusion.1.quarters, bf16[4096,2048]{1,0:T(8,128)(2,1)} %weight.1), custom_call_target="tpu_custom_call" | custom-call | flops 17179869184 | bytes 1 | tf_op jit(solution)/shard_map/down0/pallas_call | solution.py:179
  91.8 2.4 %own0.1.rest_0_ = f32[128,2048]{1,0:T(8,128)S(1)} custom-call(bf16[128,1024]{1,0:T(8,128)(2,1)} %hide0.1.one, bf16[128,1024]{1,0:T(8,128)(2,1)S(1)} %collective-permute-done.22.two, bf16[2,1024,2048]{2,1,0:T(8,128)(2,1)S(1)} %down0.1.weights), custom_call_target="tpu_custom_call" | custom-call | flops 17179869184 | bytes 1 | tf_op jit(solution)/shard_map/own0/pallas_call | solution.py:202
  94.2 4.0 %down2.1.weights = bf16[2,1024,2048]{2,1,0:T(8,128)(2,1)S(1)} custom-call(s32[2]{0:T(128)S(1)} %pad_add_fusion.quarters, bf16[4096,2048]{1,0:T(8,128)(2,1)} %weight.1), custom_call_target="tpu_custom_call" | custom-call | flops 17179869184 | bytes 1 | tf_op jit(solution)/shard_map/down2/pallas_call | solution.py:179
  98.2 5.6 %collective-permute-done.23.got_up = bf16[256,1024]{1,0:T(8,128)(2,1)S(1)} collective-permute-done((bf16[256,1024]{1,0:T(8,128)(2,1)S(1)}, bf16[256,1024]{1,0:T(8,128)(2,1)S(1)}, u32[]{:S(2)}, u32[]{:S(2)}) %collective-permute-start.23) | collective-permute-done | bytes 524320 | tf_op jit(solution)/shard_map/b1/ppermute | solution.py:69
  105.4 2.7 %collective-permute-start.30 = (bf16[256,1024]{1,0:T(8,128)(2,1)S(1)}, bf16[256,1024]{1,0:T(8,128)(2,1)S(1)}, u32[]{:S(2)}, u32[]{:S(2)}) collective-permute-start(bf16[256,1024]{1,0:T(8,128)(2,1)S(1)} %hide1.1.one), channel_id=1, source_target_pairs={{0,1},{1,0},{2,3},{3,2},{4,5},{5,4},{6,7},{7,6},{8,9},{9,8},{10,11... | collective-permute-start | bytes 1572872 | tf_op jit(solution)/shard_map/hide1/ppermute | solution.py:69
  108.7 6.3 %collective-permute-done.24.got_up = bf16[128,1024]{1,0:T(8,128)(2,1)S(1)} collective-permute-done((bf16[128,1024]{1,0:T(8,128)(2,1)S(1)}, bf16[128,1024]{1,0:T(8,128)(2,1)S(1)}, u32[]{:S(2)}, u32[]{:S(2)}) %collective-permute-start.24) | collective-permute-done | bytes 262176 | tf_op jit(solution)/shard_map/b2/ppermute | solution.py:69
  115.2 2.5 %rest0.1 = f32[128,2048]{1,0:T(8,128)S(1)} custom-call(bf16[128,1024]{1,0:T(8,128)(2,1)} %collective-permute-done.27.one, bf16[128,1024]{1,0:T(8,128)(2,1)S(1)} %collective-permute-done.28.two, bf16[2,1024,2048]{2,1,0:T(8,128)(2,1)S(1)} %down2.1.weights, f32[128,2048]{1,0:T(8,128)S(1)} %own0.1.rest_0_), custom_call_target="tpu_custom_call" | custom-call | flops 17179869184 | bytes 1 | tf_op jit(solution)/shard_map/rest0/pallas_call | solution.py:202
  121.5 3.7 %collective-permute-start.31 = (bf16[64,2048]{1,0:T(8,128)(2,1)S(1)}, bf16[64,2048]{1,0:T(8,128)(2,1)S(1)}, u32[]{:S(2)}, u32[]{:S(2)}) collective-permute-start(bf16[64,2048]{1,0:T(8,128)(2,1)S(1)} %get-tuple-element.149), channel_id=1, source_target_pairs={{1,4},{3,6},{4,1},{6,3},{9,12},{11,14},{12,9},{14,11},{17,20},{19,... | collective-permute-start | bytes 786440 | tf_op jit(solution)/shard_map/out0/ppermute | solution.py:93
  125.2 2.6 %own1.1.rest_0_ = f32[256,2048]{1,0:T(8,128)S(1)} custom-call(bf16[256,1024]{1,0:T(8,128)(2,1)S(1)} %hide1.1.one, bf16[256,1024]{1,0:T(8,128)(2,1)S(1)} %collective-permute-done.30.two, bf16[2,1024,2048]{2,1,0:T(8,128)(2,1)S(1)} %down0.1.weights), custom_call_target="tpu_custom_call" | custom-call | flops 17179869184 | bytes 1 | tf_op jit(solution)/shard_map/own1/pallas_call | solution.py:202
  131.9 3.4 %collective-permute-done.32 = bf16[32,2048]{1,0:T(8,128)(2,1)S(1)} collective-permute-done((bf16[32,2048]{1,0:T(8,128)(2,1)S(1)}, bf16[32,2048]{1,0:T(8,128)(2,1)S(1)}, u32[]{:S(2)}, u32[]{:S(2)}) %collective-permute-start.32) | collective-permute-done | bytes 131104 | tf_op jit(solution)/shard_map/mix0/ppermute | solution.py:69
  137.4 2.6 %rest1.1 = f32[256,2048]{1,0:T(8,128)S(1)} custom-call(bf16[256,1024]{1,0:T(8,128)(2,1)S(1)} %collective-permute-done.26.one, bf16[256,1024]{1,0:T(8,128)(2,1)S(1)} %collective-permute-done.34.two, bf16[2,1024,2048]{2,1,0:T(8,128)(2,1)S(1)} %down2.1.weights, f32[256,2048]{1,0:T(8,128)S(1)} %own1.1.rest_0_), custom_call_target="tpu_custom_call" | custom-call | flops 17179869184 | bytes 1 | tf_op jit(solution)/shard_map/rest1/pallas_call | solution.py:202
  140.6 3.7 %collective-permute-done.35.got = bf16[32,2048]{1,0:T(8,128)(2,1)S(1)} collective-permute-done((bf16[32,2048]{1,0:T(8,128)(2,1)S(1)}, bf16[32,2048]{1,0:T(8,128)(2,1)S(1)}, u32[]{:S(2)}, u32[]{:S(2)}) %collective-permute-start.35) | collective-permute-done | bytes 131104 | tf_op jit(solution)/shard_map/far_out0/ppermute | solution.py:73
  148.6 3.7 %collective-permute-start.40 = (bf16[64,2048]{1,0:T(8,128)(2,1)S(1)}, bf16[64,2048]{1,0:T(8,128)(2,1)S(1)}, u32[]{:S(2)}, u32[]{:S(2)}) collective-permute-start(bf16[64,2048]{1,0:T(8,128)(2,1)S(1)} %get-tuple-element.147), channel_id=1, source_target_pairs={{1,4},{3,6},{4,1},{6,3},{9,12},{11,14},{12,9},{14,11},{17,20},{19,... | collective-permute-start | bytes 786440 | tf_op jit(solution)/shard_map/out2/ppermute | solution.py:93
  152.2 4.0 %collective-permute-done.39 = bf16[128,2048]{1,0:T(8,128)(2,1)S(1)} collective-permute-done((bf16[128,2048]{1,0:T(8,128)(2,1)S(1)}, bf16[128,2048]{1,0:T(8,128)(2,1)S(1)}, u32[]{:S(2)}, u32[]{:S(2)}) %collective-permute-start.39) | collective-permute-done | bytes 524320 | tf_op jit(solution)/shard_map/out1/ppermute | solution.py:93
  157.0 4.5 %collective-permute-done.40 = bf16[64,2048]{1,0:T(8,128)(2,1)S(1)} collective-permute-done((bf16[64,2048]{1,0:T(8,128)(2,1)S(1)}, bf16[64,2048]{1,0:T(8,128)(2,1)S(1)}, u32[]{:S(2)}, u32[]{:S(2)}) %collective-permute-start.40) | collective-permute-done | bytes 262176 | tf_op jit(solution)/shard_map/out2/ppermute | solution.py:93
  163.0 2.8 %collective-permute-done.41 = bf16[32,2048]{1,0:T(8,128)(2,1)S(1)} collective-permute-done((bf16[32,2048]{1,0:T(8,128)(2,1)S(1)}, bf16[32,2048]{1,0:T(8,128)(2,1)S(1)}, u32[]{:S(2)}, u32[]{:S(2)}) %collective-permute-start.41) | collective-permute-done | bytes 131104 | tf_op jit(solution)/shard_map/mix2/ppermute | solution.py:69
  166.4 10.8 %collective-permute-done.44.got = bf16[64,2048]{1,0:T(8,128)(2,1)S(1)} collective-permute-done((bf16[64,2048]{1,0:T(8,128)(2,1)S(1)}, bf16[64,2048]{1,0:T(8,128)(2,1)S(1)}, u32[]{:S(2)}, u32[]{:S(2)}) %collective-permute-start.44) | collective-permute-done | bytes 262176 | tf_op jit(solution)/shard_map/far_out1/ppermute | solution.py:73
  (139 shorter events, 58.7 us)
Async XLA Ops:
  2.8 17.0 %collective-permute-start = (bf16[32,2048]{1,0:T(8,128)(2,1)S(1)}, bf16[32,2048]{1,0:T(8,128)(2,1)S(1)}, u32[]{:S(2)}, u32[]{:S(2)}) collective-permute-start(bf16[32,2048]{1,0:T(8,128)(2,1)S(1)} %get-tuple-element.75), channel_id=1, source_target_pairs={{0,8},{4,12},{8,0},{12,4},{1,9},{5,13},{9,1},{13,5},{2,10},{6,14},... | collective-permute-start | bytes 393224 | tf_op jit(solution)/shard_map/far0/ppermute | solution.py:73
  24.6 13.8 %collective-permute-start.1 = (bf16[64,2048]{1,0:T(8,128)(2,1)S(1)}, bf16[64,2048]{1,0:T(8,128)(2,1)S(1)}, u32[]{:S(2)}, u32[]{:S(2)}) collective-permute-start(bf16[64,2048]{1,0:T(8,128)(2,1)S(1)} %get-tuple-element.79), channel_id=1, source_target_pairs={{0,8},{4,12},{8,0},{12,4},{1,9},{5,13},{9,1},{13,5},{2,10},{6,14},... | collective-permute-start | bytes 786440 | tf_op jit(solution)/shard_map/far1/ppermute | solution.py:73
  24.8 14.0 %collective-permute-start.4 = (bf16[64,2048]{1,0:T(8,128)(2,1)S(1)}, bf16[64,2048]{1,0:T(8,128)(2,1)S(1)}, u32[]{:S(2)}, u32[]{:S(2)}) collective-permute-start(bf16[64,2048]{1,0:T(8,128)(2,1)S(1)} %pad_maximum_fusion.4), channel_id=1, source_target_pairs={{0,4},{1,0},{2,6},{3,2},{4,5},{5,1},{6,7},{7,3},{8,12},{9,8},{10,1... | collective-permute-start | bytes 786440 | tf_op jit(solution)/shard_map/arr0/ppermute | solution.py:93
  26.4 12.4 %collective-permute-start.5 = (bf16[64,2048]{1,0:T(8,128)(2,1)S(1)}, bf16[64,2048]{1,0:T(8,128)(2,1)S(1)}, u32[]{:S(2)}, u32[]{:S(2)}) collective-permute-start(bf16[64,2048]{1,0:T(8,128)(2,1)S(1)} %pad_maximum_fusion.4), channel_id=1, source_target_pairs={{1,4},{3,6},{4,1},{6,3},{9,12},{11,14},{12,9},{14,11},{17,20},{19,... | collective-permute-start | bytes 786440 | tf_op jit(solution)/shard_map/arr0/ppermute | solution.py:93
  38.8 15.2 %collective-permute-start.3 = (bf16[32,2048]{1,0:T(8,128)(2,1)S(1)}, bf16[32,2048]{1,0:T(8,128)(2,1)S(1)}, u32[]{:S(2)}, u32[]{:S(2)}) collective-permute-start(bf16[32,2048]{1,0:T(8,128)(2,1)S(1)} %get-tuple-element.84), channel_id=1, source_target_pairs={{0,8},{4,12},{8,0},{12,4},{1,9},{5,13},{9,1},{13,5},{2,10},{6,14},... | collective-permute-start | bytes 393224 | tf_op jit(solution)/shard_map/far2/ppermute | solution.py:73
  40.6 9.1 %collective-permute-start.7 = (bf16[2,128,1024]{2,1,0:T(8,128)(2,1)S(1)}, bf16[2,128,1024]{2,1,0:T(8,128)(2,1)S(1)}, u32[]{:S(2)}, u32[]{:S(2)}) collective-permute-start(bf16[2,128,1024]{2,1,0:T(8,128)(2,1)S(1)} %a0.1), channel_id=1, source_target_pairs={{0,1},{1,0},{2,3},{3,2},{4,5},{5,4},{6,7},{7,6},{8,9},{9,8},{10,11... | collective-permute-start | bytes 1572872 | tf_op jit(solution)/shard_map/a0/ppermute | solution.py:69
  46.0 10.1 %collective-permute-start.10 = (bf16[128,2048]{1,0:T(8,128)(2,1)S(1)}, bf16[128,2048]{1,0:T(8,128)(2,1)S(1)}, u32[]{:S(2)}, u32[]{:S(2)}) collective-permute-start(bf16[128,2048]{1,0:T(8,128)(2,1)S(1)} %pad_maximum_fusion.2), channel_id=1, source_target_pairs={{0,4},{1,0},{2,6},{3,2},{4,5},{5,1},{6,7},{7,3},{8,12},{9,8},{10,1... | collective-permute-start | bytes 1572872 | tf_op jit(solution)/shard_map/arr1/ppermute | solution.py:93
  47.4 12.5 %collective-permute-start.11 = (bf16[128,2048]{1,0:T(8,128)(2,1)S(1)}, bf16[128,2048]{1,0:T(8,128)(2,1)S(1)}, u32[]{:S(2)}, u32[]{:S(2)}) collective-permute-start(bf16[128,2048]{1,0:T(8,128)(2,1)S(1)} %pad_maximum_fusion.2), channel_id=1, source_target_pairs={{1,4},{3,6},{4,1},{6,3},{9,12},{11,14},{12,9},{14,11},{17,20},{19,... | collective-permute-start | bytes 1572872 | tf_op jit(solution)/shard_map/arr1/ppermute | solution.py:93
  51.1 21.9 %collective-permute-start.14 = (bf16[128,1024]{1,0:T(8,128)(2,1)S(1)}, bf16[128,1024]{1,0:T(8,128)(2,1)S(1)}, u32[]{:S(2)}, u32[]{:S(2)}) collective-permute-start(bf16[128,1024]{1,0:T(8,128)(2,1)S(1)} %get-tuple-element.90), channel_id=1, source_target_pairs={{0,2},{1,3},{2,0},{3,1},{4,6},{5,7},{6,4},{7,5},{8,10},{9,11},{10,... | collective-permute-start | bytes 786440 | tf_op jit(solution)/shard_map/b0/ppermute | solution.py:69
  54.0 14.5 %collective-permute-start.9 = (bf16[32,2048]{1,0:T(8,128)(2,1)S(1)}, bf16[32,2048]{1,0:T(8,128)(2,1)S(1)}, u32[]{:S(2)}, u32[]{:S(2)}) collective-permute-start(bf16[32,2048]{1,0:T(8,128)(2,1)S(1)} %broadcast_select_fusion.20), channel_id=1, source_target_pairs={{0,2},{1,3},{2,0},{3,1},{4,6},{5,7},{6,4},{7,5},{8,10},{9,11},{10,... | collective-permute-start | bytes 393224 | tf_op jit(solution)/shard_map/sel2/ppermute | solution.py:69
  54.3 18.7 %collective-permute-start.15 = (bf16[128,1024]{1,0:T(8,128)(2,1)S(1)}, bf16[128,1024]{1,0:T(8,128)(2,1)S(1)}, u32[]{:S(2)}, u32[]{:S(2)}) collective-permute-start(bf16[128,1024]{1,0:T(8,128)(2,1)S(1)} %get-tuple-element.100), channel_id=1, source_target_pairs={{0,2},{1,3},{2,0},{3,1},{4,6},{5,7},{6,4},{7,5},{8,10},{9,11},{10,... | collective-permute-start | bytes 786440 | tf_op jit(solution)/shard_map/b0/ppermute | solution.py:69
  65.6 9.6 %collective-permute-start.16 = (bf16[2,256,1024]{2,1,0:T(8,128)(2,1)S(1)}, bf16[2,256,1024]{2,1,0:T(8,128)(2,1)S(1)}, u32[]{:S(2)}, u32[]{:S(2)}) collective-permute-start(bf16[2,256,1024]{2,1,0:T(8,128)(2,1)S(1)} %c1.1), channel_id=1, source_target_pairs={{0,1},{1,0},{2,3},{3,2},{4,5},{5,4},{6,7},{7,6},{8,9},{9,8},{10,11... | collective-permute-start | bytes 3145736 | tf_op jit(solution)/shard_map/c1/ppermute | solution.py:69
  68.6 9.3 %collective-permute-start.13 = (bf16[64,2048]{1,0:T(8,128)(2,1)S(1)}, bf16[64,2048]{1,0:T(8,128)(2,1)S(1)}, u32[]{:S(2)}, u32[]{:S(2)}) collective-permute-start(bf16[64,2048]{1,0:T(8,128)(2,1)S(1)} %pad_maximum_fusion.5), channel_id=1, source_target_pairs={{0,4},{1,0},{2,6},{3,2},{4,5},{5,1},{6,7},{7,3},{8,12},{9,8},{10,1... | collective-permute-start | bytes 786440 | tf_op jit(solution)/shard_map/arr2/ppermute | solution.py:93
  68.7 10.6 %collective-permute-start.17 = (bf16[64,2048]{1,0:T(8,128)(2,1)S(1)}, bf16[64,2048]{1,0:T(8,128)(2,1)S(1)}, u32[]{:S(2)}, u32[]{:S(2)}) collective-permute-start(bf16[64,2048]{1,0:T(8,128)(2,1)S(1)} %pad_maximum_fusion.5), channel_id=1, source_target_pairs={{1,4},{3,6},{4,1},{6,3},{9,12},{11,14},{12,9},{14,11},{17,20},{19,... | collective-permute-start | bytes 786440 | tf_op jit(solution)/shard_map/arr2/ppermute | solution.py:93
  73.9 17.8 %collective-permute-start.22 = (bf16[128,1024]{1,0:T(8,128)(2,1)}, bf16[128,1024]{1,0:T(8,128)(2,1)S(1)}, u32[]{:S(2)}, u32[]{:S(2)}) collective-permute-start(bf16[128,1024]{1,0:T(8,128)(2,1)} %hide0.1.one), channel_id=1, source_target_pairs={{0,1},{1,0},{2,3},{3,2},{4,5},{5,4},{6,7},{7,6},{8,9},{9,8},{10,11... | collective-permute-start | bytes 786440 | tf_op jit(solution)/shard_map/hide0/ppermute | solution.py:69
  73.9 29.8 %collective-permute-start.21 = (bf16[256,1024]{1,0:T(8,128)(2,1)S(1)}, bf16[256,1024]{1,0:T(8,128)(2,1)S(1)}, u32[]{:S(2)}, u32[]{:S(2)}) collective-permute-start(bf16[256,1024]{1,0:T(8,128)(2,1)S(1)} %get-tuple-element.97), channel_id=1, source_target_pairs={{0,2},{1,3},{2,0},{3,1},{4,6},{5,7},{6,4},{7,5},{8,10},{9,11},{10,... | collective-permute-start | bytes 1572872 | tf_op jit(solution)/shard_map/b1/ppermute | solution.py:69
  75.2 33.1 %collective-permute-start.27 = (bf16[128,1024]{1,0:T(8,128)(2,1)}, bf16[128,1024]{1,0:T(8,128)(2,1)}, u32[]{:S(2)}, u32[]{:S(2)}) collective-permute-start(bf16[128,1024]{1,0:T(8,128)(2,1)} %hide0.1.one), channel_id=1, source_target_pairs={{0,2},{1,3},{2,0},{3,1},{4,6},{5,7},{6,4},{7,5},{8,10},{9,11},{10,... | collective-permute-start | bytes 786440 | tf_op jit(solution)/shard_map/hide0/ppermute | solution.py:69
  78.0 25.8 %collective-permute-start.23 = (bf16[256,1024]{1,0:T(8,128)(2,1)S(1)}, bf16[256,1024]{1,0:T(8,128)(2,1)S(1)}, u32[]{:S(2)}, u32[]{:S(2)}) collective-permute-start(bf16[256,1024]{1,0:T(8,128)(2,1)S(1)} %get-tuple-element.113), channel_id=1, source_target_pairs={{0,2},{1,3},{2,0},{3,1},{4,6},{5,7},{6,4},{7,5},{8,10},{9,11},{10,... | collective-permute-start | bytes 1572872 | tf_op jit(solution)/shard_map/b1/ppermute | solution.py:69
  86.0 29.1 %collective-permute-start.20 = (bf16[128,1024]{1,0:T(8,128)(2,1)S(1)}, bf16[128,1024]{1,0:T(8,128)(2,1)S(1)}, u32[]{:S(2)}, u32[]{:S(2)}) collective-permute-start(bf16[128,1024]{1,0:T(8,128)(2,1)S(1)} %get-tuple-element.107), channel_id=1, source_target_pairs={{0,2},{1,3},{2,0},{3,1},{4,6},{5,7},{6,4},{7,5},{8,10},{9,11},{10,... | collective-permute-start | bytes 786440 | tf_op jit(solution)/shard_map/b2/ppermute | solution.py:69
  103.8 11.2 %collective-permute-start.24 = (bf16[128,1024]{1,0:T(8,128)(2,1)S(1)}, bf16[128,1024]{1,0:T(8,128)(2,1)S(1)}, u32[]{:S(2)}, u32[]{:S(2)}) collective-permute-start(bf16[128,1024]{1,0:T(8,128)(2,1)S(1)} %get-tuple-element.116), channel_id=1, source_target_pairs={{0,2},{1,3},{2,0},{3,1},{4,6},{5,7},{6,4},{7,5},{8,10},{9,11},{10,... | collective-permute-start | bytes 786440 | tf_op jit(solution)/shard_map/b2/ppermute | solution.py:69
  105.4 16.0 %collective-permute-start.30 = (bf16[256,1024]{1,0:T(8,128)(2,1)S(1)}, bf16[256,1024]{1,0:T(8,128)(2,1)S(1)}, u32[]{:S(2)}, u32[]{:S(2)}) collective-permute-start(bf16[256,1024]{1,0:T(8,128)(2,1)S(1)} %hide1.1.one), channel_id=1, source_target_pairs={{0,1},{1,0},{2,3},{3,2},{4,5},{5,4},{6,7},{7,6},{8,9},{9,8},{10,11... | collective-permute-start | bytes 1572872 | tf_op jit(solution)/shard_map/hide1/ppermute | solution.py:69
  108.1 22.3 %collective-permute-start.26 = (bf16[256,1024]{1,0:T(8,128)(2,1)S(1)}, bf16[256,1024]{1,0:T(8,128)(2,1)S(1)}, u32[]{:S(2)}, u32[]{:S(2)}) collective-permute-start(bf16[256,1024]{1,0:T(8,128)(2,1)S(1)} %hide1.1.one), channel_id=1, source_target_pairs={{0,2},{1,3},{2,0},{3,1},{4,6},{5,7},{6,4},{7,5},{8,10},{9,11},{10,... | collective-permute-start | bytes 1572872 | tf_op jit(solution)/shard_map/hide1/ppermute | solution.py:69
  117.8 10.0 %collective-permute-start.29 = (bf16[64,2048]{1,0:T(8,128)(2,1)S(1)}, bf16[64,2048]{1,0:T(8,128)(2,1)S(1)}, u32[]{:S(2)}, u32[]{:S(2)}) collective-permute-start(bf16[64,2048]{1,0:T(8,128)(2,1)S(1)} %get-tuple-element.148), channel_id=1, source_target_pairs={{0,1},{1,5},{2,3},{3,7},{4,0},{5,4},{6,2},{7,6},{8,9},{9,13},{10,1... | collective-permute-start | bytes 786440 | tf_op jit(solution)/shard_map/out0/ppermute | solution.py:93
  118.5 11.8 %collective-permute-start.33 = (bf16[128,1024]{1,0:T(8,128)(2,1)S(1)}, bf16[128,1024]{1,0:T(8,128)(2,1)S(1)}, u32[]{:S(2)}, u32[]{:S(2)}) collective-permute-start(bf16[128,1024]{1,0:T(8,128)(2,1)S(1)} %hide2.1.one), channel_id=1, source_target_pairs={{0,1},{1,0},{2,3},{3,2},{4,5},{5,4},{6,7},{7,6},{8,9},{9,8},{10,11... | collective-permute-start | bytes 786440 | tf_op jit(solution)/shard_map/hide2/ppermute | solution.py:69
  120.2 24.1 %collective-permute-start.25 = (bf16[128,1024]{1,0:T(8,128)(2,1)S(1)}, bf16[128,1024]{1,0:T(8,128)(2,1)S(1)}, u32[]{:S(2)}, u32[]{:S(2)}) collective-permute-start(bf16[128,1024]{1,0:T(8,128)(2,1)S(1)} %hide2.1.one), channel_id=1, source_target_pairs={{0,2},{1,3},{2,0},{3,1},{4,6},{5,7},{6,4},{7,5},{8,10},{9,11},{10,... | collective-permute-start | bytes 786440 | tf_op jit(solution)/shard_map/hide2/ppermute | solution.py:69
  135.3 9.0 %collective-permute-start.35 = (bf16[32,2048]{1,0:T(8,128)(2,1)S(1)}, bf16[32,2048]{1,0:T(8,128)(2,1)S(1)}, u32[]{:S(2)}, u32[]{:S(2)}) collective-permute-start(bf16[32,2048]{1,0:T(8,128)(2,1)S(1)} %convert_select_fusion.5), channel_id=1, source_target_pairs={{0,8},{4,12},{8,0},{12,4},{1,9},{5,13},{9,1},{13,5},{2,10},{6,14},... | collective-permute-start | bytes 393224 | tf_op jit(solution)/shard_map/far_out0/ppermute | solution.py:73
  140.1 12.1 %collective-permute-start.38 = (bf16[128,2048]{1,0:T(8,128)(2,1)S(1)}, bf16[128,2048]{1,0:T(8,128)(2,1)S(1)}, u32[]{:S(2)}, u32[]{:S(2)}) collective-permute-start(bf16[128,2048]{1,0:T(8,128)(2,1)S(1)} %get-tuple-element.143), channel_id=1, source_target_pairs={{0,1},{1,5},{2,3},{3,7},{4,0},{5,4},{6,2},{7,6},{8,9},{9,13},{10,1... | collective-permute-start | bytes 1572872 | tf_op jit(solution)/shard_map/out1/ppermute | solution.py:93
  145.0 11.2 %collective-permute-start.39 = (bf16[128,2048]{1,0:T(8,128)(2,1)S(1)}, bf16[128,2048]{1,0:T(8,128)(2,1)S(1)}, u32[]{:S(2)}, u32[]{:S(2)}) collective-permute-start(bf16[128,2048]{1,0:T(8,128)(2,1)S(1)} %get-tuple-element.142), channel_id=1, source_target_pairs={{1,4},{3,6},{4,1},{6,3},{9,12},{11,14},{12,9},{14,11},{17,20},{19,... | collective-permute-start | bytes 1572872 | tf_op jit(solution)/shard_map/out1/ppermute | solution.py:93
  148.5 8.5 %collective-permute-start.37 = (bf16[64,2048]{1,0:T(8,128)(2,1)S(1)}, bf16[64,2048]{1,0:T(8,128)(2,1)S(1)}, u32[]{:S(2)}, u32[]{:S(2)}) collective-permute-start(bf16[64,2048]{1,0:T(8,128)(2,1)S(1)} %get-tuple-element.146), channel_id=1, source_target_pairs={{0,1},{1,5},{2,3},{3,7},{4,0},{5,4},{6,2},{7,6},{8,9},{9,13},{10,1... | collective-permute-start | bytes 786440 | tf_op jit(solution)/shard_map/out2/ppermute | solution.py:93
  148.6 12.9 %collective-permute-start.40 = (bf16[64,2048]{1,0:T(8,128)(2,1)S(1)}, bf16[64,2048]{1,0:T(8,128)(2,1)S(1)}, u32[]{:S(2)}, u32[]{:S(2)}) collective-permute-start(bf16[64,2048]{1,0:T(8,128)(2,1)S(1)} %get-tuple-element.147), channel_id=1, source_target_pairs={{1,4},{3,6},{4,1},{6,3},{9,12},{11,14},{12,9},{14,11},{17,20},{19,... | collective-permute-start | bytes 786440 | tf_op jit(solution)/shard_map/out2/ppermute | solution.py:93
  162.3 15.0 %collective-permute-start.44 = (bf16[64,2048]{1,0:T(8,128)(2,1)S(1)}, bf16[64,2048]{1,0:T(8,128)(2,1)S(1)}, u32[]{:S(2)}, u32[]{:S(2)}) collective-permute-start(bf16[64,2048]{1,0:T(8,128)(2,1)S(1)} %convert_select_fusion.2), channel_id=1, source_target_pairs={{0,8},{4,12},{8,0},{12,4},{1,9},{5,13},{9,1},{13,5},{2,10},{6,14},... | collective-permute-start | bytes 786440 | tf_op jit(solution)/shard_map/far_out1/ppermute | solution.py:73
  165.9 13.0 %collective-permute-start.43 = (bf16[32,2048]{1,0:T(8,128)(2,1)S(1)}, bf16[32,2048]{1,0:T(8,128)(2,1)S(1)}, u32[]{:S(2)}, u32[]{:S(2)}) collective-permute-start(bf16[32,2048]{1,0:T(8,128)(2,1)S(1)} %convert_select_fusion.4), channel_id=1, source_target_pairs={{0,8},{4,12},{8,0},{12,4},{1,9},{5,13},{9,1},{13,5},{2,10},{6,14},... | collective-permute-start | bytes 393224 | tf_op jit(solution)/shard_map/far_out2/ppermute | solution.py:73
  (21 other events, 112.8 us)

commit v3 on v2

--- a/solution.py
+++ b/solution.py
@@ -7,16 +7,17 @@
 from jax.experimental.pallas import tpu as pltpu
 from jax.sharding import PartitionSpec as P
 
-ROWS = (32, 64, 32)
+ROWS = (32, 48, 48)
 ORDER = (
     "far0", "load3", "load1", "sel0", "far1", "load2", "arr0", "load0", "sel1", "far2", "take0", "a0", "c0",
-    "arr1", "b0", "d0", "sel2", "take1", "a1", "c1", "b1", "arr2", "hide0", "d1", "take2", "a2", "c2", "b2",
-    "d2", "down0", "own0", "down2", "hide1", "forward0", "hide2", "rest0", "out0", "own1", "mix0", "forward1",
-    "own2", "far_out0", "rest1", "forward2", "out1", "end0", "rest2", "out2", "mix1", "mix2", "far_out1",
+    "arr1", "b0", "d0", "sel2", "take1", "a1", "c1", "b1", "arr2", "d1", "hide0", "take2", "a2", "c2", "b2",
+    "d2", "down0", "own0", "forward0", "down2", "rest0", "out0", "hide1", "mix0", "hide2", "far_out0", "own1",
+    "forward1", "own2", "rest1", "out1", "forward2", "end0", "rest2", "out2", "mix1", "mix2", "far_out1",
     "far_out2", "end1", "end2",
 )
 TILE = 256
 COST = 1 << 34
+LOAD_COST = 1 << 30
 VMEM = 10 << 20
 
 
@@ -123,7 +124,7 @@
         out_specs=pl.BlockSpec(memory_space=pltpu.VMEM),
         scratch_shapes=[pltpu.SemaphoreType.DMA((2, 4))],
         compiler_params=pltpu.CompilerParams(vmem_limit_bytes=VMEM),
-        cost_estimate=pl.CostEstimate(flops=COST, bytes_accessed=1, transcendentals=0),
+        cost_estimate=pl.CostEstimate(flops=LOAD_COST, bytes_accessed=1, transcendentals=0),
     )(quarter.reshape(1).astype(jnp.int32), gate_weight, up_weight)
 
 
@@ -227,7 +228,7 @@
         in_specs=[near] * 2,
         out_specs=[near] * count,
         compiler_params=pltpu.CompilerParams(vmem_limit_bytes=VMEM),
-        cost_estimate=pl.CostEstimate(flops=COST, bytes_accessed=1, transcendentals=0),
+        cost_estimate=pl.CostEstimate(flops=LOAD_COST, bytes_accessed=1, transcendentals=0),
     )(values, scales.T)
 
 

time: 180 us -> 172 us (0.956)
  waiting for transfers between devices: 54.2 us -> 49.7 us
  Pallas kernels: 60.3 us -> 56.6 us
    ppermute x12, waiting for transfers between devices: 14.7 us -> 28.1 us  [over_both(): return lax.ppermute(array, ('tp', 'seq'), pairs)]
    ppermute x6, waiting for transfers between devices: 21 us -> 8.68 us  [over_tp(): return lax.ppermute(array, 'tp', [(i, i ^ bit) for i in range(4)])]
    ppermute x6, starting transfers between devices: 6.57 us -> 12.8 us  [over_tp(): return lax.ppermute(array, 'tp', [(i, i ^ bit) for i in range(4)])]
    ppermute x27, waiting for transfers between devices: 18.4 us -> 12.9 us  [over_seq(): return lax.ppermute(array, 'seq', [(i, i ^ bit) for i in range(4)])]
    ppermute x12, starting transfers between devices: 23.8 us -> 19.1 us  [over_both(): return lax.ppermute(array, ('tp', 'seq'), pairs)]
    ppermute x27, starting transfers between devices: 23.1 us -> 20.3 us  [over_seq(): return lax.ppermute(array, 'seq', [(i, i ^ bit) for i in range(4)])]
    pallas_call x6, Pallas kernels: 13 us -> 10.8 us  [products(): pl.pallas_call(functools.partial(products_kernel, total is not None), out...]
  transfers between devices with their start and end apart: 45 -> 45, of which waited for: 14 -> 17; matrix products, arithmetic and copies ran while one was open for 1% -> 1% of each run, Pallas kernels for 33% -> 32%
where the time goes in v3:
time: 172 us
  Pallas kernels  56.6 us (33%)
  starting transfers between devices  52.2 us (30%)
  waiting for transfers between devices  49.7 us (29%)
  local copies, waits for them, and re-layouts  10.1 us (6%)
  other arithmetic  2.14 us (1%)
    ppermute x12, waiting for transfers between devices, over_both(): return lax.ppermute(array, ('tp', 'seq'), pairs)  28.1 us
    pallas_call x12, Pallas kernels, sums(): pl.pallas_call(functools.partial(sums_kernel, got is not None, split), ou...  21.1 us
    ppermute x27, starting transfers between devices, over_seq(): return lax.ppermute(array, 'seq', [(i, i ^ bit) for i in range(4)])  20.3 us
    ppermute x12, starting transfers between devices, over_both(): return lax.ppermute(array, ('tp', 'seq'), pairs)  19.1 us
    pallas_call x4, Pallas kernels, load(): pl.pallas_call(load_kernel, out_shape=jax.ShapeDtypeStruct((2, deep, widt...  14 us
    ppermute x27, waiting for transfers between devices, over_seq(): return lax.ppermute(array, 'seq', [(i, i ^ bit) for i in range(4)])  12.9 us
    ppermute x6, starting transfers between devices, over_tp(): return lax.ppermute(array, 'tp', [(i, i ^ bit) for i in range(4)])  12.8 us
    pallas_call x6, Pallas kernels, products(): pl.pallas_call(functools.partial(products_kernel, total is not None), out...  10.8 us
  transfers between devices with their start and end apart: 45, of which 17 were waited for; matrix products, arithmetic and copies ran while one was open for 1% of the time, Pallas kernels for 32%

profile of v3, /device:TPU:1, one launch (start us, length us, event | category | flops | bytes accessed | tf_op | source)
XLA Modules:
  0.0 172.0 jit_solution(18094956038137278405)
XLA Ops:
  2.8 3.2 %collective-permute-start = (bf16[32,2048]{1,0:T(8,128)(2,1)S(1)}, bf16[32,2048]{1,0:T(8,128)(2,1)S(1)}, u32[]{:S(2)}, u32[]{:S(2)}) collective-permute-start(bf16[32,2048]{1,0:T(8,128)(2,1)S(1)} %get-tuple-element.74), channel_id=1, source_target_pairs={{0,8},{4,12},{8,0},{12,4},{1,9},{5,13},{9,1},{13,5},{2,10},{6,14},... | collective-permute-start | bytes 393224 | tf_op jit(solution)/shard_map/far0/ppermute | solution.py:74
  6.0 3.5 %load3.1.weights = bf16[2,2048,1024]{2,1,0:T(8,128)(2,1)S(1)} custom-call(s32[1]{0:T(128)} %bitcast.2.quarter, bf16[2048,4096]{1,0:T(8,128)(2,1)} %gate_weight.3, bf16[2048,4096]{1,0:T(8,128)(2,1)} %up_weight.7), custom_call_target="tpu_custom_call" | custom-call | flops 1073741824 | bytes 1 | tf_op jit(solution)/shard_map/load3/pallas_call | solution.py:120
  9.6 3.3 %copy-done.1 = bf16[2,2048,1024]{2,1,0:T(8,128)(2,1)} copy-done((bf16[2,2048,1024]{2,1,0:T(8,128)(2,1)}, bf16[2,2048,1024]{2,1,0:T(8,128)(2,1)S(1)}, u32[]{:S(2)}) %copy-start.1) | copy-done | bytes 8388632
  12.8 3.5 %load1.1.weights = bf16[2,2048,1024]{2,1,0:T(8,128)(2,1)S(1)} custom-call(s32[1]{0:T(128)} %bitcast.1.quarter, bf16[2048,4096]{1,0:T(8,128)(2,1)} %gate_weight.3, bf16[2048,4096]{1,0:T(8,128)(2,1)} %up_weight.7), custom_call_target="tpu_custom_call" | custom-call | flops 1073741824 | bytes 1 | tf_op jit(solution)/shard_map/load1/pallas_call | solution.py:120
  16.4 3.3 %copy-done = bf16[2,2048,1024]{2,1,0:T(8,128)(2,1)} copy-done((bf16[2,2048,1024]{2,1,0:T(8,128)(2,1)}, bf16[2,2048,1024]{2,1,0:T(8,128)(2,1)S(1)}, u32[]{:S(2)}) %copy-start) | copy-done | bytes 8388632
  21.2 3.5 %load2.1.weights = bf16[2,2048,1024]{2,1,0:T(8,128)(2,1)S(1)} custom-call(s32[1]{0:T(128)} %bitcast.4.quarter, bf16[2048,4096]{1,0:T(8,128)(2,1)} %gate_weight.3, bf16[2048,4096]{1,0:T(8,128)(2,1)} %up_weight.7), custom_call_target="tpu_custom_call" | custom-call | flops 1073741824 | bytes 1 | tf_op jit(solution)/shard_map/load2/pallas_call | solution.py:120
  24.8 4.9 %collective-permute-start.5 = (bf16[64,2048]{1,0:T(8,128)(2,1)S(1)}, bf16[64,2048]{1,0:T(8,128)(2,1)S(1)}, u32[]{:S(2)}, u32[]{:S(2)}) collective-permute-start(bf16[64,2048]{1,0:T(8,128)(2,1)S(1)} %pad_maximum_fusion.5), channel_id=1, source_target_pairs={{1,4},{3,6},{4,1},{6,3},{9,12},{11,14},{12,9},{14,11},{17,20},{19,... | collective-permute-start | bytes 786440 | tf_op jit(solution)/shard_map/arr0/ppermute | solution.py:94
  29.7 3.5 %load0.1.weights = bf16[2,2048,1024]{2,1,0:T(8,128)(2,1)S(1)} custom-call(s32[1]{0:T(128)} %bitcast.3.quarter, bf16[2048,4096]{1,0:T(8,128)(2,1)} %gate_weight.3, bf16[2048,4096]{1,0:T(8,128)(2,1)} %up_weight.7), custom_call_target="tpu_custom_call" | custom-call | flops 1073741824 | bytes 1 | tf_op jit(solution)/shard_map/load0/pallas_call | solution.py:120
  35.9 4.2 %collective-permute-done.4 = bf16[64,2048]{1,0:T(8,128)(2,1)S(1)} collective-permute-done((bf16[64,2048]{1,0:T(8,128)(2,1)S(1)}, bf16[64,2048]{1,0:T(8,128)(2,1)S(1)}, u32[]{:S(2)}, u32[]{:S(2)}) %collective-permute-start.4) | collective-permute-done | bytes 262176 | tf_op jit(solution)/shard_map/arr0/ppermute | solution.py:94
  47.2 2.1 %collective-permute-start.8 = (bf16[2,128,1024]{2,1,0:T(8,128)(2,1)S(1)}, bf16[2,128,1024]{2,1,0:T(8,128)(2,1)S(1)}, u32[]{:S(2)}, u32[]{:S(2)}) collective-permute-start(bf16[2,128,1024]{2,1,0:T(8,128)(2,1)S(1)} %c0.1), channel_id=1, source_target_pairs={{0,1},{1,0},{2,3},{3,2},{4,5},{5,4},{6,7},{7,6},{8,9},{9,8},{10,11... | collective-permute-start | bytes 1572872 | tf_op jit(solution)/shard_map/c0/ppermute | solution.py:70
  53.7 4.2 %collective-permute-done.10 = bf16[96,2048]{1,0:T(8,128)(2,1)S(1)} collective-permute-done((bf16[96,2048]{1,0:T(8,128)(2,1)S(1)}, bf16[96,2048]{1,0:T(8,128)(2,1)S(1)}, u32[]{:S(2)}, u32[]{:S(2)}) %collective-permute-start.10) | collective-permute-done | bytes 393248 | tf_op jit(solution)/shard_map/arr1/ppermute | solution.py:94
  60.7 2.0 %c1.1 = bf16[2,192,1024]{2,1,0:T(8,128)(2,1)S(1)} custom-call(bf16[192,2048]{1,0:T(8,128)(2,1)S(1)} %pad_maximum_fusion.some, bf16[2,2048,1024]{2,1,0:T(8,128)(2,1)S(1)} %bitcast.8), custom_call_target="tpu_custom_call" | custom-call | flops 17179869184 | bytes 1 | tf_op jit(solution)/shard_map/c1/pallas_call | solution.py:149
  65.1 2.2 %collective-permute-start.17 = (bf16[96,2048]{1,0:T(8,128)(2,1)S(1)}, bf16[96,2048]{1,0:T(8,128)(2,1)S(1)}, u32[]{:S(2)}, u32[]{:S(2)}) collective-permute-start(bf16[96,2048]{1,0:T(8,128)(2,1)S(1)} %pad_maximum_fusion.4), channel_id=1, source_target_pairs={{1,4},{3,6},{4,1},{6,3},{9,12},{11,14},{12,9},{14,11},{17,20},{19,... | collective-permute-start | bytes 1179656 | tf_op jit(solution)/shard_map/arr2/ppermute | solution.py:94
  67.6 2.0 %d1.1.held = f32[2,192,1024]{2,1,0:T(8,128)S(1)} custom-call(bf16[192,2048]{1,0:T(8,128)(2,1)S(1)} %pad_maximum_fusion.some, bf16[2,2048,1024]{2,1,0:T(8,128)(2,1)S(1)} %load0.1.weights, bf16[2,192,1024]{2,1,0:T(8,128)(2,1)S(1)} %collective-permute-done.15.rest_0_), custom_call_target="tpu_custom_call" | custom-call | flops 17179869184 | bytes 1 | tf_op jit(solution)/shard_map/d1/pallas_call | solution.py:149
  73.7 4.9 %collective-permute-done.13 = bf16[96,2048]{1,0:T(8,128)(2,1)S(1)} collective-permute-done((bf16[96,2048]{1,0:T(8,128)(2,1)S(1)}, bf16[96,2048]{1,0:T(8,128)(2,1)S(1)}, u32[]{:S(2)}, u32[]{:S(2)}) %collective-permute-start.13) | collective-permute-done | bytes 393248 | tf_op jit(solution)/shard_map/arr2/ppermute | solution.py:94
  82.6 2.0 %c2.1 = bf16[2,192,1024]{2,1,0:T(8,128)(2,1)S(1)} custom-call(bf16[192,2048]{1,0:T(8,128)(2,1)S(1)} %pad_maximum_fusion.1.some, bf16[2,2048,1024]{2,1,0:T(8,128)(2,1)S(1)} %bitcast.8), custom_call_target="tpu_custom_call" | custom-call | flops 17179869184 | bytes 1 | tf_op jit(solution)/shard_map/c2/pallas_call | solution.py:149
  87.2 2.0 %d2.1.held = f32[2,192,1024]{2,1,0:T(8,128)S(1)} custom-call(bf16[192,2048]{1,0:T(8,128)(2,1)S(1)} %pad_maximum_fusion.1.some, bf16[2,2048,1024]{2,1,0:T(8,128)(2,1)S(1)} %load0.1.weights, bf16[2,192,1024]{2,1,0:T(8,128)(2,1)S(1)} %collective-permute-done.19.rest_0_), custom_call_target="tpu_custom_call" | custom-call | flops 17179869184 | bytes 1 | tf_op jit(solution)/shard_map/d2/pallas_call | solution.py:149
  89.2 4.0 %down0.1.weights = bf16[2,1024,2048]{2,1,0:T(8,128)(2,1)S(1)} custom-call(s32[2]{0:T(128)S(1)} %pad_add_fusion.quarters, bf16[4096,2048]{1,0:T(8,128)(2,1)} %weight.1), custom_call_target="tpu_custom_call" | custom-call | flops 17179869184 | bytes 1 | tf_op jit(solution)/shard_map/down0/pallas_call | solution.py:180
  97.1 4.0 %down2.1.weights = bf16[2,1024,2048]{2,1,0:T(8,128)(2,1)S(1)} custom-call(s32[2]{0:T(128)S(1)} %pad_add_fusion.1.quarters, bf16[4096,2048]{1,0:T(8,128)(2,1)} %weight.1), custom_call_target="tpu_custom_call" | custom-call | flops 17179869184 | bytes 1 | tf_op jit(solution)/shard_map/down2/pallas_call | solution.py:180
  103.0 3.3 %collective-permute-start.27 = (bf16[64,2048]{1,0:T(8,128)(2,1)S(1)}, bf16[64,2048]{1,0:T(8,128)(2,1)S(1)}, u32[]{:S(2)}, u32[]{:S(2)}) collective-permute-start(bf16[64,2048]{1,0:T(8,128)(2,1)S(1)} %get-tuple-element.149), channel_id=1, source_target_pairs={{1,4},{3,6},{4,1},{6,3},{9,12},{11,14},{12,9},{14,11},{17,20},{19,... | collective-permute-start | bytes 786440 | tf_op jit(solution)/shard_map/out0/ppermute | solution.py:94
  106.7 4.8 %collective-permute-done.27 = bf16[64,2048]{1,0:T(8,128)(2,1)S(1)} collective-permute-done((bf16[64,2048]{1,0:T(8,128)(2,1)S(1)}, bf16[64,2048]{1,0:T(8,128)(2,1)S(1)}, u32[]{:S(2)}, u32[]{:S(2)}) %collective-permute-start.27) | collective-permute-done | bytes 262176 | tf_op jit(solution)/shard_map/out0/ppermute | solution.py:94
  111.7 2.1 %collective-permute-done.28.got_up = bf16[192,1024]{1,0:T(8,128)(2,1)S(1)} collective-permute-done((bf16[192,1024]{1,0:T(8,128)(2,1)S(1)}, bf16[192,1024]{1,0:T(8,128)(2,1)S(1)}, u32[]{:S(2)}, u32[]{:S(2)}) %collective-permute-start.28) | collective-permute-done | bytes 393248 | tf_op jit(solution)/shard_map/b2/ppermute | solution.py:70
  116.5 8.6 %collective-permute-done.31 = bf16[32,2048]{1,0:T(8,128)(2,1)S(1)} collective-permute-done((bf16[32,2048]{1,0:T(8,128)(2,1)S(1)}, bf16[32,2048]{1,0:T(8,128)(2,1)S(1)}, u32[]{:S(2)}, u32[]{:S(2)}) %collective-permute-start.31) | collective-permute-done | bytes 131104 | tf_op jit(solution)/shard_map/mix0/ppermute | solution.py:70
  134.5 2.3 %collective-permute-start.39 = (bf16[96,2048]{1,0:T(8,128)(2,1)S(1)}, bf16[96,2048]{1,0:T(8,128)(2,1)S(1)}, u32[]{:S(2)}, u32[]{:S(2)}) collective-permute-start(bf16[96,2048]{1,0:T(8,128)(2,1)S(1)} %get-tuple-element.140), channel_id=1, source_target_pairs={{1,4},{3,6},{4,1},{6,3},{9,12},{11,14},{12,9},{14,11},{17,20},{19,... | collective-permute-start | bytes 1179656 | tf_op jit(solution)/shard_map/out1/ppermute | solution.py:94
  136.8 2.0 %rest2.1 = f32[192,2048]{1,0:T(8,128)S(1)} custom-call(bf16[192,1024]{1,0:T(8,128)(2,1)S(1)} %collective-permute-done.29.one, bf16[192,1024]{1,0:T(8,128)(2,1)S(1)} %collective-permute-done.36.two, bf16[2,1024,2048]{2,1,0:T(8,128)(2,1)S(1)} %down2.1.weights, f32[192,2048]{1,0:T(8,128)S(1)} %own2.1.rest_0_), custom_call_target="tpu_custom_call" | custom-call | flops 17179869184 | bytes 1 | tf_op jit(solution)/shard_map/rest2/pallas_call | solution.py:203
  139.0 3.3 %collective-permute-start.40 = (bf16[96,2048]{1,0:T(8,128)(2,1)S(1)}, bf16[96,2048]{1,0:T(8,128)(2,1)S(1)}, u32[]{:S(2)}, u32[]{:S(2)}) collective-permute-start(bf16[96,2048]{1,0:T(8,128)(2,1)S(1)} %get-tuple-element.143), channel_id=1, source_target_pairs={{1,4},{3,6},{4,1},{6,3},{9,12},{11,14},{12,9},{14,11},{17,20},{19,... | collective-permute-start | bytes 1179656 | tf_op jit(solution)/shard_map/out2/ppermute | solution.py:94
  142.3 2.1 %collective-permute-done.39 = bf16[96,2048]{1,0:T(8,128)(2,1)S(1)} collective-permute-done((bf16[96,2048]{1,0:T(8,128)(2,1)S(1)}, bf16[96,2048]{1,0:T(8,128)(2,1)S(1)}, u32[]{:S(2)}, u32[]{:S(2)}) %collective-permute-start.39) | collective-permute-done | bytes 393248 | tf_op jit(solution)/shard_map/out1/ppermute | solution.py:94
  146.6 6.5 %collective-permute-done.40 = bf16[96,2048]{1,0:T(8,128)(2,1)S(1)} collective-permute-done((bf16[96,2048]{1,0:T(8,128)(2,1)S(1)}, bf16[96,2048]{1,0:T(8,128)(2,1)S(1)}, u32[]{:S(2)}, u32[]{:S(2)}) %collective-permute-start.40) | collective-permute-done | bytes 393248 | tf_op jit(solution)/shard_map/out2/ppermute | solution.py:94
  154.5 4.4 %collective-permute-start.44 = (bf16[48,2048]{1,0:T(8,128)(2,1)S(1)}, bf16[48,2048]{1,0:T(8,128)(2,1)S(1)}, u32[]{:S(2)}, u32[]{:S(2)}) collective-permute-start(bf16[48,2048]{1,0:T(8,128)(2,1)S(1)} %convert_select_fusion.4), channel_id=1, source_target_pairs={{0,8},{4,12},{8,0},{12,4},{1,9},{5,13},{9,1},{13,5},{2,10},{6,14},... | collective-permute-start | bytes 589832 | tf_op jit(solution)/shard_map/far_out1/ppermute | solution.py:74
  158.9 3.2 %collective-permute-start.43 = (bf16[48,2048]{1,0:T(8,128)(2,1)S(1)}, bf16[48,2048]{1,0:T(8,128)(2,1)S(1)}, u32[]{:S(2)}, u32[]{:S(2)}) collective-permute-start(bf16[48,2048]{1,0:T(8,128)(2,1)S(1)} %convert_select_fusion.3), channel_id=1, source_target_pairs={{0,8},{4,12},{8,0},{12,4},{1,9},{5,13},{9,1},{13,5},{2,10},{6,14},... | collective-permute-start | bytes 589832 | tf_op jit(solution)/shard_map/far_out2/ppermute | solution.py:74
  162.2 6.4 %collective-permute-done.44.got = bf16[48,2048]{1,0:T(8,128)(2,1)S(1)} collective-permute-done((bf16[48,2048]{1,0:T(8,128)(2,1)S(1)}, bf16[48,2048]{1,0:T(8,128)(2,1)S(1)}, u32[]{:S(2)}, u32[]{:S(2)}) %collective-permute-start.44) | collective-permute-done | bytes 196640 | tf_op jit(solution)/shard_map/far_out1/ppermute | solution.py:74
  168.8 2.2 %collective-permute-done.43.got = bf16[48,2048]{1,0:T(8,128)(2,1)S(1)} collective-permute-done((bf16[48,2048]{1,0:T(8,128)(2,1)S(1)}, bf16[48,2048]{1,0:T(8,128)(2,1)S(1)}, u32[]{:S(2)}, u32[]{:S(2)}) %collective-permute-start.43) | collective-permute-done | bytes 196640 | tf_op jit(solution)/shard_map/far_out2/ppermute | solution.py:74
  (139 shorter events, 57.2 us)
Async XLA Ops:
  2.8 16.9 %collective-permute-start = (bf16[32,2048]{1,0:T(8,128)(2,1)S(1)}, bf16[32,2048]{1,0:T(8,128)(2,1)S(1)}, u32[]{:S(2)}, u32[]{:S(2)}) collective-permute-start(bf16[32,2048]{1,0:T(8,128)(2,1)S(1)} %get-tuple-element.74), channel_id=1, source_target_pairs={{0,8},{4,12},{8,0},{12,4},{1,9},{5,13},{9,1},{13,5},{2,10},{6,14},... | collective-permute-start | bytes 393224 | tf_op jit(solution)/shard_map/far0/ppermute | solution.py:74
  21.1 12.1 %collective-permute-start.1 = (bf16[48,2048]{1,0:T(8,128)(2,1)S(1)}, bf16[48,2048]{1,0:T(8,128)(2,1)S(1)}, u32[]{:S(2)}, u32[]{:S(2)}) collective-permute-start(bf16[48,2048]{1,0:T(8,128)(2,1)S(1)} %get-tuple-element.78), channel_id=1, source_target_pairs={{0,8},{4,12},{8,0},{12,4},{1,9},{5,13},{9,1},{13,5},{2,10},{6,14},... | collective-permute-start | bytes 589832 | tf_op jit(solution)/shard_map/far1/ppermute | solution.py:74
  24.8 15.3 %collective-permute-start.5 = (bf16[64,2048]{1,0:T(8,128)(2,1)S(1)}, bf16[64,2048]{1,0:T(8,128)(2,1)S(1)}, u32[]{:S(2)}, u32[]{:S(2)}) collective-permute-start(bf16[64,2048]{1,0:T(8,128)(2,1)S(1)} %pad_maximum_fusion.5), channel_id=1, source_target_pairs={{1,4},{3,6},{4,1},{6,3},{9,12},{11,14},{12,9},{14,11},{17,20},{19,... | collective-permute-start | bytes 786440 | tf_op jit(solution)/shard_map/arr0/ppermute | solution.py:94
  29.7 10.5 %collective-permute-start.4 = (bf16[64,2048]{1,0:T(8,128)(2,1)S(1)}, bf16[64,2048]{1,0:T(8,128)(2,1)S(1)}, u32[]{:S(2)}, u32[]{:S(2)}) collective-permute-start(bf16[64,2048]{1,0:T(8,128)(2,1)S(1)} %pad_maximum_fusion.5), channel_id=1, source_target_pairs={{0,4},{1,0},{2,6},{3,2},{4,5},{5,1},{6,7},{7,3},{8,12},{9,8},{10,1... | collective-permute-start | bytes 786440 | tf_op jit(solution)/shard_map/arr0/ppermute | solution.py:94
  33.3 11.8 %collective-permute-start.6 = (bf16[48,2048]{1,0:T(8,128)(2,1)S(1)}, bf16[48,2048]{1,0:T(8,128)(2,1)S(1)}, u32[]{:S(2)}, u32[]{:S(2)}) collective-permute-start(bf16[48,2048]{1,0:T(8,128)(2,1)S(1)} %broadcast_select_fusion.19), channel_id=1, source_target_pairs={{0,2},{1,3},{2,0},{3,1},{4,6},{5,7},{6,4},{7,5},{8,10},{9,11},{10,... | collective-permute-start | bytes 589832 | tf_op jit(solution)/shard_map/sel1/ppermute | solution.py:70
  34.1 18.2 %collective-permute-start.3 = (bf16[48,2048]{1,0:T(8,128)(2,1)S(1)}, bf16[48,2048]{1,0:T(8,128)(2,1)S(1)}, u32[]{:S(2)}, u32[]{:S(2)}) collective-permute-start(bf16[48,2048]{1,0:T(8,128)(2,1)S(1)} %get-tuple-element.83), channel_id=1, source_target_pairs={{0,8},{4,12},{8,0},{12,4},{1,9},{5,13},{9,1},{13,5},{2,10},{6,14},... | collective-permute-start | bytes 589832 | tf_op jit(solution)/shard_map/far2/ppermute | solution.py:74
  45.2 13.1 %collective-permute-start.11 = (bf16[96,2048]{1,0:T(8,128)(2,1)S(1)}, bf16[96,2048]{1,0:T(8,128)(2,1)S(1)}, u32[]{:S(2)}, u32[]{:S(2)}) collective-permute-start(bf16[96,2048]{1,0:T(8,128)(2,1)S(1)} %pad_maximum_fusion.3), channel_id=1, source_target_pairs={{1,4},{3,6},{4,1},{6,3},{9,12},{11,14},{12,9},{14,11},{17,20},{19,... | collective-permute-start | bytes 1179656 | tf_op jit(solution)/shard_map/arr1/ppermute | solution.py:94
  47.1 10.8 %collective-permute-start.10 = (bf16[96,2048]{1,0:T(8,128)(2,1)S(1)}, bf16[96,2048]{1,0:T(8,128)(2,1)S(1)}, u32[]{:S(2)}, u32[]{:S(2)}) collective-permute-start(bf16[96,2048]{1,0:T(8,128)(2,1)S(1)} %pad_maximum_fusion.3), channel_id=1, source_target_pairs={{0,4},{1,0},{2,6},{3,2},{4,5},{5,1},{6,7},{7,3},{8,12},{9,8},{10,1... | collective-permute-start | bytes 1179656 | tf_op jit(solution)/shard_map/arr1/ppermute | solution.py:94
  50.6 20.5 %collective-permute-start.14 = (bf16[128,1024]{1,0:T(8,128)(2,1)S(1)}, bf16[128,1024]{1,0:T(8,128)(2,1)S(1)}, u32[]{:S(2)}, u32[]{:S(2)}) collective-permute-start(bf16[128,1024]{1,0:T(8,128)(2,1)S(1)} %get-tuple-element.89), channel_id=1, source_target_pairs={{0,2},{1,3},{2,0},{3,1},{4,6},{5,7},{6,4},{7,5},{8,10},{9,11},{10,... | collective-permute-start | bytes 786440 | tf_op jit(solution)/shard_map/b0/ppermute | solution.py:70
  52.3 12.7 %collective-permute-start.9 = (bf16[48,2048]{1,0:T(8,128)(2,1)S(1)}, bf16[48,2048]{1,0:T(8,128)(2,1)S(1)}, u32[]{:S(2)}, u32[]{:S(2)}) collective-permute-start(bf16[48,2048]{1,0:T(8,128)(2,1)S(1)} %broadcast_select_fusion.16), channel_id=1, source_target_pairs={{0,2},{1,3},{2,0},{3,1},{4,6},{5,7},{6,4},{7,5},{8,10},{9,11},{10,... | collective-permute-start | bytes 589832 | tf_op jit(solution)/shard_map/sel2/ppermute | solution.py:70
  63.2 7.9 %collective-permute-start.16 = (bf16[128,1024]{1,0:T(8,128)(2,1)S(1)}, bf16[128,1024]{1,0:T(8,128)(2,1)S(1)}, u32[]{:S(2)}, u32[]{:S(2)}) collective-permute-start(bf16[128,1024]{1,0:T(8,128)(2,1)S(1)} %get-tuple-element.100), channel_id=1, source_target_pairs={{0,2},{1,3},{2,0},{3,1},{4,6},{5,7},{6,4},{7,5},{8,10},{9,11},{10,... | collective-permute-start | bytes 786440 | tf_op jit(solution)/shard_map/b0/ppermute | solution.py:70
  65.1 15.1 %collective-permute-start.17 = (bf16[96,2048]{1,0:T(8,128)(2,1)S(1)}, bf16[96,2048]{1,0:T(8,128)(2,1)S(1)}, u32[]{:S(2)}, u32[]{:S(2)}) collective-permute-start(bf16[96,2048]{1,0:T(8,128)(2,1)S(1)} %pad_maximum_fusion.4), channel_id=1, source_target_pairs={{1,4},{3,6},{4,1},{6,3},{9,12},{11,14},{12,9},{14,11},{17,20},{19,... | collective-permute-start | bytes 1179656 | tf_op jit(solution)/shard_map/arr2/ppermute | solution.py:94
  67.3 11.3 %collective-permute-start.13 = (bf16[96,2048]{1,0:T(8,128)(2,1)S(1)}, bf16[96,2048]{1,0:T(8,128)(2,1)S(1)}, u32[]{:S(2)}, u32[]{:S(2)}) collective-permute-start(bf16[96,2048]{1,0:T(8,128)(2,1)S(1)} %pad_maximum_fusion.4), channel_id=1, source_target_pairs={{0,4},{1,0},{2,6},{3,2},{4,5},{5,1},{6,7},{7,3},{8,12},{9,8},{10,1... | collective-permute-start | bytes 1179656 | tf_op jit(solution)/shard_map/arr2/ppermute | solution.py:94
  71.3 21.9 %collective-permute-start.22 = (bf16[128,1024]{1,0:T(8,128)(2,1)S(1)}, bf16[128,1024]{1,0:T(8,128)(2,1)S(1)}, u32[]{:S(2)}, u32[]{:S(2)}) collective-permute-start(bf16[128,1024]{1,0:T(8,128)(2,1)S(1)} %hide0.1.one), channel_id=1, source_target_pairs={{0,1},{1,0},{2,3},{3,2},{4,5},{5,4},{6,7},{7,6},{8,9},{9,8},{10,11... | collective-permute-start | bytes 786440 | tf_op jit(solution)/shard_map/hide0/ppermute | solution.py:70
  72.2 24.0 %collective-permute-start.21 = (bf16[128,1024]{1,0:T(8,128)(2,1)S(1)}, bf16[128,1024]{1,0:T(8,128)(2,1)S(1)}, u32[]{:S(2)}, u32[]{:S(2)}) collective-permute-start(bf16[128,1024]{1,0:T(8,128)(2,1)S(1)} %hide0.1.one), channel_id=1, source_target_pairs={{0,2},{1,3},{2,0},{3,1},{4,6},{5,7},{6,4},{7,5},{8,10},{9,11},{10,... | collective-permute-start | bytes 786440 | tf_op jit(solution)/shard_map/hide0/ppermute | solution.py:70
  73.2 29.8 %collective-permute-start.25 = (bf16[192,1024]{1,0:T(8,128)(2,1)S(1)}, bf16[192,1024]{1,0:T(8,128)(2,1)S(1)}, u32[]{:S(2)}, u32[]{:S(2)}) collective-permute-start(bf16[192,1024]{1,0:T(8,128)(2,1)S(1)} %get-tuple-element.96), channel_id=1, source_target_pairs={{0,2},{1,3},{2,0},{3,1},{4,6},{5,7},{6,4},{7,5},{8,10},{9,11},{10,... | collective-permute-start | bytes 1179656 | tf_op jit(solution)/shard_map/b1/ppermute | solution.py:70
  78.6 24.3 %collective-permute-start.26 = (bf16[192,1024]{1,0:T(8,128)(2,1)S(1)}, bf16[192,1024]{1,0:T(8,128)(2,1)S(1)}, u32[]{:S(2)}, u32[]{:S(2)}) collective-permute-start(bf16[192,1024]{1,0:T(8,128)(2,1)S(1)} %get-tuple-element.114), channel_id=1, source_target_pairs={{0,2},{1,3},{2,0},{3,1},{4,6},{5,7},{6,4},{7,5},{8,10},{9,11},{10,... | collective-permute-start | bytes 1179656 | tf_op jit(solution)/shard_map/b1/ppermute | solution.py:70
  87.1 26.7 %collective-permute-start.20 = (bf16[192,1024]{1,0:T(8,128)(2,1)S(1)}, bf16[192,1024]{1,0:T(8,128)(2,1)S(1)}, u32[]{:S(2)}, u32[]{:S(2)}) collective-permute-start(bf16[192,1024]{1,0:T(8,128)(2,1)S(1)} %get-tuple-element.106), channel_id=1, source_target_pairs={{0,2},{1,3},{2,0},{3,1},{4,6},{5,7},{6,4},{7,5},{8,10},{9,11},{10,... | collective-permute-start | bytes 1179656 | tf_op jit(solution)/shard_map/b2/ppermute | solution.py:70
  93.2 20.6 %collective-permute-start.28 = (bf16[192,1024]{1,0:T(8,128)(2,1)S(1)}, bf16[192,1024]{1,0:T(8,128)(2,1)S(1)}, u32[]{:S(2)}, u32[]{:S(2)}) collective-permute-start(bf16[192,1024]{1,0:T(8,128)(2,1)S(1)} %get-tuple-element.118), channel_id=1, source_target_pairs={{0,2},{1,3},{2,0},{3,1},{4,6},{5,7},{6,4},{7,5},{8,10},{9,11},{10,... | collective-permute-start | bytes 1179656 | tf_op jit(solution)/shard_map/b2/ppermute | solution.py:70
  103.0 8.5 %collective-permute-start.27 = (bf16[64,2048]{1,0:T(8,128)(2,1)S(1)}, bf16[64,2048]{1,0:T(8,128)(2,1)S(1)}, u32[]{:S(2)}, u32[]{:S(2)}) collective-permute-start(bf16[64,2048]{1,0:T(8,128)(2,1)S(1)} %get-tuple-element.149), channel_id=1, source_target_pairs={{1,4},{3,6},{4,1},{6,3},{9,12},{11,14},{12,9},{14,11},{17,20},{19,... | collective-permute-start | bytes 786440 | tf_op jit(solution)/shard_map/out0/ppermute | solution.py:94
  106.6 18.6 %collective-permute-start.32 = (bf16[192,1024]{1,0:T(8,128)(2,1)S(1)}, bf16[192,1024]{1,0:T(8,128)(2,1)S(1)}, u32[]{:S(2)}, u32[]{:S(2)}) collective-permute-start(bf16[192,1024]{1,0:T(8,128)(2,1)S(1)} %hide1.1.one), channel_id=1, source_target_pairs={{0,1},{1,0},{2,3},{3,2},{4,5},{5,4},{6,7},{7,6},{8,9},{9,8},{10,11... | collective-permute-start | bytes 1179656 | tf_op jit(solution)/shard_map/hide1/ppermute | solution.py:70
  106.7 20.5 %collective-permute-start.30 = (bf16[192,1024]{1,0:T(8,128)(2,1)S(1)}, bf16[192,1024]{1,0:T(8,128)(2,1)S(1)}, u32[]{:S(2)}, u32[]{:S(2)}) collective-permute-start(bf16[192,1024]{1,0:T(8,128)(2,1)S(1)} %hide1.1.one), channel_id=1, source_target_pairs={{0,2},{1,3},{2,0},{3,1},{4,6},{5,7},{6,4},{7,5},{8,10},{9,11},{10,... | collective-permute-start | bytes 1179656 | tf_op jit(solution)/shard_map/hide1/ppermute | solution.py:70
  111.7 13.4 %collective-permute-start.31 = (bf16[32,2048]{1,0:T(8,128)(2,1)S(1)}, bf16[32,2048]{1,0:T(8,128)(2,1)S(1)}, u32[]{:S(2)}, u32[]{:S(2)}) collective-permute-start(bf16[32,2048]{1,0:T(8,128)(2,1)S(1)} %select_convert_fusion.5), channel_id=1, source_target_pairs={{0,2},{1,3},{2,0},{3,1},{4,6},{5,7},{6,4},{7,5},{8,10},{9,11},{10,... | collective-permute-start | bytes 393224 | tf_op jit(solution)/shard_map/mix0/ppermute | solution.py:70
  114.1 14.8 %collective-permute-start.33 = (bf16[192,1024]{1,0:T(8,128)(2,1)S(1)}, bf16[192,1024]{1,0:T(8,128)(2,1)S(1)}, u32[]{:S(2)}, u32[]{:S(2)}) collective-permute-start(bf16[192,1024]{1,0:T(8,128)(2,1)S(1)} %hide2.1.one), channel_id=1, source_target_pairs={{0,1},{1,0},{2,3},{3,2},{4,5},{5,4},{6,7},{7,6},{8,9},{9,8},{10,11... | collective-permute-start | bytes 1179656 | tf_op jit(solution)/shard_map/hide2/ppermute | solution.py:70
  115.5 18.1 %collective-permute-start.29 = (bf16[192,1024]{1,0:T(8,128)(2,1)S(1)}, bf16[192,1024]{1,0:T(8,128)(2,1)S(1)}, u32[]{:S(2)}, u32[]{:S(2)}) collective-permute-start(bf16[192,1024]{1,0:T(8,128)(2,1)S(1)} %hide2.1.one), channel_id=1, source_target_pairs={{0,2},{1,3},{2,0},{3,1},{4,6},{5,7},{6,4},{7,5},{8,10},{9,11},{10,... | collective-permute-start | bytes 1179656 | tf_op jit(solution)/shard_map/hide2/ppermute | solution.py:70
  125.1 8.5 %collective-permute-start.35 = (bf16[32,2048]{1,0:T(8,128)(2,1)S(1)}, bf16[32,2048]{1,0:T(8,128)(2,1)S(1)}, u32[]{:S(2)}, u32[]{:S(2)}) collective-permute-start(bf16[32,2048]{1,0:T(8,128)(2,1)S(1)} %convert_select_fusion.5), channel_id=1, source_target_pairs={{0,8},{4,12},{8,0},{12,4},{1,9},{5,13},{9,1},{13,5},{2,10},{6,14},... | collective-permute-start | bytes 393224 | tf_op jit(solution)/shard_map/far_out0/ppermute | solution.py:74
  134.5 9.9 %collective-permute-start.39 = (bf16[96,2048]{1,0:T(8,128)(2,1)S(1)}, bf16[96,2048]{1,0:T(8,128)(2,1)S(1)}, u32[]{:S(2)}, u32[]{:S(2)}) collective-permute-start(bf16[96,2048]{1,0:T(8,128)(2,1)S(1)} %get-tuple-element.140), channel_id=1, source_target_pairs={{1,4},{3,6},{4,1},{6,3},{9,12},{11,14},{12,9},{14,11},{17,20},{19,... | collective-permute-start | bytes 1179656 | tf_op jit(solution)/shard_map/out1/ppermute | solution.py:94
  138.9 7.7 %collective-permute-start.37 = (bf16[96,2048]{1,0:T(8,128)(2,1)S(1)}, bf16[96,2048]{1,0:T(8,128)(2,1)S(1)}, u32[]{:S(2)}, u32[]{:S(2)}) collective-permute-start(bf16[96,2048]{1,0:T(8,128)(2,1)S(1)} %get-tuple-element.142), channel_id=1, source_target_pairs={{0,1},{1,5},{2,3},{3,7},{4,0},{5,4},{6,2},{7,6},{8,9},{9,13},{10,1... | collective-permute-start | bytes 1179656 | tf_op jit(solution)/shard_map/out2/ppermute | solution.py:94
  139.0 14.1 %collective-permute-start.40 = (bf16[96,2048]{1,0:T(8,128)(2,1)S(1)}, bf16[96,2048]{1,0:T(8,128)(2,1)S(1)}, u32[]{:S(2)}, u32[]{:S(2)}) collective-permute-start(bf16[96,2048]{1,0:T(8,128)(2,1)S(1)} %get-tuple-element.143), channel_id=1, source_target_pairs={{1,4},{3,6},{4,1},{6,3},{9,12},{11,14},{12,9},{14,11},{17,20},{19,... | collective-permute-start | bytes 1179656 | tf_op jit(solution)/shard_map/out2/ppermute | solution.py:94
  144.6 9.8 %collective-permute-start.42 = (bf16[48,2048]{1,0:T(8,128)(2,1)S(1)}, bf16[48,2048]{1,0:T(8,128)(2,1)S(1)}, u32[]{:S(2)}, u32[]{:S(2)}) collective-permute-start(bf16[48,2048]{1,0:T(8,128)(2,1)S(1)} %select_convert_fusion.4), channel_id=1, source_target_pairs={{0,2},{1,3},{2,0},{3,1},{4,6},{5,7},{6,4},{7,5},{8,10},{9,11},{10,... | collective-permute-start | bytes 589832 | tf_op jit(solution)/shard_map/mix1/ppermute | solution.py:70
  154.5 14.1 %collective-permute-start.44 = (bf16[48,2048]{1,0:T(8,128)(2,1)S(1)}, bf16[48,2048]{1,0:T(8,128)(2,1)S(1)}, u32[]{:S(2)}, u32[]{:S(2)}) collective-permute-start(bf16[48,2048]{1,0:T(8,128)(2,1)S(1)} %convert_select_fusion.4), channel_id=1, source_target_pairs={{0,8},{4,12},{8,0},{12,4},{1,9},{5,13},{9,1},{13,5},{2,10},{6,14},... | collective-permute-start | bytes 589832 | tf_op jit(solution)/shard_map/far_out1/ppermute | solution.py:74
  158.9 12.1 %collective-permute-start.43 = (bf16[48,2048]{1,0:T(8,128)(2,1)S(1)}, bf16[48,2048]{1,0:T(8,128)(2,1)S(1)}, u32[]{:S(2)}, u32[]{:S(2)}) collective-permute-start(bf16[48,2048]{1,0:T(8,128)(2,1)S(1)} %convert_select_fusion.3), channel_id=1, source_target_pairs={{0,8},{4,12},{8,0},{12,4},{1,9},{5,13},{9,1},{13,5},{2,10},{6,14},... | collective-permute-start | bytes 589832 | tf_op jit(solution)/shard_map/far_out2/ppermute | solution.py:74
  (21 other events, 100.7 us)

commit v4 on v3

--- a/solution.py
+++ b/solution.py
@@ -9,7 +9,7 @@
 
 ROWS = (32, 48, 48)
 ORDER = (
-    "far0", "load3", "load1", "sel0", "far1", "load2", "arr0", "load0", "sel1", "far2", "take0", "a0", "c0",
+    "far0", "load3", "sel0", "far1", "load1", "arr0", "load2", "load0", "sel1", "far2", "take0", "a0", "c0",
     "arr1", "b0", "d0", "sel2", "take1", "a1", "c1", "b1", "arr2", "d1", "hide0", "take2", "a2", "c2", "b2",
     "d2", "down0", "own0", "forward0", "down2", "rest0", "out0", "hide1", "mix0", "hide2", "far_out0", "own1",
     "forward1", "own2", "rest1", "out1", "forward2", "end0", "rest2", "out2", "mix1", "mix2", "far_out1",
@@ -18,7 +18,7 @@
 TILE = 256
 COST = 1 << 34
 LOAD_COST = 1 << 30
-VMEM = 10 << 20
+VMEM = 6 << 20
 
 
 def blocks(array):
@@ -125,7 +125,7 @@
         scratch_shapes=[pltpu.SemaphoreType.DMA((2, 4))],
         compiler_params=pltpu.CompilerParams(vmem_limit_bytes=VMEM),
         cost_estimate=pl.CostEstimate(flops=LOAD_COST, bytes_accessed=1, transcendentals=0),
-    )(quarter.reshape(1).astype(jnp.int32), gate_weight, up_weight)
+    )(quarter, gate_weight, up_weight)
 
 
 def sums_kernel(has_got, split, some, weights, *rest):
@@ -185,7 +185,7 @@
         scratch_shapes=[pltpu.SemaphoreType.DMA((2, 4))],
         compiler_params=pltpu.CompilerParams(vmem_limit_bytes=VMEM),
         cost_estimate=pl.CostEstimate(flops=COST, bytes_accessed=1, transcendentals=0),
-    )(jnp.stack(quarters).astype(jnp.int32), weight)
+    )(quarters, weight)
 
 
 def products_kernel(has_total, one, two, weights, *rest):
@@ -297,8 +297,12 @@
 
     def __init__(self, tokens_values, tokens_scales, gate_weight, up_weight, down_weight):
         tp, seq = lax.axis_index("tp"), lax.axis_index("seq")
-        self.seq, self.x, self.core = seq, seq >> 1, seq & 1
-        self.high, self.even = tp >> 1, (tp ^ seq) & 1 == 0
+        x, core, high = seq >> 1, seq & 1, tp >> 1
+        facts = x == 0, core == 0, (tp ^ seq) & 1 == 0, high == x
+        quarters = [(seq ^ bits).reshape(1) for bits in range(4)]
+        pairs = [jnp.stack([seq ^ bits, seq ^ bits ^ 1]) for bits in (0, 2)]
+        facts, self.quarters, self.pairs, gate_weight = lax.optimization_barrier((facts, quarters, pairs, gate_weight))
+        self.first_x, self.first_core, self.even, self.same_half = facts
         self.gate_weight = pltpu.with_memory_space_constraint(gate_weight, pltpu.HBM)
         self.up_weight = pltpu.with_memory_space_constraint(up_weight, pltpu.HBM)
         self.down_weight = pltpu.with_memory_space_constraint(down_weight, pltpu.HBM)
@@ -324,14 +328,14 @@
     def sel(self, i):
         part, other = self.held["far", i]
         other = self.now(other)
-        sent = jnp.where(self.high == self.x, other, part)
-        kept = jnp.where(self.high == self.x, part, other)
+        sent = jnp.where(self.same_half, other, part)
+        kept = jnp.where(self.same_half, part, other)
         self.held["sel", i] = kept, over_seq(sent, 2)
         self.last = sent
 
     def arr(self, i):
         kept, got = self.held["sel", i]
-        pair = arrange(self.x == 0, kept, self.now(got))
+        pair = arrange(self.first_x, kept, self.now(got))
         self.held["arr", i] = pair, over_both(pair, FIRST_IN), over_both(pair, SECOND)
         self.last = pair
 
@@ -340,11 +344,11 @@
         first = self.now(first)
         own = jnp.where(self.even, pair, first)
         others = jnp.where(self.even, first, second)
-        self.held["take", i] = self.last = arrange(self.core == 0, own, others)
+        self.held["take", i] = self.last = arrange(self.first_core, own, others)
 
     def load(self, bits):
         gate_weight = self.now(self.gate_weight)
-        self.held["load", bits] = self.last = load(gate_weight, self.up_weight, self.seq ^ bits)
+        self.held["load", bits] = self.last = load(gate_weight, self.up_weight, self.quarters[bits])
 
     def part(self, i, bits, got=None, kind=jnp.bfloat16, split=False):
         some = self.now(self.held["take", i])
@@ -372,8 +376,7 @@
         self.last = hidden
 
     def down(self, bits):
-        quarters = [self.seq ^ bits, self.seq ^ bits ^ 1]
-        self.held["down", bits] = self.last = load_rows(self.now(self.down_weight), quarters)
+        self.held["down", bits] = self.last = load_rows(self.now(self.down_weight), self.pairs[bits // 2])
 
     def own(self, i):
         hidden, far, near = self.held["hide", i]
@@ -391,8 +394,8 @@
         partial_sum = self.now(self.held["rest", i])
         half = partial_sum.shape[0] // 2
         low, top = partial_sum[:half], partial_sum[half:]
-        own = jnp.where(self.core == 0, low, top)
-        others = jnp.where(self.core == 0, top, low)
+        own = jnp.where(self.first_core, low, top)
+        others = jnp.where(self.first_core, top, low)
         one, two = narrow(jnp.where(self.even, others, own)), narrow(others)
         self.held["out", i] = own, over_both(one, FIRST_OUT), over_both(two, SECOND)
         self.last = one
@@ -402,16 +405,16 @@
         pair = wide(self.now(first)) + jnp.where(self.even, own, wide(second))
         rows = pair.shape[0] // 2
         low, top = pair[:rows], pair[rows:]
-        kept = jnp.where(self.x == 0, low, top)
-        sent = narrow(jnp.where(self.x == 0, top, low))
+        kept = jnp.where(self.first_x, low, top)
+        sent = narrow(jnp.where(self.first_x, top, low))
         self.held["mix", i] = kept, over_seq(sent, 2)
         self.last = sent
 
     def far_out(self, i):
         kept, got = self.held["mix", i]
         got = self.now(got)
-        sent = jnp.where(self.high == self.x, got, narrow(kept))
-        kept = jnp.where(self.high == self.x, kept, wide(got))
+        sent = jnp.where(self.same_half, got, narrow(kept))
+        kept = jnp.where(self.same_half, kept, wide(got))
         self.held["far_out", i] = kept, over_tp(sent, 2)
         self.last = sent
 

time: 172 us -> 167 us (0.971)
  local copies, waits for them, and re-layouts: 10.1 us -> 1.73 us
  starting transfers between devices: 52.2 us -> 54.2 us
    unnamed x16 -> x4, local copies, waits for them, and re-layouts: 10.1 us -> 1.73 us
    ppermute x6, waiting for transfers between devices: 8.68 us -> 13 us  [over_tp(): return lax.ppermute(array, 'tp', [(i, i ^ bit) for i in range(4)])]
    ppermute x12, waiting for transfers between devices: 28.1 us -> 23.9 us  [over_both(): return lax.ppermute(array, ('tp', 'seq'), pairs)]
    ppermute x12, starting transfers between devices: 19.1 us -> 23.1 us  [over_both(): return lax.ppermute(array, ('tp', 'seq'), pairs)]
    ppermute x6, starting transfers between devices: 12.8 us -> 9.39 us  [over_tp(): return lax.ppermute(array, 'tp', [(i, i ^ bit) for i in range(4)])]
  transfers between devices with their start and end apart: 45 -> 45, of which waited for: 17 -> 17; matrix products, arithmetic and copies ran while one was open for 1% -> 1% of each run, Pallas kernels for 32% -> 33%
where the time goes in v4:
time: 167 us
  Pallas kernels  56.7 us (34%)
  starting transfers between devices  54.2 us (32%)
  waiting for transfers between devices  51 us (31%)
  other arithmetic  2.08 us (1%)
  local copies, waits for them, and re-layouts  1.73 us (1%)
    ppermute x12, waiting for transfers between devices, over_both(): return lax.ppermute(array, ('tp', 'seq'), pairs)  23.9 us
    ppermute x12, starting transfers between devices, over_both(): return lax.ppermute(array, ('tp', 'seq'), pairs)  23.1 us
    ppermute x27, starting transfers between devices, over_seq(): return lax.ppermute(array, 'seq', [(i, i ^ bit) for i in range(4)])  21.7 us
    pallas_call x12, Pallas kernels, sums(): pl.pallas_call(functools.partial(sums_kernel, got is not None, split), ou...  21.2 us
    ppermute x27, waiting for transfers between devices, over_seq(): return lax.ppermute(array, 'seq', [(i, i ^ bit) for i in range(4)])  14.1 us
    pallas_call x4, Pallas kernels, load(): pl.pallas_call(load_kernel, out_shape=jax.ShapeDtypeStruct((2, deep, widt...  14 us
    ppermute x6, waiting for transfers between devices, over_tp(): return lax.ppermute(array, 'tp', [(i, i ^ bit) for i in range(4)])  13 us
    pallas_call x6, Pallas kernels, products(): pl.pallas_call(functools.partial(products_kernel, total is not None), out...  10.9 us
  transfers between devices with their start and end apart: 45, of which 17 were waited for; matrix products, arithmetic and copies ran while one was open for 1% of the time, Pallas kernels for 33%

profile of v4, /device:TPU:1, one launch (start us, length us, event | category | flops | bytes accessed | tf_op | source)
XLA Modules:
  0.0 167.0 jit_solution(11828364061431381817)
XLA Ops:
  2.8 3.2 %collective-permute-start = (bf16[32,2048]{1,0:T(8,128)(2,1)S(1)}, bf16[32,2048]{1,0:T(8,128)(2,1)S(1)}, u32[]{:S(2)}, u32[]{:S(2)}) collective-permute-start(bf16[32,2048]{1,0:T(8,128)(2,1)S(1)} %get-tuple-element.89), channel_id=1, source_target_pairs={{0,8},{4,12},{8,0},{12,4},{1,9},{5,13},{9,1},{13,5},{2,10},{6,14},... | collective-permute-start | bytes 393224 | tf_op jit(solution)/shard_map/far0/ppermute | solution.py:74
  6.1 3.5 %load3.1.weights = bf16[2,2048,1024]{2,1,0:T(8,128)(2,1)S(1)} custom-call(s32[1]{0:T(128)} %bitcast.3.quarter, bf16[2048,4096]{1,0:T(8,128)(2,1)} %gate_weight.3, bf16[2048,4096]{1,0:T(8,128)(2,1)} %up_weight.7), custom_call_target="tpu_custom_call" | custom-call | flops 1073741824 | bytes 1 | tf_op jit(solution)/shard_map/load3/pallas_call | solution.py:120
  9.6 2.4 %collective-permute-done = bf16[32,2048]{1,0:T(8,128)(2,1)S(1)} collective-permute-done((bf16[32,2048]{1,0:T(8,128)(2,1)S(1)}, bf16[32,2048]{1,0:T(8,128)(2,1)S(1)}, u32[]{:S(2)}, u32[]{:S(2)}) %collective-permute-start) | collective-permute-done | bytes 131104 | tf_op jit(solution)/shard_map/far0/ppermute | solution.py:74
  13.1 3.5 %load1.1.weights = bf16[2,2048,1024]{2,1,0:T(8,128)(2,1)S(1)} custom-call(s32[1]{0:T(128)} %bitcast.1.quarter, bf16[2048,4096]{1,0:T(8,128)(2,1)} %gate_weight.3, bf16[2048,4096]{1,0:T(8,128)(2,1)} %up_weight.7), custom_call_target="tpu_custom_call" | custom-call | flops 1073741824 | bytes 1 | tf_op jit(solution)/shard_map/load1/pallas_call | solution.py:120
  16.7 7.4 %collective-permute-start.5 = (bf16[64,2048]{1,0:T(8,128)(2,1)S(1)}, bf16[64,2048]{1,0:T(8,128)(2,1)S(1)}, u32[]{:S(2)}, u32[]{:S(2)}) collective-permute-start(bf16[64,2048]{1,0:T(8,128)(2,1)S(1)} %pad_maximum_fusion.5), channel_id=1, source_target_pairs={{1,4},{3,6},{4,1},{6,3},{9,12},{11,14},{12,9},{14,11},{17,20},{19,... | collective-permute-start | bytes 786440 | tf_op jit(solution)/shard_map/arr0/ppermute | solution.py:94
  24.2 3.5 %load2.1.weights = bf16[2,2048,1024]{2,1,0:T(8,128)(2,1)S(1)} custom-call(s32[1]{0:T(128)} %bitcast.2.quarter, bf16[2048,4096]{1,0:T(8,128)(2,1)} %gate_weight.3, bf16[2048,4096]{1,0:T(8,128)(2,1)} %up_weight.7), custom_call_target="tpu_custom_call" | custom-call | flops 1073741824 | bytes 1 | tf_op jit(solution)/shard_map/load2/pallas_call | solution.py:120
  27.7 3.5 %load0.1.weights = bf16[2,2048,1024]{2,1,0:T(8,128)(2,1)S(1)} custom-call(s32[1]{0:T(128)} %bitcast.quarter, bf16[2048,4096]{1,0:T(8,128)(2,1)} %gate_weight.3, bf16[2048,4096]{1,0:T(8,128)(2,1)} %up_weight.7), custom_call_target="tpu_custom_call" | custom-call | flops 1073741824 | bytes 1 | tf_op jit(solution)/shard_map/load0/pallas_call | solution.py:120
  37.5 2.8 %collective-permute-start.11 = (bf16[96,2048]{1,0:T(8,128)(2,1)S(1)}, bf16[96,2048]{1,0:T(8,128)(2,1)S(1)}, u32[]{:S(2)}, u32[]{:S(2)}) collective-permute-start(bf16[96,2048]{1,0:T(8,128)(2,1)S(1)} %pad_maximum_fusion.3), channel_id=1, source_target_pairs={{1,4},{3,6},{4,1},{6,3},{9,12},{11,14},{12,9},{14,11},{17,20},{19,... | collective-permute-start | bytes 1179656 | tf_op jit(solution)/shard_map/arr1/ppermute | solution.py:94
  46.0 6.0 %collective-permute-done.10 = bf16[96,2048]{1,0:T(8,128)(2,1)S(1)} collective-permute-done((bf16[96,2048]{1,0:T(8,128)(2,1)S(1)}, bf16[96,2048]{1,0:T(8,128)(2,1)S(1)}, u32[]{:S(2)}, u32[]{:S(2)}) %collective-permute-start.10) | collective-permute-done | bytes 393248 | tf_op jit(solution)/shard_map/arr1/ppermute | solution.py:94
  52.3 2.0 %a1.1 = bf16[2,192,1024]{2,1,0:T(8,128)(2,1)S(1)} custom-call(bf16[192,2048]{1,0:T(8,128)(2,1)S(1)} %pad_maximum_fusion.some, bf16[2,2048,1024]{2,1,0:T(8,128)(2,1)S(1)} %load3.1.weights), custom_call_target="tpu_custom_call" | custom-call | flops 17179869184 | bytes 1 | tf_op jit(solution)/shard_map/a1/pallas_call | solution.py:149
  54.4 2.0 %c1.1 = bf16[2,192,1024]{2,1,0:T(8,128)(2,1)S(1)} custom-call(bf16[192,2048]{1,0:T(8,128)(2,1)S(1)} %pad_maximum_fusion.some, bf16[2,2048,1024]{2,1,0:T(8,128)(2,1)S(1)} %load1.1.weights), custom_call_target="tpu_custom_call" | custom-call | flops 17179869184 | bytes 1 | tf_op jit(solution)/shard_map/c1/pallas_call | solution.py:149
  62.3 2.0 %d1.1.held = f32[2,192,1024]{2,1,0:T(8,128)S(1)} custom-call(bf16[192,2048]{1,0:T(8,128)(2,1)S(1)} %pad_maximum_fusion.some, bf16[2,2048,1024]{2,1,0:T(8,128)(2,1)S(1)} %load0.1.weights, bf16[2,192,1024]{2,1,0:T(8,128)(2,1)S(1)} %collective-permute-done.15.rest_0_), custom_call_target="tpu_custom_call" | custom-call | flops 17179869184 | bytes 1 | tf_op jit(solution)/shard_map/d1/pallas_call | solution.py:149
  68.2 4.9 %collective-permute-done.13 = bf16[96,2048]{1,0:T(8,128)(2,1)S(1)} collective-permute-done((bf16[96,2048]{1,0:T(8,128)(2,1)S(1)}, bf16[96,2048]{1,0:T(8,128)(2,1)S(1)}, u32[]{:S(2)}, u32[]{:S(2)}) %collective-permute-start.13) | collective-permute-done | bytes 393248 | tf_op jit(solution)/shard_map/arr2/ppermute | solution.py:94
  73.7 2.0 %a2.1 = bf16[2,192,1024]{2,1,0:T(8,128)(2,1)S(1)} custom-call(bf16[192,2048]{1,0:T(8,128)(2,1)S(1)} %pad_maximum_fusion.1.some, bf16[2,2048,1024]{2,1,0:T(8,128)(2,1)S(1)} %load3.1.weights), custom_call_target="tpu_custom_call" | custom-call | flops 17179869184 | bytes 1 | tf_op jit(solution)/shard_map/a2/pallas_call | solution.py:149
  75.8 2.0 %c2.1 = bf16[2,192,1024]{2,1,0:T(8,128)(2,1)S(1)} custom-call(bf16[192,2048]{1,0:T(8,128)(2,1)S(1)} %pad_maximum_fusion.1.some, bf16[2,2048,1024]{2,1,0:T(8,128)(2,1)S(1)} %load1.1.weights), custom_call_target="tpu_custom_call" | custom-call | flops 17179869184 | bytes 1 | tf_op jit(solution)/shard_map/c2/pallas_call | solution.py:149
  81.5 2.0 %d2.1.held = f32[2,192,1024]{2,1,0:T(8,128)S(1)} custom-call(bf16[192,2048]{1,0:T(8,128)(2,1)S(1)} %pad_maximum_fusion.1.some, bf16[2,2048,1024]{2,1,0:T(8,128)(2,1)S(1)} %load0.1.weights, bf16[2,192,1024]{2,1,0:T(8,128)(2,1)S(1)} %collective-permute-done.19.rest_0_), custom_call_target="tpu_custom_call" | custom-call | flops 17179869184 | bytes 1 | tf_op jit(solution)/shard_map/d2/pallas_call | solution.py:149
  83.5 4.0 %down0.1.weights = bf16[2,1024,2048]{2,1,0:T(8,128)(2,1)S(1)} custom-call(s32[2]{0:T(128)S(1)} %get-tuple-element.128.quarters, bf16[4096,2048]{1,0:T(8,128)(2,1)} %weight.1), custom_call_target="tpu_custom_call" | custom-call | flops 17179869184 | bytes 1 | tf_op jit(solution)/shard_map/down0/pallas_call | solution.py:180
  90.3 4.0 %down2.1.weights = bf16[2,1024,2048]{2,1,0:T(8,128)(2,1)S(1)} custom-call(s32[2]{0:T(128)S(1)} %get-tuple-element.132.quarters, bf16[4096,2048]{1,0:T(8,128)(2,1)} %weight.1), custom_call_target="tpu_custom_call" | custom-call | flops 17179869184 | bytes 1 | tf_op jit(solution)/shard_map/down2/pallas_call | solution.py:180
  96.3 3.2 %collective-permute-start.27 = (bf16[64,2048]{1,0:T(8,128)(2,1)S(1)}, bf16[64,2048]{1,0:T(8,128)(2,1)S(1)}, u32[]{:S(2)}, u32[]{:S(2)}) collective-permute-start(bf16[64,2048]{1,0:T(8,128)(2,1)S(1)} %get-tuple-element.171), channel_id=1, source_target_pairs={{1,4},{3,6},{4,1},{6,3},{9,12},{11,14},{12,9},{14,11},{17,20},{19,... | collective-permute-start | bytes 786440 | tf_op jit(solution)/shard_map/out0/ppermute | solution.py:94
  101.1 3.6 %collective-permute-done.27 = bf16[64,2048]{1,0:T(8,128)(2,1)S(1)} collective-permute-done((bf16[64,2048]{1,0:T(8,128)(2,1)S(1)}, bf16[64,2048]{1,0:T(8,128)(2,1)S(1)}, u32[]{:S(2)}, u32[]{:S(2)}) %collective-permute-start.27) | collective-permute-done | bytes 262176 | tf_op jit(solution)/shard_map/out0/ppermute | solution.py:94
  106.1 2.2 %collective-permute-done.28.got_up = bf16[192,1024]{1,0:T(8,128)(2,1)S(1)} collective-permute-done((bf16[192,1024]{1,0:T(8,128)(2,1)S(1)}, bf16[192,1024]{1,0:T(8,128)(2,1)S(1)}, u32[]{:S(2)}, u32[]{:S(2)}) %collective-permute-start.28) | collective-permute-done | bytes 393248 | tf_op jit(solution)/shard_map/b2/ppermute | solution.py:70
  110.4 9.1 %collective-permute-done.31 = bf16[32,2048]{1,0:T(8,128)(2,1)S(1)} collective-permute-done((bf16[32,2048]{1,0:T(8,128)(2,1)S(1)}, bf16[32,2048]{1,0:T(8,128)(2,1)S(1)}, u32[]{:S(2)}, u32[]{:S(2)}) %collective-permute-start.31) | collective-permute-done | bytes 131104 | tf_op jit(solution)/shard_map/mix0/ppermute | solution.py:70
  123.2 2.0 %own2.1.rest_0_ = f32[192,2048]{1,0:T(8,128)S(1)} custom-call(bf16[192,1024]{1,0:T(8,128)(2,1)S(1)} %hide2.1.one, bf16[192,1024]{1,0:T(8,128)(2,1)S(1)} %collective-permute-done.33.two, bf16[2,1024,2048]{2,1,0:T(8,128)(2,1)S(1)} %down0.1.weights), custom_call_target="tpu_custom_call" | custom-call | flops 17179869184 | bytes 1 | tf_op jit(solution)/shard_map/own2/pallas_call | solution.py:203
  125.2 2.0 %rest1.1 = f32[192,2048]{1,0:T(8,128)S(1)} custom-call(bf16[192,1024]{1,0:T(8,128)(2,1)S(1)} %collective-permute-done.30.one, bf16[192,1024]{1,0:T(8,128)(2,1)S(1)} %collective-permute-done.34.two, bf16[2,1024,2048]{2,1,0:T(8,128)(2,1)S(1)} %down2.1.weights, f32[192,2048]{1,0:T(8,128)S(1)} %own1.1.rest_0_), custom_call_target="tpu_custom_call" | custom-call | flops 17179869184 | bytes 1 | tf_op jit(solution)/shard_map/rest1/pallas_call | solution.py:203
  129.0 2.4 %collective-permute-start.39 = (bf16[96,2048]{1,0:T(8,128)(2,1)S(1)}, bf16[96,2048]{1,0:T(8,128)(2,1)S(1)}, u32[]{:S(2)}, u32[]{:S(2)}) collective-permute-start(bf16[96,2048]{1,0:T(8,128)(2,1)S(1)} %get-tuple-element.162), channel_id=1, source_target_pairs={{1,4},{3,6},{4,1},{6,3},{9,12},{11,14},{12,9},{14,11},{17,20},{19,... | collective-permute-start | bytes 1179656 | tf_op jit(solution)/shard_map/out1/ppermute | solution.py:94
  131.4 2.0 %rest2.1 = f32[192,2048]{1,0:T(8,128)S(1)} custom-call(bf16[192,1024]{1,0:T(8,128)(2,1)S(1)} %collective-permute-done.29.one, bf16[192,1024]{1,0:T(8,128)(2,1)S(1)} %collective-permute-done.36.two, bf16[2,1024,2048]{2,1,0:T(8,128)(2,1)S(1)} %down2.1.weights, f32[192,2048]{1,0:T(8,128)S(1)} %own2.1.rest_0_), custom_call_target="tpu_custom_call" | custom-call | flops 17179869184 | bytes 1 | tf_op jit(solution)/shard_map/rest2/pallas_call | solution.py:203
  133.6 3.2 %collective-permute-start.40 = (bf16[96,2048]{1,0:T(8,128)(2,1)S(1)}, bf16[96,2048]{1,0:T(8,128)(2,1)S(1)}, u32[]{:S(2)}, u32[]{:S(2)}) collective-permute-start(bf16[96,2048]{1,0:T(8,128)(2,1)S(1)} %get-tuple-element.165), channel_id=1, source_target_pairs={{1,4},{3,6},{4,1},{6,3},{9,12},{11,14},{12,9},{14,11},{17,20},{19,... | collective-permute-start | bytes 1179656 | tf_op jit(solution)/shard_map/out2/ppermute | solution.py:94
  142.0 5.5 %collective-permute-done.40 = bf16[96,2048]{1,0:T(8,128)(2,1)S(1)} collective-permute-done((bf16[96,2048]{1,0:T(8,128)(2,1)S(1)}, bf16[96,2048]{1,0:T(8,128)(2,1)S(1)}, u32[]{:S(2)}, u32[]{:S(2)}) %collective-permute-start.40) | collective-permute-done | bytes 393248 | tf_op jit(solution)/shard_map/out2/ppermute | solution.py:94
  149.0 2.4 %collective-permute-start.44 = (bf16[48,2048]{1,0:T(8,128)(2,1)S(1)}, bf16[48,2048]{1,0:T(8,128)(2,1)S(1)}, u32[]{:S(2)}, u32[]{:S(2)}) collective-permute-start(bf16[48,2048]{1,0:T(8,128)(2,1)S(1)} %convert_select_fusion.4), channel_id=1, source_target_pairs={{0,8},{4,12},{8,0},{12,4},{1,9},{5,13},{9,1},{13,5},{2,10},{6,14},... | collective-permute-start | bytes 589832 | tf_op jit(solution)/shard_map/far_out1/ppermute | solution.py:74
  152.6 2.6 %collective-permute-start.43 = (bf16[48,2048]{1,0:T(8,128)(2,1)S(1)}, bf16[48,2048]{1,0:T(8,128)(2,1)S(1)}, u32[]{:S(2)}, u32[]{:S(2)}) collective-permute-start(bf16[48,2048]{1,0:T(8,128)(2,1)S(1)} %convert_select_fusion.3), channel_id=1, source_target_pairs={{0,8},{4,12},{8,0},{12,4},{1,9},{5,13},{9,1},{13,5},{2,10},{6,14},... | collective-permute-start | bytes 589832 | tf_op jit(solution)/shard_map/far_out2/ppermute | solution.py:74
  155.2 7.9 %collective-permute-done.44.got = bf16[48,2048]{1,0:T(8,128)(2,1)S(1)} collective-permute-done((bf16[48,2048]{1,0:T(8,128)(2,1)S(1)}, bf16[48,2048]{1,0:T(8,128)(2,1)S(1)}, u32[]{:S(2)}, u32[]{:S(2)}) %collective-permute-start.44) | collective-permute-done | bytes 196640 | tf_op jit(solution)/shard_map/far_out1/ppermute | solution.py:74
  163.4 2.6 %collective-permute-done.43.got = bf16[48,2048]{1,0:T(8,128)(2,1)S(1)} collective-permute-done((bf16[48,2048]{1,0:T(8,128)(2,1)S(1)}, bf16[48,2048]{1,0:T(8,128)(2,1)S(1)}, u32[]{:S(2)}, u32[]{:S(2)}) %collective-permute-start.43) | collective-permute-done | bytes 196640 | tf_op jit(solution)/shard_map/far_out2/ppermute | solution.py:74
  (124 shorter events, 54.2 us)
Async XLA Ops:
  2.8 9.2 %collective-permute-start = (bf16[32,2048]{1,0:T(8,128)(2,1)S(1)}, bf16[32,2048]{1,0:T(8,128)(2,1)S(1)}, u32[]{:S(2)}, u32[]{:S(2)}) collective-permute-start(bf16[32,2048]{1,0:T(8,128)(2,1)S(1)} %get-tuple-element.89), channel_id=1, source_target_pairs={{0,8},{4,12},{8,0},{12,4},{1,9},{5,13},{9,1},{13,5},{2,10},{6,14},... | collective-permute-start | bytes 393224 | tf_op jit(solution)/shard_map/far0/ppermute | solution.py:74
  13.1 18.1 %collective-permute-start.1 = (bf16[48,2048]{1,0:T(8,128)(2,1)S(1)}, bf16[48,2048]{1,0:T(8,128)(2,1)S(1)}, u32[]{:S(2)}, u32[]{:S(2)}) collective-permute-start(bf16[48,2048]{1,0:T(8,128)(2,1)S(1)} %get-tuple-element.94), channel_id=1, source_target_pairs={{0,8},{4,12},{8,0},{12,4},{1,9},{5,13},{9,1},{13,5},{2,10},{6,14},... | collective-permute-start | bytes 589832 | tf_op jit(solution)/shard_map/far1/ppermute | solution.py:74
  16.7 15.9 %collective-permute-start.5 = (bf16[64,2048]{1,0:T(8,128)(2,1)S(1)}, bf16[64,2048]{1,0:T(8,128)(2,1)S(1)}, u32[]{:S(2)}, u32[]{:S(2)}) collective-permute-start(bf16[64,2048]{1,0:T(8,128)(2,1)S(1)} %pad_maximum_fusion.5), channel_id=1, source_target_pairs={{1,4},{3,6},{4,1},{6,3},{9,12},{11,14},{12,9},{14,11},{17,20},{19,... | collective-permute-start | bytes 786440 | tf_op jit(solution)/shard_map/arr0/ppermute | solution.py:94
  24.1 8.6 %collective-permute-start.4 = (bf16[64,2048]{1,0:T(8,128)(2,1)S(1)}, bf16[64,2048]{1,0:T(8,128)(2,1)S(1)}, u32[]{:S(2)}, u32[]{:S(2)}) collective-permute-start(bf16[64,2048]{1,0:T(8,128)(2,1)S(1)} %pad_maximum_fusion.5), channel_id=1, source_target_pairs={{0,4},{1,0},{2,6},{3,2},{4,5},{5,1},{6,7},{7,3},{8,12},{9,8},{10,1... | collective-permute-start | bytes 786440 | tf_op jit(solution)/shard_map/arr0/ppermute | solution.py:94
  31.6 13.1 %collective-permute-start.3 = (bf16[48,2048]{1,0:T(8,128)(2,1)S(1)}, bf16[48,2048]{1,0:T(8,128)(2,1)S(1)}, u32[]{:S(2)}, u32[]{:S(2)}) collective-permute-start(bf16[48,2048]{1,0:T(8,128)(2,1)S(1)} %get-tuple-element.103), channel_id=1, source_target_pairs={{0,8},{4,12},{8,0},{12,4},{1,9},{5,13},{9,1},{13,5},{2,10},{6,14},... | collective-permute-start | bytes 589832 | tf_op jit(solution)/shard_map/far2/ppermute | solution.py:74
  34.3 7.3 %collective-permute-start.7 = (bf16[2,128,1024]{2,1,0:T(8,128)(2,1)S(1)}, bf16[2,128,1024]{2,1,0:T(8,128)(2,1)S(1)}, u32[]{:S(2)}, u32[]{:S(2)}) collective-permute-start(bf16[2,128,1024]{2,1,0:T(8,128)(2,1)S(1)} %a0.1), channel_id=1, source_target_pairs={{0,1},{1,0},{2,3},{3,2},{4,5},{5,4},{6,7},{7,6},{8,9},{9,8},{10,11... | collective-permute-start | bytes 1572872 | tf_op jit(solution)/shard_map/a0/ppermute | solution.py:70
  37.5 14.6 %collective-permute-start.11 = (bf16[96,2048]{1,0:T(8,128)(2,1)S(1)}, bf16[96,2048]{1,0:T(8,128)(2,1)S(1)}, u32[]{:S(2)}, u32[]{:S(2)}) collective-permute-start(bf16[96,2048]{1,0:T(8,128)(2,1)S(1)} %pad_maximum_fusion.3), channel_id=1, source_target_pairs={{1,4},{3,6},{4,1},{6,3},{9,12},{11,14},{12,9},{14,11},{17,20},{19,... | collective-permute-start | bytes 1179656 | tf_op jit(solution)/shard_map/arr1/ppermute | solution.py:94
  40.2 11.8 %collective-permute-start.10 = (bf16[96,2048]{1,0:T(8,128)(2,1)S(1)}, bf16[96,2048]{1,0:T(8,128)(2,1)S(1)}, u32[]{:S(2)}, u32[]{:S(2)}) collective-permute-start(bf16[96,2048]{1,0:T(8,128)(2,1)S(1)} %pad_maximum_fusion.3), channel_id=1, source_target_pairs={{0,4},{1,0},{2,6},{3,2},{4,5},{5,1},{6,7},{7,3},{8,12},{9,8},{10,1... | collective-permute-start | bytes 1179656 | tf_op jit(solution)/shard_map/arr1/ppermute | solution.py:94
  42.9 22.0 %collective-permute-start.14 = (bf16[128,1024]{1,0:T(8,128)(2,1)S(1)}, bf16[128,1024]{1,0:T(8,128)(2,1)S(1)}, u32[]{:S(2)}, u32[]{:S(2)}) collective-permute-start(bf16[128,1024]{1,0:T(8,128)(2,1)S(1)} %get-tuple-element.109), channel_id=1, source_target_pairs={{0,2},{1,3},{2,0},{3,1},{4,6},{5,7},{6,4},{7,5},{8,10},{9,11},{10,... | collective-permute-start | bytes 786440 | tf_op jit(solution)/shard_map/b0/ppermute | solution.py:70
  44.7 15.3 %collective-permute-start.9 = (bf16[48,2048]{1,0:T(8,128)(2,1)S(1)}, bf16[48,2048]{1,0:T(8,128)(2,1)S(1)}, u32[]{:S(2)}, u32[]{:S(2)}) collective-permute-start(bf16[48,2048]{1,0:T(8,128)(2,1)S(1)} %broadcast_select_fusion.16), channel_id=1, source_target_pairs={{0,2},{1,3},{2,0},{3,1},{4,6},{5,7},{6,4},{7,5},{8,10},{9,11},{10,... | collective-permute-start | bytes 589832 | tf_op jit(solution)/shard_map/sel2/ppermute | solution.py:70
  57.0 7.9 %collective-permute-start.16 = (bf16[128,1024]{1,0:T(8,128)(2,1)S(1)}, bf16[128,1024]{1,0:T(8,128)(2,1)S(1)}, u32[]{:S(2)}, u32[]{:S(2)}) collective-permute-start(bf16[128,1024]{1,0:T(8,128)(2,1)S(1)} %get-tuple-element.120), channel_id=1, source_target_pairs={{0,2},{1,3},{2,0},{3,1},{4,6},{5,7},{6,4},{7,5},{8,10},{9,11},{10,... | collective-permute-start | bytes 786440 | tf_op jit(solution)/shard_map/b0/ppermute | solution.py:70
  60.1 13.3 %collective-permute-start.17 = (bf16[96,2048]{1,0:T(8,128)(2,1)S(1)}, bf16[96,2048]{1,0:T(8,128)(2,1)S(1)}, u32[]{:S(2)}, u32[]{:S(2)}) collective-permute-start(bf16[96,2048]{1,0:T(8,128)(2,1)S(1)} %pad_maximum_fusion.4), channel_id=1, source_target_pairs={{1,4},{3,6},{4,1},{6,3},{9,12},{11,14},{12,9},{14,11},{17,20},{19,... | collective-permute-start | bytes 1179656 | tf_op jit(solution)/shard_map/arr2/ppermute | solution.py:94
  62.0 11.1 %collective-permute-start.13 = (bf16[96,2048]{1,0:T(8,128)(2,1)S(1)}, bf16[96,2048]{1,0:T(8,128)(2,1)S(1)}, u32[]{:S(2)}, u32[]{:S(2)}) collective-permute-start(bf16[96,2048]{1,0:T(8,128)(2,1)S(1)} %pad_maximum_fusion.4), channel_id=1, source_target_pairs={{0,4},{1,0},{2,6},{3,2},{4,5},{5,1},{6,7},{7,3},{8,12},{9,8},{10,1... | collective-permute-start | bytes 1179656 | tf_op jit(solution)/shard_map/arr2/ppermute | solution.py:94
  65.0 22.5 %collective-permute-start.22 = (bf16[128,1024]{1,0:T(8,128)(2,1)S(1)}, bf16[128,1024]{1,0:T(8,128)(2,1)S(1)}, u32[]{:S(2)}, u32[]{:S(2)}) collective-permute-start(bf16[128,1024]{1,0:T(8,128)(2,1)S(1)} %hide0.1.one), channel_id=1, source_target_pairs={{0,1},{1,0},{2,3},{3,2},{4,5},{5,4},{6,7},{7,6},{8,9},{9,8},{10,11... | collective-permute-start | bytes 786440 | tf_op jit(solution)/shard_map/hide0/ppermute | solution.py:70
  66.7 22.7 %collective-permute-start.21 = (bf16[128,1024]{1,0:T(8,128)(2,1)S(1)}, bf16[128,1024]{1,0:T(8,128)(2,1)S(1)}, u32[]{:S(2)}, u32[]{:S(2)}) collective-permute-start(bf16[128,1024]{1,0:T(8,128)(2,1)S(1)} %hide0.1.one), channel_id=1, source_target_pairs={{0,2},{1,3},{2,0},{3,1},{4,6},{5,7},{6,4},{7,5},{8,10},{9,11},{10,... | collective-permute-start | bytes 786440 | tf_op jit(solution)/shard_map/hide0/ppermute | solution.py:70
  67.2 29.1 %collective-permute-start.25 = (bf16[192,1024]{1,0:T(8,128)(2,1)S(1)}, bf16[192,1024]{1,0:T(8,128)(2,1)S(1)}, u32[]{:S(2)}, u32[]{:S(2)}) collective-permute-start(bf16[192,1024]{1,0:T(8,128)(2,1)S(1)} %get-tuple-element.116), channel_id=1, source_target_pairs={{0,2},{1,3},{2,0},{3,1},{4,6},{5,7},{6,4},{7,5},{8,10},{9,11},{10,... | collective-permute-start | bytes 1179656 | tf_op jit(solution)/shard_map/b1/ppermute | solution.py:70
  73.1 23.2 %collective-permute-start.26 = (bf16[192,1024]{1,0:T(8,128)(2,1)S(1)}, bf16[192,1024]{1,0:T(8,128)(2,1)S(1)}, u32[]{:S(2)}, u32[]{:S(2)}) collective-permute-start(bf16[192,1024]{1,0:T(8,128)(2,1)S(1)} %get-tuple-element.136), channel_id=1, source_target_pairs={{0,2},{1,3},{2,0},{3,1},{4,6},{5,7},{6,4},{7,5},{8,10},{9,11},{10,... | collective-permute-start | bytes 1179656 | tf_op jit(solution)/shard_map/b1/ppermute | solution.py:70
  80.3 28.0 %collective-permute-start.20 = (bf16[192,1024]{1,0:T(8,128)(2,1)S(1)}, bf16[192,1024]{1,0:T(8,128)(2,1)S(1)}, u32[]{:S(2)}, u32[]{:S(2)}) collective-permute-start(bf16[192,1024]{1,0:T(8,128)(2,1)S(1)} %get-tuple-element.126), channel_id=1, source_target_pairs={{0,2},{1,3},{2,0},{3,1},{4,6},{5,7},{6,4},{7,5},{8,10},{9,11},{10,... | collective-permute-start | bytes 1179656 | tf_op jit(solution)/shard_map/b2/ppermute | solution.py:70
  87.5 20.7 %collective-permute-start.28 = (bf16[192,1024]{1,0:T(8,128)(2,1)S(1)}, bf16[192,1024]{1,0:T(8,128)(2,1)S(1)}, u32[]{:S(2)}, u32[]{:S(2)}) collective-permute-start(bf16[192,1024]{1,0:T(8,128)(2,1)S(1)} %get-tuple-element.140), channel_id=1, source_target_pairs={{0,2},{1,3},{2,0},{3,1},{4,6},{5,7},{6,4},{7,5},{8,10},{9,11},{10,... | collective-permute-start | bytes 1179656 | tf_op jit(solution)/shard_map/b2/ppermute | solution.py:70
  96.3 8.4 %collective-permute-start.27 = (bf16[64,2048]{1,0:T(8,128)(2,1)S(1)}, bf16[64,2048]{1,0:T(8,128)(2,1)S(1)}, u32[]{:S(2)}, u32[]{:S(2)}) collective-permute-start(bf16[64,2048]{1,0:T(8,128)(2,1)S(1)} %get-tuple-element.171), channel_id=1, source_target_pairs={{1,4},{3,6},{4,1},{6,3},{9,12},{11,14},{12,9},{14,11},{17,20},{19,... | collective-permute-start | bytes 786440 | tf_op jit(solution)/shard_map/out0/ppermute | solution.py:94
  99.8 19.9 %collective-permute-start.32 = (bf16[192,1024]{1,0:T(8,128)(2,1)S(1)}, bf16[192,1024]{1,0:T(8,128)(2,1)S(1)}, u32[]{:S(2)}, u32[]{:S(2)}) collective-permute-start(bf16[192,1024]{1,0:T(8,128)(2,1)S(1)} %hide1.1.one), channel_id=1, source_target_pairs={{0,1},{1,0},{2,3},{3,2},{4,5},{5,4},{6,7},{7,6},{8,9},{9,8},{10,11... | collective-permute-start | bytes 1179656 | tf_op jit(solution)/shard_map/hide1/ppermute | solution.py:70
  99.9 21.8 %collective-permute-start.30 = (bf16[192,1024]{1,0:T(8,128)(2,1)S(1)}, bf16[192,1024]{1,0:T(8,128)(2,1)S(1)}, u32[]{:S(2)}, u32[]{:S(2)}) collective-permute-start(bf16[192,1024]{1,0:T(8,128)(2,1)S(1)} %hide1.1.one), channel_id=1, source_target_pairs={{0,2},{1,3},{2,0},{3,1},{4,6},{5,7},{6,4},{7,5},{8,10},{9,11},{10,... | collective-permute-start | bytes 1179656 | tf_op jit(solution)/shard_map/hide1/ppermute | solution.py:70
  104.9 14.7 %collective-permute-start.31 = (bf16[32,2048]{1,0:T(8,128)(2,1)S(1)}, bf16[32,2048]{1,0:T(8,128)(2,1)S(1)}, u32[]{:S(2)}, u32[]{:S(2)}) collective-permute-start(bf16[32,2048]{1,0:T(8,128)(2,1)S(1)} %select_convert_fusion.5), channel_id=1, source_target_pairs={{0,2},{1,3},{2,0},{3,1},{4,6},{5,7},{6,4},{7,5},{8,10},{9,11},{10,... | collective-permute-start | bytes 393224 | tf_op jit(solution)/shard_map/mix0/ppermute | solution.py:70
  108.6 14.6 %collective-permute-start.33 = (bf16[192,1024]{1,0:T(8,128)(2,1)S(1)}, bf16[192,1024]{1,0:T(8,128)(2,1)S(1)}, u32[]{:S(2)}, u32[]{:S(2)}) collective-permute-start(bf16[192,1024]{1,0:T(8,128)(2,1)S(1)} %hide2.1.one), channel_id=1, source_target_pairs={{0,1},{1,0},{2,3},{3,2},{4,5},{5,4},{6,7},{7,6},{8,9},{9,8},{10,11... | collective-permute-start | bytes 1179656 | tf_op jit(solution)/shard_map/hide2/ppermute | solution.py:70
  109.9 18.9 %collective-permute-start.29 = (bf16[192,1024]{1,0:T(8,128)(2,1)S(1)}, bf16[192,1024]{1,0:T(8,128)(2,1)S(1)}, u32[]{:S(2)}, u32[]{:S(2)}) collective-permute-start(bf16[192,1024]{1,0:T(8,128)(2,1)S(1)} %hide2.1.one), channel_id=1, source_target_pairs={{0,2},{1,3},{2,0},{3,1},{4,6},{5,7},{6,4},{7,5},{8,10},{9,11},{10,... | collective-permute-start | bytes 1179656 | tf_op jit(solution)/shard_map/hide2/ppermute | solution.py:70
  119.6 9.3 %collective-permute-start.35 = (bf16[32,2048]{1,0:T(8,128)(2,1)S(1)}, bf16[32,2048]{1,0:T(8,128)(2,1)S(1)}, u32[]{:S(2)}, u32[]{:S(2)}) collective-permute-start(bf16[32,2048]{1,0:T(8,128)(2,1)S(1)} %convert_select_fusion.5), channel_id=1, source_target_pairs={{0,8},{4,12},{8,0},{12,4},{1,9},{5,13},{9,1},{13,5},{2,10},{6,14},... | collective-permute-start | bytes 393224 | tf_op jit(solution)/shard_map/far_out0/ppermute | solution.py:74
  129.0 9.7 %collective-permute-start.39 = (bf16[96,2048]{1,0:T(8,128)(2,1)S(1)}, bf16[96,2048]{1,0:T(8,128)(2,1)S(1)}, u32[]{:S(2)}, u32[]{:S(2)}) collective-permute-start(bf16[96,2048]{1,0:T(8,128)(2,1)S(1)} %get-tuple-element.162), channel_id=1, source_target_pairs={{1,4},{3,6},{4,1},{6,3},{9,12},{11,14},{12,9},{14,11},{17,20},{19,... | collective-permute-start | bytes 1179656 | tf_op jit(solution)/shard_map/out1/ppermute | solution.py:94
  133.5 8.5 %collective-permute-start.37 = (bf16[96,2048]{1,0:T(8,128)(2,1)S(1)}, bf16[96,2048]{1,0:T(8,128)(2,1)S(1)}, u32[]{:S(2)}, u32[]{:S(2)}) collective-permute-start(bf16[96,2048]{1,0:T(8,128)(2,1)S(1)} %get-tuple-element.164), channel_id=1, source_target_pairs={{0,1},{1,5},{2,3},{3,7},{4,0},{5,4},{6,2},{7,6},{8,9},{9,13},{10,1... | collective-permute-start | bytes 1179656 | tf_op jit(solution)/shard_map/out2/ppermute | solution.py:94
  133.6 13.9 %collective-permute-start.40 = (bf16[96,2048]{1,0:T(8,128)(2,1)S(1)}, bf16[96,2048]{1,0:T(8,128)(2,1)S(1)}, u32[]{:S(2)}, u32[]{:S(2)}) collective-permute-start(bf16[96,2048]{1,0:T(8,128)(2,1)S(1)} %get-tuple-element.165), channel_id=1, source_target_pairs={{1,4},{3,6},{4,1},{6,3},{9,12},{11,14},{12,9},{14,11},{17,20},{19,... | collective-permute-start | bytes 1179656 | tf_op jit(solution)/shard_map/out2/ppermute | solution.py:94
  138.9 10.0 %collective-permute-start.42 = (bf16[48,2048]{1,0:T(8,128)(2,1)S(1)}, bf16[48,2048]{1,0:T(8,128)(2,1)S(1)}, u32[]{:S(2)}, u32[]{:S(2)}) collective-permute-start(bf16[48,2048]{1,0:T(8,128)(2,1)S(1)} %select_convert_fusion.4), channel_id=1, source_target_pairs={{0,2},{1,3},{2,0},{3,1},{4,6},{5,7},{6,4},{7,5},{8,10},{9,11},{10,... | collective-permute-start | bytes 589832 | tf_op jit(solution)/shard_map/mix1/ppermute | solution.py:70
  149.0 14.1 %collective-permute-start.44 = (bf16[48,2048]{1,0:T(8,128)(2,1)S(1)}, bf16[48,2048]{1,0:T(8,128)(2,1)S(1)}, u32[]{:S(2)}, u32[]{:S(2)}) collective-permute-start(bf16[48,2048]{1,0:T(8,128)(2,1)S(1)} %convert_select_fusion.4), channel_id=1, source_target_pairs={{0,8},{4,12},{8,0},{12,4},{1,9},{5,13},{9,1},{13,5},{2,10},{6,14},... | collective-permute-start | bytes 589832 | tf_op jit(solution)/shard_map/far_out1/ppermute | solution.py:74
  152.6 13.4 %collective-permute-start.43 = (bf16[48,2048]{1,0:T(8,128)(2,1)S(1)}, bf16[48,2048]{1,0:T(8,128)(2,1)S(1)}, u32[]{:S(2)}, u32[]{:S(2)}) collective-permute-start(bf16[48,2048]{1,0:T(8,128)(2,1)S(1)} %convert_select_fusion.3), channel_id=1, source_target_pairs={{0,8},{4,12},{8,0},{12,4},{1,9},{5,13},{9,1},{13,5},{2,10},{6,14},... | collective-permute-start | bytes 589832 | tf_op jit(solution)/shard_map/far_out2/ppermute | solution.py:74
  (15 other events, 56.0 us)

commit v5 on v4

--- a/solution.py
+++ b/solution.py
@@ -7,13 +7,13 @@
 from jax.experimental.pallas import tpu as pltpu
 from jax.sharding import PartitionSpec as P
 
-ROWS = (32, 48, 48)
+ROWS = (32, 64, 32)
 ORDER = (
     "far0", "load3", "sel0", "far1", "load1", "arr0", "load2", "load0", "sel1", "far2", "take0", "a0", "c0",
-    "arr1", "b0", "d0", "sel2", "take1", "a1", "c1", "b1", "arr2", "d1", "hide0", "take2", "a2", "c2", "b2",
-    "d2", "down0", "own0", "forward0", "down2", "rest0", "out0", "hide1", "mix0", "hide2", "far_out0", "own1",
-    "forward1", "own2", "rest1", "out1", "forward2", "end0", "rest2", "out2", "mix1", "mix2", "far_out1",
-    "far_out2", "end1", "end2",
+    "b0", "arr1", "d0", "sel2", "take1", "a1", "c1", "b1", "d1", "hide0", "arr2", "take2", "a2", "c2",
+    "down0", "forward0", "own0", "hide1", "b2", "d2", "down2", "rest0", "out0", "own1", "forward1", "hide2",
+    "rest1", "out1", "mix0", "own2", "far_out0", "forward2", "mix1", "rest2", "out2", "end0", "mix2",
+    "far_out1", "far_out2", "end1", "end2",
 )
 TILE = 256
 COST = 1 << 34

time: 167 us -> 179 us (1.072)
  waiting for transfers between devices: 51 us -> 68.1 us
  starting transfers between devices: 54.2 us -> 48.9 us
    ppermute x27, waiting for transfers between devices: 14.1 us -> 24.5 us  [over_seq(): return lax.ppermute(array, 'seq', [(i, i ^ bit) for i in range(4)])]
    ppermute x27, starting transfers between devices: 21.7 us -> 17.2 us  [over_seq(): return lax.ppermute(array, 'seq', [(i, i ^ bit) for i in range(4)])]
    ppermute x12, waiting for transfers between devices: 23.9 us -> 27.8 us  [over_both(): return lax.ppermute(array, ('tp', 'seq'), pairs)]
    ppermute x6, waiting for transfers between devices: 13 us -> 15.9 us  [over_tp(): return lax.ppermute(array, 'tp', [(i, i ^ bit) for i in range(4)])]
    ppermute x6, starting transfers between devices: 9.39 us -> 7.48 us  [over_tp(): return lax.ppermute(array, 'tp', [(i, i ^ bit) for i in range(4)])]
  transfers between devices with their start and end apart: 45 -> 45, of which waited for: 17 -> 13; matrix products, arithmetic and copies ran while one was open for 1% -> 1% of each run, Pallas kernels for 33% -> 31%
where the time goes in v5:
time: 179 us
  waiting for transfers between devices  68.1 us (38%)
  Pallas kernels  56.6 us (32%)
  starting transfers between devices  48.9 us (27%)
  other arithmetic  2.21 us (1%)
    ppermute x12, waiting for transfers between devices, over_both(): return lax.ppermute(array, ('tp', 'seq'), pairs)  27.8 us
    ppermute x27, waiting for transfers between devices, over_seq(): return lax.ppermute(array, 'seq', [(i, i ^ bit) for i in range(4)])  24.5 us
    ppermute x12, starting transfers between devices, over_both(): return lax.ppermute(array, ('tp', 'seq'), pairs)  24.2 us
    pallas_call x12, Pallas kernels, sums(): pl.pallas_call(functools.partial(sums_kernel, got is not None, split), ou...  21.1 us
    ppermute x27, starting transfers between devices, over_seq(): return lax.ppermute(array, 'seq', [(i, i ^ bit) for i in range(4)])  17.2 us
    ppermute x6, waiting for transfers between devices, over_tp(): return lax.ppermute(array, 'tp', [(i, i ^ bit) for i in range(4)])  15.9 us
    pallas_call x4, Pallas kernels, load(): pl.pallas_call(load_kernel, out_shape=jax.ShapeDtypeStruct((2, deep, widt...  14 us
    pallas_call x6, Pallas kernels, products(): pl.pallas_call(functools.partial(products_kernel, total is not None), out...  10.9 us
  transfers between devices with their start and end apart: 45, of which 13 were waited for; matrix products, arithmetic and copies ran while one was open for 1% of the time, Pallas kernels for 31%

profile of v5, /device:TPU:1, one launch (start us, length us, event | category | flops | bytes accessed | tf_op | source)
XLA Modules:
  0.0 178.8 jit_solution(9648301979015901693)
XLA Ops:
  2.8 3.2 %collective-permute-start = (bf16[32,2048]{1,0:T(8,128)(2,1)S(1)}, bf16[32,2048]{1,0:T(8,128)(2,1)S(1)}, u32[]{:S(2)}, u32[]{:S(2)}) collective-permute-start(bf16[32,2048]{1,0:T(8,128)(2,1)S(1)} %get-tuple-element.89), channel_id=1, source_target_pairs={{0,8},{4,12},{8,0},{12,4},{1,9},{5,13},{9,1},{13,5},{2,10},{6,14},... | collective-permute-start | bytes 393224 | tf_op jit(solution)/shard_map/far0/ppermute | solution.py:74
  6.1 3.5 %load3.1.weights = bf16[2,2048,1024]{2,1,0:T(8,128)(2,1)S(1)} custom-call(s32[1]{0:T(128)} %bitcast.3.quarter, bf16[2048,4096]{1,0:T(8,128)(2,1)} %gate_weight.3, bf16[2048,4096]{1,0:T(8,128)(2,1)} %up_weight.7), custom_call_target="tpu_custom_call" | custom-call | flops 1073741824 | bytes 1 | tf_op jit(solution)/shard_map/load3/pallas_call | solution.py:120
  9.6 2.4 %collective-permute-done = bf16[32,2048]{1,0:T(8,128)(2,1)S(1)} collective-permute-done((bf16[32,2048]{1,0:T(8,128)(2,1)S(1)}, bf16[32,2048]{1,0:T(8,128)(2,1)S(1)}, u32[]{:S(2)}, u32[]{:S(2)}) %collective-permute-start) | collective-permute-done | bytes 131104 | tf_op jit(solution)/shard_map/far0/ppermute | solution.py:74
  13.1 3.5 %load1.1.weights = bf16[2,2048,1024]{2,1,0:T(8,128)(2,1)S(1)} custom-call(s32[1]{0:T(128)} %bitcast.1.quarter, bf16[2048,4096]{1,0:T(8,128)(2,1)} %gate_weight.3, bf16[2048,4096]{1,0:T(8,128)(2,1)} %up_weight.7), custom_call_target="tpu_custom_call" | custom-call | flops 1073741824 | bytes 1 | tf_op jit(solution)/shard_map/load1/pallas_call | solution.py:120
  16.7 7.4 %collective-permute-start.5 = (bf16[64,2048]{1,0:T(8,128)(2,1)S(1)}, bf16[64,2048]{1,0:T(8,128)(2,1)S(1)}, u32[]{:S(2)}, u32[]{:S(2)}) collective-permute-start(bf16[64,2048]{1,0:T(8,128)(2,1)S(1)} %pad_maximum_fusion.4), channel_id=1, source_target_pairs={{1,4},{3,6},{4,1},{6,3},{9,12},{11,14},{12,9},{14,11},{17,20},{19,... | collective-permute-start | bytes 786440 | tf_op jit(solution)/shard_map/arr0/ppermute | solution.py:94
  24.2 3.5 %load2.1.weights = bf16[2,2048,1024]{2,1,0:T(8,128)(2,1)S(1)} custom-call(s32[1]{0:T(128)} %bitcast.2.quarter, bf16[2048,4096]{1,0:T(8,128)(2,1)} %gate_weight.3, bf16[2048,4096]{1,0:T(8,128)(2,1)} %up_weight.7), custom_call_target="tpu_custom_call" | custom-call | flops 1073741824 | bytes 1 | tf_op jit(solution)/shard_map/load2/pallas_call | solution.py:120
  27.7 3.5 %load0.1.weights = bf16[2,2048,1024]{2,1,0:T(8,128)(2,1)S(1)} custom-call(s32[1]{0:T(128)} %bitcast.quarter, bf16[2048,4096]{1,0:T(8,128)(2,1)} %gate_weight.3, bf16[2048,4096]{1,0:T(8,128)(2,1)} %up_weight.7), custom_call_target="tpu_custom_call" | custom-call | flops 1073741824 | bytes 1 | tf_op jit(solution)/shard_map/load0/pallas_call | solution.py:120
  39.0 2.7 %collective-permute-start.12 = (bf16[128,2048]{1,0:T(8,128)(2,1)S(1)}, bf16[128,2048]{1,0:T(8,128)(2,1)S(1)}, u32[]{:S(2)}, u32[]{:S(2)}) collective-permute-start(bf16[128,2048]{1,0:T(8,128)(2,1)S(1)} %pad_maximum_fusion.2), channel_id=1, source_target_pairs={{1,4},{3,6},{4,1},{6,3},{9,12},{11,14},{12,9},{14,11},{17,20},{19,... | collective-permute-start | bytes 1572872 | tf_op jit(solution)/shard_map/arr1/ppermute | solution.py:94
  44.9 10.3 %collective-permute-done.11 = bf16[128,2048]{1,0:T(8,128)(2,1)S(1)} collective-permute-done((bf16[128,2048]{1,0:T(8,128)(2,1)S(1)}, bf16[128,2048]{1,0:T(8,128)(2,1)S(1)}, u32[]{:S(2)}, u32[]{:S(2)}) %collective-permute-start.11) | collective-permute-done | bytes 524320 | tf_op jit(solution)/shard_map/arr1/ppermute | solution.py:94
  55.5 2.5 %a1.1 = bf16[2,256,1024]{2,1,0:T(8,128)(2,1)S(1)} custom-call(bf16[256,2048]{1,0:T(8,128)(2,1)S(1)} %pad_maximum_fusion.some, bf16[2,2048,1024]{2,1,0:T(8,128)(2,1)S(1)} %load3.1.weights), custom_call_target="tpu_custom_call" | custom-call | flops 17179869184 | bytes 1 | tf_op jit(solution)/shard_map/a1/pallas_call | solution.py:149
  58.1 2.5 %c1.1 = bf16[2,256,1024]{2,1,0:T(8,128)(2,1)S(1)} custom-call(bf16[256,2048]{1,0:T(8,128)(2,1)S(1)} %pad_maximum_fusion.some, bf16[2,2048,1024]{2,1,0:T(8,128)(2,1)S(1)} %load1.1.weights), custom_call_target="tpu_custom_call" | custom-call | flops 17179869184 | bytes 1 | tf_op jit(solution)/shard_map/c1/pallas_call | solution.py:149
  61.2 2.3 %b1.1 = (bf16[256,1024]{1,0:T(8,128)(2,1)S(1)}, bf16[256,1024]{1,0:T(8,128)(2,1)S(1)}) custom-call(bf16[256,2048]{1,0:T(8,128)(2,1)S(1)} %pad_maximum_fusion.some, bf16[2,2048,1024]{2,1,0:T(8,128)(2,1)S(1)} %load2.1.weights, bf16[2,256,1024]{2,1,0:T(8,128)(2,1)S(1)} %collective-permute-done.13.rest_0_), custom_call_target="tpu_custom_call" | custom-call | flops 17179869184 | bytes 1 | tf_op jit(solution)/shard_map/b1/pallas_call | solution.py:149
  63.5 2.5 %d1.1.held = f32[2,256,1024]{2,1,0:T(8,128)S(1)} custom-call(bf16[256,2048]{1,0:T(8,128)(2,1)S(1)} %pad_maximum_fusion.some, bf16[2,2048,1024]{2,1,0:T(8,128)(2,1)S(1)} %load0.1.weights, bf16[2,256,1024]{2,1,0:T(8,128)(2,1)S(1)} %collective-permute-done.14.rest_0_), custom_call_target="tpu_custom_call" | custom-call | flops 17179869184 | bytes 1 | tf_op jit(solution)/shard_map/d1/pallas_call | solution.py:149
  66.7 2.8 %collective-permute-start.17 = (bf16[64,2048]{1,0:T(8,128)(2,1)S(1)}, bf16[64,2048]{1,0:T(8,128)(2,1)S(1)}, u32[]{:S(2)}, u32[]{:S(2)}) collective-permute-start(bf16[64,2048]{1,0:T(8,128)(2,1)S(1)} %pad_maximum_fusion.5), channel_id=1, source_target_pairs={{1,4},{3,6},{4,1},{6,3},{9,12},{11,14},{12,9},{14,11},{17,20},{19,... | collective-permute-start | bytes 786440 | tf_op jit(solution)/shard_map/arr2/ppermute | solution.py:94
  72.9 1.9 %collective-permute-done.17 = bf16[64,2048]{1,0:T(8,128)(2,1)S(1)} collective-permute-done((bf16[64,2048]{1,0:T(8,128)(2,1)S(1)}, bf16[64,2048]{1,0:T(8,128)(2,1)S(1)}, u32[]{:S(2)}, u32[]{:S(2)}) %collective-permute-start.17) | collective-permute-done | bytes 262176 | tf_op jit(solution)/shard_map/arr2/ppermute | solution.py:94
  77.9 4.0 %down0.1.weights = bf16[2,1024,2048]{2,1,0:T(8,128)(2,1)S(1)} custom-call(s32[2]{0:T(128)S(1)} %get-tuple-element.123.quarters, bf16[4096,2048]{1,0:T(8,128)(2,1)} %weight.1), custom_call_target="tpu_custom_call" | custom-call | flops 17179869184 | bytes 1 | tf_op jit(solution)/shard_map/down0/pallas_call | solution.py:180
  84.1 15.4 %collective-permute-done.20.got_up = bf16[256,1024]{1,0:T(8,128)(2,1)S(1)} collective-permute-done((bf16[256,1024]{1,0:T(8,128)(2,1)S(1)}, bf16[256,1024]{1,0:T(8,128)(2,1)S(1)}, u32[]{:S(2)}, u32[]{:S(2)}) %collective-permute-start.20) | collective-permute-done | bytes 524320 | tf_op jit(solution)/shard_map/b1/ppermute | solution.py:70
  104.5 4.0 %down2.1.weights = bf16[2,1024,2048]{2,1,0:T(8,128)(2,1)S(1)} custom-call(s32[2]{0:T(128)S(1)} %get-tuple-element.135.quarters, bf16[4096,2048]{1,0:T(8,128)(2,1)} %weight.1), custom_call_target="tpu_custom_call" | custom-call | flops 17179869184 | bytes 1 | tf_op jit(solution)/shard_map/down2/pallas_call | solution.py:180
  108.6 1.5 rest0.1
  111.6 4.0 %collective-permute-start.32 = (bf16[64,2048]{1,0:T(8,128)(2,1)S(1)}, bf16[64,2048]{1,0:T(8,128)(2,1)S(1)}, u32[]{:S(2)}, u32[]{:S(2)}) collective-permute-start(bf16[64,2048]{1,0:T(8,128)(2,1)S(1)} %get-tuple-element.168), channel_id=1, source_target_pairs={{1,4},{3,6},{4,1},{6,3},{9,12},{11,14},{12,9},{14,11},{17,20},{19,... | collective-permute-start | bytes 786440 | tf_op jit(solution)/shard_map/out0/ppermute | solution.py:94
  115.6 2.5 %own1.1.rest_0_ = f32[256,2048]{1,0:T(8,128)S(1)} custom-call(bf16[256,1024]{1,0:T(8,128)(2,1)S(1)} %hide1.1.one, bf16[256,1024]{1,0:T(8,128)(2,1)S(1)} %collective-permute-done.26.two, bf16[2,1024,2048]{2,1,0:T(8,128)(2,1)S(1)} %down0.1.weights), custom_call_target="tpu_custom_call" | custom-call | flops 17179869184 | bytes 1 | tf_op jit(solution)/shard_map/own1/pallas_call | solution.py:203
  118.1 6.5 %collective-permute-done.27.got_up = bf16[128,1024]{1,0:T(8,128)(2,1)S(1)} collective-permute-done((bf16[128,1024]{1,0:T(8,128)(2,1)S(1)}, bf16[128,1024]{1,0:T(8,128)(2,1)S(1)}, u32[]{:S(2)}, u32[]{:S(2)}) %collective-permute-start.27) | collective-permute-done | bytes 262176 | tf_op jit(solution)/shard_map/b2/ppermute | solution.py:70
  127.0 2.5 %rest1.1 = f32[256,2048]{1,0:T(8,128)S(1)} custom-call(bf16[256,1024]{1,0:T(8,128)(2,1)S(1)} %collective-permute-done.30.one, bf16[256,1024]{1,0:T(8,128)(2,1)S(1)} %collective-permute-done.31.two, bf16[2,1024,2048]{2,1,0:T(8,128)(2,1)S(1)} %down2.1.weights, f32[256,2048]{1,0:T(8,128)S(1)} %own1.1.rest_0_), custom_call_target="tpu_custom_call" | custom-call | flops 17179869184 | bytes 1 | tf_op jit(solution)/shard_map/rest1/pallas_call | solution.py:203
  131.1 4.2 %collective-permute-start.36 = (bf16[128,2048]{1,0:T(8,128)(2,1)S(1)}, bf16[128,2048]{1,0:T(8,128)(2,1)S(1)}, u32[]{:S(2)}, u32[]{:S(2)}) collective-permute-start(bf16[128,2048]{1,0:T(8,128)(2,1)S(1)} %get-tuple-element.162), channel_id=1, source_target_pairs={{1,4},{3,6},{4,1},{6,3},{9,12},{11,14},{12,9},{14,11},{17,20},{19,... | collective-permute-start | bytes 1572872 | tf_op jit(solution)/shard_map/out1/ppermute | solution.py:94
  135.3 1.5 own2.1.rest_0_
  136.8 1.7 collective-permute-start.39
  140.0 8.7 %collective-permute-done.36 = bf16[128,2048]{1,0:T(8,128)(2,1)S(1)} collective-permute-done((bf16[128,2048]{1,0:T(8,128)(2,1)S(1)}, bf16[128,2048]{1,0:T(8,128)(2,1)S(1)}, u32[]{:S(2)}, u32[]{:S(2)}) %collective-permute-start.36) | collective-permute-done | bytes 524320 | tf_op jit(solution)/shard_map/out1/ppermute | solution.py:94
  151.3 2.0 %collective-permute-start.40 = (bf16[64,2048]{1,0:T(8,128)(2,1)S(1)}, bf16[64,2048]{1,0:T(8,128)(2,1)S(1)}, u32[]{:S(2)}, u32[]{:S(2)}) collective-permute-start(bf16[64,2048]{1,0:T(8,128)(2,1)S(1)} %get-tuple-element.167), channel_id=1, source_target_pairs={{1,4},{3,6},{4,1},{6,3},{9,12},{11,14},{12,9},{14,11},{17,20},{19,... | collective-permute-start | bytes 786440 | tf_op jit(solution)/shard_map/out2/ppermute | solution.py:94
  154.6 4.4 %collective-permute-done.40 = bf16[64,2048]{1,0:T(8,128)(2,1)S(1)} collective-permute-done((bf16[64,2048]{1,0:T(8,128)(2,1)S(1)}, bf16[64,2048]{1,0:T(8,128)(2,1)S(1)}, u32[]{:S(2)}, u32[]{:S(2)}) %collective-permute-start.40) | collective-permute-done | bytes 262176 | tf_op jit(solution)/shard_map/out2/ppermute | solution.py:94
  160.8 2.5 %collective-permute-done.41 = bf16[32,2048]{1,0:T(8,128)(2,1)S(1)} collective-permute-done((bf16[32,2048]{1,0:T(8,128)(2,1)S(1)}, bf16[32,2048]{1,0:T(8,128)(2,1)S(1)}, u32[]{:S(2)}, u32[]{:S(2)}) %collective-permute-start.41) | collective-permute-done | bytes 131104 | tf_op jit(solution)/shard_map/mix2/ppermute | solution.py:70
  164.2 11.0 %collective-permute-done.44.got = bf16[64,2048]{1,0:T(8,128)(2,1)S(1)} collective-permute-done((bf16[64,2048]{1,0:T(8,128)(2,1)S(1)}, bf16[64,2048]{1,0:T(8,128)(2,1)S(1)}, u32[]{:S(2)}, u32[]{:S(2)}) %collective-permute-start.44) | collective-permute-done | bytes 262176 | tf_op jit(solution)/shard_map/far_out1/ppermute | solution.py:74
  175.5 2.4 %collective-permute-done.43.got = bf16[32,2048]{1,0:T(8,128)(2,1)S(1)} collective-permute-done((bf16[32,2048]{1,0:T(8,128)(2,1)S(1)}, bf16[32,2048]{1,0:T(8,128)(2,1)S(1)}, u32[]{:S(2)}, u32[]{:S(2)}) %collective-permute-start.43) | collective-permute-done | bytes 131104 | tf_op jit(solution)/shard_map/far_out2/ppermute | solution.py:74
  (124 shorter events, 44.2 us)
Async XLA Ops:
  2.8 9.2 %collective-permute-start = (bf16[32,2048]{1,0:T(8,128)(2,1)S(1)}, bf16[32,2048]{1,0:T(8,128)(2,1)S(1)}, u32[]{:S(2)}, u32[]{:S(2)}) collective-permute-start(bf16[32,2048]{1,0:T(8,128)(2,1)S(1)} %get-tuple-element.89), channel_id=1, source_target_pairs={{0,8},{4,12},{8,0},{12,4},{1,9},{5,13},{9,1},{13,5},{2,10},{6,14},... | collective-permute-start | bytes 393224 | tf_op jit(solution)/shard_map/far0/ppermute | solution.py:74
  13.1 18.1 %collective-permute-start.1 = (bf16[64,2048]{1,0:T(8,128)(2,1)S(1)}, bf16[64,2048]{1,0:T(8,128)(2,1)S(1)}, u32[]{:S(2)}, u32[]{:S(2)}) collective-permute-start(bf16[64,2048]{1,0:T(8,128)(2,1)S(1)} %get-tuple-element.94), channel_id=1, source_target_pairs={{0,8},{4,12},{8,0},{12,4},{1,9},{5,13},{9,1},{13,5},{2,10},{6,14},... | collective-permute-start | bytes 786440 | tf_op jit(solution)/shard_map/far1/ppermute | solution.py:74
  16.7 16.6 %collective-permute-start.5 = (bf16[64,2048]{1,0:T(8,128)(2,1)S(1)}, bf16[64,2048]{1,0:T(8,128)(2,1)S(1)}, u32[]{:S(2)}, u32[]{:S(2)}) collective-permute-start(bf16[64,2048]{1,0:T(8,128)(2,1)S(1)} %pad_maximum_fusion.4), channel_id=1, source_target_pairs={{1,4},{3,6},{4,1},{6,3},{9,12},{11,14},{12,9},{14,11},{17,20},{19,... | collective-permute-start | bytes 786440 | tf_op jit(solution)/shard_map/arr0/ppermute | solution.py:94
  24.1 9.2 %collective-permute-start.4 = (bf16[64,2048]{1,0:T(8,128)(2,1)S(1)}, bf16[64,2048]{1,0:T(8,128)(2,1)S(1)}, u32[]{:S(2)}, u32[]{:S(2)}) collective-permute-start(bf16[64,2048]{1,0:T(8,128)(2,1)S(1)} %pad_maximum_fusion.4), channel_id=1, source_target_pairs={{0,4},{1,0},{2,6},{3,2},{4,5},{5,1},{6,7},{7,3},{8,12},{9,8},{10,1... | collective-permute-start | bytes 786440 | tf_op jit(solution)/shard_map/arr0/ppermute | solution.py:94
  31.6 12.9 %collective-permute-start.3 = (bf16[32,2048]{1,0:T(8,128)(2,1)S(1)}, bf16[32,2048]{1,0:T(8,128)(2,1)S(1)}, u32[]{:S(2)}, u32[]{:S(2)}) collective-permute-start(bf16[32,2048]{1,0:T(8,128)(2,1)S(1)} %get-tuple-element.103), channel_id=1, source_target_pairs={{0,8},{4,12},{8,0},{12,4},{1,9},{5,13},{9,1},{13,5},{2,10},{6,14},... | collective-permute-start | bytes 393224 | tf_op jit(solution)/shard_map/far2/ppermute | solution.py:74
  38.3 27.7 %collective-permute-start.10 = (bf16[128,1024]{1,0:T(8,128)(2,1)S(1)}, bf16[128,1024]{1,0:T(8,128)(2,1)S(1)}, u32[]{:S(2)}, u32[]{:S(2)}) collective-permute-start(bf16[128,1024]{1,0:T(8,128)(2,1)S(1)} %get-tuple-element.108), channel_id=1, source_target_pairs={{0,2},{1,3},{2,0},{3,1},{4,6},{5,7},{6,4},{7,5},{8,10},{9,11},{10,... | collective-permute-start | bytes 786440 | tf_op jit(solution)/shard_map/b0/ppermute | solution.py:70
  39.0 16.1 %collective-permute-start.12 = (bf16[128,2048]{1,0:T(8,128)(2,1)S(1)}, bf16[128,2048]{1,0:T(8,128)(2,1)S(1)}, u32[]{:S(2)}, u32[]{:S(2)}) collective-permute-start(bf16[128,2048]{1,0:T(8,128)(2,1)S(1)} %pad_maximum_fusion.2), channel_id=1, source_target_pairs={{1,4},{3,6},{4,1},{6,3},{9,12},{11,14},{12,9},{14,11},{17,20},{19,... | collective-permute-start | bytes 1572872 | tf_op jit(solution)/shard_map/arr1/ppermute | solution.py:94
  41.7 13.5 %collective-permute-start.11 = (bf16[128,2048]{1,0:T(8,128)(2,1)S(1)}, bf16[128,2048]{1,0:T(8,128)(2,1)S(1)}, u32[]{:S(2)}, u32[]{:S(2)}) collective-permute-start(bf16[128,2048]{1,0:T(8,128)(2,1)S(1)} %pad_maximum_fusion.2), channel_id=1, source_target_pairs={{0,4},{1,0},{2,6},{3,2},{4,5},{5,1},{6,7},{7,3},{8,12},{9,8},{10,1... | collective-permute-start | bytes 1572872 | tf_op jit(solution)/shard_map/arr1/ppermute | solution.py:94
  41.8 24.3 %collective-permute-start.15 = (bf16[128,1024]{1,0:T(8,128)(2,1)S(1)}, bf16[128,1024]{1,0:T(8,128)(2,1)S(1)}, u32[]{:S(2)}, u32[]{:S(2)}) collective-permute-start(bf16[128,1024]{1,0:T(8,128)(2,1)S(1)} %get-tuple-element.119), channel_id=1, source_target_pairs={{0,2},{1,3},{2,0},{3,1},{4,6},{5,7},{6,4},{7,5},{8,10},{9,11},{10,... | collective-permute-start | bytes 786440 | tf_op jit(solution)/shard_map/b0/ppermute | solution.py:70
  44.5 21.8 %collective-permute-start.9 = (bf16[32,2048]{1,0:T(8,128)(2,1)S(1)}, bf16[32,2048]{1,0:T(8,128)(2,1)S(1)}, u32[]{:S(2)}, u32[]{:S(2)}) collective-permute-start(bf16[32,2048]{1,0:T(8,128)(2,1)S(1)} %broadcast_select_fusion.20), channel_id=1, source_target_pairs={{0,2},{1,3},{2,0},{3,1},{4,6},{5,7},{6,4},{7,5},{8,10},{9,11},{10,... | collective-permute-start | bytes 393224 | tf_op jit(solution)/shard_map/sel2/ppermute | solution.py:70
  69.5 12.4 %collective-permute-start.24 = (bf16[128,1024]{1,0:T(8,128)(2,1)S(1)}, bf16[128,1024]{1,0:T(8,128)(2,1)S(1)}, u32[]{:S(2)}, u32[]{:S(2)}) collective-permute-start(bf16[128,1024]{1,0:T(8,128)(2,1)S(1)} %hide0.1.one), channel_id=1, source_target_pairs={{0,2},{1,3},{2,0},{3,1},{4,6},{5,7},{6,4},{7,5},{8,10},{9,11},{10,... | collective-permute-start | bytes 786440 | tf_op jit(solution)/shard_map/hide0/ppermute | solution.py:70
  70.8 11.8 %collective-permute-start.19 = (bf16[128,1024]{1,0:T(8,128)(2,1)S(1)}, bf16[128,1024]{1,0:T(8,128)(2,1)S(1)}, u32[]{:S(2)}, u32[]{:S(2)}) collective-permute-start(bf16[128,1024]{1,0:T(8,128)(2,1)S(1)} %hide0.1.one), channel_id=1, source_target_pairs={{0,1},{1,0},{2,3},{3,2},{4,5},{5,4},{6,7},{7,6},{8,9},{9,8},{10,11... | collective-permute-start | bytes 786440 | tf_op jit(solution)/shard_map/hide0/ppermute | solution.py:70
  70.8 28.6 %collective-permute-start.18 = (bf16[256,1024]{1,0:T(8,128)(2,1)S(1)}, bf16[256,1024]{1,0:T(8,128)(2,1)S(1)}, u32[]{:S(2)}, u32[]{:S(2)}) collective-permute-start(bf16[256,1024]{1,0:T(8,128)(2,1)S(1)} %get-tuple-element.116), channel_id=1, source_target_pairs={{0,2},{1,3},{2,0},{3,1},{4,6},{5,7},{6,4},{7,5},{8,10},{9,11},{10,... | collective-permute-start | bytes 1572872 | tf_op jit(solution)/shard_map/b1/ppermute | solution.py:70
  71.9 27.5 %collective-permute-start.20 = (bf16[256,1024]{1,0:T(8,128)(2,1)S(1)}, bf16[256,1024]{1,0:T(8,128)(2,1)S(1)}, u32[]{:S(2)}, u32[]{:S(2)}) collective-permute-start(bf16[256,1024]{1,0:T(8,128)(2,1)S(1)} %get-tuple-element.129), channel_id=1, source_target_pairs={{0,2},{1,3},{2,0},{3,1},{4,6},{5,7},{6,4},{7,5},{8,10},{9,11},{10,... | collective-permute-start | bytes 1572872 | tf_op jit(solution)/shard_map/b1/ppermute | solution.py:70
  77.8 25.2 %collective-permute-start.22 = (bf16[2,128,1024]{2,1,0:T(8,128)(2,1)S(1)}, bf16[2,128,1024]{2,1,0:T(8,128)(2,1)S(1)}, u32[]{:S(2)}, u32[]{:S(2)}) collective-permute-start(bf16[2,128,1024]{2,1,0:T(8,128)(2,1)S(1)} %c2.1), channel_id=1, source_target_pairs={{0,1},{1,0},{2,3},{3,2},{4,5},{5,4},{6,7},{7,6},{8,9},{9,8},{10,11... | collective-permute-start | bytes 1572872 | tf_op jit(solution)/shard_map/c2/ppermute | solution.py:70
  82.0 19.4 %collective-permute-start.21 = (bf16[2,128,1024]{2,1,0:T(8,128)(2,1)S(1)}, bf16[2,128,1024]{2,1,0:T(8,128)(2,1)S(1)}, u32[]{:S(2)}, u32[]{:S(2)}) collective-permute-start(bf16[2,128,1024]{2,1,0:T(8,128)(2,1)S(1)} %a2.1), channel_id=1, source_target_pairs={{0,1},{1,0},{2,3},{3,2},{4,5},{5,4},{6,7},{7,6},{8,9},{9,8},{10,11... | collective-permute-start | bytes 1572872 | tf_op jit(solution)/shard_map/a2/ppermute | solution.py:70
  82.5 26.0 %collective-permute-start.25 = (bf16[128,1024]{1,0:T(8,128)(2,1)S(1)}, bf16[128,1024]{1,0:T(8,128)(2,1)S(1)}, u32[]{:S(2)}, u32[]{:S(2)}) collective-permute-start(bf16[128,1024]{1,0:T(8,128)(2,1)S(1)} %collective-permute-done.24.one), channel_id=1, source_target_pairs={{0,1},{1,0},{2,3},{3,2},{4,5},{5,4},{6,7},{7,6},{8,9},{9,8},{10,11... | collective-permute-start | bytes 786440 | tf_op jit(solution)/shard_map/forward0/ppermute | solution.py:70
  99.8 18.3 %collective-permute-start.30 = (bf16[256,1024]{1,0:T(8,128)(2,1)S(1)}, bf16[256,1024]{1,0:T(8,128)(2,1)S(1)}, u32[]{:S(2)}, u32[]{:S(2)}) collective-permute-start(bf16[256,1024]{1,0:T(8,128)(2,1)S(1)} %hide1.1.one), channel_id=1, source_target_pairs={{0,2},{1,3},{2,0},{3,1},{4,6},{5,7},{6,4},{7,5},{8,10},{9,11},{10,... | collective-permute-start | bytes 1572872 | tf_op jit(solution)/shard_map/hide1/ppermute | solution.py:70
  101.1 10.5 %collective-permute-start.26 = (bf16[256,1024]{1,0:T(8,128)(2,1)S(1)}, bf16[256,1024]{1,0:T(8,128)(2,1)S(1)}, u32[]{:S(2)}, u32[]{:S(2)}) collective-permute-start(bf16[256,1024]{1,0:T(8,128)(2,1)S(1)} %hide1.1.one), channel_id=1, source_target_pairs={{0,1},{1,0},{2,3},{3,2},{4,5},{5,4},{6,7},{7,6},{8,9},{9,8},{10,11... | collective-permute-start | bytes 1572872 | tf_op jit(solution)/shard_map/hide1/ppermute | solution.py:70
  102.7 22.0 %collective-permute-start.23 = (bf16[128,1024]{1,0:T(8,128)(2,1)S(1)}, bf16[128,1024]{1,0:T(8,128)(2,1)S(1)}, u32[]{:S(2)}, u32[]{:S(2)}) collective-permute-start(bf16[128,1024]{1,0:T(8,128)(2,1)S(1)} %get-tuple-element.132), channel_id=1, source_target_pairs={{0,2},{1,3},{2,0},{3,1},{4,6},{5,7},{6,4},{7,5},{8,10},{9,11},{10,... | collective-permute-start | bytes 786440 | tf_op jit(solution)/shard_map/b2/ppermute | solution.py:70
  110.1 19.6 %collective-permute-start.29 = (bf16[64,2048]{1,0:T(8,128)(2,1)S(1)}, bf16[64,2048]{1,0:T(8,128)(2,1)S(1)}, u32[]{:S(2)}, u32[]{:S(2)}) collective-permute-start(bf16[64,2048]{1,0:T(8,128)(2,1)S(1)} %get-tuple-element.169), channel_id=1, source_target_pairs={{0,1},{1,5},{2,3},{3,7},{4,0},{5,4},{6,2},{7,6},{8,9},{9,13},{10,1... | collective-permute-start | bytes 786440 | tf_op jit(solution)/shard_map/out0/ppermute | solution.py:94
  110.7 14.0 %collective-permute-start.27 = (bf16[128,1024]{1,0:T(8,128)(2,1)S(1)}, bf16[128,1024]{1,0:T(8,128)(2,1)S(1)}, u32[]{:S(2)}, u32[]{:S(2)}) collective-permute-start(bf16[128,1024]{1,0:T(8,128)(2,1)S(1)} %get-tuple-element.140), channel_id=1, source_target_pairs={{0,2},{1,3},{2,0},{3,1},{4,6},{5,7},{6,4},{7,5},{8,10},{9,11},{10,... | collective-permute-start | bytes 786440 | tf_op jit(solution)/shard_map/b2/ppermute | solution.py:70
  111.6 18.1 %collective-permute-start.32 = (bf16[64,2048]{1,0:T(8,128)(2,1)S(1)}, bf16[64,2048]{1,0:T(8,128)(2,1)S(1)}, u32[]{:S(2)}, u32[]{:S(2)}) collective-permute-start(bf16[64,2048]{1,0:T(8,128)(2,1)S(1)} %get-tuple-element.168), channel_id=1, source_target_pairs={{1,4},{3,6},{4,1},{6,3},{9,12},{11,14},{12,9},{14,11},{17,20},{19,... | collective-permute-start | bytes 786440 | tf_op jit(solution)/shard_map/out0/ppermute | solution.py:94
  125.7 9.6 %collective-permute-start.34 = (bf16[128,1024]{1,0:T(8,128)(2,1)S(1)}, bf16[128,1024]{1,0:T(8,128)(2,1)S(1)}, u32[]{:S(2)}, u32[]{:S(2)}) collective-permute-start(bf16[128,1024]{1,0:T(8,128)(2,1)S(1)} %hide2.1.one), channel_id=1, source_target_pairs={{0,1},{1,0},{2,3},{3,2},{4,5},{5,4},{6,7},{7,6},{8,9},{9,8},{10,11... | collective-permute-start | bytes 786440 | tf_op jit(solution)/shard_map/hide2/ppermute | solution.py:70
  125.7 12.8 %collective-permute-start.28 = (bf16[128,1024]{1,0:T(8,128)(2,1)S(1)}, bf16[128,1024]{1,0:T(8,128)(2,1)S(1)}, u32[]{:S(2)}, u32[]{:S(2)}) collective-permute-start(bf16[128,1024]{1,0:T(8,128)(2,1)S(1)} %hide2.1.one), channel_id=1, source_target_pairs={{0,2},{1,3},{2,0},{3,1},{4,6},{5,7},{6,4},{7,5},{8,10},{9,11},{10,... | collective-permute-start | bytes 786440 | tf_op jit(solution)/shard_map/hide2/ppermute | solution.py:70
  131.1 8.9 %collective-permute-start.35 = (bf16[128,2048]{1,0:T(8,128)(2,1)S(1)}, bf16[128,2048]{1,0:T(8,128)(2,1)S(1)}, u32[]{:S(2)}, u32[]{:S(2)}) collective-permute-start(bf16[128,2048]{1,0:T(8,128)(2,1)S(1)} %get-tuple-element.163), channel_id=1, source_target_pairs={{0,1},{1,5},{2,3},{3,7},{4,0},{5,4},{6,2},{7,6},{8,9},{9,13},{10,1... | collective-permute-start | bytes 1572872 | tf_op jit(solution)/shard_map/out1/ppermute | solution.py:94
  131.1 17.6 %collective-permute-start.36 = (bf16[128,2048]{1,0:T(8,128)(2,1)S(1)}, bf16[128,2048]{1,0:T(8,128)(2,1)S(1)}, u32[]{:S(2)}, u32[]{:S(2)}) collective-permute-start(bf16[128,2048]{1,0:T(8,128)(2,1)S(1)} %get-tuple-element.162), channel_id=1, source_target_pairs={{1,4},{3,6},{4,1},{6,3},{9,12},{11,14},{12,9},{14,11},{17,20},{19,... | collective-permute-start | bytes 1572872 | tf_op jit(solution)/shard_map/out1/ppermute | solution.py:94
  136.8 14.4 %collective-permute-start.39 = (bf16[32,2048]{1,0:T(8,128)(2,1)S(1)}, bf16[32,2048]{1,0:T(8,128)(2,1)S(1)}, u32[]{:S(2)}, u32[]{:S(2)}) collective-permute-start(bf16[32,2048]{1,0:T(8,128)(2,1)S(1)} %convert_select_fusion.5), channel_id=1, source_target_pairs={{0,8},{4,12},{8,0},{12,4},{1,9},{5,13},{9,1},{13,5},{2,10},{6,14},... | collective-permute-start | bytes 393224 | tf_op jit(solution)/shard_map/far_out0/ppermute | solution.py:74
  138.6 11.1 %collective-permute-start.37 = (bf16[128,1024]{1,0:T(8,128)(2,1)S(1)}, bf16[128,1024]{1,0:T(8,128)(2,1)S(1)}, u32[]{:S(2)}, u32[]{:S(2)}) collective-permute-start(bf16[128,1024]{1,0:T(8,128)(2,1)S(1)} %collective-permute-done.28.one), channel_id=1, source_target_pairs={{0,1},{1,0},{2,3},{3,2},{4,5},{5,4},{6,7},{7,6},{8,9},{9,8},{10,11... | collective-permute-start | bytes 786440 | tf_op jit(solution)/shard_map/forward2/ppermute | solution.py:70
  149.0 11.0 %collective-permute-start.42 = (bf16[64,2048]{1,0:T(8,128)(2,1)S(1)}, bf16[64,2048]{1,0:T(8,128)(2,1)S(1)}, u32[]{:S(2)}, u32[]{:S(2)}) collective-permute-start(bf16[64,2048]{1,0:T(8,128)(2,1)S(1)} %select_convert_fusion.2), channel_id=1, source_target_pairs={{0,2},{1,3},{2,0},{3,1},{4,6},{5,7},{6,4},{7,5},{8,10},{9,11},{10,... | collective-permute-start | bytes 786440 | tf_op jit(solution)/shard_map/mix1/ppermute | solution.py:70
  160.2 15.0 %collective-permute-start.44 = (bf16[64,2048]{1,0:T(8,128)(2,1)S(1)}, bf16[64,2048]{1,0:T(8,128)(2,1)S(1)}, u32[]{:S(2)}, u32[]{:S(2)}) collective-permute-start(bf16[64,2048]{1,0:T(8,128)(2,1)S(1)} %convert_select_fusion.2), channel_id=1, source_target_pairs={{0,8},{4,12},{8,0},{12,4},{1,9},{5,13},{9,1},{13,5},{2,10},{6,14},... | collective-permute-start | bytes 786440 | tf_op jit(solution)/shard_map/far_out1/ppermute | solution.py:74
  163.3 14.6 %collective-permute-start.43 = (bf16[32,2048]{1,0:T(8,128)(2,1)S(1)}, bf16[32,2048]{1,0:T(8,128)(2,1)S(1)}, u32[]{:S(2)}, u32[]{:S(2)}) collective-permute-start(bf16[32,2048]{1,0:T(8,128)(2,1)S(1)} %convert_select_fusion.4), channel_id=1, source_target_pairs={{0,8},{4,12},{8,0},{12,4},{1,9},{5,13},{9,1},{13,5},{2,10},{6,14},... | collective-permute-start | bytes 393224 | tf_op jit(solution)/shard_map/far_out2/ppermute | solution.py:74
  (15 other events, 65.2 us)

commit v6 on v5

--- a/solution.py
+++ b/solution.py
@@ -7,12 +7,12 @@
 from jax.experimental.pallas import tpu as pltpu
 from jax.sharding import PartitionSpec as P
 
-ROWS = (32, 64, 32)
+ROWS = (48, 48, 32)
 ORDER = (
     "far0", "load3", "sel0", "far1", "load1", "arr0", "load2", "load0", "sel1", "far2", "take0", "a0", "c0",
-    "b0", "arr1", "d0", "sel2", "take1", "a1", "c1", "b1", "d1", "hide0", "arr2", "take2", "a2", "c2",
-    "down0", "forward0", "own0", "hide1", "b2", "d2", "down2", "rest0", "out0", "own1", "forward1", "hide2",
-    "rest1", "out1", "mix0", "own2", "far_out0", "forward2", "mix1", "rest2", "out2", "end0", "mix2",
+    "b0", "arr1", "d0", "sel2", "take1", "a1", "c1", "hide0", "b1", "arr2", "d1", "take2", "a2", "c2",
+    "down0", "own0", "forward0", "hide1", "b2", "d2", "down2", "rest0", "out0", "own1", "forward1", "hide2",
+    "rest1", "out1", "mix0", "own2", "far_out0", "forward2", "rest2", "out2", "mix1", "end0", "mix2",
     "far_out1", "far_out2", "end1", "end2",
 )
 TILE = 256

time: 179 us -> 166 us (0.927)
  waiting for transfers between devices: 68.1 us -> 49.9 us
  starting transfers between devices: 48.9 us -> 54.3 us
    ppermute x12, waiting for transfers between devices: 27.8 us -> 12.1 us  [over_both(): return lax.ppermute(array, ('tp', 'seq'), pairs)]
    ppermute x6, starting transfers between devices: 7.48 us -> 12.1 us  [over_tp(): return lax.ppermute(array, 'tp', [(i, i ^ bit) for i in range(4)])]
    ppermute x27, waiting for transfers between devices: 24.5 us -> 21 us  [over_seq(): return lax.ppermute(array, 'seq', [(i, i ^ bit) for i in range(4)])]
  transfers between devices with their start and end apart: 45 -> 45, of which waited for: 13 -> 14; matrix products, arithmetic and copies ran while one was open for 1% -> 1% of each run, Pallas kernels for 31% -> 33%
where the time goes in v6:
time: 166 us
  Pallas kernels  56.7 us (34%)
  starting transfers between devices  54.3 us (33%)
  waiting for transfers between devices  49.9 us (30%)
  other arithmetic  2.04 us (1%)
  local copies, waits for them, and re-layouts  1.73 us (1%)
    ppermute x12, starting transfers between devices, over_both(): return lax.ppermute(array, ('tp', 'seq'), pairs)  24.2 us
    pallas_call x12, Pallas kernels, sums(): pl.pallas_call(functools.partial(sums_kernel, got is not None, split), ou...  21.2 us
    ppermute x27, waiting for transfers between devices, over_seq(): return lax.ppermute(array, 'seq', [(i, i ^ bit) for i in range(4)])  21 us
    ppermute x27, starting transfers between devices, over_seq(): return lax.ppermute(array, 'seq', [(i, i ^ bit) for i in range(4)])  18 us
    ppermute x6, waiting for transfers between devices, over_tp(): return lax.ppermute(array, 'tp', [(i, i ^ bit) for i in range(4)])  16.8 us
    pallas_call x4, Pallas kernels, load(): pl.pallas_call(load_kernel, out_shape=jax.ShapeDtypeStruct((2, deep, widt...  14 us
    ppermute x6, starting transfers between devices, over_tp(): return lax.ppermute(array, 'tp', [(i, i ^ bit) for i in range(4)])  12.1 us
    ppermute x12, waiting for transfers between devices, over_both(): return lax.ppermute(array, ('tp', 'seq'), pairs)  12.1 us
  transfers between devices with their start and end apart: 45, of which 14 were waited for; matrix products, arithmetic and copies ran while one was open for 1% of the time, Pallas kernels for 33%

profile of v6, /device:TPU:1, one launch (start us, length us, event | category | flops | bytes accessed | tf_op | source)
XLA Modules:
  0.0 166.0 jit_solution(9872808955537692733)
XLA Ops:
  2.8 3.2 %collective-permute-start = (bf16[48,2048]{1,0:T(8,128)(2,1)S(1)}, bf16[48,2048]{1,0:T(8,128)(2,1)S(1)}, u32[]{:S(2)}, u32[]{:S(2)}) collective-permute-start(bf16[48,2048]{1,0:T(8,128)(2,1)S(1)} %get-tuple-element.89), channel_id=1, source_target_pairs={{0,8},{4,12},{8,0},{12,4},{1,9},{5,13},{9,1},{13,5},{2,10},{6,14},... | collective-permute-start | bytes 589832 | tf_op jit(solution)/shard_map/far0/ppermute | solution.py:74
  6.1 3.5 %load3.1.weights = bf16[2,2048,1024]{2,1,0:T(8,128)(2,1)S(1)} custom-call(s32[1]{0:T(128)} %bitcast.3.quarter, bf16[2048,4096]{1,0:T(8,128)(2,1)} %gate_weight.3, bf16[2048,4096]{1,0:T(8,128)(2,1)} %up_weight.7), custom_call_target="tpu_custom_call" | custom-call | flops 1073741824 | bytes 1 | tf_op jit(solution)/shard_map/load3/pallas_call | solution.py:120
  9.6 5.3 %collective-permute-done = bf16[48,2048]{1,0:T(8,128)(2,1)S(1)} collective-permute-done((bf16[48,2048]{1,0:T(8,128)(2,1)S(1)}, bf16[48,2048]{1,0:T(8,128)(2,1)S(1)}, u32[]{:S(2)}, u32[]{:S(2)}) %collective-permute-start) | collective-permute-done | bytes 196640 | tf_op jit(solution)/shard_map/far0/ppermute | solution.py:74
  15.9 3.5 %load1.1.weights = bf16[2,2048,1024]{2,1,0:T(8,128)(2,1)S(1)} custom-call(s32[1]{0:T(128)} %bitcast.1.quarter, bf16[2048,4096]{1,0:T(8,128)(2,1)} %gate_weight.3, bf16[2048,4096]{1,0:T(8,128)(2,1)} %up_weight.7), custom_call_target="tpu_custom_call" | custom-call | flops 1073741824 | bytes 1 | tf_op jit(solution)/shard_map/load1/pallas_call | solution.py:120
  20.2 2.2 %collective-permute-start.4 = (bf16[96,2048]{1,0:T(8,128)(2,1)S(1)}, bf16[96,2048]{1,0:T(8,128)(2,1)S(1)}, u32[]{:S(2)}, u32[]{:S(2)}) collective-permute-start(bf16[96,2048]{1,0:T(8,128)(2,1)S(1)} %pad_maximum_fusion.3), channel_id=1, source_target_pairs={{0,4},{1,0},{2,6},{3,2},{4,5},{5,1},{6,7},{7,3},{8,12},{9,8},{10,1... | collective-permute-start | bytes 1179656 | tf_op jit(solution)/shard_map/arr0/ppermute | solution.py:94
  22.4 4.6 %collective-permute-start.5 = (bf16[96,2048]{1,0:T(8,128)(2,1)S(1)}, bf16[96,2048]{1,0:T(8,128)(2,1)S(1)}, u32[]{:S(2)}, u32[]{:S(2)}) collective-permute-start(bf16[96,2048]{1,0:T(8,128)(2,1)S(1)} %pad_maximum_fusion.3), channel_id=1, source_target_pairs={{1,4},{3,6},{4,1},{6,3},{9,12},{11,14},{12,9},{14,11},{17,20},{19,... | collective-permute-start | bytes 1179656 | tf_op jit(solution)/shard_map/arr0/ppermute | solution.py:94
  27.0 3.5 %load2.1.weights = bf16[2,2048,1024]{2,1,0:T(8,128)(2,1)S(1)} custom-call(s32[1]{0:T(128)} %bitcast.2.quarter, bf16[2048,4096]{1,0:T(8,128)(2,1)} %gate_weight.3, bf16[2048,4096]{1,0:T(8,128)(2,1)} %up_weight.7), custom_call_target="tpu_custom_call" | custom-call | flops 1073741824 | bytes 1 | tf_op jit(solution)/shard_map/load2/pallas_call | solution.py:120
  30.5 3.5 %load0.1.weights = bf16[2,2048,1024]{2,1,0:T(8,128)(2,1)S(1)} custom-call(s32[1]{0:T(128)} %bitcast.quarter, bf16[2048,4096]{1,0:T(8,128)(2,1)} %gate_weight.3, bf16[2048,4096]{1,0:T(8,128)(2,1)} %up_weight.7), custom_call_target="tpu_custom_call" | custom-call | flops 1073741824 | bytes 1 | tf_op jit(solution)/shard_map/load0/pallas_call | solution.py:120
  34.4 2.5 %collective-permute-start.3 = (bf16[32,2048]{1,0:T(8,128)(2,1)S(1)}, bf16[32,2048]{1,0:T(8,128)(2,1)S(1)}, u32[]{:S(2)}, u32[]{:S(2)}) collective-permute-start(bf16[32,2048]{1,0:T(8,128)(2,1)S(1)} %get-tuple-element.103), channel_id=1, source_target_pairs={{0,8},{4,12},{8,0},{12,4},{1,9},{5,13},{9,1},{13,5},{2,10},{6,14},... | collective-permute-start | bytes 393224 | tf_op jit(solution)/shard_map/far2/ppermute | solution.py:74
  37.2 2.0 %a0.1 = bf16[2,192,1024]{2,1,0:T(8,128)(2,1)S(1)} custom-call(bf16[192,2048]{1,0:T(8,128)(2,1)S(1)} %pad_maximum_fusion.some, bf16[2,2048,1024]{2,1,0:T(8,128)(2,1)S(1)} %load3.1.weights), custom_call_target="tpu_custom_call" | custom-call | flops 17179869184 | bytes 1 | tf_op jit(solution)/shard_map/a0/pallas_call | solution.py:149
  39.2 2.0 %c0.1 = bf16[2,192,1024]{2,1,0:T(8,128)(2,1)S(1)} custom-call(bf16[192,2048]{1,0:T(8,128)(2,1)S(1)} %pad_maximum_fusion.some, bf16[2,2048,1024]{2,1,0:T(8,128)(2,1)S(1)} %load1.1.weights), custom_call_target="tpu_custom_call" | custom-call | flops 17179869184 | bytes 1 | tf_op jit(solution)/shard_map/c0/pallas_call | solution.py:149
  43.8 2.5 %collective-permute-start.11 = (bf16[96,2048]{1,0:T(8,128)(2,1)S(1)}, bf16[96,2048]{1,0:T(8,128)(2,1)S(1)}, u32[]{:S(2)}, u32[]{:S(2)}) collective-permute-start(bf16[96,2048]{1,0:T(8,128)(2,1)S(1)} %pad_maximum_fusion.4), channel_id=1, source_target_pairs={{1,4},{3,6},{4,1},{6,3},{9,12},{11,14},{12,9},{14,11},{17,20},{19,... | collective-permute-start | bytes 1179656 | tf_op jit(solution)/shard_map/arr1/ppermute | solution.py:94
  46.6 2.0 %d0.1.held = f32[2,192,1024]{2,1,0:T(8,128)S(1)} custom-call(bf16[192,2048]{1,0:T(8,128)(2,1)S(1)} %pad_maximum_fusion.some, bf16[2,2048,1024]{2,1,0:T(8,128)(2,1)S(1)} %load0.1.weights, bf16[2,192,1024]{2,1,0:T(8,128)(2,1)S(1)} %collective-permute-done.8.rest_0_), custom_call_target="tpu_custom_call" | custom-call | flops 17179869184 | bytes 1 | tf_op jit(solution)/shard_map/d0/pallas_call | solution.py:149
  50.2 2.1 %collective-permute-done.10 = bf16[96,2048]{1,0:T(8,128)(2,1)S(1)} collective-permute-done((bf16[96,2048]{1,0:T(8,128)(2,1)S(1)}, bf16[96,2048]{1,0:T(8,128)(2,1)S(1)}, u32[]{:S(2)}, u32[]{:S(2)}) %collective-permute-start.10) | collective-permute-done | bytes 393248 | tf_op jit(solution)/shard_map/arr1/ppermute | solution.py:94
  52.4 2.6 %collective-permute-done.11 = bf16[96,2048]{1,0:T(8,128)(2,1)S(1)} collective-permute-done((bf16[96,2048]{1,0:T(8,128)(2,1)S(1)}, bf16[96,2048]{1,0:T(8,128)(2,1)S(1)}, u32[]{:S(2)}, u32[]{:S(2)}) %collective-permute-start.11) | collective-permute-done | bytes 393248 | tf_op jit(solution)/shard_map/arr1/ppermute | solution.py:94
  57.3 2.0 %c1.1 = bf16[2,192,1024]{2,1,0:T(8,128)(2,1)S(1)} custom-call(bf16[192,2048]{1,0:T(8,128)(2,1)S(1)} %pad_maximum_fusion.1.some, bf16[2,2048,1024]{2,1,0:T(8,128)(2,1)S(1)} %load1.1.weights), custom_call_target="tpu_custom_call" | custom-call | flops 17179869184 | bytes 1 | tf_op jit(solution)/shard_map/c1/pallas_call | solution.py:149
  59.8 6.0 %collective-permute-done.13.got_up = bf16[192,1024]{1,0:T(8,128)(2,1)S(1)} collective-permute-done((bf16[192,1024]{1,0:T(8,128)(2,1)S(1)}, bf16[192,1024]{1,0:T(8,128)(2,1)S(1)}, u32[]{:S(2)}, u32[]{:S(2)}) %collective-permute-start.13) | collective-permute-done | bytes 393248 | tf_op jit(solution)/shard_map/b0/ppermute | solution.py:70
  69.2 3.2 %collective-permute-start.17 = (bf16[64,2048]{1,0:T(8,128)(2,1)S(1)}, bf16[64,2048]{1,0:T(8,128)(2,1)S(1)}, u32[]{:S(2)}, u32[]{:S(2)}) collective-permute-start(bf16[64,2048]{1,0:T(8,128)(2,1)S(1)} %pad_maximum_fusion.5), channel_id=1, source_target_pairs={{1,4},{3,6},{4,1},{6,3},{9,12},{11,14},{12,9},{14,11},{17,20},{19,... | collective-permute-start | bytes 786440 | tf_op jit(solution)/shard_map/arr2/ppermute | solution.py:94
  80.4 4.0 %down0.1.weights = bf16[2,1024,2048]{2,1,0:T(8,128)(2,1)S(1)} custom-call(s32[2]{0:T(128)S(1)} %get-tuple-element.123.quarters, bf16[4096,2048]{1,0:T(8,128)(2,1)} %weight.1), custom_call_target="tpu_custom_call" | custom-call | flops 17179869184 | bytes 1 | tf_op jit(solution)/shard_map/down0/pallas_call | solution.py:180
  87.1 6.3 %collective-permute-done.20.got_up = bf16[192,1024]{1,0:T(8,128)(2,1)S(1)} collective-permute-done((bf16[192,1024]{1,0:T(8,128)(2,1)S(1)}, bf16[192,1024]{1,0:T(8,128)(2,1)S(1)}, u32[]{:S(2)}, u32[]{:S(2)}) %collective-permute-start.20) | collective-permute-done | bytes 393248 | tf_op jit(solution)/shard_map/b1/ppermute | solution.py:70
  99.3 4.0 %down2.1.weights = bf16[2,1024,2048]{2,1,0:T(8,128)(2,1)S(1)} custom-call(s32[2]{0:T(128)S(1)} %get-tuple-element.135.quarters, bf16[4096,2048]{1,0:T(8,128)(2,1)} %weight.1), custom_call_target="tpu_custom_call" | custom-call | flops 17179869184 | bytes 1 | tf_op jit(solution)/shard_map/down2/pallas_call | solution.py:180
  103.3 2.0 %rest0.1 = f32[192,2048]{1,0:T(8,128)S(1)} custom-call(bf16[192,1024]{1,0:T(8,128)(2,1)S(1)} %collective-permute-done.24.one, bf16[192,1024]{1,0:T(8,128)(2,1)S(1)} %collective-permute-done.25.two, bf16[2,1024,2048]{2,1,0:T(8,128)(2,1)S(1)} %down2.1.weights, f32[192,2048]{1,0:T(8,128)S(1)} %own0.1.rest_0_), custom_call_target="tpu_custom_call" | custom-call | flops 17179869184 | bytes 1 | tf_op jit(solution)/shard_map/rest0/pallas_call | solution.py:203
  109.3 3.0 %collective-permute-start.32 = (bf16[96,2048]{1,0:T(8,128)(2,1)S(1)}, bf16[96,2048]{1,0:T(8,128)(2,1)S(1)}, u32[]{:S(2)}, u32[]{:S(2)}) collective-permute-start(bf16[96,2048]{1,0:T(8,128)(2,1)S(1)} %get-tuple-element.164), channel_id=1, source_target_pairs={{1,4},{3,6},{4,1},{6,3},{9,12},{11,14},{12,9},{14,11},{17,20},{19,... | collective-permute-start | bytes 1179656 | tf_op jit(solution)/shard_map/out0/ppermute | solution.py:94
  112.3 4.6 %collective-permute-done.27.got_up = bf16[128,1024]{1,0:T(8,128)(2,1)S(1)} collective-permute-done((bf16[128,1024]{1,0:T(8,128)(2,1)S(1)}, bf16[128,1024]{1,0:T(8,128)(2,1)S(1)}, u32[]{:S(2)}, u32[]{:S(2)}) %collective-permute-start.27) | collective-permute-done | bytes 262176 | tf_op jit(solution)/shard_map/b2/ppermute | solution.py:70
  123.4 2.7 %collective-permute-start.39 = (bf16[96,2048]{1,0:T(8,128)(2,1)S(1)}, bf16[96,2048]{1,0:T(8,128)(2,1)S(1)}, u32[]{:S(2)}, u32[]{:S(2)}) collective-permute-start(bf16[96,2048]{1,0:T(8,128)(2,1)S(1)} %get-tuple-element.162), channel_id=1, source_target_pairs={{1,4},{3,6},{4,1},{6,3},{9,12},{11,14},{12,9},{14,11},{17,20},{19,... | collective-permute-start | bytes 1179656 | tf_op jit(solution)/shard_map/out1/ppermute | solution.py:94
  127.6 2.6 %collective-permute-done.33 = bf16[48,2048]{1,0:T(8,128)(2,1)S(1)} collective-permute-done((bf16[48,2048]{1,0:T(8,128)(2,1)S(1)}, bf16[48,2048]{1,0:T(8,128)(2,1)S(1)}, u32[]{:S(2)}, u32[]{:S(2)}) %collective-permute-start.33) | collective-permute-done | bytes 196640 | tf_op jit(solution)/shard_map/mix0/ppermute | solution.py:70
  131.1 2.6 %collective-permute-start.37 = (bf16[48,2048]{1,0:T(8,128)(2,1)S(1)}, bf16[48,2048]{1,0:T(8,128)(2,1)S(1)}, u32[]{:S(2)}, u32[]{:S(2)}) collective-permute-start(bf16[48,2048]{1,0:T(8,128)(2,1)S(1)} %convert_select_fusion.4), channel_id=1, source_target_pairs={{0,8},{4,12},{8,0},{12,4},{1,9},{5,13},{9,1},{13,5},{2,10},{6,14},... | collective-permute-start | bytes 589832 | tf_op jit(solution)/shard_map/far_out0/ppermute | solution.py:74
  137.0 6.1 %collective-permute-done.37.got = bf16[48,2048]{1,0:T(8,128)(2,1)S(1)} collective-permute-done((bf16[48,2048]{1,0:T(8,128)(2,1)S(1)}, bf16[48,2048]{1,0:T(8,128)(2,1)S(1)}, u32[]{:S(2)}, u32[]{:S(2)}) %collective-permute-start.37) | collective-permute-done | bytes 196640 | tf_op jit(solution)/shard_map/far_out0/ppermute | solution.py:74
  145.2 6.3 %collective-permute-done.40 = bf16[64,2048]{1,0:T(8,128)(2,1)S(1)} collective-permute-done((bf16[64,2048]{1,0:T(8,128)(2,1)S(1)}, bf16[64,2048]{1,0:T(8,128)(2,1)S(1)}, u32[]{:S(2)}, u32[]{:S(2)}) %collective-permute-start.40) | collective-permute-done | bytes 262176 | tf_op jit(solution)/shard_map/out2/ppermute | solution.py:94
  151.7 2.9 %collective-permute-start.41 = (bf16[32,2048]{1,0:T(8,128)(2,1)S(1)}, bf16[32,2048]{1,0:T(8,128)(2,1)S(1)}, u32[]{:S(2)}, u32[]{:S(2)}) collective-permute-start(bf16[32,2048]{1,0:T(8,128)(2,1)S(1)} %select_convert_fusion.5), channel_id=1, source_target_pairs={{0,2},{1,3},{2,0},{3,1},{4,6},{5,7},{6,4},{7,5},{8,10},{9,11},{10,... | collective-permute-start | bytes 393224 | tf_op jit(solution)/shard_map/mix2/ppermute | solution.py:70
  157.0 2.4 %collective-permute-start.43 = (bf16[32,2048]{1,0:T(8,128)(2,1)S(1)}, bf16[32,2048]{1,0:T(8,128)(2,1)S(1)}, u32[]{:S(2)}, u32[]{:S(2)}) collective-permute-start(bf16[32,2048]{1,0:T(8,128)(2,1)S(1)} %convert_select_fusion.5), channel_id=1, source_target_pairs={{0,8},{4,12},{8,0},{12,4},{1,9},{5,13},{9,1},{13,5},{2,10},{6,14},... | collective-permute-start | bytes 393224 | tf_op jit(solution)/shard_map/far_out2/ppermute | solution.py:74
  159.4 4.3 %collective-permute-done.44.got = bf16[48,2048]{1,0:T(8,128)(2,1)S(1)} collective-permute-done((bf16[48,2048]{1,0:T(8,128)(2,1)S(1)}, bf16[48,2048]{1,0:T(8,128)(2,1)S(1)}, u32[]{:S(2)}, u32[]{:S(2)}) %collective-permute-start.44) | collective-permute-done | bytes 196640 | tf_op jit(solution)/shard_map/far_out1/ppermute | solution.py:74
  (124 shorter events, 55.0 us)
Async XLA Ops:
  2.8 12.0 %collective-permute-start = (bf16[48,2048]{1,0:T(8,128)(2,1)S(1)}, bf16[48,2048]{1,0:T(8,128)(2,1)S(1)}, u32[]{:S(2)}, u32[]{:S(2)}) collective-permute-start(bf16[48,2048]{1,0:T(8,128)(2,1)S(1)} %get-tuple-element.89), channel_id=1, source_target_pairs={{0,8},{4,12},{8,0},{12,4},{1,9},{5,13},{9,1},{13,5},{2,10},{6,14},... | collective-permute-start | bytes 589832 | tf_op jit(solution)/shard_map/far0/ppermute | solution.py:74
  15.9 18.1 %collective-permute-start.1 = (bf16[48,2048]{1,0:T(8,128)(2,1)S(1)}, bf16[48,2048]{1,0:T(8,128)(2,1)S(1)}, u32[]{:S(2)}, u32[]{:S(2)}) collective-permute-start(bf16[48,2048]{1,0:T(8,128)(2,1)S(1)} %get-tuple-element.94), channel_id=1, source_target_pairs={{0,8},{4,12},{8,0},{12,4},{1,9},{5,13},{9,1},{13,5},{2,10},{6,14},... | collective-permute-start | bytes 589832 | tf_op jit(solution)/shard_map/far1/ppermute | solution.py:74
  20.2 16.7 %collective-permute-start.4 = (bf16[96,2048]{1,0:T(8,128)(2,1)S(1)}, bf16[96,2048]{1,0:T(8,128)(2,1)S(1)}, u32[]{:S(2)}, u32[]{:S(2)}) collective-permute-start(bf16[96,2048]{1,0:T(8,128)(2,1)S(1)} %pad_maximum_fusion.3), channel_id=1, source_target_pairs={{0,4},{1,0},{2,6},{3,2},{4,5},{5,1},{6,7},{7,3},{8,12},{9,8},{10,1... | collective-permute-start | bytes 1179656 | tf_op jit(solution)/shard_map/arr0/ppermute | solution.py:94
  22.4 14.4 %collective-permute-start.5 = (bf16[96,2048]{1,0:T(8,128)(2,1)S(1)}, bf16[96,2048]{1,0:T(8,128)(2,1)S(1)}, u32[]{:S(2)}, u32[]{:S(2)}) collective-permute-start(bf16[96,2048]{1,0:T(8,128)(2,1)S(1)} %pad_maximum_fusion.3), channel_id=1, source_target_pairs={{1,4},{3,6},{4,1},{6,3},{9,12},{11,14},{12,9},{14,11},{17,20},{19,... | collective-permute-start | bytes 1179656 | tf_op jit(solution)/shard_map/arr0/ppermute | solution.py:94
  34.1 9.6 %collective-permute-start.6 = (bf16[48,2048]{1,0:T(8,128)(2,1)S(1)}, bf16[48,2048]{1,0:T(8,128)(2,1)S(1)}, u32[]{:S(2)}, u32[]{:S(2)}) collective-permute-start(bf16[48,2048]{1,0:T(8,128)(2,1)S(1)} %broadcast_select_fusion.17), channel_id=1, source_target_pairs={{0,2},{1,3},{2,0},{3,1},{4,6},{5,7},{6,4},{7,5},{8,10},{9,11},{10,... | collective-permute-start | bytes 589832 | tf_op jit(solution)/shard_map/sel1/ppermute | solution.py:70
  34.4 14.2 %collective-permute-start.3 = (bf16[32,2048]{1,0:T(8,128)(2,1)S(1)}, bf16[32,2048]{1,0:T(8,128)(2,1)S(1)}, u32[]{:S(2)}, u32[]{:S(2)}) collective-permute-start(bf16[32,2048]{1,0:T(8,128)(2,1)S(1)} %get-tuple-element.103), channel_id=1, source_target_pairs={{0,8},{4,12},{8,0},{12,4},{1,9},{5,13},{9,1},{13,5},{2,10},{6,14},... | collective-permute-start | bytes 393224 | tf_op jit(solution)/shard_map/far2/ppermute | solution.py:74
  43.8 11.1 %collective-permute-start.11 = (bf16[96,2048]{1,0:T(8,128)(2,1)S(1)}, bf16[96,2048]{1,0:T(8,128)(2,1)S(1)}, u32[]{:S(2)}, u32[]{:S(2)}) collective-permute-start(bf16[96,2048]{1,0:T(8,128)(2,1)S(1)} %pad_maximum_fusion.4), channel_id=1, source_target_pairs={{1,4},{3,6},{4,1},{6,3},{9,12},{11,14},{12,9},{14,11},{17,20},{19,... | collective-permute-start | bytes 1179656 | tf_op jit(solution)/shard_map/arr1/ppermute | solution.py:94
  46.3 19.5 %collective-permute-start.12 = (bf16[192,1024]{1,0:T(8,128)(2,1)S(1)}, bf16[192,1024]{1,0:T(8,128)(2,1)S(1)}, u32[]{:S(2)}, u32[]{:S(2)}) collective-permute-start(bf16[192,1024]{1,0:T(8,128)(2,1)S(1)} %get-tuple-element.108), channel_id=1, source_target_pairs={{0,2},{1,3},{2,0},{3,1},{4,6},{5,7},{6,4},{7,5},{8,10},{9,11},{10,... | collective-permute-start | bytes 1179656 | tf_op jit(solution)/shard_map/b0/ppermute | solution.py:70
  48.6 17.2 %collective-permute-start.13 = (bf16[192,1024]{1,0:T(8,128)(2,1)S(1)}, bf16[192,1024]{1,0:T(8,128)(2,1)S(1)}, u32[]{:S(2)}, u32[]{:S(2)}) collective-permute-start(bf16[192,1024]{1,0:T(8,128)(2,1)S(1)} %get-tuple-element.116), channel_id=1, source_target_pairs={{0,2},{1,3},{2,0},{3,1},{4,6},{5,7},{6,4},{7,5},{8,10},{9,11},{10,... | collective-permute-start | bytes 1179656 | tf_op jit(solution)/shard_map/b0/ppermute | solution.py:70
  49.9 18.4 %collective-permute-start.9 = (bf16[32,2048]{1,0:T(8,128)(2,1)S(1)}, bf16[32,2048]{1,0:T(8,128)(2,1)S(1)}, u32[]{:S(2)}, u32[]{:S(2)}) collective-permute-start(bf16[32,2048]{1,0:T(8,128)(2,1)S(1)} %broadcast_select_fusion.22), channel_id=1, source_target_pairs={{0,2},{1,3},{2,0},{3,1},{4,6},{5,7},{6,4},{7,5},{8,10},{9,11},{10,... | collective-permute-start | bytes 393224 | tf_op jit(solution)/shard_map/sel2/ppermute | solution.py:70
  57.2 9.3 %collective-permute-start.14 = (bf16[2,192,1024]{2,1,0:T(8,128)(2,1)S(1)}, bf16[2,192,1024]{2,1,0:T(8,128)(2,1)S(1)}, u32[]{:S(2)}, u32[]{:S(2)}) collective-permute-start(bf16[2,192,1024]{2,1,0:T(8,128)(2,1)S(1)} %a1.1), channel_id=1, source_target_pairs={{0,1},{1,0},{2,3},{3,2},{4,5},{5,4},{6,7},{7,6},{8,9},{9,8},{10,11... | collective-permute-start | bytes 2359304 | tf_op jit(solution)/shard_map/a1/ppermute | solution.py:70
  59.3 13.1 %collective-permute-start.16 = (bf16[2,192,1024]{2,1,0:T(8,128)(2,1)S(1)}, bf16[2,192,1024]{2,1,0:T(8,128)(2,1)S(1)}, u32[]{:S(2)}, u32[]{:S(2)}) collective-permute-start(bf16[2,192,1024]{2,1,0:T(8,128)(2,1)S(1)} %c1.1), channel_id=1, source_target_pairs={{0,1},{1,0},{2,3},{3,2},{4,5},{5,4},{6,7},{7,6},{8,9},{9,8},{10,11... | collective-permute-start | bytes 2359304 | tf_op jit(solution)/shard_map/c1/ppermute | solution.py:70
  66.1 18.3 %collective-permute-start.19 = (bf16[192,1024]{1,0:T(8,128)(2,1)S(1)}, bf16[192,1024]{1,0:T(8,128)(2,1)S(1)}, u32[]{:S(2)}, u32[]{:S(2)}) collective-permute-start(bf16[192,1024]{1,0:T(8,128)(2,1)S(1)} %hide0.1.one), channel_id=1, source_target_pairs={{0,1},{1,0},{2,3},{3,2},{4,5},{5,4},{6,7},{7,6},{8,9},{9,8},{10,11... | collective-permute-start | bytes 1179656 | tf_op jit(solution)/shard_map/hide0/ppermute | solution.py:70
  66.2 20.8 %collective-permute-start.24 = (bf16[192,1024]{1,0:T(8,128)(2,1)S(1)}, bf16[192,1024]{1,0:T(8,128)(2,1)S(1)}, u32[]{:S(2)}, u32[]{:S(2)}) collective-permute-start(bf16[192,1024]{1,0:T(8,128)(2,1)S(1)} %hide0.1.one), channel_id=1, source_target_pairs={{0,2},{1,3},{2,0},{3,1},{4,6},{5,7},{6,4},{7,5},{8,10},{9,11},{10,... | collective-permute-start | bytes 1179656 | tf_op jit(solution)/shard_map/hide0/ppermute | solution.py:70
  72.4 20.9 %collective-permute-start.18 = (bf16[192,1024]{1,0:T(8,128)(2,1)S(1)}, bf16[192,1024]{1,0:T(8,128)(2,1)S(1)}, u32[]{:S(2)}, u32[]{:S(2)}) collective-permute-start(bf16[192,1024]{1,0:T(8,128)(2,1)S(1)} %get-tuple-element.119), channel_id=1, source_target_pairs={{0,2},{1,3},{2,0},{3,1},{4,6},{5,7},{6,4},{7,5},{8,10},{9,11},{10,... | collective-permute-start | bytes 1179656 | tf_op jit(solution)/shard_map/b1/ppermute | solution.py:70
  75.7 17.6 %collective-permute-start.20 = (bf16[192,1024]{1,0:T(8,128)(2,1)S(1)}, bf16[192,1024]{1,0:T(8,128)(2,1)S(1)}, u32[]{:S(2)}, u32[]{:S(2)}) collective-permute-start(bf16[192,1024]{1,0:T(8,128)(2,1)S(1)} %get-tuple-element.129), channel_id=1, source_target_pairs={{0,2},{1,3},{2,0},{3,1},{4,6},{5,7},{6,4},{7,5},{8,10},{9,11},{10,... | collective-permute-start | bytes 1179656 | tf_op jit(solution)/shard_map/b1/ppermute | solution.py:70
  78.8 16.5 %collective-permute-start.21 = (bf16[2,128,1024]{2,1,0:T(8,128)(2,1)S(1)}, bf16[2,128,1024]{2,1,0:T(8,128)(2,1)S(1)}, u32[]{:S(2)}, u32[]{:S(2)}) collective-permute-start(bf16[2,128,1024]{2,1,0:T(8,128)(2,1)S(1)} %a2.1), channel_id=1, source_target_pairs={{0,1},{1,0},{2,3},{3,2},{4,5},{5,4},{6,7},{7,6},{8,9},{9,8},{10,11... | collective-permute-start | bytes 1572872 | tf_op jit(solution)/shard_map/a2/ppermute | solution.py:70
  84.4 13.4 %collective-permute-start.22 = (bf16[2,128,1024]{2,1,0:T(8,128)(2,1)S(1)}, bf16[2,128,1024]{2,1,0:T(8,128)(2,1)S(1)}, u32[]{:S(2)}, u32[]{:S(2)}) collective-permute-start(bf16[2,128,1024]{2,1,0:T(8,128)(2,1)S(1)} %c2.1), channel_id=1, source_target_pairs={{0,1},{1,0},{2,3},{3,2},{4,5},{5,4},{6,7},{7,6},{8,9},{9,8},{10,11... | collective-permute-start | bytes 1572872 | tf_op jit(solution)/shard_map/c2/ppermute | solution.py:70
  87.0 16.4 %collective-permute-start.25 = (bf16[192,1024]{1,0:T(8,128)(2,1)S(1)}, bf16[192,1024]{1,0:T(8,128)(2,1)S(1)}, u32[]{:S(2)}, u32[]{:S(2)}) collective-permute-start(bf16[192,1024]{1,0:T(8,128)(2,1)S(1)} %collective-permute-done.24.one), channel_id=1, source_target_pairs={{0,1},{1,0},{2,3},{3,2},{4,5},{5,4},{6,7},{7,6},{8,9},{9,8},{10,11... | collective-permute-start | bytes 1179656 | tf_op jit(solution)/shard_map/forward0/ppermute | solution.py:70
  93.7 13.6 %collective-permute-start.26 = (bf16[192,1024]{1,0:T(8,128)(2,1)S(1)}, bf16[192,1024]{1,0:T(8,128)(2,1)S(1)}, u32[]{:S(2)}, u32[]{:S(2)}) collective-permute-start(bf16[192,1024]{1,0:T(8,128)(2,1)S(1)} %hide1.1.one), channel_id=1, source_target_pairs={{0,1},{1,0},{2,3},{3,2},{4,5},{5,4},{6,7},{7,6},{8,9},{9,8},{10,11... | collective-permute-start | bytes 1179656 | tf_op jit(solution)/shard_map/hide1/ppermute | solution.py:70
  95.0 14.2 %collective-permute-start.30 = (bf16[192,1024]{1,0:T(8,128)(2,1)S(1)}, bf16[192,1024]{1,0:T(8,128)(2,1)S(1)}, u32[]{:S(2)}, u32[]{:S(2)}) collective-permute-start(bf16[192,1024]{1,0:T(8,128)(2,1)S(1)} %hide1.1.one), channel_id=1, source_target_pairs={{0,2},{1,3},{2,0},{3,1},{4,6},{5,7},{6,4},{7,5},{8,10},{9,11},{10,... | collective-permute-start | bytes 1179656 | tf_op jit(solution)/shard_map/hide1/ppermute | solution.py:70
  96.6 20.4 %collective-permute-start.23 = (bf16[128,1024]{1,0:T(8,128)(2,1)S(1)}, bf16[128,1024]{1,0:T(8,128)(2,1)S(1)}, u32[]{:S(2)}, u32[]{:S(2)}) collective-permute-start(bf16[128,1024]{1,0:T(8,128)(2,1)S(1)} %get-tuple-element.132), channel_id=1, source_target_pairs={{0,2},{1,3},{2,0},{3,1},{4,6},{5,7},{6,4},{7,5},{8,10},{9,11},{10,... | collective-permute-start | bytes 786440 | tf_op jit(solution)/shard_map/b2/ppermute | solution.py:70
  105.4 15.0 %collective-permute-start.29 = (bf16[96,2048]{1,0:T(8,128)(2,1)S(1)}, bf16[96,2048]{1,0:T(8,128)(2,1)S(1)}, u32[]{:S(2)}, u32[]{:S(2)}) collective-permute-start(bf16[96,2048]{1,0:T(8,128)(2,1)S(1)} %get-tuple-element.165), channel_id=1, source_target_pairs={{0,1},{1,5},{2,3},{3,7},{4,0},{5,4},{6,2},{7,6},{8,9},{9,13},{10,1... | collective-permute-start | bytes 1179656 | tf_op jit(solution)/shard_map/out0/ppermute | solution.py:94
  107.0 9.9 %collective-permute-start.27 = (bf16[128,1024]{1,0:T(8,128)(2,1)S(1)}, bf16[128,1024]{1,0:T(8,128)(2,1)S(1)}, u32[]{:S(2)}, u32[]{:S(2)}) collective-permute-start(bf16[128,1024]{1,0:T(8,128)(2,1)S(1)} %get-tuple-element.140), channel_id=1, source_target_pairs={{0,2},{1,3},{2,0},{3,1},{4,6},{5,7},{6,4},{7,5},{8,10},{9,11},{10,... | collective-permute-start | bytes 786440 | tf_op jit(solution)/shard_map/b2/ppermute | solution.py:70
  109.3 11.1 %collective-permute-start.32 = (bf16[96,2048]{1,0:T(8,128)(2,1)S(1)}, bf16[96,2048]{1,0:T(8,128)(2,1)S(1)}, u32[]{:S(2)}, u32[]{:S(2)}) collective-permute-start(bf16[96,2048]{1,0:T(8,128)(2,1)S(1)} %get-tuple-element.164), channel_id=1, source_target_pairs={{1,4},{3,6},{4,1},{6,3},{9,12},{11,14},{12,9},{14,11},{17,20},{19,... | collective-permute-start | bytes 1179656 | tf_op jit(solution)/shard_map/out0/ppermute | solution.py:94
  118.0 12.2 %collective-permute-start.28 = (bf16[128,1024]{1,0:T(8,128)(2,1)S(1)}, bf16[128,1024]{1,0:T(8,128)(2,1)S(1)}, u32[]{:S(2)}, u32[]{:S(2)}) collective-permute-start(bf16[128,1024]{1,0:T(8,128)(2,1)S(1)} %hide2.1.one), channel_id=1, source_target_pairs={{0,2},{1,3},{2,0},{3,1},{4,6},{5,7},{6,4},{7,5},{8,10},{9,11},{10,... | collective-permute-start | bytes 786440 | tf_op jit(solution)/shard_map/hide2/ppermute | solution.py:70
  120.7 9.5 %collective-permute-start.33 = (bf16[48,2048]{1,0:T(8,128)(2,1)S(1)}, bf16[48,2048]{1,0:T(8,128)(2,1)S(1)}, u32[]{:S(2)}, u32[]{:S(2)}) collective-permute-start(bf16[48,2048]{1,0:T(8,128)(2,1)S(1)} %select_convert_fusion.4), channel_id=1, source_target_pairs={{0,2},{1,3},{2,0},{3,1},{4,6},{5,7},{6,4},{7,5},{8,10},{9,11},{10,... | collective-permute-start | bytes 589832 | tf_op jit(solution)/shard_map/mix0/ppermute | solution.py:70
  121.9 13.6 %collective-permute-start.38 = (bf16[96,2048]{1,0:T(8,128)(2,1)S(1)}, bf16[96,2048]{1,0:T(8,128)(2,1)S(1)}, u32[]{:S(2)}, u32[]{:S(2)}) collective-permute-start(bf16[96,2048]{1,0:T(8,128)(2,1)S(1)} %get-tuple-element.163), channel_id=1, source_target_pairs={{0,1},{1,5},{2,3},{3,7},{4,0},{5,4},{6,2},{7,6},{8,9},{9,13},{10,1... | collective-permute-start | bytes 1179656 | tf_op jit(solution)/shard_map/out1/ppermute | solution.py:94
  123.4 12.2 %collective-permute-start.39 = (bf16[96,2048]{1,0:T(8,128)(2,1)S(1)}, bf16[96,2048]{1,0:T(8,128)(2,1)S(1)}, u32[]{:S(2)}, u32[]{:S(2)}) collective-permute-start(bf16[96,2048]{1,0:T(8,128)(2,1)S(1)} %get-tuple-element.162), channel_id=1, source_target_pairs={{1,4},{3,6},{4,1},{6,3},{9,12},{11,14},{12,9},{14,11},{17,20},{19,... | collective-permute-start | bytes 1179656 | tf_op jit(solution)/shard_map/out1/ppermute | solution.py:94
  131.1 12.0 %collective-permute-start.37 = (bf16[48,2048]{1,0:T(8,128)(2,1)S(1)}, bf16[48,2048]{1,0:T(8,128)(2,1)S(1)}, u32[]{:S(2)}, u32[]{:S(2)}) collective-permute-start(bf16[48,2048]{1,0:T(8,128)(2,1)S(1)} %convert_select_fusion.4), channel_id=1, source_target_pairs={{0,8},{4,12},{8,0},{12,4},{1,9},{5,13},{9,1},{13,5},{2,10},{6,14},... | collective-permute-start | bytes 589832 | tf_op jit(solution)/shard_map/far_out0/ppermute | solution.py:74
  135.3 10.0 %collective-permute-start.36 = (bf16[64,2048]{1,0:T(8,128)(2,1)S(1)}, bf16[64,2048]{1,0:T(8,128)(2,1)S(1)}, u32[]{:S(2)}, u32[]{:S(2)}) collective-permute-start(bf16[64,2048]{1,0:T(8,128)(2,1)S(1)} %get-tuple-element.170), channel_id=1, source_target_pairs={{0,1},{1,5},{2,3},{3,7},{4,0},{5,4},{6,2},{7,6},{8,9},{9,13},{10,1... | collective-permute-start | bytes 786440 | tf_op jit(solution)/shard_map/out2/ppermute | solution.py:94
  135.8 18.8 %collective-permute-start.42 = (bf16[48,2048]{1,0:T(8,128)(2,1)S(1)}, bf16[48,2048]{1,0:T(8,128)(2,1)S(1)}, u32[]{:S(2)}, u32[]{:S(2)}) collective-permute-start(bf16[48,2048]{1,0:T(8,128)(2,1)S(1)} %select_convert_fusion.3), channel_id=1, source_target_pairs={{0,2},{1,3},{2,0},{3,1},{4,6},{5,7},{6,4},{7,5},{8,10},{9,11},{10,... | collective-permute-start | bytes 589832 | tf_op jit(solution)/shard_map/mix1/ppermute | solution.py:70
  (15 other events, 91.1 us)

commit v7 on v6

--- a/solution.py
+++ b/solution.py
@@ -10,12 +10,13 @@
 ROWS = (48, 48, 32)
 ORDER = (
     "far0", "load3", "sel0", "far1", "load1", "arr0", "load2", "load0", "sel1", "far2", "take0", "a0", "c0",
-    "b0", "arr1", "d0", "sel2", "take1", "a1", "c1", "hide0", "b1", "arr2", "d1", "take2", "a2", "c2",
-    "down0", "own0", "forward0", "hide1", "b2", "d2", "down2", "rest0", "out0", "own1", "forward1", "hide2",
-    "rest1", "out1", "mix0", "own2", "far_out0", "forward2", "rest2", "out2", "mix1", "end0", "mix2",
+    "b0", "arr1", "d0", "sel2", "take1", "a1", "c1", "b1", "arr2", "d1", "hide0", "take2", "a2", "c2",
+    "down0", "own0", "b2", "d2", "forward0", "down2", "hide1", "rest0", "out0", "own1", "forward1", "hide2",
+    "mix0", "rest1", "out1", "forward2", "own2", "rest2", "out2", "far_out0", "mix1", "mix2", "end0",
     "far_out1", "far_out2", "end1", "end2",
 )
 TILE = 256
+SPLIT = ()
 COST = 1 << 34
 LOAD_COST = 1 << 30
 VMEM = 6 << 20
@@ -232,7 +233,9 @@
     )(values, scales.T)
 
 
-def hide_kernel(held, got_gate, got_up, out):
+def hide_kernel(held, *rest):
+    got, out = rest[:-1], rest[-1]
+    got_gate, got_up = got if len(got) == 2 else (got[0].at[0], got[0].at[1])
     rows = 32
 
     @pl.loop(0, out.shape[0] // rows)
@@ -243,16 +246,16 @@
         out[here] = narrow(jax.nn.silu(gate) * up)
 
 
-def hide(held, got_gate, got_up):
+def hide(held, *got):
     near = pl.BlockSpec(memory_space=pltpu.VMEM)
     return pl.pallas_call(
         hide_kernel,
-        out_shape=jax.ShapeDtypeStruct(held.shape[1:], got_up.dtype),
-        in_specs=[near] * 3,
+        out_shape=jax.ShapeDtypeStruct(held.shape[1:], got[0].dtype),
+        in_specs=[near] * (1 + len(got)),
         out_specs=near,
         compiler_params=pltpu.CompilerParams(vmem_limit_bytes=VMEM),
         cost_estimate=pl.CostEstimate(flops=COST, bytes_accessed=1, transcendentals=0),
-    )(held, got_gate, got_up)
+    )(held, *got)
 
 
 def end_kernel(count, kept, got, *rest):
@@ -363,8 +366,8 @@
         self.held["c", i] = over_seq(self.part(i, 1), 1)
 
     def b(self, i):
-        both = self.part(i, 2, self.held["a", i], split=True)
-        self.held["b", i] = over_seq(both[0], 2), over_seq(both[1], 2)
+        sent = self.part(i, 2, self.held["a", i], split=i in SPLIT)
+        self.held["b", i] = [over_seq(part, 2) for part in (sent if i in SPLIT else (sent,))]
 
     def d(self, i):
         self.held["d", i] = self.part(i, 0, self.held["c", i], jnp.float32)

time: 166 us -> 168 us (1.012)
  starting transfers between devices: 54.3 us -> 49.2 us
  waiting for transfers between devices: 49.9 us -> 54.3 us
  Pallas kernels: 56.7 us -> 59.3 us
    ppermute x12, waiting for transfers between devices: 12.1 us -> 20.1 us  [over_both(): return lax.ppermute(array, ('tp', 'seq'), pairs)]
    ppermute x6, starting transfers between devices: 12.1 us -> 8.79 us  [over_tp(): return lax.ppermute(array, 'tp', [(i, i ^ bit) for i in range(4)])]
    ppermute x6, waiting for transfers between devices: 16.8 us -> 15 us  [over_tp(): return lax.ppermute(array, 'tp', [(i, i ^ bit) for i in range(4)])]
    ppermute x27 -> x24, waiting for transfers between devices: 21 us -> 19.2 us  [over_seq(): return lax.ppermute(array, 'seq', [(i, i ^ bit) for i in range(4)])]
    ppermute x27 -> x24, starting transfers between devices: 18 us -> 16.4 us  [over_seq(): return lax.ppermute(array, 'seq', [(i, i ^ bit) for i in range(4)])]
  transfers between devices with their start and end apart: 45 -> 42, of which waited for: 14 -> 14; matrix products, arithmetic and copies ran while one was open for 1% -> 1% of each run, Pallas kernels for 33% -> 34%
where the time goes in v7:
time: 168 us
  Pallas kernels  59.3 us (35%)
  waiting for transfers between devices  54.3 us (32%)
  starting transfers between devices  49.2 us (29%)
  other arithmetic  2.04 us (1%)
  local copies, waits for them, and re-layouts  1.73 us (1%)
    ppermute x12, starting transfers between devices, over_both(): return lax.ppermute(array, ('tp', 'seq'), pairs)  24 us
    pallas_call x12, Pallas kernels, sums(): pl.pallas_call(functools.partial(sums_kernel, got is not None, split), ou...  22.7 us
    ppermute x12, waiting for transfers between devices, over_both(): return lax.ppermute(array, ('tp', 'seq'), pairs)  20.1 us
    ppermute x24, waiting for transfers between devices, over_seq(): return lax.ppermute(array, 'seq', [(i, i ^ bit) for i in range(4)])  19.2 us
    ppermute x24, starting transfers between devices, over_seq(): return lax.ppermute(array, 'seq', [(i, i ^ bit) for i in range(4)])  16.4 us
    ppermute x6, waiting for transfers between devices, over_tp(): return lax.ppermute(array, 'tp', [(i, i ^ bit) for i in range(4)])  15 us
    pallas_call x4, Pallas kernels, load(): pl.pallas_call(load_kernel, out_shape=jax.ShapeDtypeStruct((2, deep, widt...  14 us
    pallas_call x6, Pallas kernels, products(): pl.pallas_call(functools.partial(products_kernel, total is not None), out...  10.9 us
  transfers between devices with their start and end apart: 42, of which 14 were waited for; matrix products, arithmetic and copies ran while one was open for 1% of the time, Pallas kernels for 34%

profile of v7, /device:TPU:1, one launch (start us, length us, event | category | flops | bytes accessed | tf_op | source)
XLA Modules:
  0.0 167.9 jit_solution(5124963166827251212)
XLA Ops:
  2.8 3.2 %collective-permute-start = (bf16[48,2048]{1,0:T(8,128)(2,1)S(1)}, bf16[48,2048]{1,0:T(8,128)(2,1)S(1)}, u32[]{:S(2)}, u32[]{:S(2)}) collective-permute-start(bf16[48,2048]{1,0:T(8,128)(2,1)S(1)} %get-tuple-element.80), channel_id=1, source_target_pairs={{0,8},{4,12},{8,0},{12,4},{1,9},{5,13},{9,1},{13,5},{2,10},{6,14},... | collective-permute-start | bytes 589832 | tf_op jit(solution)/shard_map/far0/ppermute | solution.py:75
  6.1 3.5 %load3.1.weights = bf16[2,2048,1024]{2,1,0:T(8,128)(2,1)S(1)} custom-call(s32[1]{0:T(128)} %bitcast.3.quarter, bf16[2048,4096]{1,0:T(8,128)(2,1)} %gate_weight.3, bf16[2048,4096]{1,0:T(8,128)(2,1)} %up_weight.7), custom_call_target="tpu_custom_call" | custom-call | flops 1073741824 | bytes 1 | tf_op jit(solution)/shard_map/load3/pallas_call | solution.py:121
  9.6 5.3 %collective-permute-done = bf16[48,2048]{1,0:T(8,128)(2,1)S(1)} collective-permute-done((bf16[48,2048]{1,0:T(8,128)(2,1)S(1)}, bf16[48,2048]{1,0:T(8,128)(2,1)S(1)}, u32[]{:S(2)}, u32[]{:S(2)}) %collective-permute-start) | collective-permute-done | bytes 196640 | tf_op jit(solution)/shard_map/far0/ppermute | solution.py:75
  15.9 3.5 %load1.1.weights = bf16[2,2048,1024]{2,1,0:T(8,128)(2,1)S(1)} custom-call(s32[1]{0:T(128)} %bitcast.1.quarter, bf16[2048,4096]{1,0:T(8,128)(2,1)} %gate_weight.3, bf16[2048,4096]{1,0:T(8,128)(2,1)} %up_weight.7), custom_call_target="tpu_custom_call" | custom-call | flops 1073741824 | bytes 1 | tf_op jit(solution)/shard_map/load1/pallas_call | solution.py:121
  20.2 6.7 %collective-permute-start.5 = (bf16[96,2048]{1,0:T(8,128)(2,1)S(1)}, bf16[96,2048]{1,0:T(8,128)(2,1)S(1)}, u32[]{:S(2)}, u32[]{:S(2)}) collective-permute-start(bf16[96,2048]{1,0:T(8,128)(2,1)S(1)} %pad_maximum_fusion.3), channel_id=1, source_target_pairs={{1,4},{3,6},{4,1},{6,3},{9,12},{11,14},{12,9},{14,11},{17,20},{19,... | collective-permute-start | bytes 1179656 | tf_op jit(solution)/shard_map/arr0/ppermute | solution.py:95
  27.0 3.5 %load2.1.weights = bf16[2,2048,1024]{2,1,0:T(8,128)(2,1)S(1)} custom-call(s32[1]{0:T(128)} %bitcast.2.quarter, bf16[2048,4096]{1,0:T(8,128)(2,1)} %gate_weight.3, bf16[2048,4096]{1,0:T(8,128)(2,1)} %up_weight.7), custom_call_target="tpu_custom_call" | custom-call | flops 1073741824 | bytes 1 | tf_op jit(solution)/shard_map/load2/pallas_call | solution.py:121
  30.5 3.5 %load0.1.weights = bf16[2,2048,1024]{2,1,0:T(8,128)(2,1)S(1)} custom-call(s32[1]{0:T(128)} %bitcast.quarter, bf16[2048,4096]{1,0:T(8,128)(2,1)} %gate_weight.3, bf16[2048,4096]{1,0:T(8,128)(2,1)} %up_weight.7), custom_call_target="tpu_custom_call" | custom-call | flops 1073741824 | bytes 1 | tf_op jit(solution)/shard_map/load0/pallas_call | solution.py:121
  34.4 2.5 %collective-permute-start.3 = (bf16[32,2048]{1,0:T(8,128)(2,1)S(1)}, bf16[32,2048]{1,0:T(8,128)(2,1)S(1)}, u32[]{:S(2)}, u32[]{:S(2)}) collective-permute-start(bf16[32,2048]{1,0:T(8,128)(2,1)S(1)} %get-tuple-element.94), channel_id=1, source_target_pairs={{0,8},{4,12},{8,0},{12,4},{1,9},{5,13},{9,1},{13,5},{2,10},{6,14},... | collective-permute-start | bytes 393224 | tf_op jit(solution)/shard_map/far2/ppermute | solution.py:75
  37.2 2.0 %a0.1 = bf16[2,192,1024]{2,1,0:T(8,128)(2,1)S(1)} custom-call(bf16[192,2048]{1,0:T(8,128)(2,1)S(1)} %pad_maximum_fusion.some, bf16[2,2048,1024]{2,1,0:T(8,128)(2,1)S(1)} %load3.1.weights), custom_call_target="tpu_custom_call" | custom-call | flops 17179869184 | bytes 1 | tf_op jit(solution)/shard_map/a0/pallas_call | solution.py:150
  42.2 2.0 %b0.1 = bf16[2,192,1024]{2,1,0:T(8,128)(2,1)S(1)} custom-call(bf16[192,2048]{1,0:T(8,128)(2,1)S(1)} %pad_maximum_fusion.some, bf16[2,2048,1024]{2,1,0:T(8,128)(2,1)S(1)} %load2.1.weights, bf16[2,192,1024]{2,1,0:T(8,128)(2,1)S(1)} %collective-permute-done.7.rest_0_), custom_call_target="tpu_custom_call" | custom-call | flops 17179869184 | bytes 1 | tf_op jit(solution)/shard_map/b0/pallas_call | solution.py:150
  44.3 2.9 %collective-permute-start.11 = (bf16[96,2048]{1,0:T(8,128)(2,1)S(1)}, bf16[96,2048]{1,0:T(8,128)(2,1)S(1)}, u32[]{:S(2)}, u32[]{:S(2)}) collective-permute-start(bf16[96,2048]{1,0:T(8,128)(2,1)S(1)} %pad_maximum_fusion.4), channel_id=1, source_target_pairs={{1,4},{3,6},{4,1},{6,3},{9,12},{11,14},{12,9},{14,11},{17,20},{19,... | collective-permute-start | bytes 1179656 | tf_op jit(solution)/shard_map/arr1/ppermute | solution.py:95
  47.6 2.0 %d0.1.held = f32[2,192,1024]{2,1,0:T(8,128)S(1)} custom-call(bf16[192,2048]{1,0:T(8,128)(2,1)S(1)} %pad_maximum_fusion.some, bf16[2,2048,1024]{2,1,0:T(8,128)(2,1)S(1)} %load0.1.weights, bf16[2,192,1024]{2,1,0:T(8,128)(2,1)S(1)} %collective-permute-done.8.rest_0_), custom_call_target="tpu_custom_call" | custom-call | flops 17179869184 | bytes 1 | tf_op jit(solution)/shard_map/d0/pallas_call | solution.py:150
  51.0 7.0 %collective-permute-done.10 = bf16[96,2048]{1,0:T(8,128)(2,1)S(1)} collective-permute-done((bf16[96,2048]{1,0:T(8,128)(2,1)S(1)}, bf16[96,2048]{1,0:T(8,128)(2,1)S(1)}, u32[]{:S(2)}, u32[]{:S(2)}) %collective-permute-start.10) | collective-permute-done | bytes 393248 | tf_op jit(solution)/shard_map/arr1/ppermute | solution.py:95
  62.9 2.9 %b1.1 = bf16[2,192,1024]{2,1,0:T(8,128)(2,1)} custom-call(bf16[192,2048]{1,0:T(8,128)(2,1)S(1)} %pad_maximum_fusion.1.some, bf16[2,2048,1024]{2,1,0:T(8,128)(2,1)S(1)} %load2.1.weights, bf16[2,192,1024]{2,1,0:T(8,128)(2,1)S(1)} %collective-permute-done.12.rest_0_), custom_call_target="tpu_custom_call" | custom-call | flops 17179869184 | bytes 1 | tf_op jit(solution)/shard_map/b1/pallas_call | solution.py:150
  65.8 2.4 %collective-permute-done.9 = bf16[32,2048]{1,0:T(8,128)(2,1)S(1)} collective-permute-done((bf16[32,2048]{1,0:T(8,128)(2,1)S(1)}, bf16[32,2048]{1,0:T(8,128)(2,1)S(1)}, u32[]{:S(2)}, u32[]{:S(2)}) %collective-permute-start.9) | collective-permute-done | bytes 131104 | tf_op jit(solution)/shard_map/sel2/ppermute | solution.py:71
  68.2 5.1 %collective-permute-start.16 = (bf16[64,2048]{1,0:T(8,128)(2,1)S(1)}, bf16[64,2048]{1,0:T(8,128)(2,1)S(1)}, u32[]{:S(2)}, u32[]{:S(2)}) collective-permute-start(bf16[64,2048]{1,0:T(8,128)(2,1)S(1)} %pad_maximum_fusion.5), channel_id=1, source_target_pairs={{1,4},{3,6},{4,1},{6,3},{9,12},{11,14},{12,9},{14,11},{17,20},{19,... | collective-permute-start | bytes 786440 | tf_op jit(solution)/shard_map/arr2/ppermute | solution.py:95
  73.9 2.0 %d1.1.held = f32[2,192,1024]{2,1,0:T(8,128)S(1)} custom-call(bf16[192,2048]{1,0:T(8,128)(2,1)S(1)} %pad_maximum_fusion.1.some, bf16[2,2048,1024]{2,1,0:T(8,128)(2,1)S(1)} %load0.1.weights, bf16[2,192,1024]{2,1,0:T(8,128)(2,1)S(1)} %collective-permute-done.15.rest_0_), custom_call_target="tpu_custom_call" | custom-call | flops 17179869184 | bytes 1 | tf_op jit(solution)/shard_map/d1/pallas_call | solution.py:150
  78.3 2.2 %collective-permute-done.13 = bf16[64,2048]{1,0:T(8,128)(2,1)S(1)} collective-permute-done((bf16[64,2048]{1,0:T(8,128)(2,1)S(1)}, bf16[64,2048]{1,0:T(8,128)(2,1)S(1)}, u32[]{:S(2)}, u32[]{:S(2)}) %collective-permute-start.13) | collective-permute-done | bytes 262176 | tf_op jit(solution)/shard_map/arr2/ppermute | solution.py:95
  84.3 4.0 %down0.1.weights = bf16[2,1024,2048]{2,1,0:T(8,128)(2,1)S(1)} custom-call(s32[2]{0:T(128)S(1)} %get-tuple-element.110.quarters, bf16[4096,2048]{1,0:T(8,128)(2,1)} %weight.1), custom_call_target="tpu_custom_call" | custom-call | flops 17179869184 | bytes 1 | tf_op jit(solution)/shard_map/down0/pallas_call | solution.py:181
  88.3 2.0 %own0.1.rest_0_ = f32[192,2048]{1,0:T(8,128)S(1)} custom-call(bf16[192,1024]{1,0:T(8,128)(2,1)S(1)} %hide0.1.one, bf16[192,1024]{1,0:T(8,128)(2,1)S(1)} %collective-permute-done.17.two, bf16[2,1024,2048]{2,1,0:T(8,128)(2,1)S(1)} %down0.1.weights), custom_call_target="tpu_custom_call" | custom-call | flops 17179869184 | bytes 1 | tf_op jit(solution)/shard_map/own0/pallas_call | solution.py:204
  93.6 7.4 %collective-permute-done.22.one = bf16[192,1024]{1,0:T(8,128)(2,1)S(1)} collective-permute-done((bf16[192,1024]{1,0:T(8,128)(2,1)S(1)}, bf16[192,1024]{1,0:T(8,128)(2,1)S(1)}, u32[]{:S(2)}, u32[]{:S(2)}) %collective-permute-start.22) | collective-permute-done | bytes 393248 | tf_op jit(solution)/shard_map/hide0/ppermute | solution.py:71
  103.0 4.0 %down2.1.weights = bf16[2,1024,2048]{2,1,0:T(8,128)(2,1)S(1)} custom-call(s32[2]{0:T(128)S(1)} %get-tuple-element.117.quarters, bf16[4096,2048]{1,0:T(8,128)(2,1)} %weight.1), custom_call_target="tpu_custom_call" | custom-call | flops 17179869184 | bytes 1 | tf_op jit(solution)/shard_map/down2/pallas_call | solution.py:181
  112.0 3.0 %collective-permute-start.28 = (bf16[96,2048]{1,0:T(8,128)(2,1)S(1)}, bf16[96,2048]{1,0:T(8,128)(2,1)S(1)}, u32[]{:S(2)}, u32[]{:S(2)}) collective-permute-start(bf16[96,2048]{1,0:T(8,128)(2,1)S(1)} %get-tuple-element.146), channel_id=1, source_target_pairs={{1,4},{3,6},{4,1},{6,3},{9,12},{11,14},{12,9},{14,11},{17,20},{19,... | collective-permute-start | bytes 1179656 | tf_op jit(solution)/shard_map/out0/ppermute | solution.py:95
  117.0 3.7 %collective-permute-done.26.one = bf16[192,1024]{1,0:T(8,128)(2,1)S(1)} collective-permute-done((bf16[192,1024]{1,0:T(8,128)(2,1)S(1)}, bf16[192,1024]{1,0:T(8,128)(2,1)S(1)}, u32[]{:S(2)}, u32[]{:S(2)}) %collective-permute-start.26) | collective-permute-done | bytes 393248 | tf_op jit(solution)/shard_map/hide1/ppermute | solution.py:71
  126.8 2.9 %collective-permute-done.25.one = bf16[128,1024]{1,0:T(8,128)(2,1)S(1)} collective-permute-done((bf16[128,1024]{1,0:T(8,128)(2,1)S(1)}, bf16[128,1024]{1,0:T(8,128)(2,1)S(1)}, u32[]{:S(2)}, u32[]{:S(2)}) %collective-permute-start.25) | collective-permute-done | bytes 262176 | tf_op jit(solution)/shard_map/hide2/ppermute | solution.py:71
  129.7 2.1 %collective-permute-start.31 = (bf16[128,1024]{1,0:T(8,128)(2,1)S(1)}, bf16[128,1024]{1,0:T(8,128)(2,1)S(1)}, u32[]{:S(2)}, u32[]{:S(2)}) collective-permute-start(bf16[128,1024]{1,0:T(8,128)(2,1)S(1)} %collective-permute-done.25.one), channel_id=1, source_target_pairs={{0,1},{1,0},{2,3},{3,2},{4,5},{5,4},{6,7},{7,6},{8,9},{9,8},{10,11... | collective-permute-start | bytes 786440 | tf_op jit(solution)/shard_map/forward2/ppermute | solution.py:71
  133.3 2.0 %collective-permute-start.35 = (bf16[96,2048]{1,0:T(8,128)(2,1)S(1)}, bf16[96,2048]{1,0:T(8,128)(2,1)S(1)}, u32[]{:S(2)}, u32[]{:S(2)}) collective-permute-start(bf16[96,2048]{1,0:T(8,128)(2,1)S(1)} %get-tuple-element.144), channel_id=1, source_target_pairs={{1,4},{3,6},{4,1},{6,3},{9,12},{11,14},{12,9},{14,11},{17,20},{19,... | collective-permute-start | bytes 1179656 | tf_op jit(solution)/shard_map/out1/ppermute | solution.py:95
  138.3 2.6 %collective-permute-start.36 = (bf16[64,2048]{1,0:T(8,128)(2,1)S(1)}, bf16[64,2048]{1,0:T(8,128)(2,1)S(1)}, u32[]{:S(2)}, u32[]{:S(2)}) collective-permute-start(bf16[64,2048]{1,0:T(8,128)(2,1)S(1)} %get-tuple-element.153), channel_id=1, source_target_pairs={{1,4},{3,6},{4,1},{6,3},{9,12},{11,14},{12,9},{14,11},{17,20},{19,... | collective-permute-start | bytes 786440 | tf_op jit(solution)/shard_map/out2/ppermute | solution.py:95
  141.0 5.1 %collective-permute-done.35 = bf16[96,2048]{1,0:T(8,128)(2,1)S(1)} collective-permute-done((bf16[96,2048]{1,0:T(8,128)(2,1)S(1)}, bf16[96,2048]{1,0:T(8,128)(2,1)S(1)}, u32[]{:S(2)}, u32[]{:S(2)}) %collective-permute-start.35) | collective-permute-done | bytes 393248 | tf_op jit(solution)/shard_map/out1/ppermute | solution.py:95
  146.6 5.5 %collective-permute-done.36 = bf16[64,2048]{1,0:T(8,128)(2,1)S(1)} collective-permute-done((bf16[64,2048]{1,0:T(8,128)(2,1)S(1)}, bf16[64,2048]{1,0:T(8,128)(2,1)S(1)}, u32[]{:S(2)}, u32[]{:S(2)}) %collective-permute-start.36) | collective-permute-done | bytes 262176 | tf_op jit(solution)/shard_map/out2/ppermute | solution.py:95
  154.4 2.1 %collective-permute-done.37 = bf16[32,2048]{1,0:T(8,128)(2,1)S(1)} collective-permute-done((bf16[32,2048]{1,0:T(8,128)(2,1)S(1)}, bf16[32,2048]{1,0:T(8,128)(2,1)S(1)}, u32[]{:S(2)}, u32[]{:S(2)}) %collective-permute-start.37) | collective-permute-done | bytes 131104 | tf_op jit(solution)/shard_map/mix2/ppermute | solution.py:71
  157.0 8.2 %collective-permute-done.41.got = bf16[48,2048]{1,0:T(8,128)(2,1)S(1)} collective-permute-done((bf16[48,2048]{1,0:T(8,128)(2,1)S(1)}, bf16[48,2048]{1,0:T(8,128)(2,1)S(1)}, u32[]{:S(2)}, u32[]{:S(2)}) %collective-permute-start.41) | collective-permute-done | bytes 196640 | tf_op jit(solution)/shard_map/far_out1/ppermute | solution.py:75
  (118 shorter events, 49.7 us)
Async XLA Ops:
  2.8 12.0 %collective-permute-start = (bf16[48,2048]{1,0:T(8,128)(2,1)S(1)}, bf16[48,2048]{1,0:T(8,128)(2,1)S(1)}, u32[]{:S(2)}, u32[]{:S(2)}) collective-permute-start(bf16[48,2048]{1,0:T(8,128)(2,1)S(1)} %get-tuple-element.80), channel_id=1, source_target_pairs={{0,8},{4,12},{8,0},{12,4},{1,9},{5,13},{9,1},{13,5},{2,10},{6,14},... | collective-permute-start | bytes 589832 | tf_op jit(solution)/shard_map/far0/ppermute | solution.py:75
  15.9 18.1 %collective-permute-start.1 = (bf16[48,2048]{1,0:T(8,128)(2,1)S(1)}, bf16[48,2048]{1,0:T(8,128)(2,1)S(1)}, u32[]{:S(2)}, u32[]{:S(2)}) collective-permute-start(bf16[48,2048]{1,0:T(8,128)(2,1)S(1)} %get-tuple-element.85), channel_id=1, source_target_pairs={{0,8},{4,12},{8,0},{12,4},{1,9},{5,13},{9,1},{13,5},{2,10},{6,14},... | collective-permute-start | bytes 589832 | tf_op jit(solution)/shard_map/far1/ppermute | solution.py:75
  20.2 16.7 %collective-permute-start.5 = (bf16[96,2048]{1,0:T(8,128)(2,1)S(1)}, bf16[96,2048]{1,0:T(8,128)(2,1)S(1)}, u32[]{:S(2)}, u32[]{:S(2)}) collective-permute-start(bf16[96,2048]{1,0:T(8,128)(2,1)S(1)} %pad_maximum_fusion.3), channel_id=1, source_target_pairs={{1,4},{3,6},{4,1},{6,3},{9,12},{11,14},{12,9},{14,11},{17,20},{19,... | collective-permute-start | bytes 1179656 | tf_op jit(solution)/shard_map/arr0/ppermute | solution.py:95
  26.9 10.0 %collective-permute-start.4 = (bf16[96,2048]{1,0:T(8,128)(2,1)S(1)}, bf16[96,2048]{1,0:T(8,128)(2,1)S(1)}, u32[]{:S(2)}, u32[]{:S(2)}) collective-permute-start(bf16[96,2048]{1,0:T(8,128)(2,1)S(1)} %pad_maximum_fusion.3), channel_id=1, source_target_pairs={{0,4},{1,0},{2,6},{3,2},{4,5},{5,1},{6,7},{7,3},{8,12},{9,8},{10,1... | collective-permute-start | bytes 1179656 | tf_op jit(solution)/shard_map/arr0/ppermute | solution.py:95
  34.1 10.2 %collective-permute-start.6 = (bf16[48,2048]{1,0:T(8,128)(2,1)S(1)}, bf16[48,2048]{1,0:T(8,128)(2,1)S(1)}, u32[]{:S(2)}, u32[]{:S(2)}) collective-permute-start(bf16[48,2048]{1,0:T(8,128)(2,1)S(1)} %broadcast_select_fusion.17), channel_id=1, source_target_pairs={{0,2},{1,3},{2,0},{3,1},{4,6},{5,7},{6,4},{7,5},{8,10},{9,11},{10,... | collective-permute-start | bytes 589832 | tf_op jit(solution)/shard_map/sel1/ppermute | solution.py:71
  34.4 15.3 %collective-permute-start.3 = (bf16[32,2048]{1,0:T(8,128)(2,1)S(1)}, bf16[32,2048]{1,0:T(8,128)(2,1)S(1)}, u32[]{:S(2)}, u32[]{:S(2)}) collective-permute-start(bf16[32,2048]{1,0:T(8,128)(2,1)S(1)} %get-tuple-element.94), channel_id=1, source_target_pairs={{0,8},{4,12},{8,0},{12,4},{1,9},{5,13},{9,1},{13,5},{2,10},{6,14},... | collective-permute-start | bytes 393224 | tf_op jit(solution)/shard_map/far2/ppermute | solution.py:75
  44.3 13.6 %collective-permute-start.11 = (bf16[96,2048]{1,0:T(8,128)(2,1)S(1)}, bf16[96,2048]{1,0:T(8,128)(2,1)S(1)}, u32[]{:S(2)}, u32[]{:S(2)}) collective-permute-start(bf16[96,2048]{1,0:T(8,128)(2,1)S(1)} %pad_maximum_fusion.4), channel_id=1, source_target_pairs={{1,4},{3,6},{4,1},{6,3},{9,12},{11,14},{12,9},{14,11},{17,20},{19,... | collective-permute-start | bytes 1179656 | tf_op jit(solution)/shard_map/arr1/ppermute | solution.py:95
  47.3 10.7 %collective-permute-start.10 = (bf16[96,2048]{1,0:T(8,128)(2,1)S(1)}, bf16[96,2048]{1,0:T(8,128)(2,1)S(1)}, u32[]{:S(2)}, u32[]{:S(2)}) collective-permute-start(bf16[96,2048]{1,0:T(8,128)(2,1)S(1)} %pad_maximum_fusion.4), channel_id=1, source_target_pairs={{0,4},{1,0},{2,6},{3,2},{4,5},{5,1},{6,7},{7,3},{8,12},{9,8},{10,1... | collective-permute-start | bytes 1179656 | tf_op jit(solution)/shard_map/arr1/ppermute | solution.py:95
  47.3 28.6 %collective-permute-start.14 = (bf16[2,192,1024]{2,1,0:T(8,128)(2,1)S(1)}, bf16[2,192,1024]{2,1,0:T(8,128)(2,1)S(1)}, u32[]{:S(2)}, u32[]{:S(2)}) collective-permute-start(bf16[2,192,1024]{2,1,0:T(8,128)(2,1)S(1)} %b0.1), channel_id=1, source_target_pairs={{0,2},{1,3},{2,0},{3,1},{4,6},{5,7},{6,4},{7,5},{8,10},{9,11},{10,... | collective-permute-start | bytes 2359304 | tf_op jit(solution)/shard_map/b0/ppermute | solution.py:71
  49.7 18.5 %collective-permute-start.9 = (bf16[32,2048]{1,0:T(8,128)(2,1)S(1)}, bf16[32,2048]{1,0:T(8,128)(2,1)S(1)}, u32[]{:S(2)}, u32[]{:S(2)}) collective-permute-start(bf16[32,2048]{1,0:T(8,128)(2,1)S(1)} %broadcast_select_fusion.22), channel_id=1, source_target_pairs={{0,2},{1,3},{2,0},{3,1},{4,6},{5,7},{6,4},{7,5},{8,10},{9,11},{10,... | collective-permute-start | bytes 393224 | tf_op jit(solution)/shard_map/sel2/ppermute | solution.py:71
  62.3 11.6 %collective-permute-start.15 = (bf16[2,192,1024]{2,1,0:T(8,128)(2,1)S(1)}, bf16[2,192,1024]{2,1,0:T(8,128)(2,1)S(1)}, u32[]{:S(2)}, u32[]{:S(2)}) collective-permute-start(bf16[2,192,1024]{2,1,0:T(8,128)(2,1)S(1)} %c1.1), channel_id=1, source_target_pairs={{0,1},{1,0},{2,3},{3,2},{4,5},{5,4},{6,7},{7,6},{8,9},{9,8},{10,11... | collective-permute-start | bytes 2359304 | tf_op jit(solution)/shard_map/c1/ppermute | solution.py:71
  68.2 12.3 %collective-permute-start.16 = (bf16[64,2048]{1,0:T(8,128)(2,1)S(1)}, bf16[64,2048]{1,0:T(8,128)(2,1)S(1)}, u32[]{:S(2)}, u32[]{:S(2)}) collective-permute-start(bf16[64,2048]{1,0:T(8,128)(2,1)S(1)} %pad_maximum_fusion.5), channel_id=1, source_target_pairs={{1,4},{3,6},{4,1},{6,3},{9,12},{11,14},{12,9},{14,11},{17,20},{19,... | collective-permute-start | bytes 786440 | tf_op jit(solution)/shard_map/arr2/ppermute | solution.py:95
  73.5 33.4 %collective-permute-start.21 = (bf16[2,192,1024]{2,1,0:T(8,128)(2,1)}, bf16[2,192,1024]{2,1,0:T(8,128)(2,1)}, u32[]{:S(2)}, u32[]{:S(2)}) collective-permute-start(bf16[2,192,1024]{2,1,0:T(8,128)(2,1)} %b1.1), channel_id=1, source_target_pairs={{0,2},{1,3},{2,0},{3,1},{4,6},{5,7},{6,4},{7,5},{8,10},{9,11},{10,... | collective-permute-start | bytes 2359304 | tf_op jit(solution)/shard_map/b1/ppermute | solution.py:71
  76.2 24.8 %collective-permute-start.22 = (bf16[192,1024]{1,0:T(8,128)(2,1)S(1)}, bf16[192,1024]{1,0:T(8,128)(2,1)S(1)}, u32[]{:S(2)}, u32[]{:S(2)}) collective-permute-start(bf16[192,1024]{1,0:T(8,128)(2,1)S(1)} %hide0.1.one), channel_id=1, source_target_pairs={{0,2},{1,3},{2,0},{3,1},{4,6},{5,7},{6,4},{7,5},{8,10},{9,11},{10,... | collective-permute-start | bytes 1179656 | tf_op jit(solution)/shard_map/hide0/ppermute | solution.py:71
  77.5 10.9 %collective-permute-start.17 = (bf16[192,1024]{1,0:T(8,128)(2,1)S(1)}, bf16[192,1024]{1,0:T(8,128)(2,1)S(1)}, u32[]{:S(2)}, u32[]{:S(2)}) collective-permute-start(bf16[192,1024]{1,0:T(8,128)(2,1)S(1)} %hide0.1.one), channel_id=1, source_target_pairs={{0,1},{1,0},{2,3},{3,2},{4,5},{5,4},{6,7},{7,6},{8,9},{9,8},{10,11... | collective-permute-start | bytes 1179656 | tf_op jit(solution)/shard_map/hide0/ppermute | solution.py:71
  82.2 8.2 %collective-permute-start.18 = (bf16[2,128,1024]{2,1,0:T(8,128)(2,1)S(1)}, bf16[2,128,1024]{2,1,0:T(8,128)(2,1)S(1)}, u32[]{:S(2)}, u32[]{:S(2)}) collective-permute-start(bf16[2,128,1024]{2,1,0:T(8,128)(2,1)S(1)} %a2.1), channel_id=1, source_target_pairs={{0,1},{1,0},{2,3},{3,2},{4,5},{5,4},{6,7},{7,6},{8,9},{9,8},{10,11... | collective-permute-start | bytes 1572872 | tf_op jit(solution)/shard_map/a2/ppermute | solution.py:71
  83.7 8.5 %collective-permute-start.19 = (bf16[2,128,1024]{2,1,0:T(8,128)(2,1)S(1)}, bf16[2,128,1024]{2,1,0:T(8,128)(2,1)S(1)}, u32[]{:S(2)}, u32[]{:S(2)}) collective-permute-start(bf16[2,128,1024]{2,1,0:T(8,128)(2,1)S(1)} %c2.1), channel_id=1, source_target_pairs={{0,1},{1,0},{2,3},{3,2},{4,5},{5,4},{6,7},{7,6},{8,9},{9,8},{10,11... | collective-permute-start | bytes 1572872 | tf_op jit(solution)/shard_map/c2/ppermute | solution.py:71
  91.8 30.1 %collective-permute-start.20 = (bf16[2,128,1024]{2,1,0:T(8,128)(2,1)S(1)}, bf16[2,128,1024]{2,1,0:T(8,128)(2,1)S(1)}, u32[]{:S(2)}, u32[]{:S(2)}) collective-permute-start(bf16[2,128,1024]{2,1,0:T(8,128)(2,1)S(1)} %b2.1), channel_id=1, source_target_pairs={{0,2},{1,3},{2,0},{3,1},{4,6},{5,7},{6,4},{7,5},{8,10},{9,11},{10,... | collective-permute-start | bytes 1572872 | tf_op jit(solution)/shard_map/b2/ppermute | solution.py:71
  101.1 8.1 %collective-permute-start.23 = (bf16[192,1024]{1,0:T(8,128)(2,1)S(1)}, bf16[192,1024]{1,0:T(8,128)(2,1)S(1)}, u32[]{:S(2)}, u32[]{:S(2)}) collective-permute-start(bf16[192,1024]{1,0:T(8,128)(2,1)S(1)} %collective-permute-done.22.one), channel_id=1, source_target_pairs={{0,1},{1,0},{2,3},{3,2},{4,5},{5,4},{6,7},{7,6},{8,9},{9,8},{10,11... | collective-permute-start | bytes 1179656 | tf_op jit(solution)/shard_map/forward0/ppermute | solution.py:71
  108.4 12.3 %collective-permute-start.26 = (bf16[192,1024]{1,0:T(8,128)(2,1)S(1)}, bf16[192,1024]{1,0:T(8,128)(2,1)S(1)}, u32[]{:S(2)}, u32[]{:S(2)}) collective-permute-start(bf16[192,1024]{1,0:T(8,128)(2,1)S(1)} %hide1.1.one), channel_id=1, source_target_pairs={{0,2},{1,3},{2,0},{3,1},{4,6},{5,7},{6,4},{7,5},{8,10},{9,11},{10,... | collective-permute-start | bytes 1179656 | tf_op jit(solution)/shard_map/hide1/ppermute | solution.py:71
  111.2 11.3 %collective-permute-start.27 = (bf16[96,2048]{1,0:T(8,128)(2,1)S(1)}, bf16[96,2048]{1,0:T(8,128)(2,1)S(1)}, u32[]{:S(2)}, u32[]{:S(2)}) collective-permute-start(bf16[96,2048]{1,0:T(8,128)(2,1)S(1)} %get-tuple-element.147), channel_id=1, source_target_pairs={{0,1},{1,5},{2,3},{3,7},{4,0},{5,4},{6,2},{7,6},{8,9},{9,13},{10,1... | collective-permute-start | bytes 1179656 | tf_op jit(solution)/shard_map/out0/ppermute | solution.py:95
  112.0 10.8 %collective-permute-start.28 = (bf16[96,2048]{1,0:T(8,128)(2,1)S(1)}, bf16[96,2048]{1,0:T(8,128)(2,1)S(1)}, u32[]{:S(2)}, u32[]{:S(2)}) collective-permute-start(bf16[96,2048]{1,0:T(8,128)(2,1)S(1)} %get-tuple-element.146), channel_id=1, source_target_pairs={{1,4},{3,6},{4,1},{6,3},{9,12},{11,14},{12,9},{14,11},{17,20},{19,... | collective-permute-start | bytes 1179656 | tf_op jit(solution)/shard_map/out0/ppermute | solution.py:95
  122.1 9.7 %collective-permute-start.30 = (bf16[128,1024]{1,0:T(8,128)(2,1)S(1)}, bf16[128,1024]{1,0:T(8,128)(2,1)S(1)}, u32[]{:S(2)}, u32[]{:S(2)}) collective-permute-start(bf16[128,1024]{1,0:T(8,128)(2,1)S(1)} %hide2.1.one), channel_id=1, source_target_pairs={{0,1},{1,0},{2,3},{3,2},{4,5},{5,4},{6,7},{7,6},{8,9},{9,8},{10,11... | collective-permute-start | bytes 786440 | tf_op jit(solution)/shard_map/hide2/ppermute | solution.py:71
  122.1 7.5 %collective-permute-start.25 = (bf16[128,1024]{1,0:T(8,128)(2,1)S(1)}, bf16[128,1024]{1,0:T(8,128)(2,1)S(1)}, u32[]{:S(2)}, u32[]{:S(2)}) collective-permute-start(bf16[128,1024]{1,0:T(8,128)(2,1)S(1)} %hide2.1.one), channel_id=1, source_target_pairs={{0,2},{1,3},{2,0},{3,1},{4,6},{5,7},{6,4},{7,5},{8,10},{9,11},{10,... | collective-permute-start | bytes 786440 | tf_op jit(solution)/shard_map/hide2/ppermute | solution.py:71
  123.0 13.9 %collective-permute-start.34 = (bf16[48,2048]{1,0:T(8,128)(2,1)S(1)}, bf16[48,2048]{1,0:T(8,128)(2,1)S(1)}, u32[]{:S(2)}, u32[]{:S(2)}) collective-permute-start(bf16[48,2048]{1,0:T(8,128)(2,1)S(1)} %select_convert_fusion.4), channel_id=1, source_target_pairs={{0,2},{1,3},{2,0},{3,1},{4,6},{5,7},{6,4},{7,5},{8,10},{9,11},{10,... | collective-permute-start | bytes 589832 | tf_op jit(solution)/shard_map/mix0/ppermute | solution.py:71
  126.3 14.7 %collective-permute-start.33 = (bf16[96,2048]{1,0:T(8,128)(2,1)S(1)}, bf16[96,2048]{1,0:T(8,128)(2,1)S(1)}, u32[]{:S(2)}, u32[]{:S(2)}) collective-permute-start(bf16[96,2048]{1,0:T(8,128)(2,1)S(1)} %get-tuple-element.145), channel_id=1, source_target_pairs={{0,1},{1,5},{2,3},{3,7},{4,0},{5,4},{6,2},{7,6},{8,9},{9,13},{10,1... | collective-permute-start | bytes 1179656 | tf_op jit(solution)/shard_map/out1/ppermute | solution.py:95
  133.3 12.8 %collective-permute-start.35 = (bf16[96,2048]{1,0:T(8,128)(2,1)S(1)}, bf16[96,2048]{1,0:T(8,128)(2,1)S(1)}, u32[]{:S(2)}, u32[]{:S(2)}) collective-permute-start(bf16[96,2048]{1,0:T(8,128)(2,1)S(1)} %get-tuple-element.144), channel_id=1, source_target_pairs={{1,4},{3,6},{4,1},{6,3},{9,12},{11,14},{12,9},{14,11},{17,20},{19,... | collective-permute-start | bytes 1179656 | tf_op jit(solution)/shard_map/out1/ppermute | solution.py:95
  136.8 9.8 %collective-permute-start.32 = (bf16[64,2048]{1,0:T(8,128)(2,1)S(1)}, bf16[64,2048]{1,0:T(8,128)(2,1)S(1)}, u32[]{:S(2)}, u32[]{:S(2)}) collective-permute-start(bf16[64,2048]{1,0:T(8,128)(2,1)S(1)} %get-tuple-element.152), channel_id=1, source_target_pairs={{0,1},{1,5},{2,3},{3,7},{4,0},{5,4},{6,2},{7,6},{8,9},{9,13},{10,1... | collective-permute-start | bytes 786440 | tf_op jit(solution)/shard_map/out2/ppermute | solution.py:95
  136.9 15.7 %collective-permute-start.39 = (bf16[48,2048]{1,0:T(8,128)(2,1)S(1)}, bf16[48,2048]{1,0:T(8,128)(2,1)S(1)}, u32[]{:S(2)}, u32[]{:S(2)}) collective-permute-start(bf16[48,2048]{1,0:T(8,128)(2,1)S(1)} %convert_select_fusion.4), channel_id=1, source_target_pairs={{0,8},{4,12},{8,0},{12,4},{1,9},{5,13},{9,1},{13,5},{2,10},{6,14},... | collective-permute-start | bytes 589832 | tf_op jit(solution)/shard_map/far_out0/ppermute | solution.py:75
  138.3 13.9 %collective-permute-start.36 = (bf16[64,2048]{1,0:T(8,128)(2,1)S(1)}, bf16[64,2048]{1,0:T(8,128)(2,1)S(1)}, u32[]{:S(2)}, u32[]{:S(2)}) collective-permute-start(bf16[64,2048]{1,0:T(8,128)(2,1)S(1)} %get-tuple-element.153), channel_id=1, source_target_pairs={{1,4},{3,6},{4,1},{6,3},{9,12},{11,14},{12,9},{14,11},{17,20},{19,... | collective-permute-start | bytes 786440 | tf_op jit(solution)/shard_map/out2/ppermute | solution.py:95
  153.0 12.2 %collective-permute-start.41 = (bf16[48,2048]{1,0:T(8,128)(2,1)S(1)}, bf16[48,2048]{1,0:T(8,128)(2,1)S(1)}, u32[]{:S(2)}, u32[]{:S(2)}) collective-permute-start(bf16[48,2048]{1,0:T(8,128)(2,1)S(1)} %convert_select_fusion.3), channel_id=1, source_target_pairs={{0,8},{4,12},{8,0},{12,4},{1,9},{5,13},{9,1},{13,5},{2,10},{6,14},... | collective-permute-start | bytes 589832 | tf_op jit(solution)/shard_map/far_out1/ppermute | solution.py:75
  156.6 10.4 %collective-permute-start.40 = (bf16[32,2048]{1,0:T(8,128)(2,1)S(1)}, bf16[32,2048]{1,0:T(8,128)(2,1)S(1)}, u32[]{:S(2)}, u32[]{:S(2)}) collective-permute-start(bf16[32,2048]{1,0:T(8,128)(2,1)S(1)} %convert_select_fusion.5), channel_id=1, source_target_pairs={{0,8},{4,12},{8,0},{12,4},{1,9},{5,13},{9,1},{13,5},{2,10},{6,14},... | collective-permute-start | bytes 393224 | tf_op jit(solution)/shard_map/far_out2/ppermute | solution.py:75
  (12 other events, 51.5 us)

commit v8 on v7

--- a/solution.py
+++ b/solution.py
@@ -10,13 +10,13 @@
 ROWS = (48, 48, 32)
 ORDER = (
     "far0", "load3", "sel0", "far1", "load1", "arr0", "load2", "load0", "sel1", "far2", "take0", "a0", "c0",
-    "b0", "arr1", "d0", "sel2", "take1", "a1", "c1", "b1", "arr2", "d1", "hide0", "take2", "a2", "c2",
-    "down0", "own0", "b2", "d2", "forward0", "down2", "hide1", "rest0", "out0", "own1", "forward1", "hide2",
-    "mix0", "rest1", "out1", "forward2", "own2", "rest2", "out2", "far_out0", "mix1", "mix2", "end0",
-    "far_out1", "far_out2", "end1", "end2",
+    "b0", "arr1", "d0", "sel2", "take1", "a1", "c1", "hide0", "b1", "arr2", "d1", "take2", "a2", "c2",
+    "down0", "own0", "forward0", "hide1", "b2", "d2", "down2", "rest0", "out0", "forward1", "own1", "rest1",
+    "out1", "hide2", "mix0", "mix1", "forward2", "own2", "rest2", "out2", "far_out0", "mix2", "far_out1",
+    "far_out2", "end0", "end1", "end2",
 )
 TILE = 256
-SPLIT = ()
+SPLIT = (0, 1)
 COST = 1 << 34
 LOAD_COST = 1 << 30
 VMEM = 6 << 20
@@ -296,6 +296,57 @@
     )(kept, got, *(array for pair in before for array in pair))
 
 
+def small(kernel, outs, flags, *arrays):
+    near = pl.BlockSpec(memory_space=pltpu.VMEM)
+    return pl.pallas_call(
+        kernel,
+        out_shape=[jax.ShapeDtypeStruct(*out) for out in outs],
+        in_specs=[pl.BlockSpec(memory_space=pltpu.SMEM)] + [near] * len(arrays),
+        out_specs=[near] * len(outs),
+        compiler_params=pltpu.CompilerParams(vmem_limit_bytes=VMEM),
+        cost_estimate=pl.CostEstimate(flops=COST, bytes_accessed=1, transcendentals=0),
+    )(flags, *arrays)
+
+
+def strips(array):
+    return pl.loop(0, array.shape[1] // TILE)
+
+
+def out_kernel(flags, partial_sum, own, one, two):
+    half = own.shape[0]
+    low, top = pl.ds(0, half), pl.ds(half, half)
+
+    @strips(own)
+    def strip(j):
+        here = pl.ds(pl.multiple_of(j * TILE, TILE), TILE)
+        first, last = partial_sum[low, here], partial_sum[top, here]
+        mine = jnp.where(flags[1] == 1, first, last)
+        others = jnp.where(flags[1] == 1, last, first)
+        own[:, here] = mine
+        one[:, here] = narrow(jnp.where(flags[2] == 1, others, mine))
+        two[:, here] = narrow(others)
+
+
+def mix_kernel(flags, own, got_one, got_two, kept, sent):
+    rows = kept.shape[0]
+
+    @strips(own)
+    def strip(j):
+        here = pl.ds(pl.multiple_of(j * TILE, TILE), TILE)
+        pair = wide(got_one[:, here]) + jnp.where(flags[2] == 1, own[:, here], wide(got_two[:, here]))
+        kept[:, here] = jnp.where(flags[0] == 1, pair[:rows], pair[rows:])
+        sent[:, here] = narrow(jnp.where(flags[0] == 1, pair[rows:], pair[:rows]))
+
+
+def far_out_kernel(flags, kept, got, still, sent):
+    @strips(kept)
+    def strip(j):
+        here = pl.ds(pl.multiple_of(j * TILE, TILE), TILE)
+        mine, other = kept[:, here], wide(got[:, here])
+        still[:, here] = jnp.where(flags[3] == 1, mine, other)
+        sent[:, here] = narrow(jnp.where(flags[3] == 1, other, mine))
+
+
 class Steps:
 
     def __init__(self, tokens_values, tokens_scales, gate_weight, up_weight, down_weight):
@@ -304,7 +355,10 @@
         facts = x == 0, core == 0, (tp ^ seq) & 1 == 0, high == x
         quarters = [(seq ^ bits).reshape(1) for bits in range(4)]
         pairs = [jnp.stack([seq ^ bits, seq ^ bits ^ 1]) for bits in (0, 2)]
-        facts, self.quarters, self.pairs, gate_weight = lax.optimization_barrier((facts, quarters, pairs, gate_weight))
+        flags = jnp.stack(facts).astype(jnp.int32)
+        facts, self.flags, self.quarters, self.pairs, gate_weight = lax.optimization_barrier(
+            (facts, flags, quarters, pairs, gate_weight)
+        )
         self.first_x, self.first_core, self.even, self.same_half = facts
         self.gate_weight = pltpu.with_memory_space_constraint(gate_weight, pltpu.HBM)
         self.up_weight = pltpu.with_memory_space_constraint(up_weight, pltpu.HBM)
@@ -395,29 +449,24 @@
 
     def out(self, i):
         partial_sum = self.now(self.held["rest", i])
-        half = partial_sum.shape[0] // 2
-        low, top = partial_sum[:half], partial_sum[half:]
-        own = jnp.where(self.first_core, low, top)
-        others = jnp.where(self.first_core, top, low)
-        one, two = narrow(jnp.where(self.even, others, own)), narrow(others)
+        half = partial_sum.shape[0] // 2, partial_sum.shape[1]
+        outs = (half, jnp.float32), (half, jnp.bfloat16), (half, jnp.bfloat16)
+        own, one, two = small(out_kernel, outs, self.flags, partial_sum)
         self.held["out", i] = own, over_both(one, FIRST_OUT), over_both(two, SECOND)
         self.last = one
 
     def mix(self, i):
         own, first, second = self.held["out", i]
-        pair = wide(self.now(first)) + jnp.where(self.even, own, wide(second))
-        rows = pair.shape[0] // 2
-        low, top = pair[:rows], pair[rows:]
-        kept = jnp.where(self.first_x, low, top)
-        sent = narrow(jnp.where(self.first_x, top, low))
+        shape = own.shape[0] // 2, own.shape[1]
+        outs = (shape, jnp.float32), (shape, jnp.bfloat16)
+        kept, sent = small(mix_kernel, outs, self.flags, own, self.now(first), second)
         self.held["mix", i] = kept, over_seq(sent, 2)
         self.last = sent
 
     def far_out(self, i):
         kept, got = self.held["mix", i]
-        got = self.now(got)
-        sent = jnp.where(self.same_half, got, narrow(kept))
-        kept = jnp.where(self.same_half, kept, wide(got))
+        outs = (kept.shape, jnp.float32), (kept.shape, jnp.bfloat16)
+        kept, sent = small(far_out_kernel, outs, self.flags, kept, self.now(got))
         self.held["far_out", i] = kept, over_tp(sent, 2)
         self.last = sent
 

time: 168 us -> 164 us (0.976)
  waiting for transfers between devices: 54.3 us -> 48.1 us
  Pallas kernels: 59.3 us -> 63.4 us
    pallas_call x0 -> x9, Pallas kernels: none -> 6.28 us  [small(): pl.pallas_call(kernel, out_shape=[jax.ShapeDtypeStruct(*out) for out in o...]
    ppermute x24 -> x26, waiting for transfers between devices: 19.2 us -> 15.2 us  [over_seq(): return lax.ppermute(array, 'seq', [(i, i ^ bit) for i in range(4)])]
    ppermute x24 -> x26, starting transfers between devices: 16.4 us -> 13.4 us  [over_seq(): return lax.ppermute(array, 'seq', [(i, i ^ bit) for i in range(4)])]
    ppermute x12, waiting for transfers between devices: 20.1 us -> 18.2 us  [over_both(): return lax.ppermute(array, ('tp', 'seq'), pairs)]
  transfers between devices with their start and end apart: 42 -> 44, of which waited for: 14 -> 14; matrix products, arithmetic and copies ran while one was open for 1% -> 1% of each run, Pallas kernels for 34% -> 38%
where the time goes in v8:
time: 164 us; the launch traced here: 163 us
  Pallas kernels  63.4 us (39%)
  waiting for transfers between devices  48.1 us (29%)
  starting transfers between devices  47.8 us (29%)
  local copies, waits for them, and re-layouts  1.73 us (1%)
    ppermute x12, starting transfers between devices, over_both(): return lax.ppermute(array, ('tp', 'seq'), pairs)  24.5 us
    pallas_call x12, Pallas kernels, sums(): pl.pallas_call(functools.partial(sums_kernel, got is not None, split), ou...  21.4 us
    ppermute x12, waiting for transfers between devices, over_both(): return lax.ppermute(array, ('tp', 'seq'), pairs)  18.2 us
    ppermute x26, waiting for transfers between devices, over_seq(): return lax.ppermute(array, 'seq', [(i, i ^ bit) for i in range(4)])  15.2 us
    ppermute x6, waiting for transfers between devices, over_tp(): return lax.ppermute(array, 'tp', [(i, i ^ bit) for i in range(4)])  14.8 us
    pallas_call x4, Pallas kernels, load(): pl.pallas_call(load_kernel, out_shape=jax.ShapeDtypeStruct((2, deep, widt...  14 us
    ppermute x26, starting transfers between devices, over_seq(): return lax.ppermute(array, 'seq', [(i, i ^ bit) for i in range(4)])  13.4 us
    pallas_call x6, Pallas kernels, products(): pl.pallas_call(functools.partial(products_kernel, total is not None), out...  11 us
  transfers between devices with their start and end apart: 44, of which 14 were waited for; matrix products, arithmetic and copies ran while one was open for 1% of the time, Pallas kernels for 38%

profile of v8, /device:TPU:1, one launch (start us, length us, event | category | flops | bytes accessed | tf_op | source)
XLA Modules:
  0.0 163.4 jit_solution(12671704856173614353)
XLA Ops:
  2.8 3.2 %collective-permute-start = (bf16[48,2048]{1,0:T(8,128)(2,1)S(1)}, bf16[48,2048]{1,0:T(8,128)(2,1)S(1)}, u32[]{:S(2)}, u32[]{:S(2)}) collective-permute-start(bf16[48,2048]{1,0:T(8,128)(2,1)S(1)} %get-tuple-element.109), channel_id=1, source_target_pairs={{0,8},{4,12},{8,0},{12,4},{1,9},{5,13},{9,1},{13,5},{2,10},{6,14},... | collective-permute-start | bytes 589832 | tf_op jit(solution)/shard_map/far0/ppermute | solution.py:75
  6.2 3.5 %load3.1.weights = bf16[2,2048,1024]{2,1,0:T(8,128)(2,1)S(1)} custom-call(s32[1]{0:T(128)} %bitcast.7.quarter, bf16[2048,4096]{1,0:T(8,128)(2,1)} %gate_weight.3, bf16[2048,4096]{1,0:T(8,128)(2,1)} %up_weight.7), custom_call_target="tpu_custom_call" | custom-call | flops 1073741824 | bytes 1 | tf_op jit(solution)/shard_map/load3/pallas_call | solution.py:121
  9.7 5.2 %collective-permute-done = bf16[48,2048]{1,0:T(8,128)(2,1)S(1)} collective-permute-done((bf16[48,2048]{1,0:T(8,128)(2,1)S(1)}, bf16[48,2048]{1,0:T(8,128)(2,1)S(1)}, u32[]{:S(2)}, u32[]{:S(2)}) %collective-permute-start) | collective-permute-done | bytes 196640 | tf_op jit(solution)/shard_map/far0/ppermute | solution.py:75
  15.9 3.5 %load1.1.weights = bf16[2,2048,1024]{2,1,0:T(8,128)(2,1)S(1)} custom-call(s32[1]{0:T(128)} %bitcast.5.quarter, bf16[2048,4096]{1,0:T(8,128)(2,1)} %gate_weight.3, bf16[2048,4096]{1,0:T(8,128)(2,1)} %up_weight.7), custom_call_target="tpu_custom_call" | custom-call | flops 1073741824 | bytes 1 | tf_op jit(solution)/shard_map/load1/pallas_call | solution.py:121
  20.2 2.2 %collective-permute-start.4 = (bf16[96,2048]{1,0:T(8,128)(2,1)S(1)}, bf16[96,2048]{1,0:T(8,128)(2,1)S(1)}, u32[]{:S(2)}, u32[]{:S(2)}) collective-permute-start(bf16[96,2048]{1,0:T(8,128)(2,1)S(1)} %pad_maximum_fusion.3), channel_id=1, source_target_pairs={{0,4},{1,0},{2,6},{3,2},{4,5},{5,1},{6,7},{7,3},{8,12},{9,8},{10,1... | collective-permute-start | bytes 1179656 | tf_op jit(solution)/shard_map/arr0/ppermute | solution.py:95
  22.4 4.6 %collective-permute-start.5 = (bf16[96,2048]{1,0:T(8,128)(2,1)S(1)}, bf16[96,2048]{1,0:T(8,128)(2,1)S(1)}, u32[]{:S(2)}, u32[]{:S(2)}) collective-permute-start(bf16[96,2048]{1,0:T(8,128)(2,1)S(1)} %pad_maximum_fusion.3), channel_id=1, source_target_pairs={{1,4},{3,6},{4,1},{6,3},{9,12},{11,14},{12,9},{14,11},{17,20},{19,... | collective-permute-start | bytes 1179656 | tf_op jit(solution)/shard_map/arr0/ppermute | solution.py:95
  27.0 3.5 %load2.1.weights = bf16[2,2048,1024]{2,1,0:T(8,128)(2,1)S(1)} custom-call(s32[1]{0:T(128)} %bitcast.6.quarter, bf16[2048,4096]{1,0:T(8,128)(2,1)} %gate_weight.3, bf16[2048,4096]{1,0:T(8,128)(2,1)} %up_weight.7), custom_call_target="tpu_custom_call" | custom-call | flops 1073741824 | bytes 1 | tf_op jit(solution)/shard_map/load2/pallas_call | solution.py:121
  30.5 3.5 %load0.1.weights = bf16[2,2048,1024]{2,1,0:T(8,128)(2,1)S(1)} custom-call(s32[1]{0:T(128)} %bitcast.4.quarter, bf16[2048,4096]{1,0:T(8,128)(2,1)} %gate_weight.3, bf16[2048,4096]{1,0:T(8,128)(2,1)} %up_weight.7), custom_call_target="tpu_custom_call" | custom-call | flops 1073741824 | bytes 1 | tf_op jit(solution)/shard_map/load0/pallas_call | solution.py:121
  34.4 2.5 %collective-permute-start.3 = (bf16[32,2048]{1,0:T(8,128)(2,1)S(1)}, bf16[32,2048]{1,0:T(8,128)(2,1)S(1)}, u32[]{:S(2)}, u32[]{:S(2)}) collective-permute-start(bf16[32,2048]{1,0:T(8,128)(2,1)S(1)} %get-tuple-element.123), channel_id=1, source_target_pairs={{0,8},{4,12},{8,0},{12,4},{1,9},{5,13},{9,1},{13,5},{2,10},{6,14},... | collective-permute-start | bytes 393224 | tf_op jit(solution)/shard_map/far2/ppermute | solution.py:75
  37.2 2.0 %a0.1 = bf16[2,192,1024]{2,1,0:T(8,128)(2,1)S(1)} custom-call(bf16[192,2048]{1,0:T(8,128)(2,1)S(1)} %pad_maximum_fusion.some, bf16[2,2048,1024]{2,1,0:T(8,128)(2,1)S(1)} %load3.1.weights), custom_call_target="tpu_custom_call" | custom-call | flops 17179869184 | bytes 1 | tf_op jit(solution)/shard_map/a0/pallas_call | solution.py:150
  43.8 2.5 %collective-permute-start.11 = (bf16[96,2048]{1,0:T(8,128)(2,1)S(1)}, bf16[96,2048]{1,0:T(8,128)(2,1)S(1)}, u32[]{:S(2)}, u32[]{:S(2)}) collective-permute-start(bf16[96,2048]{1,0:T(8,128)(2,1)S(1)} %pad_maximum_fusion.4), channel_id=1, source_target_pairs={{1,4},{3,6},{4,1},{6,3},{9,12},{11,14},{12,9},{14,11},{17,20},{19,... | collective-permute-start | bytes 1179656 | tf_op jit(solution)/shard_map/arr1/ppermute | solution.py:95
  50.2 2.1 %collective-permute-done.10 = bf16[96,2048]{1,0:T(8,128)(2,1)S(1)} collective-permute-done((bf16[96,2048]{1,0:T(8,128)(2,1)S(1)}, bf16[96,2048]{1,0:T(8,128)(2,1)S(1)}, u32[]{:S(2)}, u32[]{:S(2)}) %collective-permute-start.10) | collective-permute-done | bytes 393248 | tf_op jit(solution)/shard_map/arr1/ppermute | solution.py:95
  52.4 2.6 %collective-permute-done.11 = bf16[96,2048]{1,0:T(8,128)(2,1)S(1)} collective-permute-done((bf16[96,2048]{1,0:T(8,128)(2,1)S(1)}, bf16[96,2048]{1,0:T(8,128)(2,1)S(1)}, u32[]{:S(2)}, u32[]{:S(2)}) %collective-permute-start.11) | collective-permute-done | bytes 393248 | tf_op jit(solution)/shard_map/arr1/ppermute | solution.py:95
  59.9 5.9 %collective-permute-done.13.rest_1_ = bf16[192,1024]{1,0:T(8,128)(2,1)S(1)} collective-permute-done((bf16[192,1024]{1,0:T(8,128)(2,1)S(1)}, bf16[192,1024]{1,0:T(8,128)(2,1)S(1)}, u32[]{:S(2)}, u32[]{:S(2)}) %collective-permute-start.13) | collective-permute-done | bytes 393248 | tf_op jit(solution)/shard_map/b0/ppermute | solution.py:71
  69.2 3.2 %collective-permute-start.17 = (bf16[64,2048]{1,0:T(8,128)(2,1)S(1)}, bf16[64,2048]{1,0:T(8,128)(2,1)S(1)}, u32[]{:S(2)}, u32[]{:S(2)}) collective-permute-start(bf16[64,2048]{1,0:T(8,128)(2,1)S(1)} %pad_maximum_fusion.5), channel_id=1, source_target_pairs={{1,4},{3,6},{4,1},{6,3},{9,12},{11,14},{12,9},{14,11},{17,20},{19,... | collective-permute-start | bytes 786440 | tf_op jit(solution)/shard_map/arr2/ppermute | solution.py:95
  73.7 2.0 %d1.1.held = f32[2,192,1024]{2,1,0:T(8,128)S(1)} custom-call(bf16[192,2048]{1,0:T(8,128)(2,1)S(1)} %pad_maximum_fusion.1.some, bf16[2,2048,1024]{2,1,0:T(8,128)(2,1)S(1)} %load0.1.weights, bf16[2,192,1024]{2,1,0:T(8,128)(2,1)S(1)} %collective-permute-done.16.rest_0_), custom_call_target="tpu_custom_call" | custom-call | flops 17179869184 | bytes 1 | tf_op jit(solution)/shard_map/d1/pallas_call | solution.py:150
  80.4 4.0 %down0.1.weights = bf16[2,1024,2048]{2,1,0:T(8,128)(2,1)S(1)} custom-call(s32[2]{0:T(128)S(1)} %get-tuple-element.143.quarters, bf16[4096,2048]{1,0:T(8,128)(2,1)} %weight.1), custom_call_target="tpu_custom_call" | custom-call | flops 17179869184 | bytes 1 | tf_op jit(solution)/shard_map/down0/pallas_call | solution.py:181
  85.0 2.0 %own0.1.rest_0_ = f32[192,2048]{1,0:T(8,128)S(1)} custom-call(bf16[192,1024]{1,0:T(8,128)(2,1)S(1)} %hide0.1.one, bf16[192,1024]{1,0:T(8,128)(2,1)S(1)} %collective-permute-done.19.two, bf16[2,1024,2048]{2,1,0:T(8,128)(2,1)S(1)} %down0.1.weights), custom_call_target="tpu_custom_call" | custom-call | flops 17179869184 | bytes 1 | tf_op jit(solution)/shard_map/own0/pallas_call | solution.py:204
  87.1 6.2 %collective-permute-done.20.rest_1_ = bf16[192,1024]{1,0:T(8,128)(2,1)S(1)} collective-permute-done((bf16[192,1024]{1,0:T(8,128)(2,1)S(1)}, bf16[192,1024]{1,0:T(8,128)(2,1)S(1)}, u32[]{:S(2)}, u32[]{:S(2)}) %collective-permute-start.20) | collective-permute-done | bytes 393248 | tf_op jit(solution)/shard_map/b1/ppermute | solution.py:71
  99.5 4.0 %down2.1.weights = bf16[2,1024,2048]{2,1,0:T(8,128)(2,1)S(1)} custom-call(s32[2]{0:T(128)S(1)} %get-tuple-element.154.quarters, bf16[4096,2048]{1,0:T(8,128)(2,1)} %weight.1), custom_call_target="tpu_custom_call" | custom-call | flops 17179869184 | bytes 1 | tf_op jit(solution)/shard_map/down2/pallas_call | solution.py:181
  103.5 2.0 %rest0.1.partial_sum = f32[192,2048]{1,0:T(8,128)S(1)} custom-call(bf16[192,1024]{1,0:T(8,128)(2,1)S(1)} %collective-permute-done.25.one, bf16[192,1024]{1,0:T(8,128)(2,1)S(1)} %collective-permute-done.26.two, bf16[2,1024,2048]{2,1,0:T(8,128)(2,1)S(1)} %down2.1.weights, f32[192,2048]{1,0:T(8,128)S(1)} %own0.1.rest_0_), custom_call_target="tpu_custom_call" | custom-call | flops 17179869184 | bytes 1 | tf_op jit(solution)/shard_map/rest0/pallas_call | solution.py:204
  107.9 2.0 %own1.1.rest_0_ = f32[192,2048]{1,0:T(8,128)S(1)} custom-call(bf16[192,1024]{1,0:T(8,128)(2,1)S(1)} %hide1.1.one, bf16[192,1024]{1,0:T(8,128)(2,1)S(1)} %collective-permute-done.27.two, bf16[2,1024,2048]{2,1,0:T(8,128)(2,1)S(1)} %down0.1.weights), custom_call_target="tpu_custom_call" | custom-call | flops 17179869184 | bytes 1 | tf_op jit(solution)/shard_map/own1/pallas_call | solution.py:204
  109.9 2.9 %collective-permute-start.32 = (bf16[96,2048]{1,0:T(8,128)(2,1)S(1)}, bf16[96,2048]{1,0:T(8,128)(2,1)S(1)}, u32[]{:S(2)}, u32[]{:S(2)}) collective-permute-start(bf16[96,2048]{1,0:T(8,128)(2,1)S(1)} %get-tuple-element.166), channel_id=1, source_target_pairs={{1,4},{3,6},{4,1},{6,3},{9,12},{11,14},{12,9},{14,11},{17,20},{19,... | collective-permute-start | bytes 1179656 | tf_op jit(solution)/shard_map/out0/ppermute | solution.py:95
  112.8 2.0 %rest1.1.partial_sum = f32[192,2048]{1,0:T(8,128)S(1)} custom-call(bf16[192,1024]{1,0:T(8,128)(2,1)S(1)} %collective-permute-done.24.one, bf16[192,1024]{1,0:T(8,128)(2,1)S(1)} %collective-permute-done.28.two, bf16[2,1024,2048]{2,1,0:T(8,128)(2,1)S(1)} %down2.1.weights, f32[192,2048]{1,0:T(8,128)S(1)} %own1.1.rest_0_), custom_call_target="tpu_custom_call" | custom-call | flops 17179869184 | bytes 1 | tf_op jit(solution)/shard_map/rest1/pallas_call | solution.py:204
  115.7 2.6 %collective-permute-start.33 = (bf16[96,2048]{1,0:T(8,128)(2,1)S(1)}, bf16[96,2048]{1,0:T(8,128)(2,1)S(1)}, u32[]{:S(2)}, u32[]{:S(2)}) collective-permute-start(bf16[96,2048]{1,0:T(8,128)(2,1)S(1)} %get-tuple-element.169), channel_id=1, source_target_pairs={{1,4},{3,6},{4,1},{6,3},{9,12},{11,14},{12,9},{14,11},{17,20},{19,... | collective-permute-start | bytes 1179656 | tf_op jit(solution)/shard_map/out1/ppermute | solution.py:95
  121.7 6.0 %collective-permute-done.33.got_two = bf16[96,2048]{1,0:T(8,128)(2,1)S(1)} collective-permute-done((bf16[96,2048]{1,0:T(8,128)(2,1)S(1)}, bf16[96,2048]{1,0:T(8,128)(2,1)S(1)}, u32[]{:S(2)}, u32[]{:S(2)}) %collective-permute-start.33) | collective-permute-done | bytes 393248 | tf_op jit(solution)/shard_map/out1/ppermute | solution.py:95
  133.6 2.9 %collective-permute-start.38 = (bf16[64,2048]{1,0:T(8,128)(2,1)S(1)}, bf16[64,2048]{1,0:T(8,128)(2,1)S(1)}, u32[]{:S(2)}, u32[]{:S(2)}) collective-permute-start(bf16[64,2048]{1,0:T(8,128)(2,1)S(1)} %get-tuple-element.180), channel_id=1, source_target_pairs={{1,4},{3,6},{4,1},{6,3},{9,12},{11,14},{12,9},{14,11},{17,20},{19,... | collective-permute-start | bytes 786440 | tf_op jit(solution)/shard_map/out2/ppermute | solution.py:95
  137.2 2.8 %collective-permute-start.43 = (bf16[48,2048]{1,0:T(8,128)(2,1)S(1)}, bf16[48,2048]{1,0:T(8,128)(2,1)S(1)}, u32[]{:S(2)}, u32[]{:S(2)}) collective-permute-start(bf16[48,2048]{1,0:T(8,128)(2,1)S(1)} %get-tuple-element.178), channel_id=1, source_target_pairs={{0,8},{4,12},{8,0},{12,4},{1,9},{5,13},{9,1},{13,5},{2,10},{6,14},... | collective-permute-start | bytes 589832 | tf_op jit(solution)/shard_map/far_out0/ppermute | solution.py:75
  140.0 5.7 %collective-permute-done.38.got_two = bf16[64,2048]{1,0:T(8,128)(2,1)S(1)} collective-permute-done((bf16[64,2048]{1,0:T(8,128)(2,1)S(1)}, bf16[64,2048]{1,0:T(8,128)(2,1)S(1)}, u32[]{:S(2)}, u32[]{:S(2)}) %collective-permute-start.38) | collective-permute-done | bytes 262176 | tf_op jit(solution)/shard_map/out2/ppermute | solution.py:95
  148.4 2.2 %collective-permute-done.39.got = bf16[32,2048]{1,0:T(8,128)(2,1)S(1)} collective-permute-done((bf16[32,2048]{1,0:T(8,128)(2,1)S(1)}, bf16[32,2048]{1,0:T(8,128)(2,1)S(1)}, u32[]{:S(2)}, u32[]{:S(2)}) %collective-permute-start.39) | collective-permute-done | bytes 131104 | tf_op jit(solution)/shard_map/mix2/ppermute | solution.py:71
  152.7 7.2 %collective-permute-done.42.got = bf16[48,2048]{1,0:T(8,128)(2,1)S(1)} collective-permute-done((bf16[48,2048]{1,0:T(8,128)(2,1)S(1)}, bf16[48,2048]{1,0:T(8,128)(2,1)S(1)}, u32[]{:S(2)}, u32[]{:S(2)}) %collective-permute-start.42) | collective-permute-done | bytes 196640 | tf_op jit(solution)/shard_map/far_out1/ppermute | solution.py:75
  160.0 2.4 %collective-permute-done.41.got = bf16[32,2048]{1,0:T(8,128)(2,1)S(1)} collective-permute-done((bf16[32,2048]{1,0:T(8,128)(2,1)S(1)}, bf16[32,2048]{1,0:T(8,128)(2,1)S(1)}, u32[]{:S(2)}, u32[]{:S(2)}) %collective-permute-start.41) | collective-permute-done | bytes 131104 | tf_op jit(solution)/shard_map/far_out2/ppermute | solution.py:75
  (117 shorter events, 53.1 us)
Async XLA Ops:
  2.8 12.0 %collective-permute-start = (bf16[48,2048]{1,0:T(8,128)(2,1)S(1)}, bf16[48,2048]{1,0:T(8,128)(2,1)S(1)}, u32[]{:S(2)}, u32[]{:S(2)}) collective-permute-start(bf16[48,2048]{1,0:T(8,128)(2,1)S(1)} %get-tuple-element.109), channel_id=1, source_target_pairs={{0,8},{4,12},{8,0},{12,4},{1,9},{5,13},{9,1},{13,5},{2,10},{6,14},... | collective-permute-start | bytes 589832 | tf_op jit(solution)/shard_map/far0/ppermute | solution.py:75
  15.9 18.1 %collective-permute-start.1 = (bf16[48,2048]{1,0:T(8,128)(2,1)S(1)}, bf16[48,2048]{1,0:T(8,128)(2,1)S(1)}, u32[]{:S(2)}, u32[]{:S(2)}) collective-permute-start(bf16[48,2048]{1,0:T(8,128)(2,1)S(1)} %get-tuple-element.114), channel_id=1, source_target_pairs={{0,8},{4,12},{8,0},{12,4},{1,9},{5,13},{9,1},{13,5},{2,10},{6,14},... | collective-permute-start | bytes 589832 | tf_op jit(solution)/shard_map/far1/ppermute | solution.py:75
  20.2 16.7 %collective-permute-start.4 = (bf16[96,2048]{1,0:T(8,128)(2,1)S(1)}, bf16[96,2048]{1,0:T(8,128)(2,1)S(1)}, u32[]{:S(2)}, u32[]{:S(2)}) collective-permute-start(bf16[96,2048]{1,0:T(8,128)(2,1)S(1)} %pad_maximum_fusion.3), channel_id=1, source_target_pairs={{0,4},{1,0},{2,6},{3,2},{4,5},{5,1},{6,7},{7,3},{8,12},{9,8},{10,1... | collective-permute-start | bytes 1179656 | tf_op jit(solution)/shard_map/arr0/ppermute | solution.py:95
  22.4 14.4 %collective-permute-start.5 = (bf16[96,2048]{1,0:T(8,128)(2,1)S(1)}, bf16[96,2048]{1,0:T(8,128)(2,1)S(1)}, u32[]{:S(2)}, u32[]{:S(2)}) collective-permute-start(bf16[96,2048]{1,0:T(8,128)(2,1)S(1)} %pad_maximum_fusion.3), channel_id=1, source_target_pairs={{1,4},{3,6},{4,1},{6,3},{9,12},{11,14},{12,9},{14,11},{17,20},{19,... | collective-permute-start | bytes 1179656 | tf_op jit(solution)/shard_map/arr0/ppermute | solution.py:95
  34.1 9.6 %collective-permute-start.6 = (bf16[48,2048]{1,0:T(8,128)(2,1)S(1)}, bf16[48,2048]{1,0:T(8,128)(2,1)S(1)}, u32[]{:S(2)}, u32[]{:S(2)}) collective-permute-start(bf16[48,2048]{1,0:T(8,128)(2,1)S(1)} %broadcast_select_fusion.17), channel_id=1, source_target_pairs={{0,2},{1,3},{2,0},{3,1},{4,6},{5,7},{6,4},{7,5},{8,10},{9,11},{10,... | collective-permute-start | bytes 589832 | tf_op jit(solution)/shard_map/sel1/ppermute | solution.py:71
  34.4 14.2 %collective-permute-start.3 = (bf16[32,2048]{1,0:T(8,128)(2,1)S(1)}, bf16[32,2048]{1,0:T(8,128)(2,1)S(1)}, u32[]{:S(2)}, u32[]{:S(2)}) collective-permute-start(bf16[32,2048]{1,0:T(8,128)(2,1)S(1)} %get-tuple-element.123), channel_id=1, source_target_pairs={{0,8},{4,12},{8,0},{12,4},{1,9},{5,13},{9,1},{13,5},{2,10},{6,14},... | collective-permute-start | bytes 393224 | tf_op jit(solution)/shard_map/far2/ppermute | solution.py:75
  43.8 11.1 %collective-permute-start.11 = (bf16[96,2048]{1,0:T(8,128)(2,1)S(1)}, bf16[96,2048]{1,0:T(8,128)(2,1)S(1)}, u32[]{:S(2)}, u32[]{:S(2)}) collective-permute-start(bf16[96,2048]{1,0:T(8,128)(2,1)S(1)} %pad_maximum_fusion.4), channel_id=1, source_target_pairs={{1,4},{3,6},{4,1},{6,3},{9,12},{11,14},{12,9},{14,11},{17,20},{19,... | collective-permute-start | bytes 1179656 | tf_op jit(solution)/shard_map/arr1/ppermute | solution.py:95
  46.3 19.5 %collective-permute-start.12 = (bf16[192,1024]{1,0:T(8,128)(2,1)S(1)}, bf16[192,1024]{1,0:T(8,128)(2,1)S(1)}, u32[]{:S(2)}, u32[]{:S(2)}) collective-permute-start(bf16[192,1024]{1,0:T(8,128)(2,1)S(1)} %get-tuple-element.128), channel_id=1, source_target_pairs={{0,2},{1,3},{2,0},{3,1},{4,6},{5,7},{6,4},{7,5},{8,10},{9,11},{10,... | collective-permute-start | bytes 1179656 | tf_op jit(solution)/shard_map/b0/ppermute | solution.py:71
  48.6 17.2 %collective-permute-start.13 = (bf16[192,1024]{1,0:T(8,128)(2,1)S(1)}, bf16[192,1024]{1,0:T(8,128)(2,1)S(1)}, u32[]{:S(2)}, u32[]{:S(2)}) collective-permute-start(bf16[192,1024]{1,0:T(8,128)(2,1)S(1)} %get-tuple-element.136), channel_id=1, source_target_pairs={{0,2},{1,3},{2,0},{3,1},{4,6},{5,7},{6,4},{7,5},{8,10},{9,11},{10,... | collective-permute-start | bytes 1179656 | tf_op jit(solution)/shard_map/b0/ppermute | solution.py:71
  49.9 18.4 %collective-permute-start.9 = (bf16[32,2048]{1,0:T(8,128)(2,1)S(1)}, bf16[32,2048]{1,0:T(8,128)(2,1)S(1)}, u32[]{:S(2)}, u32[]{:S(2)}) collective-permute-start(bf16[32,2048]{1,0:T(8,128)(2,1)S(1)} %broadcast_select_fusion.20), channel_id=1, source_target_pairs={{0,2},{1,3},{2,0},{3,1},{4,6},{5,7},{6,4},{7,5},{8,10},{9,11},{10,... | collective-permute-start | bytes 393224 | tf_op jit(solution)/shard_map/sel2/ppermute | solution.py:71
  57.2 9.3 %collective-permute-start.14 = (bf16[2,192,1024]{2,1,0:T(8,128)(2,1)S(1)}, bf16[2,192,1024]{2,1,0:T(8,128)(2,1)S(1)}, u32[]{:S(2)}, u32[]{:S(2)}) collective-permute-start(bf16[2,192,1024]{2,1,0:T(8,128)(2,1)S(1)} %a1.1), channel_id=1, source_target_pairs={{0,1},{1,0},{2,3},{3,2},{4,5},{5,4},{6,7},{7,6},{8,9},{9,8},{10,11... | collective-permute-start | bytes 2359304 | tf_op jit(solution)/shard_map/a1/ppermute | solution.py:71
  59.3 13.1 %collective-permute-start.16 = (bf16[2,192,1024]{2,1,0:T(8,128)(2,1)S(1)}, bf16[2,192,1024]{2,1,0:T(8,128)(2,1)S(1)}, u32[]{:S(2)}, u32[]{:S(2)}) collective-permute-start(bf16[2,192,1024]{2,1,0:T(8,128)(2,1)S(1)} %c1.1), channel_id=1, source_target_pairs={{0,1},{1,0},{2,3},{3,2},{4,5},{5,4},{6,7},{7,6},{8,9},{9,8},{10,11... | collective-permute-start | bytes 2359304 | tf_op jit(solution)/shard_map/c1/ppermute | solution.py:71
  66.1 18.3 %collective-permute-start.19 = (bf16[192,1024]{1,0:T(8,128)(2,1)S(1)}, bf16[192,1024]{1,0:T(8,128)(2,1)S(1)}, u32[]{:S(2)}, u32[]{:S(2)}) collective-permute-start(bf16[192,1024]{1,0:T(8,128)(2,1)S(1)} %hide0.1.one), channel_id=1, source_target_pairs={{0,1},{1,0},{2,3},{3,2},{4,5},{5,4},{6,7},{7,6},{8,9},{9,8},{10,11... | collective-permute-start | bytes 1179656 | tf_op jit(solution)/shard_map/hide0/ppermute | solution.py:71
  66.2 20.8 %collective-permute-start.25 = (bf16[192,1024]{1,0:T(8,128)(2,1)S(1)}, bf16[192,1024]{1,0:T(8,128)(2,1)S(1)}, u32[]{:S(2)}, u32[]{:S(2)}) collective-permute-start(bf16[192,1024]{1,0:T(8,128)(2,1)S(1)} %hide0.1.one), channel_id=1, source_target_pairs={{0,2},{1,3},{2,0},{3,1},{4,6},{5,7},{6,4},{7,5},{8,10},{9,11},{10,... | collective-permute-start | bytes 1179656 | tf_op jit(solution)/shard_map/hide0/ppermute | solution.py:71
  72.4 20.9 %collective-permute-start.18 = (bf16[192,1024]{1,0:T(8,128)(2,1)S(1)}, bf16[192,1024]{1,0:T(8,128)(2,1)S(1)}, u32[]{:S(2)}, u32[]{:S(2)}) collective-permute-start(bf16[192,1024]{1,0:T(8,128)(2,1)S(1)} %get-tuple-element.139), channel_id=1, source_target_pairs={{0,2},{1,3},{2,0},{3,1},{4,6},{5,7},{6,4},{7,5},{8,10},{9,11},{10,... | collective-permute-start | bytes 1179656 | tf_op jit(solution)/shard_map/b1/ppermute | solution.py:71
  75.7 17.6 %collective-permute-start.20 = (bf16[192,1024]{1,0:T(8,128)(2,1)S(1)}, bf16[192,1024]{1,0:T(8,128)(2,1)S(1)}, u32[]{:S(2)}, u32[]{:S(2)}) collective-permute-start(bf16[192,1024]{1,0:T(8,128)(2,1)S(1)} %get-tuple-element.149), channel_id=1, source_target_pairs={{0,2},{1,3},{2,0},{3,1},{4,6},{5,7},{6,4},{7,5},{8,10},{9,11},{10,... | collective-permute-start | bytes 1179656 | tf_op jit(solution)/shard_map/b1/ppermute | solution.py:71
  78.8 16.5 %collective-permute-start.21 = (bf16[2,128,1024]{2,1,0:T(8,128)(2,1)S(1)}, bf16[2,128,1024]{2,1,0:T(8,128)(2,1)S(1)}, u32[]{:S(2)}, u32[]{:S(2)}) collective-permute-start(bf16[2,128,1024]{2,1,0:T(8,128)(2,1)S(1)} %a2.1), channel_id=1, source_target_pairs={{0,1},{1,0},{2,3},{3,2},{4,5},{5,4},{6,7},{7,6},{8,9},{9,8},{10,11... | collective-permute-start | bytes 1572872 | tf_op jit(solution)/shard_map/a2/ppermute | solution.py:71
  84.4 13.6 %collective-permute-start.22 = (bf16[2,128,1024]{2,1,0:T(8,128)(2,1)S(1)}, bf16[2,128,1024]{2,1,0:T(8,128)(2,1)S(1)}, u32[]{:S(2)}, u32[]{:S(2)}) collective-permute-start(bf16[2,128,1024]{2,1,0:T(8,128)(2,1)S(1)} %c2.1), channel_id=1, source_target_pairs={{0,1},{1,0},{2,3},{3,2},{4,5},{5,4},{6,7},{7,6},{8,9},{9,8},{10,11... | collective-permute-start | bytes 1572872 | tf_op jit(solution)/shard_map/c2/ppermute | solution.py:71
  87.0 16.5 %collective-permute-start.26 = (bf16[192,1024]{1,0:T(8,128)(2,1)S(1)}, bf16[192,1024]{1,0:T(8,128)(2,1)S(1)}, u32[]{:S(2)}, u32[]{:S(2)}) collective-permute-start(bf16[192,1024]{1,0:T(8,128)(2,1)S(1)} %collective-permute-done.25.one), channel_id=1, source_target_pairs={{0,1},{1,0},{2,3},{3,2},{4,5},{5,4},{6,7},{7,6},{8,9},{9,8},{10,11... | collective-permute-start | bytes 1179656 | tf_op jit(solution)/shard_map/forward0/ppermute | solution.py:71
  93.7 14.2 %collective-permute-start.27 = (bf16[192,1024]{1,0:T(8,128)(2,1)S(1)}, bf16[192,1024]{1,0:T(8,128)(2,1)S(1)}, u32[]{:S(2)}, u32[]{:S(2)}) collective-permute-start(bf16[192,1024]{1,0:T(8,128)(2,1)S(1)} %hide1.1.one), channel_id=1, source_target_pairs={{0,1},{1,0},{2,3},{3,2},{4,5},{5,4},{6,7},{7,6},{8,9},{9,8},{10,11... | collective-permute-start | bytes 1179656 | tf_op jit(solution)/shard_map/hide1/ppermute | solution.py:71
  95.0 12.8 %collective-permute-start.24 = (bf16[192,1024]{1,0:T(8,128)(2,1)S(1)}, bf16[192,1024]{1,0:T(8,128)(2,1)S(1)}, u32[]{:S(2)}, u32[]{:S(2)}) collective-permute-start(bf16[192,1024]{1,0:T(8,128)(2,1)S(1)} %hide1.1.one), channel_id=1, source_target_pairs={{0,2},{1,3},{2,0},{3,1},{4,6},{5,7},{6,4},{7,5},{8,10},{9,11},{10,... | collective-permute-start | bytes 1179656 | tf_op jit(solution)/shard_map/hide1/ppermute | solution.py:71
  96.8 21.6 %collective-permute-start.23 = (bf16[2,128,1024]{2,1,0:T(8,128)(2,1)S(1)}, bf16[2,128,1024]{2,1,0:T(8,128)(2,1)S(1)}, u32[]{:S(2)}, u32[]{:S(2)}) collective-permute-start(bf16[2,128,1024]{2,1,0:T(8,128)(2,1)S(1)} %b2.1), channel_id=1, source_target_pairs={{0,2},{1,3},{2,0},{3,1},{4,6},{5,7},{6,4},{7,5},{8,10},{9,11},{10,... | collective-permute-start | bytes 1572872 | tf_op jit(solution)/shard_map/b2/ppermute | solution.py:71
  106.3 12.3 %collective-permute-start.31 = (bf16[96,2048]{1,0:T(8,128)(2,1)S(1)}, bf16[96,2048]{1,0:T(8,128)(2,1)S(1)}, u32[]{:S(2)}, u32[]{:S(2)}) collective-permute-start(bf16[96,2048]{1,0:T(8,128)(2,1)S(1)} %get-tuple-element.157), channel_id=1, source_target_pairs={{0,1},{1,5},{2,3},{3,7},{4,0},{5,4},{6,2},{7,6},{8,9},{9,13},{10,1... | collective-permute-start | bytes 1179656 | tf_op jit(solution)/shard_map/out0/ppermute | solution.py:95
  115.7 12.0 %collective-permute-start.33 = (bf16[96,2048]{1,0:T(8,128)(2,1)S(1)}, bf16[96,2048]{1,0:T(8,128)(2,1)S(1)}, u32[]{:S(2)}, u32[]{:S(2)}) collective-permute-start(bf16[96,2048]{1,0:T(8,128)(2,1)S(1)} %get-tuple-element.169), channel_id=1, source_target_pairs={{1,4},{3,6},{4,1},{6,3},{9,12},{11,14},{12,9},{14,11},{17,20},{19,... | collective-permute-start | bytes 1179656 | tf_op jit(solution)/shard_map/out1/ppermute | solution.py:95
  118.5 10.3 %collective-permute-start.34 = (bf16[128,1024]{1,0:T(8,128)(2,1)S(1)}, bf16[128,1024]{1,0:T(8,128)(2,1)S(1)}, u32[]{:S(2)}, u32[]{:S(2)}) collective-permute-start(bf16[128,1024]{1,0:T(8,128)(2,1)S(1)} %hide2.1.one), channel_id=1, source_target_pairs={{0,1},{1,0},{2,3},{3,2},{4,5},{5,4},{6,7},{7,6},{8,9},{9,8},{10,11... | collective-permute-start | bytes 786440 | tf_op jit(solution)/shard_map/hide2/ppermute | solution.py:71
  118.6 10.2 %collective-permute-start.29 = (bf16[128,1024]{1,0:T(8,128)(2,1)S(1)}, bf16[128,1024]{1,0:T(8,128)(2,1)S(1)}, u32[]{:S(2)}, u32[]{:S(2)}) collective-permute-start(bf16[128,1024]{1,0:T(8,128)(2,1)S(1)} %hide2.1.one), channel_id=1, source_target_pairs={{0,2},{1,3},{2,0},{3,1},{4,6},{5,7},{6,4},{7,5},{8,10},{9,11},{10,... | collective-permute-start | bytes 786440 | tf_op jit(solution)/shard_map/hide2/ppermute | solution.py:71
  119.8 13.8 %collective-permute-start.37 = (bf16[48,2048]{1,0:T(8,128)(2,1)S(1)}, bf16[48,2048]{1,0:T(8,128)(2,1)S(1)}, u32[]{:S(2)}, u32[]{:S(2)}) collective-permute-start(bf16[48,2048]{1,0:T(8,128)(2,1)S(1)} %get-tuple-element.167), channel_id=1, source_target_pairs={{0,2},{1,3},{2,0},{3,1},{4,6},{5,7},{6,4},{7,5},{8,10},{9,11},{10,... | collective-permute-start | bytes 589832 | tf_op jit(solution)/shard_map/mix0/ppermute | solution.py:71
  128.4 19.2 %collective-permute-start.40 = (bf16[48,2048]{1,0:T(8,128)(2,1)S(1)}, bf16[48,2048]{1,0:T(8,128)(2,1)S(1)}, u32[]{:S(2)}, u32[]{:S(2)}) collective-permute-start(bf16[48,2048]{1,0:T(8,128)(2,1)S(1)} %get-tuple-element.170), channel_id=1, source_target_pairs={{0,2},{1,3},{2,0},{3,1},{4,6},{5,7},{6,4},{7,5},{8,10},{9,11},{10,... | collective-permute-start | bytes 589832 | tf_op jit(solution)/shard_map/mix1/ppermute | solution.py:71
  133.6 12.1 %collective-permute-start.38 = (bf16[64,2048]{1,0:T(8,128)(2,1)S(1)}, bf16[64,2048]{1,0:T(8,128)(2,1)S(1)}, u32[]{:S(2)}, u32[]{:S(2)}) collective-permute-start(bf16[64,2048]{1,0:T(8,128)(2,1)S(1)} %get-tuple-element.180), channel_id=1, source_target_pairs={{1,4},{3,6},{4,1},{6,3},{9,12},{11,14},{12,9},{14,11},{17,20},{19,... | collective-permute-start | bytes 786440 | tf_op jit(solution)/shard_map/out2/ppermute | solution.py:95
  137.2 15.3 %collective-permute-start.43 = (bf16[48,2048]{1,0:T(8,128)(2,1)S(1)}, bf16[48,2048]{1,0:T(8,128)(2,1)S(1)}, u32[]{:S(2)}, u32[]{:S(2)}) collective-permute-start(bf16[48,2048]{1,0:T(8,128)(2,1)S(1)} %get-tuple-element.178), channel_id=1, source_target_pairs={{0,8},{4,12},{8,0},{12,4},{1,9},{5,13},{9,1},{13,5},{2,10},{6,14},... | collective-permute-start | bytes 589832 | tf_op jit(solution)/shard_map/far_out0/ppermute | solution.py:75
  148.3 11.5 %collective-permute-start.42 = (bf16[48,2048]{1,0:T(8,128)(2,1)S(1)}, bf16[48,2048]{1,0:T(8,128)(2,1)S(1)}, u32[]{:S(2)}, u32[]{:S(2)}) collective-permute-start(bf16[48,2048]{1,0:T(8,128)(2,1)S(1)} %get-tuple-element.185), channel_id=1, source_target_pairs={{0,8},{4,12},{8,0},{12,4},{1,9},{5,13},{9,1},{13,5},{2,10},{6,14},... | collective-permute-start | bytes 589832 | tf_op jit(solution)/shard_map/far_out1/ppermute | solution.py:75
  151.2 11.2 %collective-permute-start.41 = (bf16[32,2048]{1,0:T(8,128)(2,1)S(1)}, bf16[32,2048]{1,0:T(8,128)(2,1)S(1)}, u32[]{:S(2)}, u32[]{:S(2)}) collective-permute-start(bf16[32,2048]{1,0:T(8,128)(2,1)S(1)} %get-tuple-element.188), channel_id=1, source_target_pairs={{0,8},{4,12},{8,0},{12,4},{1,9},{5,13},{9,1},{13,5},{2,10},{6,14},... | collective-permute-start | bytes 393224 | tf_op jit(solution)/shard_map/far_out2/ppermute | solution.py:75
  (14 other events, 72.3 us)

commit v9 on v8

--- a/solution.py
+++ b/solution.py
@@ -12,8 +12,8 @@
     "far0", "load3", "sel0", "far1", "load1", "arr0", "load2", "load0", "sel1", "far2", "take0", "a0", "c0",
     "b0", "arr1", "d0", "sel2", "take1", "a1", "c1", "hide0", "b1", "arr2", "d1", "take2", "a2", "c2",
     "down0", "own0", "forward0", "hide1", "b2", "d2", "down2", "rest0", "out0", "forward1", "own1", "rest1",
-    "out1", "hide2", "mix0", "mix1", "forward2", "own2", "rest2", "out2", "far_out0", "mix2", "far_out1",
-    "far_out2", "end0", "end1", "end2",
+    "out1", "hide2", "mix0", "mix1", "far_out0", "forward2", "own2", "rest2", "out2", "far_out1", "mix2",
+    "end0", "far_out2", "end1", "end2",
 )
 TILE = 256
 SPLIT = (0, 1)

time: 164 us -> 165 us (level)
    ppermute x6, waiting for transfers between devices: 14.8 us -> 8.81 us  [over_tp(): return lax.ppermute(array, 'tp', [(i, i ^ bit) for i in range(4)])]
    ppermute x12, waiting for transfers between devices: 18.2 us -> 22.4 us  [over_both(): return lax.ppermute(array, ('tp', 'seq'), pairs)]
    ppermute x26, waiting for transfers between devices: 15.2 us -> 18.1 us  [over_seq(): return lax.ppermute(array, 'seq', [(i, i ^ bit) for i in range(4)])]
where the time goes in v9:
time: 165 us; the launch traced here: 164 us
  Pallas kernels  63.4 us (38%)
  waiting for transfers between devices  49.3 us (30%)
  starting transfers between devices  47.2 us (29%)
  local copies, waits for them, and re-layouts  1.73 us (1%)
    ppermute x12, starting transfers between devices, over_both(): return lax.ppermute(array, ('tp', 'seq'), pairs)  24.4 us
    ppermute x12, waiting for transfers between devices, over_both(): return lax.ppermute(array, ('tp', 'seq'), pairs)  22.4 us
    pallas_call x12, Pallas kernels, sums(): pl.pallas_call(functools.partial(sums_kernel, got is not None, split), ou...  21.4 us
    ppermute x26, waiting for transfers between devices, over_seq(): return lax.ppermute(array, 'seq', [(i, i ^ bit) for i in range(4)])  18.1 us
    pallas_call x4, Pallas kernels, load(): pl.pallas_call(load_kernel, out_shape=jax.ShapeDtypeStruct((2, deep, widt...  14 us
    ppermute x26, starting transfers between devices, over_seq(): return lax.ppermute(array, 'seq', [(i, i ^ bit) for i in range(4)])  13.7 us
    pallas_call x6, Pallas kernels, products(): pl.pallas_call(functools.partial(products_kernel, total is not None), out...  11 us
    ppermute x6, starting transfers between devices, over_tp(): return lax.ppermute(array, 'tp', [(i, i ^ bit) for i in range(4)])  9.15 us
  transfers between devices with their start and end apart: 44, of which 14 were waited for; matrix products, arithmetic and copies ran while one was open for 1% of the time, Pallas kernels for 38%

profile of v9, /device:TPU:1, one launch (start us, length us, event | category | flops | bytes accessed | tf_op | source)
XLA Modules:
  0.0 164.0 jit_solution(15729736360753208219)
XLA Ops:
  2.8 3.2 %collective-permute-start = (bf16[48,2048]{1,0:T(8,128)(2,1)S(1)}, bf16[48,2048]{1,0:T(8,128)(2,1)S(1)}, u32[]{:S(2)}, u32[]{:S(2)}) collective-permute-start(bf16[48,2048]{1,0:T(8,128)(2,1)S(1)} %get-tuple-element.109), channel_id=1, source_target_pairs={{0,8},{4,12},{8,0},{12,4},{1,9},{5,13},{9,1},{13,5},{2,10},{6,14},... | collective-permute-start | bytes 589832 | tf_op jit(solution)/shard_map/far0/ppermute | solution.py:75
  6.2 3.5 %load3.1.weights = bf16[2,2048,1024]{2,1,0:T(8,128)(2,1)S(1)} custom-call(s32[1]{0:T(128)} %bitcast.7.quarter, bf16[2048,4096]{1,0:T(8,128)(2,1)} %gate_weight.3, bf16[2048,4096]{1,0:T(8,128)(2,1)} %up_weight.7), custom_call_target="tpu_custom_call" | custom-call | flops 1073741824 | bytes 1 | tf_op jit(solution)/shard_map/load3/pallas_call | solution.py:121
  9.7 5.2 %collective-permute-done = bf16[48,2048]{1,0:T(8,128)(2,1)S(1)} collective-permute-done((bf16[48,2048]{1,0:T(8,128)(2,1)S(1)}, bf16[48,2048]{1,0:T(8,128)(2,1)S(1)}, u32[]{:S(2)}, u32[]{:S(2)}) %collective-permute-start) | collective-permute-done | bytes 196640 | tf_op jit(solution)/shard_map/far0/ppermute | solution.py:75
  15.9 3.5 %load1.1.weights = bf16[2,2048,1024]{2,1,0:T(8,128)(2,1)S(1)} custom-call(s32[1]{0:T(128)} %bitcast.5.quarter, bf16[2048,4096]{1,0:T(8,128)(2,1)} %gate_weight.3, bf16[2048,4096]{1,0:T(8,128)(2,1)} %up_weight.7), custom_call_target="tpu_custom_call" | custom-call | flops 1073741824 | bytes 1 | tf_op jit(solution)/shard_map/load1/pallas_call | solution.py:121
  20.2 2.2 %collective-permute-start.4 = (bf16[96,2048]{1,0:T(8,128)(2,1)S(1)}, bf16[96,2048]{1,0:T(8,128)(2,1)S(1)}, u32[]{:S(2)}, u32[]{:S(2)}) collective-permute-start(bf16[96,2048]{1,0:T(8,128)(2,1)S(1)} %pad_maximum_fusion.3), channel_id=1, source_target_pairs={{0,4},{1,0},{2,6},{3,2},{4,5},{5,1},{6,7},{7,3},{8,12},{9,8},{10,1... | collective-permute-start | bytes 1179656 | tf_op jit(solution)/shard_map/arr0/ppermute | solution.py:95
  22.4 4.6 %collective-permute-start.5 = (bf16[96,2048]{1,0:T(8,128)(2,1)S(1)}, bf16[96,2048]{1,0:T(8,128)(2,1)S(1)}, u32[]{:S(2)}, u32[]{:S(2)}) collective-permute-start(bf16[96,2048]{1,0:T(8,128)(2,1)S(1)} %pad_maximum_fusion.3), channel_id=1, source_target_pairs={{1,4},{3,6},{4,1},{6,3},{9,12},{11,14},{12,9},{14,11},{17,20},{19,... | collective-permute-start | bytes 1179656 | tf_op jit(solution)/shard_map/arr0/ppermute | solution.py:95
  27.0 3.5 %load2.1.weights = bf16[2,2048,1024]{2,1,0:T(8,128)(2,1)S(1)} custom-call(s32[1]{0:T(128)} %bitcast.6.quarter, bf16[2048,4096]{1,0:T(8,128)(2,1)} %gate_weight.3, bf16[2048,4096]{1,0:T(8,128)(2,1)} %up_weight.7), custom_call_target="tpu_custom_call" | custom-call | flops 1073741824 | bytes 1 | tf_op jit(solution)/shard_map/load2/pallas_call | solution.py:121
  30.5 3.5 %load0.1.weights = bf16[2,2048,1024]{2,1,0:T(8,128)(2,1)S(1)} custom-call(s32[1]{0:T(128)} %bitcast.4.quarter, bf16[2048,4096]{1,0:T(8,128)(2,1)} %gate_weight.3, bf16[2048,4096]{1,0:T(8,128)(2,1)} %up_weight.7), custom_call_target="tpu_custom_call" | custom-call | flops 1073741824 | bytes 1 | tf_op jit(solution)/shard_map/load0/pallas_call | solution.py:121
  34.4 2.5 %collective-permute-start.3 = (bf16[32,2048]{1,0:T(8,128)(2,1)S(1)}, bf16[32,2048]{1,0:T(8,128)(2,1)S(1)}, u32[]{:S(2)}, u32[]{:S(2)}) collective-permute-start(bf16[32,2048]{1,0:T(8,128)(2,1)S(1)} %get-tuple-element.123), channel_id=1, source_target_pairs={{0,8},{4,12},{8,0},{12,4},{1,9},{5,13},{9,1},{13,5},{2,10},{6,14},... | collective-permute-start | bytes 393224 | tf_op jit(solution)/shard_map/far2/ppermute | solution.py:75
  37.2 2.0 %a0.1 = bf16[2,192,1024]{2,1,0:T(8,128)(2,1)S(1)} custom-call(bf16[192,2048]{1,0:T(8,128)(2,1)S(1)} %pad_maximum_fusion.some, bf16[2,2048,1024]{2,1,0:T(8,128)(2,1)S(1)} %load3.1.weights), custom_call_target="tpu_custom_call" | custom-call | flops 17179869184 | bytes 1 | tf_op jit(solution)/shard_map/a0/pallas_call | solution.py:150
  43.8 2.5 %collective-permute-start.11 = (bf16[96,2048]{1,0:T(8,128)(2,1)S(1)}, bf16[96,2048]{1,0:T(8,128)(2,1)S(1)}, u32[]{:S(2)}, u32[]{:S(2)}) collective-permute-start(bf16[96,2048]{1,0:T(8,128)(2,1)S(1)} %pad_maximum_fusion.4), channel_id=1, source_target_pairs={{1,4},{3,6},{4,1},{6,3},{9,12},{11,14},{12,9},{14,11},{17,20},{19,... | collective-permute-start | bytes 1179656 | tf_op jit(solution)/shard_map/arr1/ppermute | solution.py:95
  46.6 2.0 %d0.1.held = f32[2,192,1024]{2,1,0:T(8,128)S(1)} custom-call(bf16[192,2048]{1,0:T(8,128)(2,1)S(1)} %pad_maximum_fusion.some, bf16[2,2048,1024]{2,1,0:T(8,128)(2,1)S(1)} %load0.1.weights, bf16[2,192,1024]{2,1,0:T(8,128)(2,1)S(1)} %collective-permute-done.8.rest_0_), custom_call_target="tpu_custom_call" | custom-call | flops 17179869184 | bytes 1 | tf_op jit(solution)/shard_map/d0/pallas_call | solution.py:150
  50.2 2.1 %collective-permute-done.10 = bf16[96,2048]{1,0:T(8,128)(2,1)S(1)} collective-permute-done((bf16[96,2048]{1,0:T(8,128)(2,1)S(1)}, bf16[96,2048]{1,0:T(8,128)(2,1)S(1)}, u32[]{:S(2)}, u32[]{:S(2)}) %collective-permute-start.10) | collective-permute-done | bytes 393248 | tf_op jit(solution)/shard_map/arr1/ppermute | solution.py:95
  52.4 2.6 %collective-permute-done.11 = bf16[96,2048]{1,0:T(8,128)(2,1)S(1)} collective-permute-done((bf16[96,2048]{1,0:T(8,128)(2,1)S(1)}, bf16[96,2048]{1,0:T(8,128)(2,1)S(1)}, u32[]{:S(2)}, u32[]{:S(2)}) %collective-permute-start.11) | collective-permute-done | bytes 393248 | tf_op jit(solution)/shard_map/arr1/ppermute | solution.py:95
  59.9 5.9 %collective-permute-done.13.rest_1_ = bf16[192,1024]{1,0:T(8,128)(2,1)S(1)} collective-permute-done((bf16[192,1024]{1,0:T(8,128)(2,1)S(1)}, bf16[192,1024]{1,0:T(8,128)(2,1)S(1)}, u32[]{:S(2)}, u32[]{:S(2)}) %collective-permute-start.13) | collective-permute-done | bytes 393248 | tf_op jit(solution)/shard_map/b0/ppermute | solution.py:71
  69.2 3.2 %collective-permute-start.17 = (bf16[64,2048]{1,0:T(8,128)(2,1)S(1)}, bf16[64,2048]{1,0:T(8,128)(2,1)S(1)}, u32[]{:S(2)}, u32[]{:S(2)}) collective-permute-start(bf16[64,2048]{1,0:T(8,128)(2,1)S(1)} %pad_maximum_fusion.5), channel_id=1, source_target_pairs={{1,4},{3,6},{4,1},{6,3},{9,12},{11,14},{12,9},{14,11},{17,20},{19,... | collective-permute-start | bytes 786440 | tf_op jit(solution)/shard_map/arr2/ppermute | solution.py:95
  80.4 4.0 %down0.1.weights = bf16[2,1024,2048]{2,1,0:T(8,128)(2,1)S(1)} custom-call(s32[2]{0:T(128)S(1)} %get-tuple-element.143.quarters, bf16[4096,2048]{1,0:T(8,128)(2,1)} %weight.1), custom_call_target="tpu_custom_call" | custom-call | flops 17179869184 | bytes 1 | tf_op jit(solution)/shard_map/down0/pallas_call | solution.py:181
  85.0 2.0 %own0.1.rest_0_ = f32[192,2048]{1,0:T(8,128)S(1)} custom-call(bf16[192,1024]{1,0:T(8,128)(2,1)S(1)} %hide0.1.one, bf16[192,1024]{1,0:T(8,128)(2,1)S(1)} %collective-permute-done.19.two, bf16[2,1024,2048]{2,1,0:T(8,128)(2,1)S(1)} %down0.1.weights), custom_call_target="tpu_custom_call" | custom-call | flops 17179869184 | bytes 1 | tf_op jit(solution)/shard_map/own0/pallas_call | solution.py:204
  87.1 6.2 %collective-permute-done.20.rest_1_ = bf16[192,1024]{1,0:T(8,128)(2,1)S(1)} collective-permute-done((bf16[192,1024]{1,0:T(8,128)(2,1)S(1)}, bf16[192,1024]{1,0:T(8,128)(2,1)S(1)}, u32[]{:S(2)}, u32[]{:S(2)}) %collective-permute-start.20) | collective-permute-done | bytes 393248 | tf_op jit(solution)/shard_map/b1/ppermute | solution.py:71
  99.5 4.0 %down2.1.weights = bf16[2,1024,2048]{2,1,0:T(8,128)(2,1)S(1)} custom-call(s32[2]{0:T(128)S(1)} %get-tuple-element.154.quarters, bf16[4096,2048]{1,0:T(8,128)(2,1)} %weight.1), custom_call_target="tpu_custom_call" | custom-call | flops 17179869184 | bytes 1 | tf_op jit(solution)/shard_map/down2/pallas_call | solution.py:181
  103.5 2.0 %rest0.1.partial_sum = f32[192,2048]{1,0:T(8,128)S(1)} custom-call(bf16[192,1024]{1,0:T(8,128)(2,1)S(1)} %collective-permute-done.25.one, bf16[192,1024]{1,0:T(8,128)(2,1)S(1)} %collective-permute-done.26.two, bf16[2,1024,2048]{2,1,0:T(8,128)(2,1)S(1)} %down2.1.weights, f32[192,2048]{1,0:T(8,128)S(1)} %own0.1.rest_0_), custom_call_target="tpu_custom_call" | custom-call | flops 17179869184 | bytes 1 | tf_op jit(solution)/shard_map/rest0/pallas_call | solution.py:204
  107.9 2.0 %own1.1.rest_0_ = f32[192,2048]{1,0:T(8,128)S(1)} custom-call(bf16[192,1024]{1,0:T(8,128)(2,1)S(1)} %hide1.1.one, bf16[192,1024]{1,0:T(8,128)(2,1)S(1)} %collective-permute-done.27.two, bf16[2,1024,2048]{2,1,0:T(8,128)(2,1)S(1)} %down0.1.weights), custom_call_target="tpu_custom_call" | custom-call | flops 17179869184 | bytes 1 | tf_op jit(solution)/shard_map/own1/pallas_call | solution.py:204
  109.9 2.9 %collective-permute-start.31 = (bf16[96,2048]{1,0:T(8,128)(2,1)S(1)}, bf16[96,2048]{1,0:T(8,128)(2,1)S(1)}, u32[]{:S(2)}, u32[]{:S(2)}) collective-permute-start(bf16[96,2048]{1,0:T(8,128)(2,1)S(1)} %get-tuple-element.165), channel_id=1, source_target_pairs={{1,4},{3,6},{4,1},{6,3},{9,12},{11,14},{12,9},{14,11},{17,20},{19,... | collective-permute-start | bytes 1179656 | tf_op jit(solution)/shard_map/out0/ppermute | solution.py:95
  112.8 2.0 %rest1.1.partial_sum = f32[192,2048]{1,0:T(8,128)S(1)} custom-call(bf16[192,1024]{1,0:T(8,128)(2,1)S(1)} %collective-permute-done.24.one, bf16[192,1024]{1,0:T(8,128)(2,1)S(1)} %collective-permute-done.28.two, bf16[2,1024,2048]{2,1,0:T(8,128)(2,1)S(1)} %down2.1.weights, f32[192,2048]{1,0:T(8,128)S(1)} %own1.1.rest_0_), custom_call_target="tpu_custom_call" | custom-call | flops 17179869184 | bytes 1 | tf_op jit(solution)/shard_map/rest1/pallas_call | solution.py:204
  115.7 2.6 %collective-permute-start.34 = (bf16[96,2048]{1,0:T(8,128)(2,1)S(1)}, bf16[96,2048]{1,0:T(8,128)(2,1)S(1)}, u32[]{:S(2)}, u32[]{:S(2)}) collective-permute-start(bf16[96,2048]{1,0:T(8,128)(2,1)S(1)} %get-tuple-element.170), channel_id=1, source_target_pairs={{1,4},{3,6},{4,1},{6,3},{9,12},{11,14},{12,9},{14,11},{17,20},{19,... | collective-permute-start | bytes 1179656 | tf_op jit(solution)/shard_map/out1/ppermute | solution.py:95
  121.7 6.0 %collective-permute-done.34.got_two = bf16[96,2048]{1,0:T(8,128)(2,1)S(1)} collective-permute-done((bf16[96,2048]{1,0:T(8,128)(2,1)S(1)}, bf16[96,2048]{1,0:T(8,128)(2,1)S(1)}, u32[]{:S(2)}, u32[]{:S(2)}) %collective-permute-start.34) | collective-permute-done | bytes 393248 | tf_op jit(solution)/shard_map/out1/ppermute | solution.py:95
  131.0 2.1 %collective-permute-start.41 = (bf16[48,2048]{1,0:T(8,128)(2,1)S(1)}, bf16[48,2048]{1,0:T(8,128)(2,1)S(1)}, u32[]{:S(2)}, u32[]{:S(2)}) collective-permute-start(bf16[48,2048]{1,0:T(8,128)(2,1)S(1)} %get-tuple-element.173), channel_id=1, source_target_pairs={{0,8},{4,12},{8,0},{12,4},{1,9},{5,13},{9,1},{13,5},{2,10},{6,14},... | collective-permute-start | bytes 589832 | tf_op jit(solution)/shard_map/far_out0/ppermute | solution.py:75
  138.2 2.0 %collective-permute-start.37 = (bf16[64,2048]{1,0:T(8,128)(2,1)S(1)}, bf16[64,2048]{1,0:T(8,128)(2,1)S(1)}, u32[]{:S(2)}, u32[]{:S(2)}) collective-permute-start(bf16[64,2048]{1,0:T(8,128)(2,1)S(1)} %get-tuple-element.178), channel_id=1, source_target_pairs={{0,1},{1,5},{2,3},{3,7},{4,0},{5,4},{6,2},{7,6},{8,9},{9,13},{10,1... | collective-permute-start | bytes 786440 | tf_op jit(solution)/shard_map/out2/ppermute | solution.py:95
  143.0 2.4 %collective-permute-done.37.got_one = bf16[64,2048]{1,0:T(8,128)(2,1)S(1)} collective-permute-done((bf16[64,2048]{1,0:T(8,128)(2,1)S(1)}, bf16[64,2048]{1,0:T(8,128)(2,1)S(1)}, u32[]{:S(2)}, u32[]{:S(2)}) %collective-permute-start.37) | collective-permute-done | bytes 262176 | tf_op jit(solution)/shard_map/out2/ppermute | solution.py:95
  145.5 7.5 %collective-permute-done.39.got_two = bf16[64,2048]{1,0:T(8,128)(2,1)S(1)} collective-permute-done((bf16[64,2048]{1,0:T(8,128)(2,1)S(1)}, bf16[64,2048]{1,0:T(8,128)(2,1)S(1)}, u32[]{:S(2)}, u32[]{:S(2)}) %collective-permute-start.39) | collective-permute-done | bytes 262176 | tf_op jit(solution)/shard_map/out2/ppermute | solution.py:95
  153.9 3.6 %collective-permute-done.40.got = bf16[32,2048]{1,0:T(8,128)(2,1)S(1)} collective-permute-done((bf16[32,2048]{1,0:T(8,128)(2,1)S(1)}, bf16[32,2048]{1,0:T(8,128)(2,1)S(1)}, u32[]{:S(2)}, u32[]{:S(2)}) %collective-permute-start.40) | collective-permute-done | bytes 131104 | tf_op jit(solution)/shard_map/mix2/ppermute | solution.py:71
  159.5 3.6 %collective-permute-done.42.got = bf16[32,2048]{1,0:T(8,128)(2,1)S(1)} collective-permute-done((bf16[32,2048]{1,0:T(8,128)(2,1)S(1)}, bf16[32,2048]{1,0:T(8,128)(2,1)S(1)}, u32[]{:S(2)}, u32[]{:S(2)}) %collective-permute-start.42) | collective-permute-done | bytes 131104 | tf_op jit(solution)/shard_map/far_out2/ppermute | solution.py:75
  (117 shorter events, 55.6 us)
Async XLA Ops:
  2.8 12.0 %collective-permute-start = (bf16[48,2048]{1,0:T(8,128)(2,1)S(1)}, bf16[48,2048]{1,0:T(8,128)(2,1)S(1)}, u32[]{:S(2)}, u32[]{:S(2)}) collective-permute-start(bf16[48,2048]{1,0:T(8,128)(2,1)S(1)} %get-tuple-element.109), channel_id=1, source_target_pairs={{0,8},{4,12},{8,0},{12,4},{1,9},{5,13},{9,1},{13,5},{2,10},{6,14},... | collective-permute-start | bytes 589832 | tf_op jit(solution)/shard_map/far0/ppermute | solution.py:75
  15.9 18.1 %collective-permute-start.1 = (bf16[48,2048]{1,0:T(8,128)(2,1)S(1)}, bf16[48,2048]{1,0:T(8,128)(2,1)S(1)}, u32[]{:S(2)}, u32[]{:S(2)}) collective-permute-start(bf16[48,2048]{1,0:T(8,128)(2,1)S(1)} %get-tuple-element.114), channel_id=1, source_target_pairs={{0,8},{4,12},{8,0},{12,4},{1,9},{5,13},{9,1},{13,5},{2,10},{6,14},... | collective-permute-start | bytes 589832 | tf_op jit(solution)/shard_map/far1/ppermute | solution.py:75
  20.2 16.7 %collective-permute-start.4 = (bf16[96,2048]{1,0:T(8,128)(2,1)S(1)}, bf16[96,2048]{1,0:T(8,128)(2,1)S(1)}, u32[]{:S(2)}, u32[]{:S(2)}) collective-permute-start(bf16[96,2048]{1,0:T(8,128)(2,1)S(1)} %pad_maximum_fusion.3), channel_id=1, source_target_pairs={{0,4},{1,0},{2,6},{3,2},{4,5},{5,1},{6,7},{7,3},{8,12},{9,8},{10,1... | collective-permute-start | bytes 1179656 | tf_op jit(solution)/shard_map/arr0/ppermute | solution.py:95
  22.4 14.4 %collective-permute-start.5 = (bf16[96,2048]{1,0:T(8,128)(2,1)S(1)}, bf16[96,2048]{1,0:T(8,128)(2,1)S(1)}, u32[]{:S(2)}, u32[]{:S(2)}) collective-permute-start(bf16[96,2048]{1,0:T(8,128)(2,1)S(1)} %pad_maximum_fusion.3), channel_id=1, source_target_pairs={{1,4},{3,6},{4,1},{6,3},{9,12},{11,14},{12,9},{14,11},{17,20},{19,... | collective-permute-start | bytes 1179656 | tf_op jit(solution)/shard_map/arr0/ppermute | solution.py:95
  34.1 9.6 %collective-permute-start.6 = (bf16[48,2048]{1,0:T(8,128)(2,1)S(1)}, bf16[48,2048]{1,0:T(8,128)(2,1)S(1)}, u32[]{:S(2)}, u32[]{:S(2)}) collective-permute-start(bf16[48,2048]{1,0:T(8,128)(2,1)S(1)} %broadcast_select_fusion.17), channel_id=1, source_target_pairs={{0,2},{1,3},{2,0},{3,1},{4,6},{5,7},{6,4},{7,5},{8,10},{9,11},{10,... | collective-permute-start | bytes 589832 | tf_op jit(solution)/shard_map/sel1/ppermute | solution.py:71
  34.4 14.2 %collective-permute-start.3 = (bf16[32,2048]{1,0:T(8,128)(2,1)S(1)}, bf16[32,2048]{1,0:T(8,128)(2,1)S(1)}, u32[]{:S(2)}, u32[]{:S(2)}) collective-permute-start(bf16[32,2048]{1,0:T(8,128)(2,1)S(1)} %get-tuple-element.123), channel_id=1, source_target_pairs={{0,8},{4,12},{8,0},{12,4},{1,9},{5,13},{9,1},{13,5},{2,10},{6,14},... | collective-permute-start | bytes 393224 | tf_op jit(solution)/shard_map/far2/ppermute | solution.py:75
  43.8 11.1 %collective-permute-start.11 = (bf16[96,2048]{1,0:T(8,128)(2,1)S(1)}, bf16[96,2048]{1,0:T(8,128)(2,1)S(1)}, u32[]{:S(2)}, u32[]{:S(2)}) collective-permute-start(bf16[96,2048]{1,0:T(8,128)(2,1)S(1)} %pad_maximum_fusion.4), channel_id=1, source_target_pairs={{1,4},{3,6},{4,1},{6,3},{9,12},{11,14},{12,9},{14,11},{17,20},{19,... | collective-permute-start | bytes 1179656 | tf_op jit(solution)/shard_map/arr1/ppermute | solution.py:95
  46.3 19.5 %collective-permute-start.12 = (bf16[192,1024]{1,0:T(8,128)(2,1)S(1)}, bf16[192,1024]{1,0:T(8,128)(2,1)S(1)}, u32[]{:S(2)}, u32[]{:S(2)}) collective-permute-start(bf16[192,1024]{1,0:T(8,128)(2,1)S(1)} %get-tuple-element.128), channel_id=1, source_target_pairs={{0,2},{1,3},{2,0},{3,1},{4,6},{5,7},{6,4},{7,5},{8,10},{9,11},{10,... | collective-permute-start | bytes 1179656 | tf_op jit(solution)/shard_map/b0/ppermute | solution.py:71
  48.6 17.2 %collective-permute-start.13 = (bf16[192,1024]{1,0:T(8,128)(2,1)S(1)}, bf16[192,1024]{1,0:T(8,128)(2,1)S(1)}, u32[]{:S(2)}, u32[]{:S(2)}) collective-permute-start(bf16[192,1024]{1,0:T(8,128)(2,1)S(1)} %get-tuple-element.136), channel_id=1, source_target_pairs={{0,2},{1,3},{2,0},{3,1},{4,6},{5,7},{6,4},{7,5},{8,10},{9,11},{10,... | collective-permute-start | bytes 1179656 | tf_op jit(solution)/shard_map/b0/ppermute | solution.py:71
  49.9 18.4 %collective-permute-start.9 = (bf16[32,2048]{1,0:T(8,128)(2,1)S(1)}, bf16[32,2048]{1,0:T(8,128)(2,1)S(1)}, u32[]{:S(2)}, u32[]{:S(2)}) collective-permute-start(bf16[32,2048]{1,0:T(8,128)(2,1)S(1)} %broadcast_select_fusion.20), channel_id=1, source_target_pairs={{0,2},{1,3},{2,0},{3,1},{4,6},{5,7},{6,4},{7,5},{8,10},{9,11},{10,... | collective-permute-start | bytes 393224 | tf_op jit(solution)/shard_map/sel2/ppermute | solution.py:71
  57.2 9.3 %collective-permute-start.14 = (bf16[2,192,1024]{2,1,0:T(8,128)(2,1)S(1)}, bf16[2,192,1024]{2,1,0:T(8,128)(2,1)S(1)}, u32[]{:S(2)}, u32[]{:S(2)}) collective-permute-start(bf16[2,192,1024]{2,1,0:T(8,128)(2,1)S(1)} %a1.1), channel_id=1, source_target_pairs={{0,1},{1,0},{2,3},{3,2},{4,5},{5,4},{6,7},{7,6},{8,9},{9,8},{10,11... | collective-permute-start | bytes 2359304 | tf_op jit(solution)/shard_map/a1/ppermute | solution.py:71
  59.3 13.1 %collective-permute-start.16 = (bf16[2,192,1024]{2,1,0:T(8,128)(2,1)S(1)}, bf16[2,192,1024]{2,1,0:T(8,128)(2,1)S(1)}, u32[]{:S(2)}, u32[]{:S(2)}) collective-permute-start(bf16[2,192,1024]{2,1,0:T(8,128)(2,1)S(1)} %c1.1), channel_id=1, source_target_pairs={{0,1},{1,0},{2,3},{3,2},{4,5},{5,4},{6,7},{7,6},{8,9},{9,8},{10,11... | collective-permute-start | bytes 2359304 | tf_op jit(solution)/shard_map/c1/ppermute | solution.py:71
  66.1 18.3 %collective-permute-start.19 = (bf16[192,1024]{1,0:T(8,128)(2,1)S(1)}, bf16[192,1024]{1,0:T(8,128)(2,1)S(1)}, u32[]{:S(2)}, u32[]{:S(2)}) collective-permute-start(bf16[192,1024]{1,0:T(8,128)(2,1)S(1)} %hide0.1.one), channel_id=1, source_target_pairs={{0,1},{1,0},{2,3},{3,2},{4,5},{5,4},{6,7},{7,6},{8,9},{9,8},{10,11... | collective-permute-start | bytes 1179656 | tf_op jit(solution)/shard_map/hide0/ppermute | solution.py:71
  66.2 20.8 %collective-permute-start.25 = (bf16[192,1024]{1,0:T(8,128)(2,1)S(1)}, bf16[192,1024]{1,0:T(8,128)(2,1)S(1)}, u32[]{:S(2)}, u32[]{:S(2)}) collective-permute-start(bf16[192,1024]{1,0:T(8,128)(2,1)S(1)} %hide0.1.one), channel_id=1, source_target_pairs={{0,2},{1,3},{2,0},{3,1},{4,6},{5,7},{6,4},{7,5},{8,10},{9,11},{10,... | collective-permute-start | bytes 1179656 | tf_op jit(solution)/shard_map/hide0/ppermute | solution.py:71
  72.4 20.9 %collective-permute-start.18 = (bf16[192,1024]{1,0:T(8,128)(2,1)S(1)}, bf16[192,1024]{1,0:T(8,128)(2,1)S(1)}, u32[]{:S(2)}, u32[]{:S(2)}) collective-permute-start(bf16[192,1024]{1,0:T(8,128)(2,1)S(1)} %get-tuple-element.139), channel_id=1, source_target_pairs={{0,2},{1,3},{2,0},{3,1},{4,6},{5,7},{6,4},{7,5},{8,10},{9,11},{10,... | collective-permute-start | bytes 1179656 | tf_op jit(solution)/shard_map/b1/ppermute | solution.py:71
  75.7 17.6 %collective-permute-start.20 = (bf16[192,1024]{1,0:T(8,128)(2,1)S(1)}, bf16[192,1024]{1,0:T(8,128)(2,1)S(1)}, u32[]{:S(2)}, u32[]{:S(2)}) collective-permute-start(bf16[192,1024]{1,0:T(8,128)(2,1)S(1)} %get-tuple-element.149), channel_id=1, source_target_pairs={{0,2},{1,3},{2,0},{3,1},{4,6},{5,7},{6,4},{7,5},{8,10},{9,11},{10,... | collective-permute-start | bytes 1179656 | tf_op jit(solution)/shard_map/b1/ppermute | solution.py:71
  78.8 16.5 %collective-permute-start.21 = (bf16[2,128,1024]{2,1,0:T(8,128)(2,1)S(1)}, bf16[2,128,1024]{2,1,0:T(8,128)(2,1)S(1)}, u32[]{:S(2)}, u32[]{:S(2)}) collective-permute-start(bf16[2,128,1024]{2,1,0:T(8,128)(2,1)S(1)} %a2.1), channel_id=1, source_target_pairs={{0,1},{1,0},{2,3},{3,2},{4,5},{5,4},{6,7},{7,6},{8,9},{9,8},{10,11... | collective-permute-start | bytes 1572872 | tf_op jit(solution)/shard_map/a2/ppermute | solution.py:71
  84.4 13.6 %collective-permute-start.22 = (bf16[2,128,1024]{2,1,0:T(8,128)(2,1)S(1)}, bf16[2,128,1024]{2,1,0:T(8,128)(2,1)S(1)}, u32[]{:S(2)}, u32[]{:S(2)}) collective-permute-start(bf16[2,128,1024]{2,1,0:T(8,128)(2,1)S(1)} %c2.1), channel_id=1, source_target_pairs={{0,1},{1,0},{2,3},{3,2},{4,5},{5,4},{6,7},{7,6},{8,9},{9,8},{10,11... | collective-permute-start | bytes 1572872 | tf_op jit(solution)/shard_map/c2/ppermute | solution.py:71
  87.0 16.5 %collective-permute-start.26 = (bf16[192,1024]{1,0:T(8,128)(2,1)S(1)}, bf16[192,1024]{1,0:T(8,128)(2,1)S(1)}, u32[]{:S(2)}, u32[]{:S(2)}) collective-permute-start(bf16[192,1024]{1,0:T(8,128)(2,1)S(1)} %collective-permute-done.25.one), channel_id=1, source_target_pairs={{0,1},{1,0},{2,3},{3,2},{4,5},{5,4},{6,7},{7,6},{8,9},{9,8},{10,11... | collective-permute-start | bytes 1179656 | tf_op jit(solution)/shard_map/forward0/ppermute | solution.py:71
  93.7 14.2 %collective-permute-start.27 = (bf16[192,1024]{1,0:T(8,128)(2,1)S(1)}, bf16[192,1024]{1,0:T(8,128)(2,1)S(1)}, u32[]{:S(2)}, u32[]{:S(2)}) collective-permute-start(bf16[192,1024]{1,0:T(8,128)(2,1)S(1)} %hide1.1.one), channel_id=1, source_target_pairs={{0,1},{1,0},{2,3},{3,2},{4,5},{5,4},{6,7},{7,6},{8,9},{9,8},{10,11... | collective-permute-start | bytes 1179656 | tf_op jit(solution)/shard_map/hide1/ppermute | solution.py:71
  95.0 12.8 %collective-permute-start.24 = (bf16[192,1024]{1,0:T(8,128)(2,1)S(1)}, bf16[192,1024]{1,0:T(8,128)(2,1)S(1)}, u32[]{:S(2)}, u32[]{:S(2)}) collective-permute-start(bf16[192,1024]{1,0:T(8,128)(2,1)S(1)} %hide1.1.one), channel_id=1, source_target_pairs={{0,2},{1,3},{2,0},{3,1},{4,6},{5,7},{6,4},{7,5},{8,10},{9,11},{10,... | collective-permute-start | bytes 1179656 | tf_op jit(solution)/shard_map/hide1/ppermute | solution.py:71
  96.8 21.6 %collective-permute-start.23 = (bf16[2,128,1024]{2,1,0:T(8,128)(2,1)S(1)}, bf16[2,128,1024]{2,1,0:T(8,128)(2,1)S(1)}, u32[]{:S(2)}, u32[]{:S(2)}) collective-permute-start(bf16[2,128,1024]{2,1,0:T(8,128)(2,1)S(1)} %b2.1), channel_id=1, source_target_pairs={{0,2},{1,3},{2,0},{3,1},{4,6},{5,7},{6,4},{7,5},{8,10},{9,11},{10,... | collective-permute-start | bytes 1572872 | tf_op jit(solution)/shard_map/b2/ppermute | solution.py:71
  106.3 12.3 %collective-permute-start.30 = (bf16[96,2048]{1,0:T(8,128)(2,1)S(1)}, bf16[96,2048]{1,0:T(8,128)(2,1)S(1)}, u32[]{:S(2)}, u32[]{:S(2)}) collective-permute-start(bf16[96,2048]{1,0:T(8,128)(2,1)S(1)} %get-tuple-element.157), channel_id=1, source_target_pairs={{0,1},{1,5},{2,3},{3,7},{4,0},{5,4},{6,2},{7,6},{8,9},{9,13},{10,1... | collective-permute-start | bytes 1179656 | tf_op jit(solution)/shard_map/out0/ppermute | solution.py:95
  109.9 9.1 %collective-permute-start.31 = (bf16[96,2048]{1,0:T(8,128)(2,1)S(1)}, bf16[96,2048]{1,0:T(8,128)(2,1)S(1)}, u32[]{:S(2)}, u32[]{:S(2)}) collective-permute-start(bf16[96,2048]{1,0:T(8,128)(2,1)S(1)} %get-tuple-element.165), channel_id=1, source_target_pairs={{1,4},{3,6},{4,1},{6,3},{9,12},{11,14},{12,9},{14,11},{17,20},{19,... | collective-permute-start | bytes 1179656 | tf_op jit(solution)/shard_map/out0/ppermute | solution.py:95
  115.7 12.0 %collective-permute-start.34 = (bf16[96,2048]{1,0:T(8,128)(2,1)S(1)}, bf16[96,2048]{1,0:T(8,128)(2,1)S(1)}, u32[]{:S(2)}, u32[]{:S(2)}) collective-permute-start(bf16[96,2048]{1,0:T(8,128)(2,1)S(1)} %get-tuple-element.170), channel_id=1, source_target_pairs={{1,4},{3,6},{4,1},{6,3},{9,12},{11,14},{12,9},{14,11},{17,20},{19,... | collective-permute-start | bytes 1179656 | tf_op jit(solution)/shard_map/out1/ppermute | solution.py:95
  118.5 16.0 %collective-permute-start.35 = (bf16[128,1024]{1,0:T(8,128)(2,1)S(1)}, bf16[128,1024]{1,0:T(8,128)(2,1)S(1)}, u32[]{:S(2)}, u32[]{:S(2)}) collective-permute-start(bf16[128,1024]{1,0:T(8,128)(2,1)S(1)} %hide2.1.one), channel_id=1, source_target_pairs={{0,1},{1,0},{2,3},{3,2},{4,5},{5,4},{6,7},{7,6},{8,9},{9,8},{10,11... | collective-permute-start | bytes 786440 | tf_op jit(solution)/shard_map/hide2/ppermute | solution.py:71
  118.6 14.5 %collective-permute-start.29 = (bf16[128,1024]{1,0:T(8,128)(2,1)S(1)}, bf16[128,1024]{1,0:T(8,128)(2,1)S(1)}, u32[]{:S(2)}, u32[]{:S(2)}) collective-permute-start(bf16[128,1024]{1,0:T(8,128)(2,1)S(1)} %hide2.1.one), channel_id=1, source_target_pairs={{0,2},{1,3},{2,0},{3,1},{4,6},{5,7},{6,4},{7,5},{8,10},{9,11},{10,... | collective-permute-start | bytes 786440 | tf_op jit(solution)/shard_map/hide2/ppermute | solution.py:71
  119.8 10.6 %collective-permute-start.32 = (bf16[48,2048]{1,0:T(8,128)(2,1)S(1)}, bf16[48,2048]{1,0:T(8,128)(2,1)S(1)}, u32[]{:S(2)}, u32[]{:S(2)}) collective-permute-start(bf16[48,2048]{1,0:T(8,128)(2,1)S(1)} %get-tuple-element.167), channel_id=1, source_target_pairs={{0,2},{1,3},{2,0},{3,1},{4,6},{5,7},{6,4},{7,5},{8,10},{9,11},{10,... | collective-permute-start | bytes 589832 | tf_op jit(solution)/shard_map/mix0/ppermute | solution.py:71
  128.4 11.8 %collective-permute-start.38 = (bf16[48,2048]{1,0:T(8,128)(2,1)S(1)}, bf16[48,2048]{1,0:T(8,128)(2,1)S(1)}, u32[]{:S(2)}, u32[]{:S(2)}) collective-permute-start(bf16[48,2048]{1,0:T(8,128)(2,1)S(1)} %get-tuple-element.171), channel_id=1, source_target_pairs={{0,2},{1,3},{2,0},{3,1},{4,6},{5,7},{6,4},{7,5},{8,10},{9,11},{10,... | collective-permute-start | bytes 589832 | tf_op jit(solution)/shard_map/mix1/ppermute | solution.py:71
  131.0 22.7 %collective-permute-start.41 = (bf16[48,2048]{1,0:T(8,128)(2,1)S(1)}, bf16[48,2048]{1,0:T(8,128)(2,1)S(1)}, u32[]{:S(2)}, u32[]{:S(2)}) collective-permute-start(bf16[48,2048]{1,0:T(8,128)(2,1)S(1)} %get-tuple-element.173), channel_id=1, source_target_pairs={{0,8},{4,12},{8,0},{12,4},{1,9},{5,13},{9,1},{13,5},{2,10},{6,14},... | collective-permute-start | bytes 589832 | tf_op jit(solution)/shard_map/far_out0/ppermute | solution.py:75
  140.2 12.8 %collective-permute-start.39 = (bf16[64,2048]{1,0:T(8,128)(2,1)S(1)}, bf16[64,2048]{1,0:T(8,128)(2,1)S(1)}, u32[]{:S(2)}, u32[]{:S(2)}) collective-permute-start(bf16[64,2048]{1,0:T(8,128)(2,1)S(1)} %get-tuple-element.183), channel_id=1, source_target_pairs={{1,4},{3,6},{4,1},{6,3},{9,12},{11,14},{12,9},{14,11},{17,20},{19,... | collective-permute-start | bytes 786440 | tf_op jit(solution)/shard_map/out2/ppermute | solution.py:95
  142.8 16.5 %collective-permute-start.43 = (bf16[48,2048]{1,0:T(8,128)(2,1)S(1)}, bf16[48,2048]{1,0:T(8,128)(2,1)S(1)}, u32[]{:S(2)}, u32[]{:S(2)}) collective-permute-start(bf16[48,2048]{1,0:T(8,128)(2,1)S(1)} %get-tuple-element.181), channel_id=1, source_target_pairs={{0,8},{4,12},{8,0},{12,4},{1,9},{5,13},{9,1},{13,5},{2,10},{6,14},... | collective-permute-start | bytes 589832 | tf_op jit(solution)/shard_map/far_out1/ppermute | solution.py:75
  (14 other events, 68.9 us)

commit v10 on v9

--- a/solution.py
+++ b/solution.py
@@ -11,8 +11,8 @@
 ORDER = (
     "far0", "load3", "sel0", "far1", "load1", "arr0", "load2", "load0", "sel1", "far2", "take0", "a0", "c0",
     "b0", "arr1", "d0", "sel2", "take1", "a1", "c1", "hide0", "b1", "arr2", "d1", "take2", "a2", "c2",
-    "down0", "own0", "forward0", "hide1", "b2", "d2", "down2", "rest0", "out0", "forward1", "own1", "rest1",
-    "out1", "hide2", "mix0", "mix1", "far_out0", "forward2", "own2", "rest2", "out2", "far_out1", "mix2",
+    "down0", "own0", "forward0", "down2", "rest0", "out0", "hide1", "b2", "d2", "forward1", "own1", "mix0",
+    "rest1", "out1", "hide2", "far_out0", "mix1", "forward2", "own2", "rest2", "out2", "far_out1", "mix2",
     "end0", "far_out2", "end1", "end2",
 )
 TILE = 256

time: 165 us -> 173 us (1.048)
  waiting for transfers between devices: 49.3 us -> 53.7 us
  starting transfers between devices: 47.2 us -> 51.5 us
    ppermute x26, starting transfers between devices: 13.7 us -> 17.7 us  [over_seq(): return lax.ppermute(array, 'seq', [(i, i ^ bit) for i in range(4)])]
    ppermute x12, waiting for transfers between devices: 22.4 us -> 26.2 us  [over_both(): return lax.ppermute(array, ('tp', 'seq'), pairs)]
    ppermute x6, waiting for transfers between devices: 8.81 us -> 11.1 us  [over_tp(): return lax.ppermute(array, 'tp', [(i, i ^ bit) for i in range(4)])]
    ppermute x12, starting transfers between devices: 24.4 us -> 26.4 us  [over_both(): return lax.ppermute(array, ('tp', 'seq'), pairs)]
  transfers between devices with their start and end apart: 44 -> 44, of which waited for: 14 -> 13; matrix products, arithmetic and copies ran while one was open for 1% -> 1% of each run, Pallas kernels for 38% -> 36%
where the time goes in v10:
time: 173 us
  Pallas kernels  63.5 us (37%)
  waiting for transfers between devices  53.7 us (31%)
  starting transfers between devices  51.5 us (30%)
  local copies, waits for them, and re-layouts  1.74 us (1%)
    ppermute x12, starting transfers between devices, over_both(): return lax.ppermute(array, ('tp', 'seq'), pairs)  26.4 us
    ppermute x12, waiting for transfers between devices, over_both(): return lax.ppermute(array, ('tp', 'seq'), pairs)  26.2 us
    pallas_call x12, Pallas kernels, sums(): pl.pallas_call(functools.partial(sums_kernel, got is not None, split), ou...  21.4 us
    ppermute x26, starting transfers between devices, over_seq(): return lax.ppermute(array, 'seq', [(i, i ^ bit) for i in range(4)])  17.7 us
    ppermute x26, waiting for transfers between devices, over_seq(): return lax.ppermute(array, 'seq', [(i, i ^ bit) for i in range(4)])  16.4 us
    pallas_call x4, Pallas kernels, load(): pl.pallas_call(load_kernel, out_shape=jax.ShapeDtypeStruct((2, deep, widt...  14 us
    ppermute x6, waiting for transfers between devices, over_tp(): return lax.ppermute(array, 'tp', [(i, i ^ bit) for i in range(4)])  11.1 us
    pallas_call x6, Pallas kernels, products(): pl.pallas_call(functools.partial(products_kernel, total is not None), out...  11.1 us
  transfers between devices with their start and end apart: 44, of which 13 were waited for; matrix products, arithmetic and copies ran while one was open for 1% of the time, Pallas kernels for 36%

profile of v10, /device:TPU:1, one launch (start us, length us, event | category | flops | bytes accessed | tf_op | source)
XLA Modules:
  0.0 172.9 jit_solution(11427068663295466813)
XLA Ops:
  2.8 3.2 %collective-permute-start = (bf16[48,2048]{1,0:T(8,128)(2,1)S(1)}, bf16[48,2048]{1,0:T(8,128)(2,1)S(1)}, u32[]{:S(2)}, u32[]{:S(2)}) collective-permute-start(bf16[48,2048]{1,0:T(8,128)(2,1)S(1)} %get-tuple-element.109), channel_id=1, source_target_pairs={{0,8},{4,12},{8,0},{12,4},{1,9},{5,13},{9,1},{13,5},{2,10},{6,14},... | collective-permute-start | bytes 589832 | tf_op jit(solution)/shard_map/far0/ppermute | solution.py:75
  6.2 3.5 %load3.1.weights = bf16[2,2048,1024]{2,1,0:T(8,128)(2,1)S(1)} custom-call(s32[1]{0:T(128)} %bitcast.7.quarter, bf16[2048,4096]{1,0:T(8,128)(2,1)} %gate_weight.3, bf16[2048,4096]{1,0:T(8,128)(2,1)} %up_weight.7), custom_call_target="tpu_custom_call" | custom-call | flops 1073741824 | bytes 1 | tf_op jit(solution)/shard_map/load3/pallas_call | solution.py:121
  9.7 5.2 %collective-permute-done = bf16[48,2048]{1,0:T(8,128)(2,1)S(1)} collective-permute-done((bf16[48,2048]{1,0:T(8,128)(2,1)S(1)}, bf16[48,2048]{1,0:T(8,128)(2,1)S(1)}, u32[]{:S(2)}, u32[]{:S(2)}) %collective-permute-start) | collective-permute-done | bytes 196640 | tf_op jit(solution)/shard_map/far0/ppermute | solution.py:75
  15.9 3.5 %load1.1.weights = bf16[2,2048,1024]{2,1,0:T(8,128)(2,1)S(1)} custom-call(s32[1]{0:T(128)} %bitcast.5.quarter, bf16[2048,4096]{1,0:T(8,128)(2,1)} %gate_weight.3, bf16[2048,4096]{1,0:T(8,128)(2,1)} %up_weight.7), custom_call_target="tpu_custom_call" | custom-call | flops 1073741824 | bytes 1 | tf_op jit(solution)/shard_map/load1/pallas_call | solution.py:121
  20.2 6.7 %collective-permute-start.5 = (bf16[96,2048]{1,0:T(8,128)(2,1)S(1)}, bf16[96,2048]{1,0:T(8,128)(2,1)S(1)}, u32[]{:S(2)}, u32[]{:S(2)}) collective-permute-start(bf16[96,2048]{1,0:T(8,128)(2,1)S(1)} %pad_maximum_fusion.3), channel_id=1, source_target_pairs={{1,4},{3,6},{4,1},{6,3},{9,12},{11,14},{12,9},{14,11},{17,20},{19,... | collective-permute-start | bytes 1179656 | tf_op jit(solution)/shard_map/arr0/ppermute | solution.py:95
  27.0 3.5 %load2.1.weights = bf16[2,2048,1024]{2,1,0:T(8,128)(2,1)S(1)} custom-call(s32[1]{0:T(128)} %bitcast.6.quarter, bf16[2048,4096]{1,0:T(8,128)(2,1)} %gate_weight.3, bf16[2048,4096]{1,0:T(8,128)(2,1)} %up_weight.7), custom_call_target="tpu_custom_call" | custom-call | flops 1073741824 | bytes 1 | tf_op jit(solution)/shard_map/load2/pallas_call | solution.py:121
  30.5 3.5 %load0.1.weights = bf16[2,2048,1024]{2,1,0:T(8,128)(2,1)S(1)} custom-call(s32[1]{0:T(128)} %bitcast.4.quarter, bf16[2048,4096]{1,0:T(8,128)(2,1)} %gate_weight.3, bf16[2048,4096]{1,0:T(8,128)(2,1)} %up_weight.7), custom_call_target="tpu_custom_call" | custom-call | flops 1073741824 | bytes 1 | tf_op jit(solution)/shard_map/load0/pallas_call | solution.py:121
  34.4 2.5 %collective-permute-start.3 = (bf16[32,2048]{1,0:T(8,128)(2,1)S(1)}, bf16[32,2048]{1,0:T(8,128)(2,1)S(1)}, u32[]{:S(2)}, u32[]{:S(2)}) collective-permute-start(bf16[32,2048]{1,0:T(8,128)(2,1)S(1)} %get-tuple-element.123), channel_id=1, source_target_pairs={{0,8},{4,12},{8,0},{12,4},{1,9},{5,13},{9,1},{13,5},{2,10},{6,14},... | collective-permute-start | bytes 393224 | tf_op jit(solution)/shard_map/far2/ppermute | solution.py:75
  44.2 2.9 %collective-permute-start.11 = (bf16[96,2048]{1,0:T(8,128)(2,1)S(1)}, bf16[96,2048]{1,0:T(8,128)(2,1)S(1)}, u32[]{:S(2)}, u32[]{:S(2)}) collective-permute-start(bf16[96,2048]{1,0:T(8,128)(2,1)S(1)} %pad_maximum_fusion.4), channel_id=1, source_target_pairs={{1,4},{3,6},{4,1},{6,3},{9,12},{11,14},{12,9},{14,11},{17,20},{19,... | collective-permute-start | bytes 1179656 | tf_op jit(solution)/shard_map/arr1/ppermute | solution.py:95
  47.5 2.0 %d0.1.held = f32[2,192,1024]{2,1,0:T(8,128)S(1)} custom-call(bf16[192,2048]{1,0:T(8,128)(2,1)S(1)} %pad_maximum_fusion.some, bf16[2,2048,1024]{2,1,0:T(8,128)(2,1)S(1)} %load0.1.weights, bf16[2,192,1024]{2,1,0:T(8,128)(2,1)S(1)} %collective-permute-done.8.rest_0_), custom_call_target="tpu_custom_call" | custom-call | flops 17179869184 | bytes 1 | tf_op jit(solution)/shard_map/d0/pallas_call | solution.py:150
  51.0 6.7 %collective-permute-done.10 = bf16[96,2048]{1,0:T(8,128)(2,1)S(1)} collective-permute-done((bf16[96,2048]{1,0:T(8,128)(2,1)S(1)}, bf16[96,2048]{1,0:T(8,128)(2,1)S(1)}, u32[]{:S(2)}, u32[]{:S(2)}) %collective-permute-start.10) | collective-permute-done | bytes 393248 | tf_op jit(solution)/shard_map/arr1/ppermute | solution.py:95
  58.1 2.0 %a1.1 = bf16[2,192,1024]{2,1,0:T(8,128)(2,1)S(1)} custom-call(bf16[192,2048]{1,0:T(8,128)(2,1)S(1)} %pad_maximum_fusion.1.some, bf16[2,2048,1024]{2,1,0:T(8,128)(2,1)S(1)} %load3.1.weights), custom_call_target="tpu_custom_call" | custom-call | flops 17179869184 | bytes 1 | tf_op jit(solution)/shard_map/a1/pallas_call | solution.py:150
  62.2 5.8 %collective-permute-done.13.rest_1_ = bf16[192,1024]{1,0:T(8,128)(2,1)S(1)} collective-permute-done((bf16[192,1024]{1,0:T(8,128)(2,1)S(1)}, bf16[192,1024]{1,0:T(8,128)(2,1)S(1)}, u32[]{:S(2)}, u32[]{:S(2)}) %collective-permute-start.13) | collective-permute-done | bytes 393248 | tf_op jit(solution)/shard_map/b0/ppermute | solution.py:71
  68.3 2.1 %collective-permute-start.20 = (bf16[192,1024]{1,0:T(8,128)(2,1)S(1)}, bf16[192,1024]{1,0:T(8,128)(2,1)S(1)}, u32[]{:S(2)}, u32[]{:S(2)}) collective-permute-start(bf16[192,1024]{1,0:T(8,128)(2,1)S(1)} %hide0.1.one), channel_id=1, source_target_pairs={{0,1},{1,0},{2,3},{3,2},{4,5},{5,4},{6,7},{7,6},{8,9},{9,8},{10,11... | collective-permute-start | bytes 1179656 | tf_op jit(solution)/shard_map/hide0/ppermute | solution.py:71
  72.9 3.3 %collective-permute-start.17 = (bf16[64,2048]{1,0:T(8,128)(2,1)S(1)}, bf16[64,2048]{1,0:T(8,128)(2,1)S(1)}, u32[]{:S(2)}, u32[]{:S(2)}) collective-permute-start(bf16[64,2048]{1,0:T(8,128)(2,1)S(1)} %pad_maximum_fusion.5), channel_id=1, source_target_pairs={{1,4},{3,6},{4,1},{6,3},{9,12},{11,14},{12,9},{14,11},{17,20},{19,... | collective-permute-start | bytes 786440 | tf_op jit(solution)/shard_map/arr2/ppermute | solution.py:95
  77.6 2.0 %d1.1.held = f32[2,192,1024]{2,1,0:T(8,128)S(1)} custom-call(bf16[192,2048]{1,0:T(8,128)(2,1)S(1)} %pad_maximum_fusion.1.some, bf16[2,2048,1024]{2,1,0:T(8,128)(2,1)S(1)} %load0.1.weights, bf16[2,192,1024]{2,1,0:T(8,128)(2,1)S(1)} %collective-permute-done.16.rest_0_), custom_call_target="tpu_custom_call" | custom-call | flops 17179869184 | bytes 1 | tf_op jit(solution)/shard_map/d1/pallas_call | solution.py:150
  79.7 4.0 %collective-permute-done.15 = bf16[64,2048]{1,0:T(8,128)(2,1)S(1)} collective-permute-done((bf16[64,2048]{1,0:T(8,128)(2,1)S(1)}, bf16[64,2048]{1,0:T(8,128)(2,1)S(1)}, u32[]{:S(2)}, u32[]{:S(2)}) %collective-permute-start.15) | collective-permute-done | bytes 262176 | tf_op jit(solution)/shard_map/arr2/ppermute | solution.py:95
  88.1 4.0 %down0.1.weights = bf16[2,1024,2048]{2,1,0:T(8,128)(2,1)S(1)} custom-call(s32[2]{0:T(128)S(1)} %get-tuple-element.143.quarters, bf16[4096,2048]{1,0:T(8,128)(2,1)} %weight.1), custom_call_target="tpu_custom_call" | custom-call | flops 17179869184 | bytes 1 | tf_op jit(solution)/shard_map/down0/pallas_call | solution.py:181
  92.7 2.0 %own0.1.rest_0_ = f32[192,2048]{1,0:T(8,128)S(1)} custom-call(bf16[192,1024]{1,0:T(8,128)(2,1)S(1)} %hide0.1.one, bf16[192,1024]{1,0:T(8,128)(2,1)S(1)} %collective-permute-done.20.two, bf16[2,1024,2048]{2,1,0:T(8,128)(2,1)S(1)} %down0.1.weights), custom_call_target="tpu_custom_call" | custom-call | flops 17179869184 | bytes 1 | tf_op jit(solution)/shard_map/own0/pallas_call | solution.py:204
  94.8 4.0 %down2.1.weights = bf16[2,1024,2048]{2,1,0:T(8,128)(2,1)S(1)} custom-call(s32[2]{0:T(128)S(1)} %get-tuple-element.149.quarters, bf16[4096,2048]{1,0:T(8,128)(2,1)} %weight.1), custom_call_target="tpu_custom_call" | custom-call | flops 17179869184 | bytes 1 | tf_op jit(solution)/shard_map/down2/pallas_call | solution.py:181
  98.8 2.0 %rest0.1.partial_sum = f32[192,2048]{1,0:T(8,128)S(1)} custom-call(bf16[192,1024]{1,0:T(8,128)(2,1)S(1)} %collective-permute-done.19.one, bf16[192,1024]{1,0:T(8,128)(2,1)S(1)} %collective-permute-done.21.two, bf16[2,1024,2048]{2,1,0:T(8,128)(2,1)S(1)} %down2.1.weights, f32[192,2048]{1,0:T(8,128)S(1)} %own0.1.rest_0_), custom_call_target="tpu_custom_call" | custom-call | flops 17179869184 | bytes 1 | tf_op jit(solution)/shard_map/rest0/pallas_call | solution.py:204
  103.8 3.1 %collective-permute-start.29 = (bf16[96,2048]{1,0:T(8,128)(2,1)S(1)}, bf16[96,2048]{1,0:T(8,128)(2,1)S(1)}, u32[]{:S(2)}, u32[]{:S(2)}) collective-permute-start(bf16[96,2048]{1,0:T(8,128)(2,1)S(1)} %get-tuple-element.162), channel_id=1, source_target_pairs={{1,4},{3,6},{4,1},{6,3},{9,12},{11,14},{12,9},{14,11},{17,20},{19,... | collective-permute-start | bytes 1179656 | tf_op jit(solution)/shard_map/out0/ppermute | solution.py:95
  111.2 2.0 %collective-permute-done.26.one = bf16[192,1024]{1,0:T(8,128)(2,1)S(1)} collective-permute-done((bf16[192,1024]{1,0:T(8,128)(2,1)S(1)}, bf16[192,1024]{1,0:T(8,128)(2,1)S(1)}, u32[]{:S(2)}, u32[]{:S(2)}) %collective-permute-start.26) | collective-permute-done | bytes 393248 | tf_op jit(solution)/shard_map/hide1/ppermute | solution.py:71
  114.5 2.0 %own1.1.rest_0_ = f32[192,2048]{1,0:T(8,128)S(1)} custom-call(bf16[192,1024]{1,0:T(8,128)(2,1)S(1)} %hide1.1.one, bf16[192,1024]{1,0:T(8,128)(2,1)S(1)} %collective-permute-done.28.two, bf16[2,1024,2048]{2,1,0:T(8,128)(2,1)S(1)} %down0.1.weights), custom_call_target="tpu_custom_call" | custom-call | flops 17179869184 | bytes 1 | tf_op jit(solution)/shard_map/own1/pallas_call | solution.py:204
  117.6 2.0 %rest1.1.partial_sum = f32[192,2048]{1,0:T(8,128)S(1)} custom-call(bf16[192,1024]{1,0:T(8,128)(2,1)S(1)} %collective-permute-done.26.one, bf16[192,1024]{1,0:T(8,128)(2,1)S(1)} %collective-permute-done.30.two, bf16[2,1024,2048]{2,1,0:T(8,128)(2,1)S(1)} %down2.1.weights, f32[192,2048]{1,0:T(8,128)S(1)} %own1.1.rest_0_), custom_call_target="tpu_custom_call" | custom-call | flops 17179869184 | bytes 1 | tf_op jit(solution)/shard_map/rest1/pallas_call | solution.py:204
  120.4 4.0 %collective-permute-done.25.rest_0_ = bf16[2,128,1024]{2,1,0:T(8,128)(2,1)S(1)} collective-permute-done((bf16[2,128,1024]{2,1,0:T(8,128)(2,1)S(1)}, bf16[2,128,1024]{2,1,0:T(8,128)(2,1)S(1)}, u32[]{:S(2)}, u32[]{:S(2)}) %collective-permute-start.25) | collective-permute-done | bytes 524320 | tf_op jit(solution)/shard_map/b2/ppermute | solution.py:71
  128.7 3.6 %collective-permute-start.34 = (bf16[96,2048]{1,0:T(8,128)(2,1)S(1)}, bf16[96,2048]{1,0:T(8,128)(2,1)S(1)}, u32[]{:S(2)}, u32[]{:S(2)}) collective-permute-start(bf16[96,2048]{1,0:T(8,128)(2,1)S(1)} %get-tuple-element.172), channel_id=1, source_target_pairs={{1,4},{3,6},{4,1},{6,3},{9,12},{11,14},{12,9},{14,11},{17,20},{19,... | collective-permute-start | bytes 1179656 | tf_op jit(solution)/shard_map/out1/ppermute | solution.py:95
  133.4 8.7 %collective-permute-done.34.got_two = bf16[96,2048]{1,0:T(8,128)(2,1)S(1)} collective-permute-done((bf16[96,2048]{1,0:T(8,128)(2,1)S(1)}, bf16[96,2048]{1,0:T(8,128)(2,1)S(1)}, u32[]{:S(2)}, u32[]{:S(2)}) %collective-permute-start.34) | collective-permute-done | bytes 393248 | tf_op jit(solution)/shard_map/out1/ppermute | solution.py:95
  148.1 3.8 %collective-permute-start.39 = (bf16[64,2048]{1,0:T(8,128)(2,1)S(1)}, bf16[64,2048]{1,0:T(8,128)(2,1)S(1)}, u32[]{:S(2)}, u32[]{:S(2)}) collective-permute-start(bf16[64,2048]{1,0:T(8,128)(2,1)S(1)} %get-tuple-element.183), channel_id=1, source_target_pairs={{1,4},{3,6},{4,1},{6,3},{9,12},{11,14},{12,9},{14,11},{17,20},{19,... | collective-permute-start | bytes 786440 | tf_op jit(solution)/shard_map/out2/ppermute | solution.py:95
  153.8 6.7 %collective-permute-done.39.got_two = bf16[64,2048]{1,0:T(8,128)(2,1)S(1)} collective-permute-done((bf16[64,2048]{1,0:T(8,128)(2,1)S(1)}, bf16[64,2048]{1,0:T(8,128)(2,1)S(1)}, u32[]{:S(2)}, u32[]{:S(2)}) %collective-permute-start.39) | collective-permute-done | bytes 262176 | tf_op jit(solution)/shard_map/out2/ppermute | solution.py:95
  162.2 2.9 %collective-permute-done.40.got = bf16[32,2048]{1,0:T(8,128)(2,1)S(1)} collective-permute-done((bf16[32,2048]{1,0:T(8,128)(2,1)S(1)}, bf16[32,2048]{1,0:T(8,128)(2,1)S(1)}, u32[]{:S(2)}, u32[]{:S(2)}) %collective-permute-start.40) | collective-permute-done | bytes 131104 | tf_op jit(solution)/shard_map/mix2/ppermute | solution.py:71
  166.0 5.9 %collective-permute-done.42.got = bf16[32,2048]{1,0:T(8,128)(2,1)S(1)} collective-permute-done((bf16[32,2048]{1,0:T(8,128)(2,1)S(1)}, bf16[32,2048]{1,0:T(8,128)(2,1)S(1)}, u32[]{:S(2)}, u32[]{:S(2)}) %collective-permute-start.42) | collective-permute-done | bytes 131104 | tf_op jit(solution)/shard_map/far_out2/ppermute | solution.py:75
  (124 shorter events, 52.4 us)
Async XLA Ops:
  2.8 12.0 %collective-permute-start = (bf16[48,2048]{1,0:T(8,128)(2,1)S(1)}, bf16[48,2048]{1,0:T(8,128)(2,1)S(1)}, u32[]{:S(2)}, u32[]{:S(2)}) collective-permute-start(bf16[48,2048]{1,0:T(8,128)(2,1)S(1)} %get-tuple-element.109), channel_id=1, source_target_pairs={{0,8},{4,12},{8,0},{12,4},{1,9},{5,13},{9,1},{13,5},{2,10},{6,14},... | collective-permute-start | bytes 589832 | tf_op jit(solution)/shard_map/far0/ppermute | solution.py:75
  15.9 18.1 %collective-permute-start.1 = (bf16[48,2048]{1,0:T(8,128)(2,1)S(1)}, bf16[48,2048]{1,0:T(8,128)(2,1)S(1)}, u32[]{:S(2)}, u32[]{:S(2)}) collective-permute-start(bf16[48,2048]{1,0:T(8,128)(2,1)S(1)} %get-tuple-element.114), channel_id=1, source_target_pairs={{0,8},{4,12},{8,0},{12,4},{1,9},{5,13},{9,1},{13,5},{2,10},{6,14},... | collective-permute-start | bytes 589832 | tf_op jit(solution)/shard_map/far1/ppermute | solution.py:75
  20.2 16.7 %collective-permute-start.5 = (bf16[96,2048]{1,0:T(8,128)(2,1)S(1)}, bf16[96,2048]{1,0:T(8,128)(2,1)S(1)}, u32[]{:S(2)}, u32[]{:S(2)}) collective-permute-start(bf16[96,2048]{1,0:T(8,128)(2,1)S(1)} %pad_maximum_fusion.3), channel_id=1, source_target_pairs={{1,4},{3,6},{4,1},{6,3},{9,12},{11,14},{12,9},{14,11},{17,20},{19,... | collective-permute-start | bytes 1179656 | tf_op jit(solution)/shard_map/arr0/ppermute | solution.py:95
  26.9 10.0 %collective-permute-start.4 = (bf16[96,2048]{1,0:T(8,128)(2,1)S(1)}, bf16[96,2048]{1,0:T(8,128)(2,1)S(1)}, u32[]{:S(2)}, u32[]{:S(2)}) collective-permute-start(bf16[96,2048]{1,0:T(8,128)(2,1)S(1)} %pad_maximum_fusion.3), channel_id=1, source_target_pairs={{0,4},{1,0},{2,6},{3,2},{4,5},{5,1},{6,7},{7,3},{8,12},{9,8},{10,1... | collective-permute-start | bytes 1179656 | tf_op jit(solution)/shard_map/arr0/ppermute | solution.py:95
  34.1 10.0 %collective-permute-start.6 = (bf16[48,2048]{1,0:T(8,128)(2,1)S(1)}, bf16[48,2048]{1,0:T(8,128)(2,1)S(1)}, u32[]{:S(2)}, u32[]{:S(2)}) collective-permute-start(bf16[48,2048]{1,0:T(8,128)(2,1)S(1)} %broadcast_select_fusion.17), channel_id=1, source_target_pairs={{0,2},{1,3},{2,0},{3,1},{4,6},{5,7},{6,4},{7,5},{8,10},{9,11},{10,... | collective-permute-start | bytes 589832 | tf_op jit(solution)/shard_map/sel1/ppermute | solution.py:71
  34.4 15.1 %collective-permute-start.3 = (bf16[32,2048]{1,0:T(8,128)(2,1)S(1)}, bf16[32,2048]{1,0:T(8,128)(2,1)S(1)}, u32[]{:S(2)}, u32[]{:S(2)}) collective-permute-start(bf16[32,2048]{1,0:T(8,128)(2,1)S(1)} %get-tuple-element.123), channel_id=1, source_target_pairs={{0,8},{4,12},{8,0},{12,4},{1,9},{5,13},{9,1},{13,5},{2,10},{6,14},... | collective-permute-start | bytes 393224 | tf_op jit(solution)/shard_map/far2/ppermute | solution.py:75
  44.2 13.6 %collective-permute-start.11 = (bf16[96,2048]{1,0:T(8,128)(2,1)S(1)}, bf16[96,2048]{1,0:T(8,128)(2,1)S(1)}, u32[]{:S(2)}, u32[]{:S(2)}) collective-permute-start(bf16[96,2048]{1,0:T(8,128)(2,1)S(1)} %pad_maximum_fusion.4), channel_id=1, source_target_pairs={{1,4},{3,6},{4,1},{6,3},{9,12},{11,14},{12,9},{14,11},{17,20},{19,... | collective-permute-start | bytes 1179656 | tf_op jit(solution)/shard_map/arr1/ppermute | solution.py:95
  47.1 10.7 %collective-permute-start.10 = (bf16[96,2048]{1,0:T(8,128)(2,1)S(1)}, bf16[96,2048]{1,0:T(8,128)(2,1)S(1)}, u32[]{:S(2)}, u32[]{:S(2)}) collective-permute-start(bf16[96,2048]{1,0:T(8,128)(2,1)S(1)} %pad_maximum_fusion.4), channel_id=1, source_target_pairs={{0,4},{1,0},{2,6},{3,2},{4,5},{5,1},{6,7},{7,3},{8,12},{9,8},{10,1... | collective-permute-start | bytes 1179656 | tf_op jit(solution)/shard_map/arr1/ppermute | solution.py:95
  47.2 20.8 %collective-permute-start.12 = (bf16[192,1024]{1,0:T(8,128)(2,1)S(1)}, bf16[192,1024]{1,0:T(8,128)(2,1)S(1)}, u32[]{:S(2)}, u32[]{:S(2)}) collective-permute-start(bf16[192,1024]{1,0:T(8,128)(2,1)S(1)} %get-tuple-element.128), channel_id=1, source_target_pairs={{0,2},{1,3},{2,0},{3,1},{4,6},{5,7},{6,4},{7,5},{8,10},{9,11},{10,... | collective-permute-start | bytes 1179656 | tf_op jit(solution)/shard_map/b0/ppermute | solution.py:71
  49.5 23.3 %collective-permute-start.9 = (bf16[32,2048]{1,0:T(8,128)(2,1)S(1)}, bf16[32,2048]{1,0:T(8,128)(2,1)S(1)}, u32[]{:S(2)}, u32[]{:S(2)}) collective-permute-start(bf16[32,2048]{1,0:T(8,128)(2,1)S(1)} %broadcast_select_fusion.20), channel_id=1, source_target_pairs={{0,2},{1,3},{2,0},{3,1},{4,6},{5,7},{6,4},{7,5},{8,10},{9,11},{10,... | collective-permute-start | bytes 393224 | tf_op jit(solution)/shard_map/sel2/ppermute | solution.py:71
  50.8 17.2 %collective-permute-start.13 = (bf16[192,1024]{1,0:T(8,128)(2,1)S(1)}, bf16[192,1024]{1,0:T(8,128)(2,1)S(1)}, u32[]{:S(2)}, u32[]{:S(2)}) collective-permute-start(bf16[192,1024]{1,0:T(8,128)(2,1)S(1)} %get-tuple-element.136), channel_id=1, source_target_pairs={{0,2},{1,3},{2,0},{3,1},{4,6},{5,7},{6,4},{7,5},{8,10},{9,11},{10,... | collective-permute-start | bytes 1179656 | tf_op jit(solution)/shard_map/b0/ppermute | solution.py:71
  60.1 10.8 %collective-permute-start.14 = (bf16[2,192,1024]{2,1,0:T(8,128)(2,1)S(1)}, bf16[2,192,1024]{2,1,0:T(8,128)(2,1)S(1)}, u32[]{:S(2)}, u32[]{:S(2)}) collective-permute-start(bf16[2,192,1024]{2,1,0:T(8,128)(2,1)S(1)} %a1.1), channel_id=1, source_target_pairs={{0,1},{1,0},{2,3},{3,2},{4,5},{5,4},{6,7},{7,6},{8,9},{9,8},{10,11... | collective-permute-start | bytes 2359304 | tf_op jit(solution)/shard_map/a1/ppermute | solution.py:71
  68.3 23.8 %collective-permute-start.20 = (bf16[192,1024]{1,0:T(8,128)(2,1)S(1)}, bf16[192,1024]{1,0:T(8,128)(2,1)S(1)}, u32[]{:S(2)}, u32[]{:S(2)}) collective-permute-start(bf16[192,1024]{1,0:T(8,128)(2,1)S(1)} %hide0.1.one), channel_id=1, source_target_pairs={{0,1},{1,0},{2,3},{3,2},{4,5},{5,4},{6,7},{7,6},{8,9},{9,8},{10,11... | collective-permute-start | bytes 1179656 | tf_op jit(solution)/shard_map/hide0/ppermute | solution.py:71
  70.3 24.4 %collective-permute-start.19 = (bf16[192,1024]{1,0:T(8,128)(2,1)S(1)}, bf16[192,1024]{1,0:T(8,128)(2,1)S(1)}, u32[]{:S(2)}, u32[]{:S(2)}) collective-permute-start(bf16[192,1024]{1,0:T(8,128)(2,1)S(1)} %hide0.1.one), channel_id=1, source_target_pairs={{0,2},{1,3},{2,0},{3,1},{4,6},{5,7},{6,4},{7,5},{8,10},{9,11},{10,... | collective-permute-start | bytes 1179656 | tf_op jit(solution)/shard_map/hide0/ppermute | solution.py:71
  72.9 12.0 %collective-permute-start.17 = (bf16[64,2048]{1,0:T(8,128)(2,1)S(1)}, bf16[64,2048]{1,0:T(8,128)(2,1)S(1)}, u32[]{:S(2)}, u32[]{:S(2)}) collective-permute-start(bf16[64,2048]{1,0:T(8,128)(2,1)S(1)} %pad_maximum_fusion.5), channel_id=1, source_target_pairs={{1,4},{3,6},{4,1},{6,3},{9,12},{11,14},{12,9},{14,11},{17,20},{19,... | collective-permute-start | bytes 786440 | tf_op jit(solution)/shard_map/arr2/ppermute | solution.py:95
  76.1 7.5 %collective-permute-start.15 = (bf16[64,2048]{1,0:T(8,128)(2,1)S(1)}, bf16[64,2048]{1,0:T(8,128)(2,1)S(1)}, u32[]{:S(2)}, u32[]{:S(2)}) collective-permute-start(bf16[64,2048]{1,0:T(8,128)(2,1)S(1)} %pad_maximum_fusion.5), channel_id=1, source_target_pairs={{0,4},{1,0},{2,6},{3,2},{4,5},{5,1},{6,7},{7,3},{8,12},{9,8},{10,1... | collective-permute-start | bytes 786440 | tf_op jit(solution)/shard_map/arr2/ppermute | solution.py:95
  76.4 25.3 %collective-permute-start.18 = (bf16[192,1024]{1,0:T(8,128)(2,1)S(1)}, bf16[192,1024]{1,0:T(8,128)(2,1)S(1)}, u32[]{:S(2)}, u32[]{:S(2)}) collective-permute-start(bf16[192,1024]{1,0:T(8,128)(2,1)S(1)} %get-tuple-element.139), channel_id=1, source_target_pairs={{0,2},{1,3},{2,0},{3,1},{4,6},{5,7},{6,4},{7,5},{8,10},{9,11},{10,... | collective-permute-start | bytes 1179656 | tf_op jit(solution)/shard_map/b1/ppermute | solution.py:71
  83.7 18.0 %collective-permute-start.22 = (bf16[192,1024]{1,0:T(8,128)(2,1)S(1)}, bf16[192,1024]{1,0:T(8,128)(2,1)S(1)}, u32[]{:S(2)}, u32[]{:S(2)}) collective-permute-start(bf16[192,1024]{1,0:T(8,128)(2,1)S(1)} %get-tuple-element.154), channel_id=1, source_target_pairs={{0,2},{1,3},{2,0},{3,1},{4,6},{5,7},{6,4},{7,5},{8,10},{9,11},{10,... | collective-permute-start | bytes 1179656 | tf_op jit(solution)/shard_map/b1/ppermute | solution.py:71
  88.0 20.4 %collective-permute-start.24 = (bf16[2,128,1024]{2,1,0:T(8,128)(2,1)S(1)}, bf16[2,128,1024]{2,1,0:T(8,128)(2,1)S(1)}, u32[]{:S(2)}, u32[]{:S(2)}) collective-permute-start(bf16[2,128,1024]{2,1,0:T(8,128)(2,1)S(1)} %c2.1), channel_id=1, source_target_pairs={{0,1},{1,0},{2,3},{3,2},{4,5},{5,4},{6,7},{7,6},{8,9},{9,8},{10,11... | collective-permute-start | bytes 1572872 | tf_op jit(solution)/shard_map/c2/ppermute | solution.py:71
  92.1 11.7 %collective-permute-start.23 = (bf16[2,128,1024]{2,1,0:T(8,128)(2,1)S(1)}, bf16[2,128,1024]{2,1,0:T(8,128)(2,1)S(1)}, u32[]{:S(2)}, u32[]{:S(2)}) collective-permute-start(bf16[2,128,1024]{2,1,0:T(8,128)(2,1)S(1)} %a2.1), channel_id=1, source_target_pairs={{0,1},{1,0},{2,3},{3,2},{4,5},{5,4},{6,7},{7,6},{8,9},{9,8},{10,11... | collective-permute-start | bytes 1572872 | tf_op jit(solution)/shard_map/a2/ppermute | solution.py:71
  102.0 12.5 %collective-permute-start.28 = (bf16[192,1024]{1,0:T(8,128)(2,1)S(1)}, bf16[192,1024]{1,0:T(8,128)(2,1)S(1)}, u32[]{:S(2)}, u32[]{:S(2)}) collective-permute-start(bf16[192,1024]{1,0:T(8,128)(2,1)S(1)} %hide1.1.one), channel_id=1, source_target_pairs={{0,1},{1,0},{2,3},{3,2},{4,5},{5,4},{6,7},{7,6},{8,9},{9,8},{10,11... | collective-permute-start | bytes 1179656 | tf_op jit(solution)/shard_map/hide1/ppermute | solution.py:71
  102.5 10.7 %collective-permute-start.26 = (bf16[192,1024]{1,0:T(8,128)(2,1)S(1)}, bf16[192,1024]{1,0:T(8,128)(2,1)S(1)}, u32[]{:S(2)}, u32[]{:S(2)}) collective-permute-start(bf16[192,1024]{1,0:T(8,128)(2,1)S(1)} %hide1.1.one), channel_id=1, source_target_pairs={{0,2},{1,3},{2,0},{3,1},{4,6},{5,7},{6,4},{7,5},{8,10},{9,11},{10,... | collective-permute-start | bytes 1179656 | tf_op jit(solution)/shard_map/hide1/ppermute | solution.py:71
  102.8 13.8 %collective-permute-start.27 = (bf16[96,2048]{1,0:T(8,128)(2,1)S(1)}, bf16[96,2048]{1,0:T(8,128)(2,1)S(1)}, u32[]{:S(2)}, u32[]{:S(2)}) collective-permute-start(bf16[96,2048]{1,0:T(8,128)(2,1)S(1)} %get-tuple-element.152), channel_id=1, source_target_pairs={{0,1},{1,5},{2,3},{3,7},{4,0},{5,4},{6,2},{7,6},{8,9},{9,13},{10,1... | collective-permute-start | bytes 1179656 | tf_op jit(solution)/shard_map/out0/ppermute | solution.py:95
  103.8 12.8 %collective-permute-start.29 = (bf16[96,2048]{1,0:T(8,128)(2,1)S(1)}, bf16[96,2048]{1,0:T(8,128)(2,1)S(1)}, u32[]{:S(2)}, u32[]{:S(2)}) collective-permute-start(bf16[96,2048]{1,0:T(8,128)(2,1)S(1)} %get-tuple-element.162), channel_id=1, source_target_pairs={{1,4},{3,6},{4,1},{6,3},{9,12},{11,14},{12,9},{14,11},{17,20},{19,... | collective-permute-start | bytes 1179656 | tf_op jit(solution)/shard_map/out0/ppermute | solution.py:95
  108.4 16.0 %collective-permute-start.25 = (bf16[2,128,1024]{2,1,0:T(8,128)(2,1)S(1)}, bf16[2,128,1024]{2,1,0:T(8,128)(2,1)S(1)}, u32[]{:S(2)}, u32[]{:S(2)}) collective-permute-start(bf16[2,128,1024]{2,1,0:T(8,128)(2,1)S(1)} %b2.1), channel_id=1, source_target_pairs={{0,2},{1,3},{2,0},{3,1},{4,6},{5,7},{6,4},{7,5},{8,10},{9,11},{10,... | collective-permute-start | bytes 1572872 | tf_op jit(solution)/shard_map/b2/ppermute | solution.py:71
  117.3 11.3 %collective-permute-start.33 = (bf16[48,2048]{1,0:T(8,128)(2,1)S(1)}, bf16[48,2048]{1,0:T(8,128)(2,1)S(1)}, u32[]{:S(2)}, u32[]{:S(2)}) collective-permute-start(bf16[48,2048]{1,0:T(8,128)(2,1)S(1)} %get-tuple-element.163), channel_id=1, source_target_pairs={{0,2},{1,3},{2,0},{3,1},{4,6},{5,7},{6,4},{7,5},{8,10},{9,11},{10,... | collective-permute-start | bytes 589832 | tf_op jit(solution)/shard_map/mix0/ppermute | solution.py:71
  124.7 19.5 %collective-permute-start.35 = (bf16[128,1024]{1,0:T(8,128)(2,1)S(1)}, bf16[128,1024]{1,0:T(8,128)(2,1)S(1)}, u32[]{:S(2)}, u32[]{:S(2)}) collective-permute-start(bf16[128,1024]{1,0:T(8,128)(2,1)S(1)} %hide2.1.one), channel_id=1, source_target_pairs={{0,1},{1,0},{2,3},{3,2},{4,5},{5,4},{6,7},{7,6},{8,9},{9,8},{10,11... | collective-permute-start | bytes 786440 | tf_op jit(solution)/shard_map/hide2/ppermute | solution.py:71
  126.0 18.2 %collective-permute-start.31 = (bf16[128,1024]{1,0:T(8,128)(2,1)S(1)}, bf16[128,1024]{1,0:T(8,128)(2,1)S(1)}, u32[]{:S(2)}, u32[]{:S(2)}) collective-permute-start(bf16[128,1024]{1,0:T(8,128)(2,1)S(1)} %hide2.1.one), channel_id=1, source_target_pairs={{0,2},{1,3},{2,0},{3,1},{4,6},{5,7},{6,4},{7,5},{8,10},{9,11},{10,... | collective-permute-start | bytes 786440 | tf_op jit(solution)/shard_map/hide2/ppermute | solution.py:71
  128.7 13.5 %collective-permute-start.34 = (bf16[96,2048]{1,0:T(8,128)(2,1)S(1)}, bf16[96,2048]{1,0:T(8,128)(2,1)S(1)}, u32[]{:S(2)}, u32[]{:S(2)}) collective-permute-start(bf16[96,2048]{1,0:T(8,128)(2,1)S(1)} %get-tuple-element.172), channel_id=1, source_target_pairs={{1,4},{3,6},{4,1},{6,3},{9,12},{11,14},{12,9},{14,11},{17,20},{19,... | collective-permute-start | bytes 1179656 | tf_op jit(solution)/shard_map/out1/ppermute | solution.py:95
  132.9 29.1 %collective-permute-start.41 = (bf16[48,2048]{1,0:T(8,128)(2,1)S(1)}, bf16[48,2048]{1,0:T(8,128)(2,1)S(1)}, u32[]{:S(2)}, u32[]{:S(2)}) collective-permute-start(bf16[48,2048]{1,0:T(8,128)(2,1)S(1)} %get-tuple-element.170), channel_id=1, source_target_pairs={{0,8},{4,12},{8,0},{12,4},{1,9},{5,13},{9,1},{13,5},{2,10},{6,14},... | collective-permute-start | bytes 589832 | tf_op jit(solution)/shard_map/far_out0/ppermute | solution.py:75
  148.1 12.4 %collective-permute-start.39 = (bf16[64,2048]{1,0:T(8,128)(2,1)S(1)}, bf16[64,2048]{1,0:T(8,128)(2,1)S(1)}, u32[]{:S(2)}, u32[]{:S(2)}) collective-permute-start(bf16[64,2048]{1,0:T(8,128)(2,1)S(1)} %get-tuple-element.183), channel_id=1, source_target_pairs={{1,4},{3,6},{4,1},{6,3},{9,12},{11,14},{12,9},{14,11},{17,20},{19,... | collective-permute-start | bytes 786440 | tf_op jit(solution)/shard_map/out2/ppermute | solution.py:95
  152.6 13.2 %collective-permute-start.43 = (bf16[48,2048]{1,0:T(8,128)(2,1)S(1)}, bf16[48,2048]{1,0:T(8,128)(2,1)S(1)}, u32[]{:S(2)}, u32[]{:S(2)}) collective-permute-start(bf16[48,2048]{1,0:T(8,128)(2,1)S(1)} %get-tuple-element.181), channel_id=1, source_target_pairs={{0,8},{4,12},{8,0},{12,4},{1,9},{5,13},{9,1},{13,5},{2,10},{6,14},... | collective-permute-start | bytes 589832 | tf_op jit(solution)/shard_map/far_out1/ppermute | solution.py:75
  (17 other events, 115.0 us)

commit v11 on v8

--- a/solution.py
+++ b/solution.py
@@ -11,7 +11,7 @@
 ORDER = (
     "far0", "load3", "sel0", "far1", "load1", "arr0", "load2", "load0", "sel1", "far2", "take0", "a0", "c0",
     "b0", "arr1", "d0", "sel2", "take1", "a1", "c1", "hide0", "b1", "arr2", "d1", "take2", "a2", "c2",
-    "down0", "own0", "forward0", "hide1", "b2", "d2", "down2", "rest0", "out0", "forward1", "own1", "rest1",
+    "down0", "own0", "forward0", "hide1", "b2", "d2", "down2", "own1", "rest0", "forward1", "out0", "rest1",
     "out1", "hide2", "mix0", "mix1", "forward2", "own2", "rest2", "out2", "far_out0", "mix2", "far_out1",
     "far_out2", "end0", "end1", "end2",
 )

time: 164 us -> 166 us (1.012)
  transfers between devices with their start and end apart: 44 -> 44, of which waited for: 14 -> 15; matrix products, arithmetic and copies ran while one was open for 1% -> 1% of each run, Pallas kernels for 38% -> 38%
where the time goes in v11:
time: 166 us; the launch traced here: 165 us
  Pallas kernels  63.4 us (38%)
  waiting for transfers between devices  49.5 us (30%)
  starting transfers between devices  48.2 us (29%)
  local copies, waits for them, and re-layouts  1.73 us (1%)
    ppermute x12, starting transfers between devices, over_both(): return lax.ppermute(array, ('tp', 'seq'), pairs)  24.5 us
    pallas_call x12, Pallas kernels, sums(): pl.pallas_call(functools.partial(sums_kernel, got is not None, split), ou...  21.4 us
    ppermute x12, waiting for transfers between devices, over_both(): return lax.ppermute(array, ('tp', 'seq'), pairs)  19.3 us
    ppermute x6, waiting for transfers between devices, over_tp(): return lax.ppermute(array, 'tp', [(i, i ^ bit) for i in range(4)])  15.1 us
    ppermute x26, waiting for transfers between devices, over_seq(): return lax.ppermute(array, 'seq', [(i, i ^ bit) for i in range(4)])  15.1 us
    pallas_call x4, Pallas kernels, load(): pl.pallas_call(load_kernel, out_shape=jax.ShapeDtypeStruct((2, deep, widt...  14 us
    ppermute x26, starting transfers between devices, over_seq(): return lax.ppermute(array, 'seq', [(i, i ^ bit) for i in range(4)])  13 us
    pallas_call x6, Pallas kernels, products(): pl.pallas_call(functools.partial(products_kernel, total is not None), out...  11 us
  transfers between devices with their start and end apart: 44, of which 15 were waited for; matrix products, arithmetic and copies ran while one was open for 1% of the time, Pallas kernels for 38%

profile of v11, /device:TPU:1, one launch (start us, length us, event | category | flops | bytes accessed | tf_op | source)
XLA Modules:
  0.0 165.2 jit_solution(2780621033858530015)
XLA Ops:
  2.8 3.2 %collective-permute-start = (bf16[48,2048]{1,0:T(8,128)(2,1)S(1)}, bf16[48,2048]{1,0:T(8,128)(2,1)S(1)}, u32[]{:S(2)}, u32[]{:S(2)}) collective-permute-start(bf16[48,2048]{1,0:T(8,128)(2,1)S(1)} %get-tuple-element.110), channel_id=1, source_target_pairs={{0,8},{4,12},{8,0},{12,4},{1,9},{5,13},{9,1},{13,5},{2,10},{6,14},... | collective-permute-start | bytes 589832 | tf_op jit(solution)/shard_map/far0/ppermute | solution.py:75
  6.2 3.5 %load3.1.weights = bf16[2,2048,1024]{2,1,0:T(8,128)(2,1)S(1)} custom-call(s32[1]{0:T(128)} %bitcast.7.quarter, bf16[2048,4096]{1,0:T(8,128)(2,1)} %gate_weight.3, bf16[2048,4096]{1,0:T(8,128)(2,1)} %up_weight.7), custom_call_target="tpu_custom_call" | custom-call | flops 1073741824 | bytes 1 | tf_op jit(solution)/shard_map/load3/pallas_call | solution.py:121
  9.7 5.2 %collective-permute-done = bf16[48,2048]{1,0:T(8,128)(2,1)S(1)} collective-permute-done((bf16[48,2048]{1,0:T(8,128)(2,1)S(1)}, bf16[48,2048]{1,0:T(8,128)(2,1)S(1)}, u32[]{:S(2)}, u32[]{:S(2)}) %collective-permute-start) | collective-permute-done | bytes 196640 | tf_op jit(solution)/shard_map/far0/ppermute | solution.py:75
  15.9 3.5 %load1.1.weights = bf16[2,2048,1024]{2,1,0:T(8,128)(2,1)S(1)} custom-call(s32[1]{0:T(128)} %bitcast.5.quarter, bf16[2048,4096]{1,0:T(8,128)(2,1)} %gate_weight.3, bf16[2048,4096]{1,0:T(8,128)(2,1)} %up_weight.7), custom_call_target="tpu_custom_call" | custom-call | flops 1073741824 | bytes 1 | tf_op jit(solution)/shard_map/load1/pallas_call | solution.py:121
  20.2 2.2 %collective-permute-start.4 = (bf16[96,2048]{1,0:T(8,128)(2,1)S(1)}, bf16[96,2048]{1,0:T(8,128)(2,1)S(1)}, u32[]{:S(2)}, u32[]{:S(2)}) collective-permute-start(bf16[96,2048]{1,0:T(8,128)(2,1)S(1)} %pad_maximum_fusion.3), channel_id=1, source_target_pairs={{0,4},{1,0},{2,6},{3,2},{4,5},{5,1},{6,7},{7,3},{8,12},{9,8},{10,1... | collective-permute-start | bytes 1179656 | tf_op jit(solution)/shard_map/arr0/ppermute | solution.py:95
  22.4 4.6 %collective-permute-start.5 = (bf16[96,2048]{1,0:T(8,128)(2,1)S(1)}, bf16[96,2048]{1,0:T(8,128)(2,1)S(1)}, u32[]{:S(2)}, u32[]{:S(2)}) collective-permute-start(bf16[96,2048]{1,0:T(8,128)(2,1)S(1)} %pad_maximum_fusion.3), channel_id=1, source_target_pairs={{1,4},{3,6},{4,1},{6,3},{9,12},{11,14},{12,9},{14,11},{17,20},{19,... | collective-permute-start | bytes 1179656 | tf_op jit(solution)/shard_map/arr0/ppermute | solution.py:95
  27.0 3.5 %load2.1.weights = bf16[2,2048,1024]{2,1,0:T(8,128)(2,1)S(1)} custom-call(s32[1]{0:T(128)} %bitcast.6.quarter, bf16[2048,4096]{1,0:T(8,128)(2,1)} %gate_weight.3, bf16[2048,4096]{1,0:T(8,128)(2,1)} %up_weight.7), custom_call_target="tpu_custom_call" | custom-call | flops 1073741824 | bytes 1 | tf_op jit(solution)/shard_map/load2/pallas_call | solution.py:121
  30.5 3.5 %load0.1.weights = bf16[2,2048,1024]{2,1,0:T(8,128)(2,1)S(1)} custom-call(s32[1]{0:T(128)} %bitcast.4.quarter, bf16[2048,4096]{1,0:T(8,128)(2,1)} %gate_weight.3, bf16[2048,4096]{1,0:T(8,128)(2,1)} %up_weight.7), custom_call_target="tpu_custom_call" | custom-call | flops 1073741824 | bytes 1 | tf_op jit(solution)/shard_map/load0/pallas_call | solution.py:121
  34.4 2.5 %collective-permute-start.3 = (bf16[32,2048]{1,0:T(8,128)(2,1)S(1)}, bf16[32,2048]{1,0:T(8,128)(2,1)S(1)}, u32[]{:S(2)}, u32[]{:S(2)}) collective-permute-start(bf16[32,2048]{1,0:T(8,128)(2,1)S(1)} %get-tuple-element.124), channel_id=1, source_target_pairs={{0,8},{4,12},{8,0},{12,4},{1,9},{5,13},{9,1},{13,5},{2,10},{6,14},... | collective-permute-start | bytes 393224 | tf_op jit(solution)/shard_map/far2/ppermute | solution.py:75
  37.2 2.0 %a0.1 = bf16[2,192,1024]{2,1,0:T(8,128)(2,1)S(1)} custom-call(bf16[192,2048]{1,0:T(8,128)(2,1)S(1)} %pad_maximum_fusion.some, bf16[2,2048,1024]{2,1,0:T(8,128)(2,1)S(1)} %load3.1.weights), custom_call_target="tpu_custom_call" | custom-call | flops 17179869184 | bytes 1 | tf_op jit(solution)/shard_map/a0/pallas_call | solution.py:150
  43.8 2.5 %collective-permute-start.11 = (bf16[96,2048]{1,0:T(8,128)(2,1)S(1)}, bf16[96,2048]{1,0:T(8,128)(2,1)S(1)}, u32[]{:S(2)}, u32[]{:S(2)}) collective-permute-start(bf16[96,2048]{1,0:T(8,128)(2,1)S(1)} %pad_maximum_fusion.4), channel_id=1, source_target_pairs={{1,4},{3,6},{4,1},{6,3},{9,12},{11,14},{12,9},{14,11},{17,20},{19,... | collective-permute-start | bytes 1179656 | tf_op jit(solution)/shard_map/arr1/ppermute | solution.py:95
  50.2 2.1 %collective-permute-done.10 = bf16[96,2048]{1,0:T(8,128)(2,1)S(1)} collective-permute-done((bf16[96,2048]{1,0:T(8,128)(2,1)S(1)}, bf16[96,2048]{1,0:T(8,128)(2,1)S(1)}, u32[]{:S(2)}, u32[]{:S(2)}) %collective-permute-start.10) | collective-permute-done | bytes 393248 | tf_op jit(solution)/shard_map/arr1/ppermute | solution.py:95
  52.4 2.6 %collective-permute-done.11 = bf16[96,2048]{1,0:T(8,128)(2,1)S(1)} collective-permute-done((bf16[96,2048]{1,0:T(8,128)(2,1)S(1)}, bf16[96,2048]{1,0:T(8,128)(2,1)S(1)}, u32[]{:S(2)}, u32[]{:S(2)}) %collective-permute-start.11) | collective-permute-done | bytes 393248 | tf_op jit(solution)/shard_map/arr1/ppermute | solution.py:95
  59.9 5.9 %collective-permute-done.13.rest_1_ = bf16[192,1024]{1,0:T(8,128)(2,1)S(1)} collective-permute-done((bf16[192,1024]{1,0:T(8,128)(2,1)S(1)}, bf16[192,1024]{1,0:T(8,128)(2,1)S(1)}, u32[]{:S(2)}, u32[]{:S(2)}) %collective-permute-start.13) | collective-permute-done | bytes 393248 | tf_op jit(solution)/shard_map/b0/ppermute | solution.py:71
  69.2 3.2 %collective-permute-start.17 = (bf16[64,2048]{1,0:T(8,128)(2,1)S(1)}, bf16[64,2048]{1,0:T(8,128)(2,1)S(1)}, u32[]{:S(2)}, u32[]{:S(2)}) collective-permute-start(bf16[64,2048]{1,0:T(8,128)(2,1)S(1)} %pad_maximum_fusion.5), channel_id=1, source_target_pairs={{1,4},{3,6},{4,1},{6,3},{9,12},{11,14},{12,9},{14,11},{17,20},{19,... | collective-permute-start | bytes 786440 | tf_op jit(solution)/shard_map/arr2/ppermute | solution.py:95
  80.4 4.0 %down0.1.weights = bf16[2,1024,2048]{2,1,0:T(8,128)(2,1)S(1)} custom-call(s32[2]{0:T(128)S(1)} %get-tuple-element.144.quarters, bf16[4096,2048]{1,0:T(8,128)(2,1)} %weight.1), custom_call_target="tpu_custom_call" | custom-call | flops 17179869184 | bytes 1 | tf_op jit(solution)/shard_map/down0/pallas_call | solution.py:181
  85.0 2.0 %own0.1.rest_0_ = f32[192,2048]{1,0:T(8,128)S(1)} custom-call(bf16[192,1024]{1,0:T(8,128)(2,1)S(1)} %hide0.1.one, bf16[192,1024]{1,0:T(8,128)(2,1)S(1)} %collective-permute-done.19.two, bf16[2,1024,2048]{2,1,0:T(8,128)(2,1)S(1)} %down0.1.weights), custom_call_target="tpu_custom_call" | custom-call | flops 17179869184 | bytes 1 | tf_op jit(solution)/shard_map/own0/pallas_call | solution.py:204
  87.1 6.2 %collective-permute-done.20.rest_1_ = bf16[192,1024]{1,0:T(8,128)(2,1)S(1)} collective-permute-done((bf16[192,1024]{1,0:T(8,128)(2,1)S(1)}, bf16[192,1024]{1,0:T(8,128)(2,1)S(1)}, u32[]{:S(2)}, u32[]{:S(2)}) %collective-permute-start.20) | collective-permute-done | bytes 393248 | tf_op jit(solution)/shard_map/b1/ppermute | solution.py:71
  99.5 4.0 %down2.1.weights = bf16[2,1024,2048]{2,1,0:T(8,128)(2,1)S(1)} custom-call(s32[2]{0:T(128)S(1)} %get-tuple-element.155.quarters, bf16[4096,2048]{1,0:T(8,128)(2,1)} %weight.1), custom_call_target="tpu_custom_call" | custom-call | flops 17179869184 | bytes 1 | tf_op jit(solution)/shard_map/down2/pallas_call | solution.py:181
  103.5 2.0 %own1.1.rest_0_ = f32[192,2048]{1,0:T(8,128)S(1)} custom-call(bf16[192,1024]{1,0:T(8,128)(2,1)S(1)} %hide1.1.one, bf16[192,1024]{1,0:T(8,128)(2,1)S(1)} %collective-permute-done.26.two, bf16[2,1024,2048]{2,1,0:T(8,128)(2,1)S(1)} %down0.1.weights), custom_call_target="tpu_custom_call" | custom-call | flops 17179869184 | bytes 1 | tf_op jit(solution)/shard_map/own1/pallas_call | solution.py:204
  105.5 2.0 %rest0.1.partial_sum = f32[192,2048]{1,0:T(8,128)S(1)} custom-call(bf16[192,1024]{1,0:T(8,128)(2,1)S(1)} %collective-permute-done.25.one, bf16[192,1024]{1,0:T(8,128)(2,1)S(1)} %collective-permute-done.27.two, bf16[2,1024,2048]{2,1,0:T(8,128)(2,1)S(1)} %down2.1.weights, f32[192,2048]{1,0:T(8,128)S(1)} %own0.1.rest_0_), custom_call_target="tpu_custom_call" | custom-call | flops 17179869184 | bytes 1 | tf_op jit(solution)/shard_map/rest0/pallas_call | solution.py:204
  110.6 2.1 %collective-permute-start.32 = (bf16[96,2048]{1,0:T(8,128)(2,1)S(1)}, bf16[96,2048]{1,0:T(8,128)(2,1)S(1)}, u32[]{:S(2)}, u32[]{:S(2)}) collective-permute-start(bf16[96,2048]{1,0:T(8,128)(2,1)S(1)} %get-tuple-element.168), channel_id=1, source_target_pairs={{1,4},{3,6},{4,1},{6,3},{9,12},{11,14},{12,9},{14,11},{17,20},{19,... | collective-permute-start | bytes 1179656 | tf_op jit(solution)/shard_map/out0/ppermute | solution.py:95
  112.7 2.0 %rest1.1.partial_sum = f32[192,2048]{1,0:T(8,128)S(1)} custom-call(bf16[192,1024]{1,0:T(8,128)(2,1)S(1)} %collective-permute-done.24.one, bf16[192,1024]{1,0:T(8,128)(2,1)S(1)} %collective-permute-done.28.two, bf16[2,1024,2048]{2,1,0:T(8,128)(2,1)S(1)} %down2.1.weights, f32[192,2048]{1,0:T(8,128)S(1)} %own1.1.rest_0_), custom_call_target="tpu_custom_call" | custom-call | flops 17179869184 | bytes 1 | tf_op jit(solution)/shard_map/rest1/pallas_call | solution.py:204
  115.5 3.5 %collective-permute-start.33 = (bf16[96,2048]{1,0:T(8,128)(2,1)S(1)}, bf16[96,2048]{1,0:T(8,128)(2,1)S(1)}, u32[]{:S(2)}, u32[]{:S(2)}) collective-permute-start(bf16[96,2048]{1,0:T(8,128)(2,1)S(1)} %get-tuple-element.171), channel_id=1, source_target_pairs={{1,4},{3,6},{4,1},{6,3},{9,12},{11,14},{12,9},{14,11},{17,20},{19,... | collective-permute-start | bytes 1179656 | tf_op jit(solution)/shard_map/out1/ppermute | solution.py:95
  121.7 2.0 %collective-permute-done.30.got_one = bf16[96,2048]{1,0:T(8,128)(2,1)S(1)} collective-permute-done((bf16[96,2048]{1,0:T(8,128)(2,1)S(1)}, bf16[96,2048]{1,0:T(8,128)(2,1)S(1)}, u32[]{:S(2)}, u32[]{:S(2)}) %collective-permute-start.30) | collective-permute-done | bytes 393248 | tf_op jit(solution)/shard_map/out1/ppermute | solution.py:95
  123.7 5.4 %collective-permute-done.33.got_two = bf16[96,2048]{1,0:T(8,128)(2,1)S(1)} collective-permute-done((bf16[96,2048]{1,0:T(8,128)(2,1)S(1)}, bf16[96,2048]{1,0:T(8,128)(2,1)S(1)}, u32[]{:S(2)}, u32[]{:S(2)}) %collective-permute-start.33) | collective-permute-done | bytes 393248 | tf_op jit(solution)/shard_map/out1/ppermute | solution.py:95
  135.6 2.4 %collective-permute-start.38 = (bf16[64,2048]{1,0:T(8,128)(2,1)S(1)}, bf16[64,2048]{1,0:T(8,128)(2,1)S(1)}, u32[]{:S(2)}, u32[]{:S(2)}) collective-permute-start(bf16[64,2048]{1,0:T(8,128)(2,1)S(1)} %get-tuple-element.182), channel_id=1, source_target_pairs={{1,4},{3,6},{4,1},{6,3},{9,12},{11,14},{12,9},{14,11},{17,20},{19,... | collective-permute-start | bytes 786440 | tf_op jit(solution)/shard_map/out2/ppermute | solution.py:95
  138.7 3.6 %collective-permute-start.43 = (bf16[48,2048]{1,0:T(8,128)(2,1)S(1)}, bf16[48,2048]{1,0:T(8,128)(2,1)S(1)}, u32[]{:S(2)}, u32[]{:S(2)}) collective-permute-start(bf16[48,2048]{1,0:T(8,128)(2,1)S(1)} %get-tuple-element.180), channel_id=1, source_target_pairs={{0,8},{4,12},{8,0},{12,4},{1,9},{5,13},{9,1},{13,5},{2,10},{6,14},... | collective-permute-start | bytes 589832 | tf_op jit(solution)/shard_map/far_out0/ppermute | solution.py:75
  142.2 5.3 %collective-permute-done.38.got_two = bf16[64,2048]{1,0:T(8,128)(2,1)S(1)} collective-permute-done((bf16[64,2048]{1,0:T(8,128)(2,1)S(1)}, bf16[64,2048]{1,0:T(8,128)(2,1)S(1)}, u32[]{:S(2)}, u32[]{:S(2)}) %collective-permute-start.38) | collective-permute-done | bytes 262176 | tf_op jit(solution)/shard_map/out2/ppermute | solution.py:95
  150.3 2.1 %collective-permute-done.39.got = bf16[32,2048]{1,0:T(8,128)(2,1)S(1)} collective-permute-done((bf16[32,2048]{1,0:T(8,128)(2,1)S(1)}, bf16[32,2048]{1,0:T(8,128)(2,1)S(1)}, u32[]{:S(2)}, u32[]{:S(2)}) %collective-permute-start.39) | collective-permute-done | bytes 131104 | tf_op jit(solution)/shard_map/mix2/ppermute | solution.py:71
  154.1 7.5 %collective-permute-done.42.got = bf16[48,2048]{1,0:T(8,128)(2,1)S(1)} collective-permute-done((bf16[48,2048]{1,0:T(8,128)(2,1)S(1)}, bf16[48,2048]{1,0:T(8,128)(2,1)S(1)}, u32[]{:S(2)}, u32[]{:S(2)}) %collective-permute-start.42) | collective-permute-done | bytes 196640 | tf_op jit(solution)/shard_map/far_out1/ppermute | solution.py:75
  161.8 2.4 %collective-permute-done.41.got = bf16[32,2048]{1,0:T(8,128)(2,1)S(1)} collective-permute-done((bf16[32,2048]{1,0:T(8,128)(2,1)S(1)}, bf16[32,2048]{1,0:T(8,128)(2,1)S(1)}, u32[]{:S(2)}, u32[]{:S(2)}) %collective-permute-start.41) | collective-permute-done | bytes 131104 | tf_op jit(solution)/shard_map/far_out2/ppermute | solution.py:75
  (117 shorter events, 55.3 us)
Async XLA Ops:
  2.8 12.0 %collective-permute-start = (bf16[48,2048]{1,0:T(8,128)(2,1)S(1)}, bf16[48,2048]{1,0:T(8,128)(2,1)S(1)}, u32[]{:S(2)}, u32[]{:S(2)}) collective-permute-start(bf16[48,2048]{1,0:T(8,128)(2,1)S(1)} %get-tuple-element.110), channel_id=1, source_target_pairs={{0,8},{4,12},{8,0},{12,4},{1,9},{5,13},{9,1},{13,5},{2,10},{6,14},... | collective-permute-start | bytes 589832 | tf_op jit(solution)/shard_map/far0/ppermute | solution.py:75
  15.9 18.1 %collective-permute-start.1 = (bf16[48,2048]{1,0:T(8,128)(2,1)S(1)}, bf16[48,2048]{1,0:T(8,128)(2,1)S(1)}, u32[]{:S(2)}, u32[]{:S(2)}) collective-permute-start(bf16[48,2048]{1,0:T(8,128)(2,1)S(1)} %get-tuple-element.115), channel_id=1, source_target_pairs={{0,8},{4,12},{8,0},{12,4},{1,9},{5,13},{9,1},{13,5},{2,10},{6,14},... | collective-permute-start | bytes 589832 | tf_op jit(solution)/shard_map/far1/ppermute | solution.py:75
  20.2 16.7 %collective-permute-start.4 = (bf16[96,2048]{1,0:T(8,128)(2,1)S(1)}, bf16[96,2048]{1,0:T(8,128)(2,1)S(1)}, u32[]{:S(2)}, u32[]{:S(2)}) collective-permute-start(bf16[96,2048]{1,0:T(8,128)(2,1)S(1)} %pad_maximum_fusion.3), channel_id=1, source_target_pairs={{0,4},{1,0},{2,6},{3,2},{4,5},{5,1},{6,7},{7,3},{8,12},{9,8},{10,1... | collective-permute-start | bytes 1179656 | tf_op jit(solution)/shard_map/arr0/ppermute | solution.py:95
  22.4 14.4 %collective-permute-start.5 = (bf16[96,2048]{1,0:T(8,128)(2,1)S(1)}, bf16[96,2048]{1,0:T(8,128)(2,1)S(1)}, u32[]{:S(2)}, u32[]{:S(2)}) collective-permute-start(bf16[96,2048]{1,0:T(8,128)(2,1)S(1)} %pad_maximum_fusion.3), channel_id=1, source_target_pairs={{1,4},{3,6},{4,1},{6,3},{9,12},{11,14},{12,9},{14,11},{17,20},{19,... | collective-permute-start | bytes 1179656 | tf_op jit(solution)/shard_map/arr0/ppermute | solution.py:95
  34.1 9.6 %collective-permute-start.6 = (bf16[48,2048]{1,0:T(8,128)(2,1)S(1)}, bf16[48,2048]{1,0:T(8,128)(2,1)S(1)}, u32[]{:S(2)}, u32[]{:S(2)}) collective-permute-start(bf16[48,2048]{1,0:T(8,128)(2,1)S(1)} %broadcast_select_fusion.17), channel_id=1, source_target_pairs={{0,2},{1,3},{2,0},{3,1},{4,6},{5,7},{6,4},{7,5},{8,10},{9,11},{10,... | collective-permute-start | bytes 589832 | tf_op jit(solution)/shard_map/sel1/ppermute | solution.py:71
  34.4 14.2 %collective-permute-start.3 = (bf16[32,2048]{1,0:T(8,128)(2,1)S(1)}, bf16[32,2048]{1,0:T(8,128)(2,1)S(1)}, u32[]{:S(2)}, u32[]{:S(2)}) collective-permute-start(bf16[32,2048]{1,0:T(8,128)(2,1)S(1)} %get-tuple-element.124), channel_id=1, source_target_pairs={{0,8},{4,12},{8,0},{12,4},{1,9},{5,13},{9,1},{13,5},{2,10},{6,14},... | collective-permute-start | bytes 393224 | tf_op jit(solution)/shard_map/far2/ppermute | solution.py:75
  43.8 11.1 %collective-permute-start.11 = (bf16[96,2048]{1,0:T(8,128)(2,1)S(1)}, bf16[96,2048]{1,0:T(8,128)(2,1)S(1)}, u32[]{:S(2)}, u32[]{:S(2)}) collective-permute-start(bf16[96,2048]{1,0:T(8,128)(2,1)S(1)} %pad_maximum_fusion.4), channel_id=1, source_target_pairs={{1,4},{3,6},{4,1},{6,3},{9,12},{11,14},{12,9},{14,11},{17,20},{19,... | collective-permute-start | bytes 1179656 | tf_op jit(solution)/shard_map/arr1/ppermute | solution.py:95
  46.3 19.5 %collective-permute-start.12 = (bf16[192,1024]{1,0:T(8,128)(2,1)S(1)}, bf16[192,1024]{1,0:T(8,128)(2,1)S(1)}, u32[]{:S(2)}, u32[]{:S(2)}) collective-permute-start(bf16[192,1024]{1,0:T(8,128)(2,1)S(1)} %get-tuple-element.129), channel_id=1, source_target_pairs={{0,2},{1,3},{2,0},{3,1},{4,6},{5,7},{6,4},{7,5},{8,10},{9,11},{10,... | collective-permute-start | bytes 1179656 | tf_op jit(solution)/shard_map/b0/ppermute | solution.py:71
  48.6 17.2 %collective-permute-start.13 = (bf16[192,1024]{1,0:T(8,128)(2,1)S(1)}, bf16[192,1024]{1,0:T(8,128)(2,1)S(1)}, u32[]{:S(2)}, u32[]{:S(2)}) collective-permute-start(bf16[192,1024]{1,0:T(8,128)(2,1)S(1)} %get-tuple-element.137), channel_id=1, source_target_pairs={{0,2},{1,3},{2,0},{3,1},{4,6},{5,7},{6,4},{7,5},{8,10},{9,11},{10,... | collective-permute-start | bytes 1179656 | tf_op jit(solution)/shard_map/b0/ppermute | solution.py:71
  49.9 18.4 %collective-permute-start.9 = (bf16[32,2048]{1,0:T(8,128)(2,1)S(1)}, bf16[32,2048]{1,0:T(8,128)(2,1)S(1)}, u32[]{:S(2)}, u32[]{:S(2)}) collective-permute-start(bf16[32,2048]{1,0:T(8,128)(2,1)S(1)} %broadcast_select_fusion.20), channel_id=1, source_target_pairs={{0,2},{1,3},{2,0},{3,1},{4,6},{5,7},{6,4},{7,5},{8,10},{9,11},{10,... | collective-permute-start | bytes 393224 | tf_op jit(solution)/shard_map/sel2/ppermute | solution.py:71
  59.3 13.1 %collective-permute-start.16 = (bf16[2,192,1024]{2,1,0:T(8,128)(2,1)S(1)}, bf16[2,192,1024]{2,1,0:T(8,128)(2,1)S(1)}, u32[]{:S(2)}, u32[]{:S(2)}) collective-permute-start(bf16[2,192,1024]{2,1,0:T(8,128)(2,1)S(1)} %c1.1), channel_id=1, source_target_pairs={{0,1},{1,0},{2,3},{3,2},{4,5},{5,4},{6,7},{7,6},{8,9},{9,8},{10,11... | collective-permute-start | bytes 2359304 | tf_op jit(solution)/shard_map/c1/ppermute | solution.py:71
  66.1 18.3 %collective-permute-start.19 = (bf16[192,1024]{1,0:T(8,128)(2,1)S(1)}, bf16[192,1024]{1,0:T(8,128)(2,1)S(1)}, u32[]{:S(2)}, u32[]{:S(2)}) collective-permute-start(bf16[192,1024]{1,0:T(8,128)(2,1)S(1)} %hide0.1.one), channel_id=1, source_target_pairs={{0,1},{1,0},{2,3},{3,2},{4,5},{5,4},{6,7},{7,6},{8,9},{9,8},{10,11... | collective-permute-start | bytes 1179656 | tf_op jit(solution)/shard_map/hide0/ppermute | solution.py:71
  66.2 20.8 %collective-permute-start.25 = (bf16[192,1024]{1,0:T(8,128)(2,1)S(1)}, bf16[192,1024]{1,0:T(8,128)(2,1)S(1)}, u32[]{:S(2)}, u32[]{:S(2)}) collective-permute-start(bf16[192,1024]{1,0:T(8,128)(2,1)S(1)} %hide0.1.one), channel_id=1, source_target_pairs={{0,2},{1,3},{2,0},{3,1},{4,6},{5,7},{6,4},{7,5},{8,10},{9,11},{10,... | collective-permute-start | bytes 1179656 | tf_op jit(solution)/shard_map/hide0/ppermute | solution.py:71
  72.4 20.9 %collective-permute-start.18 = (bf16[192,1024]{1,0:T(8,128)(2,1)S(1)}, bf16[192,1024]{1,0:T(8,128)(2,1)S(1)}, u32[]{:S(2)}, u32[]{:S(2)}) collective-permute-start(bf16[192,1024]{1,0:T(8,128)(2,1)S(1)} %get-tuple-element.140), channel_id=1, source_target_pairs={{0,2},{1,3},{2,0},{3,1},{4,6},{5,7},{6,4},{7,5},{8,10},{9,11},{10,... | collective-permute-start | bytes 1179656 | tf_op jit(solution)/shard_map/b1/ppermute | solution.py:71
  75.7 17.6 %collective-permute-start.20 = (bf16[192,1024]{1,0:T(8,128)(2,1)S(1)}, bf16[192,1024]{1,0:T(8,128)(2,1)S(1)}, u32[]{:S(2)}, u32[]{:S(2)}) collective-permute-start(bf16[192,1024]{1,0:T(8,128)(2,1)S(1)} %get-tuple-element.150), channel_id=1, source_target_pairs={{0,2},{1,3},{2,0},{3,1},{4,6},{5,7},{6,4},{7,5},{8,10},{9,11},{10,... | collective-permute-start | bytes 1179656 | tf_op jit(solution)/shard_map/b1/ppermute | solution.py:71
  78.8 16.5 %collective-permute-start.21 = (bf16[2,128,1024]{2,1,0:T(8,128)(2,1)S(1)}, bf16[2,128,1024]{2,1,0:T(8,128)(2,1)S(1)}, u32[]{:S(2)}, u32[]{:S(2)}) collective-permute-start(bf16[2,128,1024]{2,1,0:T(8,128)(2,1)S(1)} %a2.1), channel_id=1, source_target_pairs={{0,1},{1,0},{2,3},{3,2},{4,5},{5,4},{6,7},{7,6},{8,9},{9,8},{10,11... | collective-permute-start | bytes 1572872 | tf_op jit(solution)/shard_map/a2/ppermute | solution.py:71
  84.4 13.6 %collective-permute-start.22 = (bf16[2,128,1024]{2,1,0:T(8,128)(2,1)S(1)}, bf16[2,128,1024]{2,1,0:T(8,128)(2,1)S(1)}, u32[]{:S(2)}, u32[]{:S(2)}) collective-permute-start(bf16[2,128,1024]{2,1,0:T(8,128)(2,1)S(1)} %c2.1), channel_id=1, source_target_pairs={{0,1},{1,0},{2,3},{3,2},{4,5},{5,4},{6,7},{7,6},{8,9},{9,8},{10,11... | collective-permute-start | bytes 1572872 | tf_op jit(solution)/shard_map/c2/ppermute | solution.py:71
  87.0 18.5 %collective-permute-start.27 = (bf16[192,1024]{1,0:T(8,128)(2,1)S(1)}, bf16[192,1024]{1,0:T(8,128)(2,1)S(1)}, u32[]{:S(2)}, u32[]{:S(2)}) collective-permute-start(bf16[192,1024]{1,0:T(8,128)(2,1)S(1)} %collective-permute-done.25.one), channel_id=1, source_target_pairs={{0,1},{1,0},{2,3},{3,2},{4,5},{5,4},{6,7},{7,6},{8,9},{9,8},{10,11... | collective-permute-start | bytes 1179656 | tf_op jit(solution)/shard_map/forward0/ppermute | solution.py:71
  93.7 9.8 %collective-permute-start.26 = (bf16[192,1024]{1,0:T(8,128)(2,1)S(1)}, bf16[192,1024]{1,0:T(8,128)(2,1)S(1)}, u32[]{:S(2)}, u32[]{:S(2)}) collective-permute-start(bf16[192,1024]{1,0:T(8,128)(2,1)S(1)} %hide1.1.one), channel_id=1, source_target_pairs={{0,1},{1,0},{2,3},{3,2},{4,5},{5,4},{6,7},{7,6},{8,9},{9,8},{10,11... | collective-permute-start | bytes 1179656 | tf_op jit(solution)/shard_map/hide1/ppermute | solution.py:71
  95.0 12.6 %collective-permute-start.24 = (bf16[192,1024]{1,0:T(8,128)(2,1)S(1)}, bf16[192,1024]{1,0:T(8,128)(2,1)S(1)}, u32[]{:S(2)}, u32[]{:S(2)}) collective-permute-start(bf16[192,1024]{1,0:T(8,128)(2,1)S(1)} %hide1.1.one), channel_id=1, source_target_pairs={{0,2},{1,3},{2,0},{3,1},{4,6},{5,7},{6,4},{7,5},{8,10},{9,11},{10,... | collective-permute-start | bytes 1179656 | tf_op jit(solution)/shard_map/hide1/ppermute | solution.py:71
  96.8 22.3 %collective-permute-start.23 = (bf16[2,128,1024]{2,1,0:T(8,128)(2,1)S(1)}, bf16[2,128,1024]{2,1,0:T(8,128)(2,1)S(1)}, u32[]{:S(2)}, u32[]{:S(2)}) collective-permute-start(bf16[2,128,1024]{2,1,0:T(8,128)(2,1)S(1)} %b2.1), channel_id=1, source_target_pairs={{0,2},{1,3},{2,0},{3,1},{4,6},{5,7},{6,4},{7,5},{8,10},{9,11},{10,... | collective-permute-start | bytes 1572872 | tf_op jit(solution)/shard_map/b2/ppermute | solution.py:71
  109.0 10.3 %collective-permute-start.31 = (bf16[96,2048]{1,0:T(8,128)(2,1)S(1)}, bf16[96,2048]{1,0:T(8,128)(2,1)S(1)}, u32[]{:S(2)}, u32[]{:S(2)}) collective-permute-start(bf16[96,2048]{1,0:T(8,128)(2,1)S(1)} %get-tuple-element.161), channel_id=1, source_target_pairs={{0,1},{1,5},{2,3},{3,7},{4,0},{5,4},{6,2},{7,6},{8,9},{9,13},{10,1... | collective-permute-start | bytes 1179656 | tf_op jit(solution)/shard_map/out0/ppermute | solution.py:95
  110.6 9.8 %collective-permute-start.32 = (bf16[96,2048]{1,0:T(8,128)(2,1)S(1)}, bf16[96,2048]{1,0:T(8,128)(2,1)S(1)}, u32[]{:S(2)}, u32[]{:S(2)}) collective-permute-start(bf16[96,2048]{1,0:T(8,128)(2,1)S(1)} %get-tuple-element.168), channel_id=1, source_target_pairs={{1,4},{3,6},{4,1},{6,3},{9,12},{11,14},{12,9},{14,11},{17,20},{19,... | collective-permute-start | bytes 1179656 | tf_op jit(solution)/shard_map/out0/ppermute | solution.py:95
  115.5 13.6 %collective-permute-start.33 = (bf16[96,2048]{1,0:T(8,128)(2,1)S(1)}, bf16[96,2048]{1,0:T(8,128)(2,1)S(1)}, u32[]{:S(2)}, u32[]{:S(2)}) collective-permute-start(bf16[96,2048]{1,0:T(8,128)(2,1)S(1)} %get-tuple-element.171), channel_id=1, source_target_pairs={{1,4},{3,6},{4,1},{6,3},{9,12},{11,14},{12,9},{14,11},{17,20},{19,... | collective-permute-start | bytes 1179656 | tf_op jit(solution)/shard_map/out1/ppermute | solution.py:95
  119.3 11.0 %collective-permute-start.34 = (bf16[128,1024]{1,0:T(8,128)(2,1)S(1)}, bf16[128,1024]{1,0:T(8,128)(2,1)S(1)}, u32[]{:S(2)}, u32[]{:S(2)}) collective-permute-start(bf16[128,1024]{1,0:T(8,128)(2,1)S(1)} %hide2.1.one), channel_id=1, source_target_pairs={{0,1},{1,0},{2,3},{3,2},{4,5},{5,4},{6,7},{7,6},{8,9},{9,8},{10,11... | collective-permute-start | bytes 786440 | tf_op jit(solution)/shard_map/hide2/ppermute | solution.py:71
  119.4 10.9 %collective-permute-start.29 = (bf16[128,1024]{1,0:T(8,128)(2,1)S(1)}, bf16[128,1024]{1,0:T(8,128)(2,1)S(1)}, u32[]{:S(2)}, u32[]{:S(2)}) collective-permute-start(bf16[128,1024]{1,0:T(8,128)(2,1)S(1)} %hide2.1.one), channel_id=1, source_target_pairs={{0,2},{1,3},{2,0},{3,1},{4,6},{5,7},{6,4},{7,5},{8,10},{9,11},{10,... | collective-permute-start | bytes 786440 | tf_op jit(solution)/shard_map/hide2/ppermute | solution.py:71
  121.2 14.5 %collective-permute-start.37 = (bf16[48,2048]{1,0:T(8,128)(2,1)S(1)}, bf16[48,2048]{1,0:T(8,128)(2,1)S(1)}, u32[]{:S(2)}, u32[]{:S(2)}) collective-permute-start(bf16[48,2048]{1,0:T(8,128)(2,1)S(1)} %get-tuple-element.169), channel_id=1, source_target_pairs={{0,2},{1,3},{2,0},{3,1},{4,6},{5,7},{6,4},{7,5},{8,10},{9,11},{10,... | collective-permute-start | bytes 589832 | tf_op jit(solution)/shard_map/mix0/ppermute | solution.py:71
  129.9 19.2 %collective-permute-start.40 = (bf16[48,2048]{1,0:T(8,128)(2,1)S(1)}, bf16[48,2048]{1,0:T(8,128)(2,1)S(1)}, u32[]{:S(2)}, u32[]{:S(2)}) collective-permute-start(bf16[48,2048]{1,0:T(8,128)(2,1)S(1)} %get-tuple-element.172), channel_id=1, source_target_pairs={{0,2},{1,3},{2,0},{3,1},{4,6},{5,7},{6,4},{7,5},{8,10},{9,11},{10,... | collective-permute-start | bytes 589832 | tf_op jit(solution)/shard_map/mix1/ppermute | solution.py:71
  135.6 11.9 %collective-permute-start.38 = (bf16[64,2048]{1,0:T(8,128)(2,1)S(1)}, bf16[64,2048]{1,0:T(8,128)(2,1)S(1)}, u32[]{:S(2)}, u32[]{:S(2)}) collective-permute-start(bf16[64,2048]{1,0:T(8,128)(2,1)S(1)} %get-tuple-element.182), channel_id=1, source_target_pairs={{1,4},{3,6},{4,1},{6,3},{9,12},{11,14},{12,9},{14,11},{17,20},{19,... | collective-permute-start | bytes 786440 | tf_op jit(solution)/shard_map/out2/ppermute | solution.py:95
  138.7 15.2 %collective-permute-start.43 = (bf16[48,2048]{1,0:T(8,128)(2,1)S(1)}, bf16[48,2048]{1,0:T(8,128)(2,1)S(1)}, u32[]{:S(2)}, u32[]{:S(2)}) collective-permute-start(bf16[48,2048]{1,0:T(8,128)(2,1)S(1)} %get-tuple-element.180), channel_id=1, source_target_pairs={{0,8},{4,12},{8,0},{12,4},{1,9},{5,13},{9,1},{13,5},{2,10},{6,14},... | collective-permute-start | bytes 589832 | tf_op jit(solution)/shard_map/far_out0/ppermute | solution.py:75
  149.8 11.8 %collective-permute-start.42 = (bf16[48,2048]{1,0:T(8,128)(2,1)S(1)}, bf16[48,2048]{1,0:T(8,128)(2,1)S(1)}, u32[]{:S(2)}, u32[]{:S(2)}) collective-permute-start(bf16[48,2048]{1,0:T(8,128)(2,1)S(1)} %get-tuple-element.187), channel_id=1, source_target_pairs={{0,8},{4,12},{8,0},{12,4},{1,9},{5,13},{9,1},{13,5},{2,10},{6,14},... | collective-permute-start | bytes 589832 | tf_op jit(solution)/shard_map/far_out1/ppermute | solution.py:75
  153.1 11.2 %collective-permute-start.41 = (bf16[32,2048]{1,0:T(8,128)(2,1)S(1)}, bf16[32,2048]{1,0:T(8,128)(2,1)S(1)}, u32[]{:S(2)}, u32[]{:S(2)}) collective-permute-start(bf16[32,2048]{1,0:T(8,128)(2,1)S(1)} %get-tuple-element.190), channel_id=1, source_target_pairs={{0,8},{4,12},{8,0},{12,4},{1,9},{5,13},{9,1},{13,5},{2,10},{6,14},... | collective-permute-start | bytes 393224 | tf_op jit(solution)/shard_map/far_out2/ppermute | solution.py:75
  (14 other events, 75.5 us)

commit v12 on v8

--- a/solution.py
+++ b/solution.py
@@ -7,7 +7,7 @@
 from jax.experimental.pallas import tpu as pltpu
 from jax.sharding import PartitionSpec as P
 
-ROWS = (48, 48, 32)
+ROWS = (32, 48, 48)
 ORDER = (
     "far0", "load3", "sel0", "far1", "load1", "arr0", "load2", "load0", "sel1", "far2", "take0", "a0", "c0",
     "b0", "arr1", "d0", "sel2", "take1", "a1", "c1", "hide0", "b1", "arr2", "d1", "take2", "a2", "c2",

time: 164 us -> 161 us (0.982)
  waiting for transfers between devices: 48.1 us -> 43.7 us
    ppermute x26, starting transfers between devices: 13.4 us -> 17.7 us  [over_seq(): return lax.ppermute(array, 'seq', [(i, i ^ bit) for i in range(4)])]
    ppermute x26, waiting for transfers between devices: 15.2 us -> 11.8 us  [over_seq(): return lax.ppermute(array, 'seq', [(i, i ^ bit) for i in range(4)])]
    ppermute x6, starting transfers between devices: 9.85 us -> 7.26 us  [over_tp(): return lax.ppermute(array, 'tp', [(i, i ^ bit) for i in range(4)])]
  transfers between devices with their start and end apart: 44 -> 44, of which waited for: 14 -> 15; matrix products, arithmetic and copies ran while one was open for 1% -> 1% of each run, Pallas kernels for 38% -> 39%
where the time goes in v12:
time: 161 us; the launch traced here: 160 us
  Pallas kernels  63.2 us (39%)
  starting transfers between devices  49.4 us (31%)
  waiting for transfers between devices  43.7 us (27%)
  local copies, waits for them, and re-layouts  1.73 us (1%)
    ppermute x12, starting transfers between devices, over_both(): return lax.ppermute(array, ('tp', 'seq'), pairs)  24.4 us
    pallas_call x12, Pallas kernels, sums(): pl.pallas_call(functools.partial(sums_kernel, got is not None, split), ou...  21.4 us
    ppermute x12, waiting for transfers between devices, over_both(): return lax.ppermute(array, ('tp', 'seq'), pairs)  18.3 us
    ppermute x26, starting transfers between devices, over_seq(): return lax.ppermute(array, 'seq', [(i, i ^ bit) for i in range(4)])  17.7 us
    pallas_call x4, Pallas kernels, load(): pl.pallas_call(load_kernel, out_shape=jax.ShapeDtypeStruct((2, deep, widt...  14 us
    ppermute x6, waiting for transfers between devices, over_tp(): return lax.ppermute(array, 'tp', [(i, i ^ bit) for i in range(4)])  13.6 us
    ppermute x26, waiting for transfers between devices, over_seq(): return lax.ppermute(array, 'seq', [(i, i ^ bit) for i in range(4)])  11.8 us
    pallas_call x6, Pallas kernels, products(): pl.pallas_call(functools.partial(products_kernel, total is not None), out...  10.9 us
  transfers between devices with their start and end apart: 44, of which 15 were waited for; matrix products, arithmetic and copies ran while one was open for 1% of the time, Pallas kernels for 39%

profile of v12, /device:TPU:1, one launch (start us, length us, event | category | flops | bytes accessed | tf_op | source)
XLA Modules:
  0.0 160.3 jit_solution(5619725479996844373)
XLA Ops:
  2.8 3.2 %collective-permute-start = (bf16[32,2048]{1,0:T(8,128)(2,1)S(1)}, bf16[32,2048]{1,0:T(8,128)(2,1)S(1)}, u32[]{:S(2)}, u32[]{:S(2)}) collective-permute-start(bf16[32,2048]{1,0:T(8,128)(2,1)S(1)} %get-tuple-element.109), channel_id=1, source_target_pairs={{0,8},{4,12},{8,0},{12,4},{1,9},{5,13},{9,1},{13,5},{2,10},{6,14},... | collective-permute-start | bytes 393224 | tf_op jit(solution)/shard_map/far0/ppermute | solution.py:75
  6.2 3.5 %load3.1.weights = bf16[2,2048,1024]{2,1,0:T(8,128)(2,1)S(1)} custom-call(s32[1]{0:T(128)} %bitcast.7.quarter, bf16[2048,4096]{1,0:T(8,128)(2,1)} %gate_weight.3, bf16[2048,4096]{1,0:T(8,128)(2,1)} %up_weight.7), custom_call_target="tpu_custom_call" | custom-call | flops 1073741824 | bytes 1 | tf_op jit(solution)/shard_map/load3/pallas_call | solution.py:121
  9.7 2.4 %collective-permute-done = bf16[32,2048]{1,0:T(8,128)(2,1)S(1)} collective-permute-done((bf16[32,2048]{1,0:T(8,128)(2,1)S(1)}, bf16[32,2048]{1,0:T(8,128)(2,1)S(1)}, u32[]{:S(2)}, u32[]{:S(2)}) %collective-permute-start) | collective-permute-done | bytes 131104 | tf_op jit(solution)/shard_map/far0/ppermute | solution.py:75
  13.1 3.5 %load1.1.weights = bf16[2,2048,1024]{2,1,0:T(8,128)(2,1)S(1)} custom-call(s32[1]{0:T(128)} %bitcast.5.quarter, bf16[2048,4096]{1,0:T(8,128)(2,1)} %gate_weight.3, bf16[2048,4096]{1,0:T(8,128)(2,1)} %up_weight.7), custom_call_target="tpu_custom_call" | custom-call | flops 1073741824 | bytes 1 | tf_op jit(solution)/shard_map/load1/pallas_call | solution.py:121
  18.6 5.6 %collective-permute-start.5 = (bf16[64,2048]{1,0:T(8,128)(2,1)S(1)}, bf16[64,2048]{1,0:T(8,128)(2,1)S(1)}, u32[]{:S(2)}, u32[]{:S(2)}) collective-permute-start(bf16[64,2048]{1,0:T(8,128)(2,1)S(1)} %pad_maximum_fusion.5), channel_id=1, source_target_pairs={{1,4},{3,6},{4,1},{6,3},{9,12},{11,14},{12,9},{14,11},{17,20},{19,... | collective-permute-start | bytes 786440 | tf_op jit(solution)/shard_map/arr0/ppermute | solution.py:95
  24.2 3.5 %load2.1.weights = bf16[2,2048,1024]{2,1,0:T(8,128)(2,1)S(1)} custom-call(s32[1]{0:T(128)} %bitcast.6.quarter, bf16[2048,4096]{1,0:T(8,128)(2,1)} %gate_weight.3, bf16[2048,4096]{1,0:T(8,128)(2,1)} %up_weight.7), custom_call_target="tpu_custom_call" | custom-call | flops 1073741824 | bytes 1 | tf_op jit(solution)/shard_map/load2/pallas_call | solution.py:121
  27.7 3.5 %load0.1.weights = bf16[2,2048,1024]{2,1,0:T(8,128)(2,1)S(1)} custom-call(s32[1]{0:T(128)} %bitcast.4.quarter, bf16[2048,4096]{1,0:T(8,128)(2,1)} %gate_weight.3, bf16[2048,4096]{1,0:T(8,128)(2,1)} %up_weight.7), custom_call_target="tpu_custom_call" | custom-call | flops 1073741824 | bytes 1 | tf_op jit(solution)/shard_map/load0/pallas_call | solution.py:121
  38.0 2.3 %collective-permute-start.11 = (bf16[96,2048]{1,0:T(8,128)(2,1)S(1)}, bf16[96,2048]{1,0:T(8,128)(2,1)S(1)}, u32[]{:S(2)}, u32[]{:S(2)}) collective-permute-start(bf16[96,2048]{1,0:T(8,128)(2,1)S(1)} %pad_maximum_fusion.3), channel_id=1, source_target_pairs={{1,4},{3,6},{4,1},{6,3},{9,12},{11,14},{12,9},{14,11},{17,20},{19,... | collective-permute-start | bytes 1179656 | tf_op jit(solution)/shard_map/arr1/ppermute | solution.py:95
  44.3 3.6 %collective-permute-done.10 = bf16[96,2048]{1,0:T(8,128)(2,1)S(1)} collective-permute-done((bf16[96,2048]{1,0:T(8,128)(2,1)S(1)}, bf16[96,2048]{1,0:T(8,128)(2,1)S(1)}, u32[]{:S(2)}, u32[]{:S(2)}) %collective-permute-start.10) | collective-permute-done | bytes 393248 | tf_op jit(solution)/shard_map/arr1/ppermute | solution.py:95
  50.1 2.0 %a1.1 = bf16[2,192,1024]{2,1,0:T(8,128)(2,1)S(1)} custom-call(bf16[192,2048]{1,0:T(8,128)(2,1)S(1)} %pad_maximum_fusion.some, bf16[2,2048,1024]{2,1,0:T(8,128)(2,1)S(1)} %load3.1.weights), custom_call_target="tpu_custom_call" | custom-call | flops 17179869184 | bytes 1 | tf_op jit(solution)/shard_map/a1/pallas_call | solution.py:150
  52.1 2.0 %c1.1 = bf16[2,192,1024]{2,1,0:T(8,128)(2,1)S(1)} custom-call(bf16[192,2048]{1,0:T(8,128)(2,1)S(1)} %pad_maximum_fusion.some, bf16[2,2048,1024]{2,1,0:T(8,128)(2,1)S(1)} %load1.1.weights), custom_call_target="tpu_custom_call" | custom-call | flops 17179869184 | bytes 1 | tf_op jit(solution)/shard_map/c1/pallas_call | solution.py:150
  58.9 2.7 %collective-permute-start.17 = (bf16[96,2048]{1,0:T(8,128)(2,1)S(1)}, bf16[96,2048]{1,0:T(8,128)(2,1)S(1)}, u32[]{:S(2)}, u32[]{:S(2)}) collective-permute-start(bf16[96,2048]{1,0:T(8,128)(2,1)S(1)} %pad_maximum_fusion.4), channel_id=1, source_target_pairs={{1,4},{3,6},{4,1},{6,3},{9,12},{11,14},{12,9},{14,11},{17,20},{19,... | collective-permute-start | bytes 1179656 | tf_op jit(solution)/shard_map/arr2/ppermute | solution.py:95
  62.9 2.0 %d1.1.held = f32[2,192,1024]{2,1,0:T(8,128)S(1)} custom-call(bf16[192,2048]{1,0:T(8,128)(2,1)S(1)} %pad_maximum_fusion.some, bf16[2,2048,1024]{2,1,0:T(8,128)(2,1)S(1)} %load0.1.weights, bf16[2,192,1024]{2,1,0:T(8,128)(2,1)S(1)} %collective-permute-done.16.rest_0_), custom_call_target="tpu_custom_call" | custom-call | flops 17179869184 | bytes 1 | tf_op jit(solution)/shard_map/d1/pallas_call | solution.py:150
  67.2 2.2 %collective-permute-done.17 = bf16[96,2048]{1,0:T(8,128)(2,1)S(1)} collective-permute-done((bf16[96,2048]{1,0:T(8,128)(2,1)S(1)}, bf16[96,2048]{1,0:T(8,128)(2,1)S(1)}, u32[]{:S(2)}, u32[]{:S(2)}) %collective-permute-start.17) | collective-permute-done | bytes 393248 | tf_op jit(solution)/shard_map/arr2/ppermute | solution.py:95
  69.7 2.0 %a2.1 = bf16[2,192,1024]{2,1,0:T(8,128)(2,1)S(1)} custom-call(bf16[192,2048]{1,0:T(8,128)(2,1)S(1)} %pad_maximum_fusion.1.some, bf16[2,2048,1024]{2,1,0:T(8,128)(2,1)S(1)} %load3.1.weights), custom_call_target="tpu_custom_call" | custom-call | flops 17179869184 | bytes 1 | tf_op jit(solution)/shard_map/a2/pallas_call | solution.py:150
  71.7 2.0 %c2.1 = bf16[2,192,1024]{2,1,0:T(8,128)(2,1)S(1)} custom-call(bf16[192,2048]{1,0:T(8,128)(2,1)S(1)} %pad_maximum_fusion.1.some, bf16[2,2048,1024]{2,1,0:T(8,128)(2,1)S(1)} %load1.1.weights), custom_call_target="tpu_custom_call" | custom-call | flops 17179869184 | bytes 1 | tf_op jit(solution)/shard_map/c2/pallas_call | solution.py:150
  73.7 4.0 %down0.1.weights = bf16[2,1024,2048]{2,1,0:T(8,128)(2,1)S(1)} custom-call(s32[2]{0:T(128)S(1)} %get-tuple-element.143.quarters, bf16[4096,2048]{1,0:T(8,128)(2,1)} %weight.1), custom_call_target="tpu_custom_call" | custom-call | flops 17179869184 | bytes 1 | tf_op jit(solution)/shard_map/down0/pallas_call | solution.py:181
  82.8 2.0 %b2.1 = bf16[2,192,1024]{2,1,0:T(8,128)(2,1)S(1)} custom-call(bf16[192,2048]{1,0:T(8,128)(2,1)S(1)} %pad_maximum_fusion.1.some, bf16[2,2048,1024]{2,1,0:T(8,128)(2,1)S(1)} %load2.1.weights, bf16[2,192,1024]{2,1,0:T(8,128)(2,1)S(1)} %collective-permute-done.21.rest_0_), custom_call_target="tpu_custom_call" | custom-call | flops 17179869184 | bytes 1 | tf_op jit(solution)/shard_map/b2/pallas_call | solution.py:150
  85.1 2.0 %d2.1.held = f32[2,192,1024]{2,1,0:T(8,128)S(1)} custom-call(bf16[192,2048]{1,0:T(8,128)(2,1)S(1)} %pad_maximum_fusion.1.some, bf16[2,2048,1024]{2,1,0:T(8,128)(2,1)S(1)} %load0.1.weights, bf16[2,192,1024]{2,1,0:T(8,128)(2,1)S(1)} %collective-permute-done.22.rest_0_), custom_call_target="tpu_custom_call" | custom-call | flops 17179869184 | bytes 1 | tf_op jit(solution)/shard_map/d2/pallas_call | solution.py:150
  87.1 4.0 %down2.1.weights = bf16[2,1024,2048]{2,1,0:T(8,128)(2,1)S(1)} custom-call(s32[2]{0:T(128)S(1)} %get-tuple-element.154.quarters, bf16[4096,2048]{1,0:T(8,128)(2,1)} %weight.1), custom_call_target="tpu_custom_call" | custom-call | flops 17179869184 | bytes 1 | tf_op jit(solution)/shard_map/down2/pallas_call | solution.py:181
  95.0 2.0 %own1.1.rest_0_ = f32[192,2048]{1,0:T(8,128)S(1)} custom-call(bf16[192,1024]{1,0:T(8,128)(2,1)S(1)} %hide1.1.one, bf16[192,1024]{1,0:T(8,128)(2,1)S(1)} %collective-permute-done.27.two, bf16[2,1024,2048]{2,1,0:T(8,128)(2,1)S(1)} %down0.1.weights), custom_call_target="tpu_custom_call" | custom-call | flops 17179869184 | bytes 1 | tf_op jit(solution)/shard_map/own1/pallas_call | solution.py:204
  97.0 2.7 %collective-permute-start.32 = (bf16[64,2048]{1,0:T(8,128)(2,1)S(1)}, bf16[64,2048]{1,0:T(8,128)(2,1)S(1)}, u32[]{:S(2)}, u32[]{:S(2)}) collective-permute-start(bf16[64,2048]{1,0:T(8,128)(2,1)S(1)} %get-tuple-element.166), channel_id=1, source_target_pairs={{1,4},{3,6},{4,1},{6,3},{9,12},{11,14},{12,9},{14,11},{17,20},{19,... | collective-permute-start | bytes 786440 | tf_op jit(solution)/shard_map/out0/ppermute | solution.py:95
  99.7 2.0 %rest1.1.partial_sum = f32[192,2048]{1,0:T(8,128)S(1)} custom-call(bf16[192,1024]{1,0:T(8,128)(2,1)S(1)} %collective-permute-done.24.one, bf16[192,1024]{1,0:T(8,128)(2,1)S(1)} %collective-permute-done.28.two, bf16[2,1024,2048]{2,1,0:T(8,128)(2,1)S(1)} %down2.1.weights, f32[192,2048]{1,0:T(8,128)S(1)} %own1.1.rest_0_), custom_call_target="tpu_custom_call" | custom-call | flops 17179869184 | bytes 1 | tf_op jit(solution)/shard_map/rest1/pallas_call | solution.py:204
  102.6 2.8 %collective-permute-start.33 = (bf16[96,2048]{1,0:T(8,128)(2,1)S(1)}, bf16[96,2048]{1,0:T(8,128)(2,1)S(1)}, u32[]{:S(2)}, u32[]{:S(2)}) collective-permute-start(bf16[96,2048]{1,0:T(8,128)(2,1)S(1)} %get-tuple-element.169), channel_id=1, source_target_pairs={{1,4},{3,6},{4,1},{6,3},{9,12},{11,14},{12,9},{14,11},{17,20},{19,... | collective-permute-start | bytes 1179656 | tf_op jit(solution)/shard_map/out1/ppermute | solution.py:95
  105.4 2.8 %collective-permute-done.23.rest_0_ = bf16[2,192,1024]{2,1,0:T(8,128)(2,1)S(1)} collective-permute-done((bf16[2,192,1024]{2,1,0:T(8,128)(2,1)S(1)}, bf16[2,192,1024]{2,1,0:T(8,128)(2,1)S(1)}, u32[]{:S(2)}, u32[]{:S(2)}) %collective-permute-start.23) | collective-permute-done | bytes 786464 | tf_op jit(solution)/shard_map/b2/ppermute | solution.py:71
  114.6 5.7 %collective-permute-done.29.one = bf16[192,1024]{1,0:T(8,128)(2,1)S(1)} collective-permute-done((bf16[192,1024]{1,0:T(8,128)(2,1)S(1)}, bf16[192,1024]{1,0:T(8,128)(2,1)S(1)}, u32[]{:S(2)}, u32[]{:S(2)}) %collective-permute-start.29) | collective-permute-done | bytes 393248 | tf_op jit(solution)/shard_map/hide2/ppermute | solution.py:71
  121.7 2.0 %own2.1.rest_0_ = f32[192,2048]{1,0:T(8,128)S(1)} custom-call(bf16[192,1024]{1,0:T(8,128)(2,1)S(1)} %hide2.1.one, bf16[192,1024]{1,0:T(8,128)(2,1)S(1)} %collective-permute-done.34.two, bf16[2,1024,2048]{2,1,0:T(8,128)(2,1)S(1)} %down0.1.weights), custom_call_target="tpu_custom_call" | custom-call | flops 17179869184 | bytes 1 | tf_op jit(solution)/shard_map/own2/pallas_call | solution.py:204
  123.7 2.0 %rest2.1.partial_sum = f32[192,2048]{1,0:T(8,128)S(1)} custom-call(bf16[192,1024]{1,0:T(8,128)(2,1)S(1)} %collective-permute-done.29.one, bf16[192,1024]{1,0:T(8,128)(2,1)S(1)} %collective-permute-done.35.two, bf16[2,1024,2048]{2,1,0:T(8,128)(2,1)S(1)} %down2.1.weights, f32[192,2048]{1,0:T(8,128)S(1)} %own2.1.rest_0_), custom_call_target="tpu_custom_call" | custom-call | flops 17179869184 | bytes 1 | tf_op jit(solution)/shard_map/rest2/pallas_call | solution.py:204
  134.6 6.2 %collective-permute-done.38.got_two = bf16[96,2048]{1,0:T(8,128)(2,1)S(1)} collective-permute-done((bf16[96,2048]{1,0:T(8,128)(2,1)S(1)}, bf16[96,2048]{1,0:T(8,128)(2,1)S(1)}, u32[]{:S(2)}, u32[]{:S(2)}) %collective-permute-start.38) | collective-permute-done | bytes 393248 | tf_op jit(solution)/shard_map/out2/ppermute | solution.py:95
  144.0 2.4 %collective-permute-done.39.got = bf16[48,2048]{1,0:T(8,128)(2,1)S(1)} collective-permute-done((bf16[48,2048]{1,0:T(8,128)(2,1)S(1)}, bf16[48,2048]{1,0:T(8,128)(2,1)S(1)}, u32[]{:S(2)}, u32[]{:S(2)}) %collective-permute-start.39) | collective-permute-done | bytes 196640 | tf_op jit(solution)/shard_map/mix2/ppermute | solution.py:71
  147.9 8.9 %collective-permute-done.42.got = bf16[48,2048]{1,0:T(8,128)(2,1)S(1)} collective-permute-done((bf16[48,2048]{1,0:T(8,128)(2,1)S(1)}, bf16[48,2048]{1,0:T(8,128)(2,1)S(1)}, u32[]{:S(2)}, u32[]{:S(2)}) %collective-permute-start.42) | collective-permute-done | bytes 196640 | tf_op jit(solution)/shard_map/far_out1/ppermute | solution.py:75
  157.0 2.3 %collective-permute-done.41.got = bf16[48,2048]{1,0:T(8,128)(2,1)S(1)} collective-permute-done((bf16[48,2048]{1,0:T(8,128)(2,1)S(1)}, bf16[48,2048]{1,0:T(8,128)(2,1)S(1)}, u32[]{:S(2)}, u32[]{:S(2)}) %collective-permute-start.41) | collective-permute-done | bytes 196640 | tf_op jit(solution)/shard_map/far_out2/ppermute | solution.py:75
  (117 shorter events, 59.3 us)
Async XLA Ops:
  2.8 9.2 %collective-permute-start = (bf16[32,2048]{1,0:T(8,128)(2,1)S(1)}, bf16[32,2048]{1,0:T(8,128)(2,1)S(1)}, u32[]{:S(2)}, u32[]{:S(2)}) collective-permute-start(bf16[32,2048]{1,0:T(8,128)(2,1)S(1)} %get-tuple-element.109), channel_id=1, source_target_pairs={{0,8},{4,12},{8,0},{12,4},{1,9},{5,13},{9,1},{13,5},{2,10},{6,14},... | collective-permute-start | bytes 393224 | tf_op jit(solution)/shard_map/far0/ppermute | solution.py:75
  13.1 18.1 %collective-permute-start.1 = (bf16[48,2048]{1,0:T(8,128)(2,1)S(1)}, bf16[48,2048]{1,0:T(8,128)(2,1)S(1)}, u32[]{:S(2)}, u32[]{:S(2)}) collective-permute-start(bf16[48,2048]{1,0:T(8,128)(2,1)S(1)} %get-tuple-element.114), channel_id=1, source_target_pairs={{0,8},{4,12},{8,0},{12,4},{1,9},{5,13},{9,1},{13,5},{2,10},{6,14},... | collective-permute-start | bytes 589832 | tf_op jit(solution)/shard_map/far1/ppermute | solution.py:75
  16.7 15.9 %collective-permute-start.4 = (bf16[64,2048]{1,0:T(8,128)(2,1)S(1)}, bf16[64,2048]{1,0:T(8,128)(2,1)S(1)}, u32[]{:S(2)}, u32[]{:S(2)}) collective-permute-start(bf16[64,2048]{1,0:T(8,128)(2,1)S(1)} %pad_maximum_fusion.5), channel_id=1, source_target_pairs={{0,4},{1,0},{2,6},{3,2},{4,5},{5,1},{6,7},{7,3},{8,12},{9,8},{10,1... | collective-permute-start | bytes 786440 | tf_op jit(solution)/shard_map/arr0/ppermute | solution.py:95
  18.6 14.1 %collective-permute-start.5 = (bf16[64,2048]{1,0:T(8,128)(2,1)S(1)}, bf16[64,2048]{1,0:T(8,128)(2,1)S(1)}, u32[]{:S(2)}, u32[]{:S(2)}) collective-permute-start(bf16[64,2048]{1,0:T(8,128)(2,1)S(1)} %pad_maximum_fusion.5), channel_id=1, source_target_pairs={{1,4},{3,6},{4,1},{6,3},{9,12},{11,14},{12,9},{14,11},{17,20},{19,... | collective-permute-start | bytes 786440 | tf_op jit(solution)/shard_map/arr0/ppermute | solution.py:95
  31.6 11.1 %collective-permute-start.3 = (bf16[48,2048]{1,0:T(8,128)(2,1)S(1)}, bf16[48,2048]{1,0:T(8,128)(2,1)S(1)}, u32[]{:S(2)}, u32[]{:S(2)}) collective-permute-start(bf16[48,2048]{1,0:T(8,128)(2,1)S(1)} %get-tuple-element.123), channel_id=1, source_target_pairs={{0,8},{4,12},{8,0},{12,4},{1,9},{5,13},{9,1},{13,5},{2,10},{6,14},... | collective-permute-start | bytes 589832 | tf_op jit(solution)/shard_map/far2/ppermute | solution.py:75
  37.9 10.0 %collective-permute-start.10 = (bf16[96,2048]{1,0:T(8,128)(2,1)S(1)}, bf16[96,2048]{1,0:T(8,128)(2,1)S(1)}, u32[]{:S(2)}, u32[]{:S(2)}) collective-permute-start(bf16[96,2048]{1,0:T(8,128)(2,1)S(1)} %pad_maximum_fusion.3), channel_id=1, source_target_pairs={{0,4},{1,0},{2,6},{3,2},{4,5},{5,1},{6,7},{7,3},{8,12},{9,8},{10,1... | collective-permute-start | bytes 1179656 | tf_op jit(solution)/shard_map/arr1/ppermute | solution.py:95
  38.0 11.8 %collective-permute-start.11 = (bf16[96,2048]{1,0:T(8,128)(2,1)S(1)}, bf16[96,2048]{1,0:T(8,128)(2,1)S(1)}, u32[]{:S(2)}, u32[]{:S(2)}) collective-permute-start(bf16[96,2048]{1,0:T(8,128)(2,1)S(1)} %pad_maximum_fusion.3), channel_id=1, source_target_pairs={{1,4},{3,6},{4,1},{6,3},{9,12},{11,14},{12,9},{14,11},{17,20},{19,... | collective-permute-start | bytes 1179656 | tf_op jit(solution)/shard_map/arr1/ppermute | solution.py:95
  40.3 14.4 %collective-permute-start.12 = (bf16[128,1024]{1,0:T(8,128)(2,1)S(1)}, bf16[128,1024]{1,0:T(8,128)(2,1)S(1)}, u32[]{:S(2)}, u32[]{:S(2)}) collective-permute-start(bf16[128,1024]{1,0:T(8,128)(2,1)S(1)} %get-tuple-element.128), channel_id=1, source_target_pairs={{0,2},{1,3},{2,0},{3,1},{4,6},{5,7},{6,4},{7,5},{8,10},{9,11},{10,... | collective-permute-start | bytes 786440 | tf_op jit(solution)/shard_map/b0/ppermute | solution.py:71
  42.7 12.0 %collective-permute-start.13 = (bf16[128,1024]{1,0:T(8,128)(2,1)S(1)}, bf16[128,1024]{1,0:T(8,128)(2,1)S(1)}, u32[]{:S(2)}, u32[]{:S(2)}) collective-permute-start(bf16[128,1024]{1,0:T(8,128)(2,1)S(1)} %get-tuple-element.136), channel_id=1, source_target_pairs={{0,2},{1,3},{2,0},{3,1},{4,6},{5,7},{6,4},{7,5},{8,10},{9,11},{10,... | collective-permute-start | bytes 786440 | tf_op jit(solution)/shard_map/b0/ppermute | solution.py:71
  43.4 14.7 %collective-permute-start.9 = (bf16[48,2048]{1,0:T(8,128)(2,1)S(1)}, bf16[48,2048]{1,0:T(8,128)(2,1)S(1)}, u32[]{:S(2)}, u32[]{:S(2)}) collective-permute-start(bf16[48,2048]{1,0:T(8,128)(2,1)S(1)} %broadcast_select_fusion.12), channel_id=1, source_target_pairs={{0,2},{1,3},{2,0},{3,1},{4,6},{5,7},{6,4},{7,5},{8,10},{9,11},{10,... | collective-permute-start | bytes 589832 | tf_op jit(solution)/shard_map/sel2/ppermute | solution.py:71
  54.9 22.9 %collective-permute-start.19 = (bf16[128,1024]{1,0:T(8,128)(2,1)S(1)}, bf16[128,1024]{1,0:T(8,128)(2,1)S(1)}, u32[]{:S(2)}, u32[]{:S(2)}) collective-permute-start(bf16[128,1024]{1,0:T(8,128)(2,1)S(1)} %hide0.1.one), channel_id=1, source_target_pairs={{0,1},{1,0},{2,3},{3,2},{4,5},{5,4},{6,7},{7,6},{8,9},{9,8},{10,11... | collective-permute-start | bytes 786440 | tf_op jit(solution)/shard_map/hide0/ppermute | solution.py:71
  55.0 27.2 %collective-permute-start.25 = (bf16[128,1024]{1,0:T(8,128)(2,1)S(1)}, bf16[128,1024]{1,0:T(8,128)(2,1)S(1)}, u32[]{:S(2)}, u32[]{:S(2)}) collective-permute-start(bf16[128,1024]{1,0:T(8,128)(2,1)S(1)} %hide0.1.one), channel_id=1, source_target_pairs={{0,2},{1,3},{2,0},{3,1},{4,6},{5,7},{6,4},{7,5},{8,10},{9,11},{10,... | collective-permute-start | bytes 786440 | tf_op jit(solution)/shard_map/hide0/ppermute | solution.py:71
  58.9 10.4 %collective-permute-start.17 = (bf16[96,2048]{1,0:T(8,128)(2,1)S(1)}, bf16[96,2048]{1,0:T(8,128)(2,1)S(1)}, u32[]{:S(2)}, u32[]{:S(2)}) collective-permute-start(bf16[96,2048]{1,0:T(8,128)(2,1)S(1)} %pad_maximum_fusion.4), channel_id=1, source_target_pairs={{1,4},{3,6},{4,1},{6,3},{9,12},{11,14},{12,9},{14,11},{17,20},{19,... | collective-permute-start | bytes 1179656 | tf_op jit(solution)/shard_map/arr2/ppermute | solution.py:95
  61.6 18.8 %collective-permute-start.18 = (bf16[192,1024]{1,0:T(8,128)(2,1)S(1)}, bf16[192,1024]{1,0:T(8,128)(2,1)S(1)}, u32[]{:S(2)}, u32[]{:S(2)}) collective-permute-start(bf16[192,1024]{1,0:T(8,128)(2,1)S(1)} %get-tuple-element.139), channel_id=1, source_target_pairs={{0,2},{1,3},{2,0},{3,1},{4,6},{5,7},{6,4},{7,5},{8,10},{9,11},{10,... | collective-permute-start | bytes 1179656 | tf_op jit(solution)/shard_map/b1/ppermute | solution.py:71
  66.1 14.3 %collective-permute-start.20 = (bf16[192,1024]{1,0:T(8,128)(2,1)S(1)}, bf16[192,1024]{1,0:T(8,128)(2,1)S(1)}, u32[]{:S(2)}, u32[]{:S(2)}) collective-permute-start(bf16[192,1024]{1,0:T(8,128)(2,1)S(1)} %get-tuple-element.149), channel_id=1, source_target_pairs={{0,2},{1,3},{2,0},{3,1},{4,6},{5,7},{6,4},{7,5},{8,10},{9,11},{10,... | collective-permute-start | bytes 1179656 | tf_op jit(solution)/shard_map/b1/ppermute | solution.py:71
  71.7 11.1 %collective-permute-start.21 = (bf16[2,192,1024]{2,1,0:T(8,128)(2,1)S(1)}, bf16[2,192,1024]{2,1,0:T(8,128)(2,1)S(1)}, u32[]{:S(2)}, u32[]{:S(2)}) collective-permute-start(bf16[2,192,1024]{2,1,0:T(8,128)(2,1)S(1)} %a2.1), channel_id=1, source_target_pairs={{0,1},{1,0},{2,3},{3,2},{4,5},{5,4},{6,7},{7,6},{8,9},{9,8},{10,11... | collective-permute-start | bytes 2359304 | tf_op jit(solution)/shard_map/a2/ppermute | solution.py:71
  80.7 14.3 %collective-permute-start.27 = (bf16[192,1024]{1,0:T(8,128)(2,1)S(1)}, bf16[192,1024]{1,0:T(8,128)(2,1)S(1)}, u32[]{:S(2)}, u32[]{:S(2)}) collective-permute-start(bf16[192,1024]{1,0:T(8,128)(2,1)S(1)} %hide1.1.one), channel_id=1, source_target_pairs={{0,1},{1,0},{2,3},{3,2},{4,5},{5,4},{6,7},{7,6},{8,9},{9,8},{10,11... | collective-permute-start | bytes 1179656 | tf_op jit(solution)/shard_map/hide1/ppermute | solution.py:71
  81.0 14.0 %collective-permute-start.24 = (bf16[192,1024]{1,0:T(8,128)(2,1)S(1)}, bf16[192,1024]{1,0:T(8,128)(2,1)S(1)}, u32[]{:S(2)}, u32[]{:S(2)}) collective-permute-start(bf16[192,1024]{1,0:T(8,128)(2,1)S(1)} %hide1.1.one), channel_id=1, source_target_pairs={{0,2},{1,3},{2,0},{3,1},{4,6},{5,7},{6,4},{7,5},{8,10},{9,11},{10,... | collective-permute-start | bytes 1179656 | tf_op jit(solution)/shard_map/hide1/ppermute | solution.py:71
  82.2 8.9 %collective-permute-start.26 = (bf16[128,1024]{1,0:T(8,128)(2,1)S(1)}, bf16[128,1024]{1,0:T(8,128)(2,1)S(1)}, u32[]{:S(2)}, u32[]{:S(2)}) collective-permute-start(bf16[128,1024]{1,0:T(8,128)(2,1)S(1)} %collective-permute-done.25.one), channel_id=1, source_target_pairs={{0,1},{1,0},{2,3},{3,2},{4,5},{5,4},{6,7},{7,6},{8,9},{9,8},{10,11... | collective-permute-start | bytes 786440 | tf_op jit(solution)/shard_map/forward0/ppermute | solution.py:71
  84.8 23.5 %collective-permute-start.23 = (bf16[2,192,1024]{2,1,0:T(8,128)(2,1)S(1)}, bf16[2,192,1024]{2,1,0:T(8,128)(2,1)S(1)}, u32[]{:S(2)}, u32[]{:S(2)}) collective-permute-start(bf16[2,192,1024]{2,1,0:T(8,128)(2,1)S(1)} %b2.1), channel_id=1, source_target_pairs={{0,2},{1,3},{2,0},{3,1},{4,6},{5,7},{6,4},{7,5},{8,10},{9,11},{10,... | collective-permute-start | bytes 2359304 | tf_op jit(solution)/shard_map/b2/ppermute | solution.py:71
  93.3 16.4 %collective-permute-start.31 = (bf16[64,2048]{1,0:T(8,128)(2,1)S(1)}, bf16[64,2048]{1,0:T(8,128)(2,1)S(1)}, u32[]{:S(2)}, u32[]{:S(2)}) collective-permute-start(bf16[64,2048]{1,0:T(8,128)(2,1)S(1)} %get-tuple-element.157), channel_id=1, source_target_pairs={{0,1},{1,5},{2,3},{3,7},{4,0},{5,4},{6,2},{7,6},{8,9},{9,13},{10,1... | collective-permute-start | bytes 786440 | tf_op jit(solution)/shard_map/out0/ppermute | solution.py:95
  97.0 14.0 %collective-permute-start.32 = (bf16[64,2048]{1,0:T(8,128)(2,1)S(1)}, bf16[64,2048]{1,0:T(8,128)(2,1)S(1)}, u32[]{:S(2)}, u32[]{:S(2)}) collective-permute-start(bf16[64,2048]{1,0:T(8,128)(2,1)S(1)} %get-tuple-element.166), channel_id=1, source_target_pairs={{1,4},{3,6},{4,1},{6,3},{9,12},{11,14},{12,9},{14,11},{17,20},{19,... | collective-permute-start | bytes 786440 | tf_op jit(solution)/shard_map/out0/ppermute | solution.py:95
  102.5 9.5 %collective-permute-start.30 = (bf16[96,2048]{1,0:T(8,128)(2,1)S(1)}, bf16[96,2048]{1,0:T(8,128)(2,1)S(1)}, u32[]{:S(2)}, u32[]{:S(2)}) collective-permute-start(bf16[96,2048]{1,0:T(8,128)(2,1)S(1)} %get-tuple-element.161), channel_id=1, source_target_pairs={{0,1},{1,5},{2,3},{3,7},{4,0},{5,4},{6,2},{7,6},{8,9},{9,13},{10,1... | collective-permute-start | bytes 1179656 | tf_op jit(solution)/shard_map/out1/ppermute | solution.py:95
  102.6 10.9 %collective-permute-start.33 = (bf16[96,2048]{1,0:T(8,128)(2,1)S(1)}, bf16[96,2048]{1,0:T(8,128)(2,1)S(1)}, u32[]{:S(2)}, u32[]{:S(2)}) collective-permute-start(bf16[96,2048]{1,0:T(8,128)(2,1)S(1)} %get-tuple-element.169), channel_id=1, source_target_pairs={{1,4},{3,6},{4,1},{6,3},{9,12},{11,14},{12,9},{14,11},{17,20},{19,... | collective-permute-start | bytes 1179656 | tf_op jit(solution)/shard_map/out1/ppermute | solution.py:95
  108.5 13.2 %collective-permute-start.34 = (bf16[192,1024]{1,0:T(8,128)(2,1)S(1)}, bf16[192,1024]{1,0:T(8,128)(2,1)S(1)}, u32[]{:S(2)}, u32[]{:S(2)}) collective-permute-start(bf16[192,1024]{1,0:T(8,128)(2,1)S(1)} %hide2.1.one), channel_id=1, source_target_pairs={{0,1},{1,0},{2,3},{3,2},{4,5},{5,4},{6,7},{7,6},{8,9},{9,8},{10,11... | collective-permute-start | bytes 1179656 | tf_op jit(solution)/shard_map/hide2/ppermute | solution.py:71
  109.7 10.7 %collective-permute-start.29 = (bf16[192,1024]{1,0:T(8,128)(2,1)S(1)}, bf16[192,1024]{1,0:T(8,128)(2,1)S(1)}, u32[]{:S(2)}, u32[]{:S(2)}) collective-permute-start(bf16[192,1024]{1,0:T(8,128)(2,1)S(1)} %hide2.1.one), channel_id=1, source_target_pairs={{0,2},{1,3},{2,0},{3,1},{4,6},{5,7},{6,4},{7,5},{8,10},{9,11},{10,... | collective-permute-start | bytes 1179656 | tf_op jit(solution)/shard_map/hide2/ppermute | solution.py:71
  111.7 16.7 %collective-permute-start.37 = (bf16[32,2048]{1,0:T(8,128)(2,1)S(1)}, bf16[32,2048]{1,0:T(8,128)(2,1)S(1)}, u32[]{:S(2)}, u32[]{:S(2)}) collective-permute-start(bf16[32,2048]{1,0:T(8,128)(2,1)S(1)} %get-tuple-element.167), channel_id=1, source_target_pairs={{0,2},{1,3},{2,0},{3,1},{4,6},{5,7},{6,4},{7,5},{8,10},{9,11},{10,... | collective-permute-start | bytes 393224 | tf_op jit(solution)/shard_map/mix0/ppermute | solution.py:71
  114.2 28.8 %collective-permute-start.40 = (bf16[48,2048]{1,0:T(8,128)(2,1)S(1)}, bf16[48,2048]{1,0:T(8,128)(2,1)S(1)}, u32[]{:S(2)}, u32[]{:S(2)}) collective-permute-start(bf16[48,2048]{1,0:T(8,128)(2,1)S(1)} %get-tuple-element.170), channel_id=1, source_target_pairs={{0,2},{1,3},{2,0},{3,1},{4,6},{5,7},{6,4},{7,5},{8,10},{9,11},{10,... | collective-permute-start | bytes 589832 | tf_op jit(solution)/shard_map/mix1/ppermute | solution.py:71
  128.4 12.4 %collective-permute-start.38 = (bf16[96,2048]{1,0:T(8,128)(2,1)S(1)}, bf16[96,2048]{1,0:T(8,128)(2,1)S(1)}, u32[]{:S(2)}, u32[]{:S(2)}) collective-permute-start(bf16[96,2048]{1,0:T(8,128)(2,1)S(1)} %get-tuple-element.180), channel_id=1, source_target_pairs={{1,4},{3,6},{4,1},{6,3},{9,12},{11,14},{12,9},{14,11},{17,20},{19,... | collective-permute-start | bytes 1179656 | tf_op jit(solution)/shard_map/out2/ppermute | solution.py:95
  131.0 16.8 %collective-permute-start.43 = (bf16[32,2048]{1,0:T(8,128)(2,1)S(1)}, bf16[32,2048]{1,0:T(8,128)(2,1)S(1)}, u32[]{:S(2)}, u32[]{:S(2)}) collective-permute-start(bf16[32,2048]{1,0:T(8,128)(2,1)S(1)} %get-tuple-element.178), channel_id=1, source_target_pairs={{0,8},{4,12},{8,0},{12,4},{1,9},{5,13},{9,1},{13,5},{2,10},{6,14},... | collective-permute-start | bytes 393224 | tf_op jit(solution)/shard_map/far_out0/ppermute | solution.py:75
  143.7 13.1 %collective-permute-start.42 = (bf16[48,2048]{1,0:T(8,128)(2,1)S(1)}, bf16[48,2048]{1,0:T(8,128)(2,1)S(1)}, u32[]{:S(2)}, u32[]{:S(2)}) collective-permute-start(bf16[48,2048]{1,0:T(8,128)(2,1)S(1)} %get-tuple-element.185), channel_id=1, source_target_pairs={{0,8},{4,12},{8,0},{12,4},{1,9},{5,13},{9,1},{13,5},{2,10},{6,14},... | collective-permute-start | bytes 589832 | tf_op jit(solution)/shard_map/far_out1/ppermute | solution.py:75
  147.1 12.3 %collective-permute-start.41 = (bf16[48,2048]{1,0:T(8,128)(2,1)S(1)}, bf16[48,2048]{1,0:T(8,128)(2,1)S(1)}, u32[]{:S(2)}, u32[]{:S(2)}) collective-permute-start(bf16[48,2048]{1,0:T(8,128)(2,1)S(1)} %get-tuple-element.188), channel_id=1, source_target_pairs={{0,8},{4,12},{8,0},{12,4},{1,9},{5,13},{9,1},{13,5},{2,10},{6,14},... | collective-permute-start | bytes 589832 | tf_op jit(solution)/shard_map/far_out2/ppermute | solution.py:75
  (14 other events, 68.3 us)

commit v13 on v12

--- a/solution.py
+++ b/solution.py
@@ -12,8 +12,8 @@
     "far0", "load3", "sel0", "far1", "load1", "arr0", "load2", "load0", "sel1", "far2", "take0", "a0", "c0",
     "b0", "arr1", "d0", "sel2", "take1", "a1", "c1", "hide0", "b1", "arr2", "d1", "take2", "a2", "c2",
     "down0", "own0", "forward0", "hide1", "b2", "d2", "down2", "rest0", "out0", "forward1", "own1", "rest1",
-    "out1", "hide2", "mix0", "mix1", "forward2", "own2", "rest2", "out2", "far_out0", "mix2", "far_out1",
-    "far_out2", "end0", "end1", "end2",
+    "out1", "hide2", "mix0", "mix1", "forward2", "own2", "rest2", "out2", "far_out1", "far_out0", "mix2",
+    "end1", "far_out2", "end0", "end2",
 )
 TILE = 256
 SPLIT = (0, 1)

time: 161 us -> 160 us (level)
  waiting for transfers between devices: 43.7 us -> 38.8 us
  starting transfers between devices: 49.4 us -> 53.5 us
    ppermute x6, waiting for transfers between devices: 13.6 us -> 8.77 us  [over_tp(): return lax.ppermute(array, 'tp', [(i, i ^ bit) for i in range(4)])]
    ppermute x12, starting transfers between devices: 24.4 us -> 26.3 us  [over_both(): return lax.ppermute(array, ('tp', 'seq'), pairs)]
    ppermute x26, starting transfers between devices: 17.7 us -> 19.4 us  [over_seq(): return lax.ppermute(array, 'seq', [(i, i ^ bit) for i in range(4)])]
  transfers between devices with their start and end apart: 44 -> 44, of which waited for: 15 -> 13; matrix products, arithmetic and copies ran while one was open for 1% -> 1% of each run, Pallas kernels for 39% -> 39%
where the time goes in v13:
time: 160 us
  Pallas kernels  63.2 us (40%)
  starting transfers between devices  53.5 us (33%)
  waiting for transfers between devices  38.8 us (24%)
  local copies, waits for them, and re-layouts  1.73 us (1%)
    ppermute x12, starting transfers between devices, over_both(): return lax.ppermute(array, ('tp', 'seq'), pairs)  26.3 us
    pallas_call x12, Pallas kernels, sums(): pl.pallas_call(functools.partial(sums_kernel, got is not None, split), ou...  21.4 us
    ppermute x26, starting transfers between devices, over_seq(): return lax.ppermute(array, 'seq', [(i, i ^ bit) for i in range(4)])  19.4 us
    ppermute x12, waiting for transfers between devices, over_both(): return lax.ppermute(array, ('tp', 'seq'), pairs)  17.4 us
    pallas_call x4, Pallas kernels, load(): pl.pallas_call(load_kernel, out_shape=jax.ShapeDtypeStruct((2, deep, widt...  14 us
    ppermute x26, waiting for transfers between devices, over_seq(): return lax.ppermute(array, 'seq', [(i, i ^ bit) for i in range(4)])  12.6 us
    pallas_call x6, Pallas kernels, products(): pl.pallas_call(functools.partial(products_kernel, total is not None), out...  10.9 us
    ppermute x6, waiting for transfers between devices, over_tp(): return lax.ppermute(array, 'tp', [(i, i ^ bit) for i in range(4)])  8.77 us
  transfers between devices with their start and end apart: 44, of which 13 were waited for; matrix products, arithmetic and copies ran while one was open for 1% of the time, Pallas kernels for 39%

profile of v13, /device:TPU:1, one launch (start us, length us, event | category | flops | bytes accessed | tf_op | source)
XLA Modules:
  0.0 159.5 jit_solution(11436629418814890441)
XLA Ops:
  2.8 3.2 %collective-permute-start = (bf16[32,2048]{1,0:T(8,128)(2,1)S(1)}, bf16[32,2048]{1,0:T(8,128)(2,1)S(1)}, u32[]{:S(2)}, u32[]{:S(2)}) collective-permute-start(bf16[32,2048]{1,0:T(8,128)(2,1)S(1)} %get-tuple-element.109), channel_id=1, source_target_pairs={{0,8},{4,12},{8,0},{12,4},{1,9},{5,13},{9,1},{13,5},{2,10},{6,14},... | collective-permute-start | bytes 393224 | tf_op jit(solution)/shard_map/far0/ppermute | solution.py:75
  6.2 3.5 %load3.1.weights = bf16[2,2048,1024]{2,1,0:T(8,128)(2,1)S(1)} custom-call(s32[1]{0:T(128)} %bitcast.7.quarter, bf16[2048,4096]{1,0:T(8,128)(2,1)} %gate_weight.3, bf16[2048,4096]{1,0:T(8,128)(2,1)} %up_weight.7), custom_call_target="tpu_custom_call" | custom-call | flops 1073741824 | bytes 1 | tf_op jit(solution)/shard_map/load3/pallas_call | solution.py:121
  9.7 2.4 %collective-permute-done = bf16[32,2048]{1,0:T(8,128)(2,1)S(1)} collective-permute-done((bf16[32,2048]{1,0:T(8,128)(2,1)S(1)}, bf16[32,2048]{1,0:T(8,128)(2,1)S(1)}, u32[]{:S(2)}, u32[]{:S(2)}) %collective-permute-start) | collective-permute-done | bytes 131104 | tf_op jit(solution)/shard_map/far0/ppermute | solution.py:75
  13.1 3.5 %load1.1.weights = bf16[2,2048,1024]{2,1,0:T(8,128)(2,1)S(1)} custom-call(s32[1]{0:T(128)} %bitcast.5.quarter, bf16[2048,4096]{1,0:T(8,128)(2,1)} %gate_weight.3, bf16[2048,4096]{1,0:T(8,128)(2,1)} %up_weight.7), custom_call_target="tpu_custom_call" | custom-call | flops 1073741824 | bytes 1 | tf_op jit(solution)/shard_map/load1/pallas_call | solution.py:121
  18.6 5.6 %collective-permute-start.5 = (bf16[64,2048]{1,0:T(8,128)(2,1)S(1)}, bf16[64,2048]{1,0:T(8,128)(2,1)S(1)}, u32[]{:S(2)}, u32[]{:S(2)}) collective-permute-start(bf16[64,2048]{1,0:T(8,128)(2,1)S(1)} %pad_maximum_fusion.5), channel_id=1, source_target_pairs={{1,4},{3,6},{4,1},{6,3},{9,12},{11,14},{12,9},{14,11},{17,20},{19,... | collective-permute-start | bytes 786440 | tf_op jit(solution)/shard_map/arr0/ppermute | solution.py:95
  24.2 3.5 %load2.1.weights = bf16[2,2048,1024]{2,1,0:T(8,128)(2,1)S(1)} custom-call(s32[1]{0:T(128)} %bitcast.6.quarter, bf16[2048,4096]{1,0:T(8,128)(2,1)} %gate_weight.3, bf16[2048,4096]{1,0:T(8,128)(2,1)} %up_weight.7), custom_call_target="tpu_custom_call" | custom-call | flops 1073741824 | bytes 1 | tf_op jit(solution)/shard_map/load2/pallas_call | solution.py:121
  27.7 3.5 %load0.1.weights = bf16[2,2048,1024]{2,1,0:T(8,128)(2,1)S(1)} custom-call(s32[1]{0:T(128)} %bitcast.4.quarter, bf16[2048,4096]{1,0:T(8,128)(2,1)} %gate_weight.3, bf16[2048,4096]{1,0:T(8,128)(2,1)} %up_weight.7), custom_call_target="tpu_custom_call" | custom-call | flops 1073741824 | bytes 1 | tf_op jit(solution)/shard_map/load0/pallas_call | solution.py:121
  38.0 2.3 %collective-permute-start.11 = (bf16[96,2048]{1,0:T(8,128)(2,1)S(1)}, bf16[96,2048]{1,0:T(8,128)(2,1)S(1)}, u32[]{:S(2)}, u32[]{:S(2)}) collective-permute-start(bf16[96,2048]{1,0:T(8,128)(2,1)S(1)} %pad_maximum_fusion.3), channel_id=1, source_target_pairs={{1,4},{3,6},{4,1},{6,3},{9,12},{11,14},{12,9},{14,11},{17,20},{19,... | collective-permute-start | bytes 1179656 | tf_op jit(solution)/shard_map/arr1/ppermute | solution.py:95
  44.3 3.6 %collective-permute-done.10 = bf16[96,2048]{1,0:T(8,128)(2,1)S(1)} collective-permute-done((bf16[96,2048]{1,0:T(8,128)(2,1)S(1)}, bf16[96,2048]{1,0:T(8,128)(2,1)S(1)}, u32[]{:S(2)}, u32[]{:S(2)}) %collective-permute-start.10) | collective-permute-done | bytes 393248 | tf_op jit(solution)/shard_map/arr1/ppermute | solution.py:95
  52.1 2.0 %c1.1 = bf16[2,192,1024]{2,1,0:T(8,128)(2,1)S(1)} custom-call(bf16[192,2048]{1,0:T(8,128)(2,1)S(1)} %pad_maximum_fusion.some, bf16[2,2048,1024]{2,1,0:T(8,128)(2,1)S(1)} %load1.1.weights), custom_call_target="tpu_custom_call" | custom-call | flops 17179869184 | bytes 1 | tf_op jit(solution)/shard_map/c1/pallas_call | solution.py:150
  58.9 2.7 %collective-permute-start.17 = (bf16[96,2048]{1,0:T(8,128)(2,1)S(1)}, bf16[96,2048]{1,0:T(8,128)(2,1)S(1)}, u32[]{:S(2)}, u32[]{:S(2)}) collective-permute-start(bf16[96,2048]{1,0:T(8,128)(2,1)S(1)} %pad_maximum_fusion.4), channel_id=1, source_target_pairs={{1,4},{3,6},{4,1},{6,3},{9,12},{11,14},{12,9},{14,11},{17,20},{19,... | collective-permute-start | bytes 1179656 | tf_op jit(solution)/shard_map/arr2/ppermute | solution.py:95
  62.9 2.0 %d1.1.held = f32[2,192,1024]{2,1,0:T(8,128)S(1)} custom-call(bf16[192,2048]{1,0:T(8,128)(2,1)S(1)} %pad_maximum_fusion.some, bf16[2,2048,1024]{2,1,0:T(8,128)(2,1)S(1)} %load0.1.weights, bf16[2,192,1024]{2,1,0:T(8,128)(2,1)S(1)} %collective-permute-done.16.rest_0_), custom_call_target="tpu_custom_call" | custom-call | flops 17179869184 | bytes 1 | tf_op jit(solution)/shard_map/d1/pallas_call | solution.py:150
  67.2 2.2 %collective-permute-done.17 = bf16[96,2048]{1,0:T(8,128)(2,1)S(1)} collective-permute-done((bf16[96,2048]{1,0:T(8,128)(2,1)S(1)}, bf16[96,2048]{1,0:T(8,128)(2,1)S(1)}, u32[]{:S(2)}, u32[]{:S(2)}) %collective-permute-start.17) | collective-permute-done | bytes 393248 | tf_op jit(solution)/shard_map/arr2/ppermute | solution.py:95
  69.7 2.0 %a2.1 = bf16[2,192,1024]{2,1,0:T(8,128)(2,1)S(1)} custom-call(bf16[192,2048]{1,0:T(8,128)(2,1)S(1)} %pad_maximum_fusion.1.some, bf16[2,2048,1024]{2,1,0:T(8,128)(2,1)S(1)} %load3.1.weights), custom_call_target="tpu_custom_call" | custom-call | flops 17179869184 | bytes 1 | tf_op jit(solution)/shard_map/a2/pallas_call | solution.py:150
  71.7 2.0 %c2.1 = bf16[2,192,1024]{2,1,0:T(8,128)(2,1)S(1)} custom-call(bf16[192,2048]{1,0:T(8,128)(2,1)S(1)} %pad_maximum_fusion.1.some, bf16[2,2048,1024]{2,1,0:T(8,128)(2,1)S(1)} %load1.1.weights), custom_call_target="tpu_custom_call" | custom-call | flops 17179869184 | bytes 1 | tf_op jit(solution)/shard_map/c2/pallas_call | solution.py:150
  73.7 4.0 %down0.1.weights = bf16[2,1024,2048]{2,1,0:T(8,128)(2,1)S(1)} custom-call(s32[2]{0:T(128)S(1)} %get-tuple-element.143.quarters, bf16[4096,2048]{1,0:T(8,128)(2,1)} %weight.1), custom_call_target="tpu_custom_call" | custom-call | flops 17179869184 | bytes 1 | tf_op jit(solution)/shard_map/down0/pallas_call | solution.py:181
  82.8 2.0 %b2.1 = bf16[2,192,1024]{2,1,0:T(8,128)(2,1)S(1)} custom-call(bf16[192,2048]{1,0:T(8,128)(2,1)S(1)} %pad_maximum_fusion.1.some, bf16[2,2048,1024]{2,1,0:T(8,128)(2,1)S(1)} %load2.1.weights, bf16[2,192,1024]{2,1,0:T(8,128)(2,1)S(1)} %collective-permute-done.21.rest_0_), custom_call_target="tpu_custom_call" | custom-call | flops 17179869184 | bytes 1 | tf_op jit(solution)/shard_map/b2/pallas_call | solution.py:150
  85.1 2.0 %d2.1.held = f32[2,192,1024]{2,1,0:T(8,128)S(1)} custom-call(bf16[192,2048]{1,0:T(8,128)(2,1)S(1)} %pad_maximum_fusion.1.some, bf16[2,2048,1024]{2,1,0:T(8,128)(2,1)S(1)} %load0.1.weights, bf16[2,192,1024]{2,1,0:T(8,128)(2,1)S(1)} %collective-permute-done.22.rest_0_), custom_call_target="tpu_custom_call" | custom-call | flops 17179869184 | bytes 1 | tf_op jit(solution)/shard_map/d2/pallas_call | solution.py:150
  87.1 4.0 %down2.1.weights = bf16[2,1024,2048]{2,1,0:T(8,128)(2,1)S(1)} custom-call(s32[2]{0:T(128)S(1)} %get-tuple-element.154.quarters, bf16[4096,2048]{1,0:T(8,128)(2,1)} %weight.1), custom_call_target="tpu_custom_call" | custom-call | flops 17179869184 | bytes 1 | tf_op jit(solution)/shard_map/down2/pallas_call | solution.py:181
  95.0 2.0 %own1.1.rest_0_ = f32[192,2048]{1,0:T(8,128)S(1)} custom-call(bf16[192,1024]{1,0:T(8,128)(2,1)S(1)} %hide1.1.one, bf16[192,1024]{1,0:T(8,128)(2,1)S(1)} %collective-permute-done.27.two, bf16[2,1024,2048]{2,1,0:T(8,128)(2,1)S(1)} %down0.1.weights), custom_call_target="tpu_custom_call" | custom-call | flops 17179869184 | bytes 1 | tf_op jit(solution)/shard_map/own1/pallas_call | solution.py:204
  97.0 2.7 %collective-permute-start.32 = (bf16[64,2048]{1,0:T(8,128)(2,1)S(1)}, bf16[64,2048]{1,0:T(8,128)(2,1)S(1)}, u32[]{:S(2)}, u32[]{:S(2)}) collective-permute-start(bf16[64,2048]{1,0:T(8,128)(2,1)S(1)} %get-tuple-element.166), channel_id=1, source_target_pairs={{1,4},{3,6},{4,1},{6,3},{9,12},{11,14},{12,9},{14,11},{17,20},{19,... | collective-permute-start | bytes 786440 | tf_op jit(solution)/shard_map/out0/ppermute | solution.py:95
  99.7 2.0 %rest1.1.partial_sum = f32[192,2048]{1,0:T(8,128)S(1)} custom-call(bf16[192,1024]{1,0:T(8,128)(2,1)S(1)} %collective-permute-done.24.one, bf16[192,1024]{1,0:T(8,128)(2,1)S(1)} %collective-permute-done.28.two, bf16[2,1024,2048]{2,1,0:T(8,128)(2,1)S(1)} %down2.1.weights, f32[192,2048]{1,0:T(8,128)S(1)} %own1.1.rest_0_), custom_call_target="tpu_custom_call" | custom-call | flops 17179869184 | bytes 1 | tf_op jit(solution)/shard_map/rest1/pallas_call | solution.py:204
  102.6 2.8 %collective-permute-start.33 = (bf16[96,2048]{1,0:T(8,128)(2,1)S(1)}, bf16[96,2048]{1,0:T(8,128)(2,1)S(1)}, u32[]{:S(2)}, u32[]{:S(2)}) collective-permute-start(bf16[96,2048]{1,0:T(8,128)(2,1)S(1)} %get-tuple-element.169), channel_id=1, source_target_pairs={{1,4},{3,6},{4,1},{6,3},{9,12},{11,14},{12,9},{14,11},{17,20},{19,... | collective-permute-start | bytes 1179656 | tf_op jit(solution)/shard_map/out1/ppermute | solution.py:95
  105.4 2.8 %collective-permute-done.23.rest_0_ = bf16[2,192,1024]{2,1,0:T(8,128)(2,1)S(1)} collective-permute-done((bf16[2,192,1024]{2,1,0:T(8,128)(2,1)S(1)}, bf16[2,192,1024]{2,1,0:T(8,128)(2,1)S(1)}, u32[]{:S(2)}, u32[]{:S(2)}) %collective-permute-start.23) | collective-permute-done | bytes 786464 | tf_op jit(solution)/shard_map/b2/ppermute | solution.py:71
  114.6 5.7 %collective-permute-done.29.one = bf16[192,1024]{1,0:T(8,128)(2,1)S(1)} collective-permute-done((bf16[192,1024]{1,0:T(8,128)(2,1)S(1)}, bf16[192,1024]{1,0:T(8,128)(2,1)S(1)}, u32[]{:S(2)}, u32[]{:S(2)}) %collective-permute-start.29) | collective-permute-done | bytes 393248 | tf_op jit(solution)/shard_map/hide2/ppermute | solution.py:71
  121.7 2.0 %own2.1.rest_0_ = f32[192,2048]{1,0:T(8,128)S(1)} custom-call(bf16[192,1024]{1,0:T(8,128)(2,1)S(1)} %hide2.1.one, bf16[192,1024]{1,0:T(8,128)(2,1)S(1)} %collective-permute-done.34.two, bf16[2,1024,2048]{2,1,0:T(8,128)(2,1)S(1)} %down0.1.weights), custom_call_target="tpu_custom_call" | custom-call | flops 17179869184 | bytes 1 | tf_op jit(solution)/shard_map/own2/pallas_call | solution.py:204
  123.7 2.0 %rest2.1.partial_sum = f32[192,2048]{1,0:T(8,128)S(1)} custom-call(bf16[192,1024]{1,0:T(8,128)(2,1)S(1)} %collective-permute-done.29.one, bf16[192,1024]{1,0:T(8,128)(2,1)S(1)} %collective-permute-done.35.two, bf16[2,1024,2048]{2,1,0:T(8,128)(2,1)S(1)} %down2.1.weights, f32[192,2048]{1,0:T(8,128)S(1)} %own2.1.rest_0_), custom_call_target="tpu_custom_call" | custom-call | flops 17179869184 | bytes 1 | tf_op jit(solution)/shard_map/rest2/pallas_call | solution.py:204
  130.7 3.8 %collective-permute-start.39 = (bf16[96,2048]{1,0:T(8,128)(2,1)S(1)}, bf16[96,2048]{1,0:T(8,128)(2,1)S(1)}, u32[]{:S(2)}, u32[]{:S(2)}) collective-permute-start(bf16[96,2048]{1,0:T(8,128)(2,1)S(1)} %get-tuple-element.183), channel_id=1, source_target_pairs={{1,4},{3,6},{4,1},{6,3},{9,12},{11,14},{12,9},{14,11},{17,20},{19,... | collective-permute-start | bytes 1179656 | tf_op jit(solution)/shard_map/out2/ppermute | solution.py:95
  136.0 7.0 %collective-permute-done.39.got_two = bf16[96,2048]{1,0:T(8,128)(2,1)S(1)} collective-permute-done((bf16[96,2048]{1,0:T(8,128)(2,1)S(1)}, bf16[96,2048]{1,0:T(8,128)(2,1)S(1)}, u32[]{:S(2)}, u32[]{:S(2)}) %collective-permute-start.39) | collective-permute-done | bytes 393248 | tf_op jit(solution)/shard_map/out2/ppermute | solution.py:95
  143.8 3.2 %collective-permute-start.40 = (bf16[48,2048]{1,0:T(8,128)(2,1)S(1)}, bf16[48,2048]{1,0:T(8,128)(2,1)S(1)}, u32[]{:S(2)}, u32[]{:S(2)}) collective-permute-start(bf16[48,2048]{1,0:T(8,128)(2,1)S(1)} %get-tuple-element.185), channel_id=1, source_target_pairs={{0,2},{1,3},{2,0},{3,1},{4,6},{5,7},{6,4},{7,5},{8,10},{9,11},{10,... | collective-permute-start | bytes 589832 | tf_op jit(solution)/shard_map/mix2/ppermute | solution.py:71
  147.1 3.2 %collective-permute-done.40.got = bf16[48,2048]{1,0:T(8,128)(2,1)S(1)} collective-permute-done((bf16[48,2048]{1,0:T(8,128)(2,1)S(1)}, bf16[48,2048]{1,0:T(8,128)(2,1)S(1)}, u32[]{:S(2)}, u32[]{:S(2)}) %collective-permute-start.40) | collective-permute-done | bytes 196640 | tf_op jit(solution)/shard_map/mix2/ppermute | solution.py:71
  152.2 6.4 %collective-permute-done.42.got = bf16[48,2048]{1,0:T(8,128)(2,1)S(1)} collective-permute-done((bf16[48,2048]{1,0:T(8,128)(2,1)S(1)}, bf16[48,2048]{1,0:T(8,128)(2,1)S(1)}, u32[]{:S(2)}, u32[]{:S(2)}) %collective-permute-start.42) | collective-permute-done | bytes 196640 | tf_op jit(solution)/shard_map/far_out2/ppermute | solution.py:75
  (117 shorter events, 56.8 us)
Async XLA Ops:
  2.8 9.2 %collective-permute-start = (bf16[32,2048]{1,0:T(8,128)(2,1)S(1)}, bf16[32,2048]{1,0:T(8,128)(2,1)S(1)}, u32[]{:S(2)}, u32[]{:S(2)}) collective-permute-start(bf16[32,2048]{1,0:T(8,128)(2,1)S(1)} %get-tuple-element.109), channel_id=1, source_target_pairs={{0,8},{4,12},{8,0},{12,4},{1,9},{5,13},{9,1},{13,5},{2,10},{6,14},... | collective-permute-start | bytes 393224 | tf_op jit(solution)/shard_map/far0/ppermute | solution.py:75
  13.1 18.1 %collective-permute-start.1 = (bf16[48,2048]{1,0:T(8,128)(2,1)S(1)}, bf16[48,2048]{1,0:T(8,128)(2,1)S(1)}, u32[]{:S(2)}, u32[]{:S(2)}) collective-permute-start(bf16[48,2048]{1,0:T(8,128)(2,1)S(1)} %get-tuple-element.114), channel_id=1, source_target_pairs={{0,8},{4,12},{8,0},{12,4},{1,9},{5,13},{9,1},{13,5},{2,10},{6,14},... | collective-permute-start | bytes 589832 | tf_op jit(solution)/shard_map/far1/ppermute | solution.py:75
  16.7 15.9 %collective-permute-start.4 = (bf16[64,2048]{1,0:T(8,128)(2,1)S(1)}, bf16[64,2048]{1,0:T(8,128)(2,1)S(1)}, u32[]{:S(2)}, u32[]{:S(2)}) collective-permute-start(bf16[64,2048]{1,0:T(8,128)(2,1)S(1)} %pad_maximum_fusion.5), channel_id=1, source_target_pairs={{0,4},{1,0},{2,6},{3,2},{4,5},{5,1},{6,7},{7,3},{8,12},{9,8},{10,1... | collective-permute-start | bytes 786440 | tf_op jit(solution)/shard_map/arr0/ppermute | solution.py:95
  18.6 14.1 %collective-permute-start.5 = (bf16[64,2048]{1,0:T(8,128)(2,1)S(1)}, bf16[64,2048]{1,0:T(8,128)(2,1)S(1)}, u32[]{:S(2)}, u32[]{:S(2)}) collective-permute-start(bf16[64,2048]{1,0:T(8,128)(2,1)S(1)} %pad_maximum_fusion.5), channel_id=1, source_target_pairs={{1,4},{3,6},{4,1},{6,3},{9,12},{11,14},{12,9},{14,11},{17,20},{19,... | collective-permute-start | bytes 786440 | tf_op jit(solution)/shard_map/arr0/ppermute | solution.py:95
  31.6 11.1 %collective-permute-start.3 = (bf16[48,2048]{1,0:T(8,128)(2,1)S(1)}, bf16[48,2048]{1,0:T(8,128)(2,1)S(1)}, u32[]{:S(2)}, u32[]{:S(2)}) collective-permute-start(bf16[48,2048]{1,0:T(8,128)(2,1)S(1)} %get-tuple-element.123), channel_id=1, source_target_pairs={{0,8},{4,12},{8,0},{12,4},{1,9},{5,13},{9,1},{13,5},{2,10},{6,14},... | collective-permute-start | bytes 589832 | tf_op jit(solution)/shard_map/far2/ppermute | solution.py:75
  37.9 10.0 %collective-permute-start.10 = (bf16[96,2048]{1,0:T(8,128)(2,1)S(1)}, bf16[96,2048]{1,0:T(8,128)(2,1)S(1)}, u32[]{:S(2)}, u32[]{:S(2)}) collective-permute-start(bf16[96,2048]{1,0:T(8,128)(2,1)S(1)} %pad_maximum_fusion.3), channel_id=1, source_target_pairs={{0,4},{1,0},{2,6},{3,2},{4,5},{5,1},{6,7},{7,3},{8,12},{9,8},{10,1... | collective-permute-start | bytes 1179656 | tf_op jit(solution)/shard_map/arr1/ppermute | solution.py:95
  38.0 11.8 %collective-permute-start.11 = (bf16[96,2048]{1,0:T(8,128)(2,1)S(1)}, bf16[96,2048]{1,0:T(8,128)(2,1)S(1)}, u32[]{:S(2)}, u32[]{:S(2)}) collective-permute-start(bf16[96,2048]{1,0:T(8,128)(2,1)S(1)} %pad_maximum_fusion.3), channel_id=1, source_target_pairs={{1,4},{3,6},{4,1},{6,3},{9,12},{11,14},{12,9},{14,11},{17,20},{19,... | collective-permute-start | bytes 1179656 | tf_op jit(solution)/shard_map/arr1/ppermute | solution.py:95
  40.3 14.4 %collective-permute-start.12 = (bf16[128,1024]{1,0:T(8,128)(2,1)S(1)}, bf16[128,1024]{1,0:T(8,128)(2,1)S(1)}, u32[]{:S(2)}, u32[]{:S(2)}) collective-permute-start(bf16[128,1024]{1,0:T(8,128)(2,1)S(1)} %get-tuple-element.128), channel_id=1, source_target_pairs={{0,2},{1,3},{2,0},{3,1},{4,6},{5,7},{6,4},{7,5},{8,10},{9,11},{10,... | collective-permute-start | bytes 786440 | tf_op jit(solution)/shard_map/b0/ppermute | solution.py:71
  42.7 12.0 %collective-permute-start.13 = (bf16[128,1024]{1,0:T(8,128)(2,1)S(1)}, bf16[128,1024]{1,0:T(8,128)(2,1)S(1)}, u32[]{:S(2)}, u32[]{:S(2)}) collective-permute-start(bf16[128,1024]{1,0:T(8,128)(2,1)S(1)} %get-tuple-element.136), channel_id=1, source_target_pairs={{0,2},{1,3},{2,0},{3,1},{4,6},{5,7},{6,4},{7,5},{8,10},{9,11},{10,... | collective-permute-start | bytes 786440 | tf_op jit(solution)/shard_map/b0/ppermute | solution.py:71
  43.4 14.7 %collective-permute-start.9 = (bf16[48,2048]{1,0:T(8,128)(2,1)S(1)}, bf16[48,2048]{1,0:T(8,128)(2,1)S(1)}, u32[]{:S(2)}, u32[]{:S(2)}) collective-permute-start(bf16[48,2048]{1,0:T(8,128)(2,1)S(1)} %broadcast_select_fusion.12), channel_id=1, source_target_pairs={{0,2},{1,3},{2,0},{3,1},{4,6},{5,7},{6,4},{7,5},{8,10},{9,11},{10,... | collective-permute-start | bytes 589832 | tf_op jit(solution)/shard_map/sel2/ppermute | solution.py:71
  54.9 22.9 %collective-permute-start.19 = (bf16[128,1024]{1,0:T(8,128)(2,1)S(1)}, bf16[128,1024]{1,0:T(8,128)(2,1)S(1)}, u32[]{:S(2)}, u32[]{:S(2)}) collective-permute-start(bf16[128,1024]{1,0:T(8,128)(2,1)S(1)} %hide0.1.one), channel_id=1, source_target_pairs={{0,1},{1,0},{2,3},{3,2},{4,5},{5,4},{6,7},{7,6},{8,9},{9,8},{10,11... | collective-permute-start | bytes 786440 | tf_op jit(solution)/shard_map/hide0/ppermute | solution.py:71
  55.0 27.2 %collective-permute-start.25 = (bf16[128,1024]{1,0:T(8,128)(2,1)S(1)}, bf16[128,1024]{1,0:T(8,128)(2,1)S(1)}, u32[]{:S(2)}, u32[]{:S(2)}) collective-permute-start(bf16[128,1024]{1,0:T(8,128)(2,1)S(1)} %hide0.1.one), channel_id=1, source_target_pairs={{0,2},{1,3},{2,0},{3,1},{4,6},{5,7},{6,4},{7,5},{8,10},{9,11},{10,... | collective-permute-start | bytes 786440 | tf_op jit(solution)/shard_map/hide0/ppermute | solution.py:71
  58.9 10.4 %collective-permute-start.17 = (bf16[96,2048]{1,0:T(8,128)(2,1)S(1)}, bf16[96,2048]{1,0:T(8,128)(2,1)S(1)}, u32[]{:S(2)}, u32[]{:S(2)}) collective-permute-start(bf16[96,2048]{1,0:T(8,128)(2,1)S(1)} %pad_maximum_fusion.4), channel_id=1, source_target_pairs={{1,4},{3,6},{4,1},{6,3},{9,12},{11,14},{12,9},{14,11},{17,20},{19,... | collective-permute-start | bytes 1179656 | tf_op jit(solution)/shard_map/arr2/ppermute | solution.py:95
  61.6 18.8 %collective-permute-start.18 = (bf16[192,1024]{1,0:T(8,128)(2,1)S(1)}, bf16[192,1024]{1,0:T(8,128)(2,1)S(1)}, u32[]{:S(2)}, u32[]{:S(2)}) collective-permute-start(bf16[192,1024]{1,0:T(8,128)(2,1)S(1)} %get-tuple-element.139), channel_id=1, source_target_pairs={{0,2},{1,3},{2,0},{3,1},{4,6},{5,7},{6,4},{7,5},{8,10},{9,11},{10,... | collective-permute-start | bytes 1179656 | tf_op jit(solution)/shard_map/b1/ppermute | solution.py:71
  66.1 14.3 %collective-permute-start.20 = (bf16[192,1024]{1,0:T(8,128)(2,1)S(1)}, bf16[192,1024]{1,0:T(8,128)(2,1)S(1)}, u32[]{:S(2)}, u32[]{:S(2)}) collective-permute-start(bf16[192,1024]{1,0:T(8,128)(2,1)S(1)} %get-tuple-element.149), channel_id=1, source_target_pairs={{0,2},{1,3},{2,0},{3,1},{4,6},{5,7},{6,4},{7,5},{8,10},{9,11},{10,... | collective-permute-start | bytes 1179656 | tf_op jit(solution)/shard_map/b1/ppermute | solution.py:71
  71.7 11.1 %collective-permute-start.21 = (bf16[2,192,1024]{2,1,0:T(8,128)(2,1)S(1)}, bf16[2,192,1024]{2,1,0:T(8,128)(2,1)S(1)}, u32[]{:S(2)}, u32[]{:S(2)}) collective-permute-start(bf16[2,192,1024]{2,1,0:T(8,128)(2,1)S(1)} %a2.1), channel_id=1, source_target_pairs={{0,1},{1,0},{2,3},{3,2},{4,5},{5,4},{6,7},{7,6},{8,9},{9,8},{10,11... | collective-permute-start | bytes 2359304 | tf_op jit(solution)/shard_map/a2/ppermute | solution.py:71
  80.7 14.3 %collective-permute-start.27 = (bf16[192,1024]{1,0:T(8,128)(2,1)S(1)}, bf16[192,1024]{1,0:T(8,128)(2,1)S(1)}, u32[]{:S(2)}, u32[]{:S(2)}) collective-permute-start(bf16[192,1024]{1,0:T(8,128)(2,1)S(1)} %hide1.1.one), channel_id=1, source_target_pairs={{0,1},{1,0},{2,3},{3,2},{4,5},{5,4},{6,7},{7,6},{8,9},{9,8},{10,11... | collective-permute-start | bytes 1179656 | tf_op jit(solution)/shard_map/hide1/ppermute | solution.py:71
  81.0 14.0 %collective-permute-start.24 = (bf16[192,1024]{1,0:T(8,128)(2,1)S(1)}, bf16[192,1024]{1,0:T(8,128)(2,1)S(1)}, u32[]{:S(2)}, u32[]{:S(2)}) collective-permute-start(bf16[192,1024]{1,0:T(8,128)(2,1)S(1)} %hide1.1.one), channel_id=1, source_target_pairs={{0,2},{1,3},{2,0},{3,1},{4,6},{5,7},{6,4},{7,5},{8,10},{9,11},{10,... | collective-permute-start | bytes 1179656 | tf_op jit(solution)/shard_map/hide1/ppermute | solution.py:71
  82.2 8.9 %collective-permute-start.26 = (bf16[128,1024]{1,0:T(8,128)(2,1)S(1)}, bf16[128,1024]{1,0:T(8,128)(2,1)S(1)}, u32[]{:S(2)}, u32[]{:S(2)}) collective-permute-start(bf16[128,1024]{1,0:T(8,128)(2,1)S(1)} %collective-permute-done.25.one), channel_id=1, source_target_pairs={{0,1},{1,0},{2,3},{3,2},{4,5},{5,4},{6,7},{7,6},{8,9},{9,8},{10,11... | collective-permute-start | bytes 786440 | tf_op jit(solution)/shard_map/forward0/ppermute | solution.py:71
  84.8 23.5 %collective-permute-start.23 = (bf16[2,192,1024]{2,1,0:T(8,128)(2,1)S(1)}, bf16[2,192,1024]{2,1,0:T(8,128)(2,1)S(1)}, u32[]{:S(2)}, u32[]{:S(2)}) collective-permute-start(bf16[2,192,1024]{2,1,0:T(8,128)(2,1)S(1)} %b2.1), channel_id=1, source_target_pairs={{0,2},{1,3},{2,0},{3,1},{4,6},{5,7},{6,4},{7,5},{8,10},{9,11},{10,... | collective-permute-start | bytes 2359304 | tf_op jit(solution)/shard_map/b2/ppermute | solution.py:71
  93.3 16.4 %collective-permute-start.31 = (bf16[64,2048]{1,0:T(8,128)(2,1)S(1)}, bf16[64,2048]{1,0:T(8,128)(2,1)S(1)}, u32[]{:S(2)}, u32[]{:S(2)}) collective-permute-start(bf16[64,2048]{1,0:T(8,128)(2,1)S(1)} %get-tuple-element.157), channel_id=1, source_target_pairs={{0,1},{1,5},{2,3},{3,7},{4,0},{5,4},{6,2},{7,6},{8,9},{9,13},{10,1... | collective-permute-start | bytes 786440 | tf_op jit(solution)/shard_map/out0/ppermute | solution.py:95
  97.0 14.0 %collective-permute-start.32 = (bf16[64,2048]{1,0:T(8,128)(2,1)S(1)}, bf16[64,2048]{1,0:T(8,128)(2,1)S(1)}, u32[]{:S(2)}, u32[]{:S(2)}) collective-permute-start(bf16[64,2048]{1,0:T(8,128)(2,1)S(1)} %get-tuple-element.166), channel_id=1, source_target_pairs={{1,4},{3,6},{4,1},{6,3},{9,12},{11,14},{12,9},{14,11},{17,20},{19,... | collective-permute-start | bytes 786440 | tf_op jit(solution)/shard_map/out0/ppermute | solution.py:95
  102.5 9.5 %collective-permute-start.30 = (bf16[96,2048]{1,0:T(8,128)(2,1)S(1)}, bf16[96,2048]{1,0:T(8,128)(2,1)S(1)}, u32[]{:S(2)}, u32[]{:S(2)}) collective-permute-start(bf16[96,2048]{1,0:T(8,128)(2,1)S(1)} %get-tuple-element.161), channel_id=1, source_target_pairs={{0,1},{1,5},{2,3},{3,7},{4,0},{5,4},{6,2},{7,6},{8,9},{9,13},{10,1... | collective-permute-start | bytes 1179656 | tf_op jit(solution)/shard_map/out1/ppermute | solution.py:95
  102.6 10.9 %collective-permute-start.33 = (bf16[96,2048]{1,0:T(8,128)(2,1)S(1)}, bf16[96,2048]{1,0:T(8,128)(2,1)S(1)}, u32[]{:S(2)}, u32[]{:S(2)}) collective-permute-start(bf16[96,2048]{1,0:T(8,128)(2,1)S(1)} %get-tuple-element.169), channel_id=1, source_target_pairs={{1,4},{3,6},{4,1},{6,3},{9,12},{11,14},{12,9},{14,11},{17,20},{19,... | collective-permute-start | bytes 1179656 | tf_op jit(solution)/shard_map/out1/ppermute | solution.py:95
  108.5 13.2 %collective-permute-start.34 = (bf16[192,1024]{1,0:T(8,128)(2,1)S(1)}, bf16[192,1024]{1,0:T(8,128)(2,1)S(1)}, u32[]{:S(2)}, u32[]{:S(2)}) collective-permute-start(bf16[192,1024]{1,0:T(8,128)(2,1)S(1)} %hide2.1.one), channel_id=1, source_target_pairs={{0,1},{1,0},{2,3},{3,2},{4,5},{5,4},{6,7},{7,6},{8,9},{9,8},{10,11... | collective-permute-start | bytes 1179656 | tf_op jit(solution)/shard_map/hide2/ppermute | solution.py:71
  109.7 10.7 %collective-permute-start.29 = (bf16[192,1024]{1,0:T(8,128)(2,1)S(1)}, bf16[192,1024]{1,0:T(8,128)(2,1)S(1)}, u32[]{:S(2)}, u32[]{:S(2)}) collective-permute-start(bf16[192,1024]{1,0:T(8,128)(2,1)S(1)} %hide2.1.one), channel_id=1, source_target_pairs={{0,2},{1,3},{2,0},{3,1},{4,6},{5,7},{6,4},{7,5},{8,10},{9,11},{10,... | collective-permute-start | bytes 1179656 | tf_op jit(solution)/shard_map/hide2/ppermute | solution.py:71
  111.7 19.0 %collective-permute-start.37 = (bf16[32,2048]{1,0:T(8,128)(2,1)S(1)}, bf16[32,2048]{1,0:T(8,128)(2,1)S(1)}, u32[]{:S(2)}, u32[]{:S(2)}) collective-permute-start(bf16[32,2048]{1,0:T(8,128)(2,1)S(1)} %get-tuple-element.167), channel_id=1, source_target_pairs={{0,2},{1,3},{2,0},{3,1},{4,6},{5,7},{6,4},{7,5},{8,10},{9,11},{10,... | collective-permute-start | bytes 393224 | tf_op jit(solution)/shard_map/mix0/ppermute | solution.py:71
  114.2 14.2 %collective-permute-start.38 = (bf16[48,2048]{1,0:T(8,128)(2,1)S(1)}, bf16[48,2048]{1,0:T(8,128)(2,1)S(1)}, u32[]{:S(2)}, u32[]{:S(2)}) collective-permute-start(bf16[48,2048]{1,0:T(8,128)(2,1)S(1)} %get-tuple-element.170), channel_id=1, source_target_pairs={{0,2},{1,3},{2,0},{3,1},{4,6},{5,7},{6,4},{7,5},{8,10},{9,11},{10,... | collective-permute-start | bytes 589832 | tf_op jit(solution)/shard_map/mix1/ppermute | solution.py:71
  126.5 9.5 %collective-permute-start.36 = (bf16[96,2048]{1,0:T(8,128)(2,1)S(1)}, bf16[96,2048]{1,0:T(8,128)(2,1)S(1)}, u32[]{:S(2)}, u32[]{:S(2)}) collective-permute-start(bf16[96,2048]{1,0:T(8,128)(2,1)S(1)} %get-tuple-element.175), channel_id=1, source_target_pairs={{0,1},{1,5},{2,3},{3,7},{4,0},{5,4},{6,2},{7,6},{8,9},{9,13},{10,1... | collective-permute-start | bytes 1179656 | tf_op jit(solution)/shard_map/out2/ppermute | solution.py:95
  129.1 17.9 %collective-permute-start.41 = (bf16[48,2048]{1,0:T(8,128)(2,1)S(1)}, bf16[48,2048]{1,0:T(8,128)(2,1)S(1)}, u32[]{:S(2)}, u32[]{:S(2)}) collective-permute-start(bf16[48,2048]{1,0:T(8,128)(2,1)S(1)} %get-tuple-element.179), channel_id=1, source_target_pairs={{0,8},{4,12},{8,0},{12,4},{1,9},{5,13},{9,1},{13,5},{2,10},{6,14},... | collective-permute-start | bytes 589832 | tf_op jit(solution)/shard_map/far_out1/ppermute | solution.py:75
  130.7 12.3 %collective-permute-start.39 = (bf16[96,2048]{1,0:T(8,128)(2,1)S(1)}, bf16[96,2048]{1,0:T(8,128)(2,1)S(1)}, u32[]{:S(2)}, u32[]{:S(2)}) collective-permute-start(bf16[96,2048]{1,0:T(8,128)(2,1)S(1)} %get-tuple-element.183), channel_id=1, source_target_pairs={{1,4},{3,6},{4,1},{6,3},{9,12},{11,14},{12,9},{14,11},{17,20},{19,... | collective-permute-start | bytes 1179656 | tf_op jit(solution)/shard_map/out2/ppermute | solution.py:95
  135.1 16.9 %collective-permute-start.43 = (bf16[32,2048]{1,0:T(8,128)(2,1)S(1)}, bf16[32,2048]{1,0:T(8,128)(2,1)S(1)}, u32[]{:S(2)}, u32[]{:S(2)}) collective-permute-start(bf16[32,2048]{1,0:T(8,128)(2,1)S(1)} %get-tuple-element.181), channel_id=1, source_target_pairs={{0,8},{4,12},{8,0},{12,4},{1,9},{5,13},{9,1},{13,5},{2,10},{6,14},... | collective-permute-start | bytes 393224 | tf_op jit(solution)/shard_map/far_out0/ppermute | solution.py:75
  (14 other events, 69.5 us)
